TPU v7x, 32 devices: a whole 2x2x4 slice. The times are simulated.
32 devices in a mesh: fsdp: 16 (over z, y, core), seq: 2 (over x).
Axes of the slice: x: 2, y: 2, z: 4, core: 2. Of those that a mesh axis runs over, the one named last changes fastest.
Arguments:
- layer_input: bfloat16 [16, 1024, 768], P('fsdp', 'seq'), may hold values from -6 to 6
- query_weight: bfloat16 [768, 768], P('fsdp'), may hold values from -0.109375 to 0.109375
- key_weight: bfloat16 [768, 768], P('fsdp'), may hold values from -0.109375 to 0.109375
- value_weight: bfloat16 [768, 768], P('fsdp'), may hold values from -0.21875 to 0.21875
- output_weight: bfloat16 [768, 768], P('fsdp'), may hold values from -1.75 to 1.75
- expand_weight: bfloat16 [768, 3072], P('fsdp'), may hold values from -0.21875 to 0.21875
- contract_weight: bfloat16 [3072, 768], P('fsdp'), may hold values from -0.109375 to 0.109375
- attention_gain: bfloat16 [768], P('fsdp'), may hold values from 0.5 to 1.5
- feedforward_gain: bfloat16 [768], P('fsdp'), may hold values from 0.5 to 1.5
- bias_table: bfloat16 [32, 12], P('fsdp'), may hold values from -4 to 4
- valid_len: int32 [16], P('fsdp'), may hold values from 257 to 1024, as said below
- instr_len: int32 [16], P('fsdp'), may hold values from 1 to 256
- pair_flag: int32 [16], P('fsdp'), may hold values from 0 to 1
- cotangent: bfloat16 [16, 1024, 768], P('fsdp', 'seq'), may hold values from -6 to 6
Outputs:
- layer_output: bfloat16 [16, 1024, 768], P('fsdp', 'seq')
- input_grad: bfloat16 [16, 1024, 768], P('fsdp', 'seq')
- attention_gain_grad: float32 [768], P('fsdp')
- feedforward_gain_grad: float32 [768], P('fsdp')
- query_grad: float32 [768, 768], P('fsdp')
- key_grad: float32 [768, 768], P('fsdp')
- value_grad: float32 [768, 768], P('fsdp')
- output_grad: float32 [768, 768], P('fsdp')
- expand_grad: float32 [768, 3072], P('fsdp')
- contract_grad: float32 [3072, 768], P('fsdp')
- bias_grad: float32 [32, 12], P('fsdp')
Inputs may be any that keep to these rules, and one draw needn't show every extreme that they name: `valid_len`: in every aligned block of 1 row (the rows of one fsdp index) at least one row has more than 512 tokens; at least one row of all has all 1024 tokens; every row has more than 256 tokens.
All inputs are finite; a program needn't handle non-finite values.
Results may differ from a plain program's by a relative error of at most 0.02.
Values may be sent and summed in bfloat16 or wider, within the bound.
No kernel may reach another device: no remote copies, remote signals or barrier semaphores. Data moves between devices by JAX's collectives and lax.ppermute only.
A program may use at most 256 MiB of HBM per device.

v0:
```python
import jax
import jax.numpy as jnp
from jax import lax
from jax.sharding import PartitionSpec as P

BUCKETS = 32


EPS = 1e-06
far_edges = (12, 16, 23, 32, 46, 64, 91)


def bucket_table(query_pos, key_pos):
    offset = key_pos[None, :] - query_pos[:, None]
    distance = jnp.abs(offset)
    beyond = jnp.zeros_like(distance)
    for far_edge in far_edges:
        beyond = beyond + (distance >= far_edge).astype(jnp.int32)
    nearby = jnp.where(distance < 8, distance, 8 + beyond)
    return nearby + 16 * (offset > 0).astype(jnp.int32)


def visible_keys(query_pos, key_pos, valid_len, instr_len, pair_flag):
    in_valid = key_pos[None, None, :] < valid_len[:, None, None]
    guarded = (
        (pair_flag[:, None, None] == 1)
        & (query_pos[None, :, None] < instr_len[:, None, None])
        & (key_pos[None, None, :] >= instr_len[:, None, None])
    )
    return in_valid & jnp.logical_not(guarded)


def rms_scale(values):
    return lax.rsqrt(jnp.mean(values * values, axis=-1, keepdims=True) + EPS)


def norm_back(values, scale, gain, grad_out):
    normed = values * scale
    grad_normed = grad_out * gain
    grad_values = scale * (
        grad_normed - normed * jnp.mean(grad_normed * normed, axis=-1, keepdims=True)
    )
    return (grad_values, jnp.sum(grad_out * normed, axis=(0, 1)))


def gelu_tanh(values):
    return jax.nn.gelu(values, approximate=True)


def local(
    layer_input,
    query_weight,
    key_weight,
    value_weight,
    output_weight,
    expand_weight,
    contract_weight,
    attention_gain,
    feedforward_gain,
    bias_table,
    valid_len,
    instr_len,
    pair_flag,
    cotangent,
):
    f32 = jnp.float32
    bf16 = jnp.bfloat16
    row_count, local_len, model_width = layer_input.shape
    head_count = bias_table.shape[1]
    head_size = model_width // head_count
    full_len = local_len * lax.axis_size("seq")
    local_start = lax.axis_index("seq") * local_len
    query_pos = local_start + jnp.arange(local_len, dtype=jnp.int32)
    key_pos = jnp.arange(full_len, dtype=jnp.int32)
    buckets = bucket_table(query_pos, key_pos)
    onehot = buckets[:, :, None] == jnp.arange(BUCKETS, dtype=jnp.int32)[None, None, :]
    visible = visible_keys(query_pos, key_pos, valid_len, instr_len, pair_flag)
    input_wide = layer_input.astype(f32)

    def attend_probs(queries, key_heads, table_full):
        rel_bias = jnp.einsum(
            "ijb,bh->hij", onehot.astype(bf16), table_full, preferred_element_type=f32
        )
        raw_scores = jnp.einsum("rihe,rjhe->rhij", queries, key_heads, preferred_element_type=f32)
        scores = jnp.where(visible[:, None], raw_scores + rel_bias[None], -1000000000.0)
        row_peak = jnp.max(scores, axis=-1, keepdims=True)
        log_total = row_peak + jnp.log(jnp.sum(jnp.exp(scores - row_peak), axis=-1, keepdims=True))
        return (jnp.exp(scores - log_total), log_total[..., 0])

    def forward(weights):
        (
            query_full,
            key_full,
            value_full,
            output_full,
            expand_full,
            contract_full,
            gain_one,
            gain_two,
            table_full,
        ) = weights
        scale_one = rms_scale(input_wide)
        normed_low = (input_wide * scale_one * gain_one.astype(f32)).astype(bf16)

        def project(weight):
            return jnp.einsum("rtd,de->rte", normed_low, weight, preferred_element_type=f32).astype(
                bf16
            )

        query_low = project(query_full)
        key_low = project(key_full)
        value_low = project(value_full)
        key_all, value_all = (
            lax.all_gather(key_low, "seq", axis=1, tiled=True),
            lax.all_gather(value_low, "seq", axis=1, tiled=True),
        )
        queries = query_low.reshape(row_count, local_len, head_count, head_size)
        key_heads = key_all.reshape(row_count, full_len, head_count, head_size)
        value_heads = value_all.reshape(row_count, full_len, head_count, head_size)
        probs, log_total = attend_probs(queries, key_heads, table_full)
        probs_low = probs.astype(bf16)
        attended = jnp.einsum("rhij,rjhe->rihe", probs_low, value_heads, preferred_element_type=f32)
        attended = attended.reshape(row_count, local_len, model_width).astype(bf16)
        middle = input_wide + jnp.einsum(
            "rtd,de->rte", attended, output_full, preferred_element_type=f32
        )
        scale_two = rms_scale(middle)
        normed_two = (middle * scale_two * gain_two.astype(f32)).astype(bf16)
        hidden_pre = jnp.einsum("rtd,df->rtf", normed_two, expand_full, preferred_element_type=f32)
        hidden_low = gelu_tanh(hidden_pre).astype(bf16)
        result = middle + jnp.einsum(
            "rtf,fd->rtd", hidden_low, contract_full, preferred_element_type=f32
        )
        return (
            result,
            scale_one,
            normed_low,
            queries,
            key_heads,
            value_heads,
            probs,
            probs_low,
            log_total,
            attended,
            middle,
            scale_two,
            normed_two,
            hidden_pre,
            hidden_low,
        )

    stored = forward(
        (
            lax.all_gather(query_weight, "fsdp", axis=0, tiled=True),
            lax.all_gather(key_weight, "fsdp", axis=0, tiled=True),
            lax.all_gather(value_weight, "fsdp", axis=0, tiled=True),
            lax.all_gather(output_weight, "fsdp", axis=0, tiled=True),
            lax.all_gather(expand_weight, "fsdp", axis=0, tiled=True),
            lax.all_gather(contract_weight, "fsdp", axis=0, tiled=True),
            lax.all_gather(attention_gain, "fsdp", axis=0, tiled=True),
            lax.all_gather(feedforward_gain, "fsdp", axis=0, tiled=True),
            lax.all_gather(bias_table, "fsdp", axis=0, tiled=True),
        )
    )
    layer_output = stored[0].astype(bf16)
    gathered = (
        lax.all_gather(query_weight, "fsdp", axis=0, tiled=True),
        lax.all_gather(key_weight, "fsdp", axis=0, tiled=True),
        lax.all_gather(value_weight, "fsdp", axis=0, tiled=True),
        lax.all_gather(output_weight, "fsdp", axis=0, tiled=True),
        lax.all_gather(expand_weight, "fsdp", axis=0, tiled=True),
        lax.all_gather(contract_weight, "fsdp", axis=0, tiled=True),
        lax.all_gather(attention_gain, "fsdp", axis=0, tiled=True),
        lax.all_gather(feedforward_gain, "fsdp", axis=0, tiled=True),
        lax.all_gather(bias_table, "fsdp", axis=0, tiled=True),
    )
    kept = forward(gathered)
    (
        unused,
        scale_one,
        normed_low,
        queries,
        key_heads,
        value_heads,
        probs,
        probs_low,
        log_total,
        attended,
        middle,
        scale_two,
        normed_two,
        hidden_pre,
        hidden_low,
    ) = kept
    (
        query_full,
        key_full,
        value_full,
        output_full,
        expand_full,
        contract_full,
        gain_one,
        gain_two,
        table_full,
    ) = gathered
    gain_one_wide = gain_one.astype(f32)
    gain_two_wide = gain_two.astype(f32)
    contract_grad = jnp.einsum("rtf,rtd->fd", hidden_low, cotangent, preferred_element_type=f32)
    grad_hidden = jnp.einsum("rtd,fd->rtf", cotangent, contract_full, preferred_element_type=f32)
    gelu_pull = jax.vjp(gelu_tanh, hidden_pre)[1]
    grad_pre = gelu_pull(grad_hidden)[0].astype(bf16)
    expand_grad = jnp.einsum("rtd,rtf->df", normed_two, grad_pre, preferred_element_type=f32)
    grad_normed_two = jnp.einsum("rtf,df->rtd", grad_pre, expand_full, preferred_element_type=f32)
    grad_middle_norm, gain_two_grad = norm_back(middle, scale_two, gain_two_wide, grad_normed_two)
    grad_middle = cotangent.astype(f32) + grad_middle_norm
    grad_branch = grad_middle.astype(bf16)
    output_grad = jnp.einsum("rtd,rte->de", attended, grad_branch, preferred_element_type=f32)
    grad_attended = jnp.einsum(
        "rte,de->rtd", grad_branch, output_full, preferred_element_type=f32
    ).astype(bf16)
    grad_attended = grad_attended.reshape(row_count, local_len, head_count, head_size)
    grad_probs = jnp.einsum(
        "rihe,rjhe->rhij", grad_attended, value_heads, preferred_element_type=f32
    )
    row_delta = jnp.sum(probs * grad_probs, axis=-1)
    grad_scores = probs * (grad_probs - row_delta[..., None])
    bias_part = jnp.einsum(
        "hij,ijb->bh",
        jnp.sum(grad_scores, axis=0),
        onehot.astype(f32),
        precision=lax.Precision.HIGHEST,
    )
    scores_low = grad_scores.astype(bf16)
    grad_queries = jnp.einsum("rhij,rjhe->rihe", scores_low, key_heads, preferred_element_type=f32)
    grad_queries = grad_queries.reshape(row_count, local_len, model_width).astype(bf16)
    value_partial = jnp.einsum(
        "rhij,rihe->rjhe", probs_low, grad_attended, preferred_element_type=f32
    ).reshape(row_count, full_len, model_width)
    key_partial = jnp.einsum(
        "rhij,rihe->rjhe", scores_low, queries, preferred_element_type=f32
    ).reshape(row_count, full_len, model_width)
    key_summed, value_summed = (
        lax.psum_scatter(
            key_partial.astype(jnp.bfloat16), "seq", scatter_dimension=1, tiled=True
        ).astype(jnp.float32),
        lax.psum_scatter(
            value_partial.astype(jnp.bfloat16), "seq", scatter_dimension=1, tiled=True
        ).astype(jnp.float32),
    )
    grad_keys = key_summed.astype(bf16)
    grad_values = value_summed.astype(bf16)
    query_part = jnp.einsum("rtd,rte->de", normed_low, grad_queries, preferred_element_type=f32)
    key_part = jnp.einsum("rtd,rte->de", normed_low, grad_keys, preferred_element_type=f32)
    value_part = jnp.einsum("rtd,rte->de", normed_low, grad_values, preferred_element_type=f32)
    grad_normed_one = jnp.einsum(
        "rte,de->rtd", grad_queries, query_full, preferred_element_type=f32
    )
    grad_normed_one = grad_normed_one + jnp.einsum(
        "rte,de->rtd", grad_keys, key_full, preferred_element_type=f32
    )
    grad_normed_one = grad_normed_one + jnp.einsum(
        "rte,de->rtd", grad_values, value_full, preferred_element_type=f32
    )
    grad_input_norm, gain_one_grad = norm_back(
        input_wide, scale_one, gain_one_wide, grad_normed_one
    )
    input_grad = (grad_middle + grad_input_norm).astype(bf16)
    owned = (
        lax.psum_scatter(
            query_part.astype(jnp.bfloat16), "fsdp", scatter_dimension=0, tiled=True
        ).astype(jnp.float32),
        lax.psum_scatter(
            key_part.astype(jnp.bfloat16), "fsdp", scatter_dimension=0, tiled=True
        ).astype(jnp.float32),
        lax.psum_scatter(
            value_part.astype(jnp.bfloat16), "fsdp", scatter_dimension=0, tiled=True
        ).astype(jnp.float32),
        lax.psum_scatter(
            output_grad.astype(jnp.bfloat16), "fsdp", scatter_dimension=0, tiled=True
        ).astype(jnp.float32),
        lax.psum_scatter(
            expand_grad.astype(jnp.bfloat16), "fsdp", scatter_dimension=0, tiled=True
        ).astype(jnp.float32),
        lax.psum_scatter(
            contract_grad.astype(jnp.bfloat16), "fsdp", scatter_dimension=0, tiled=True
        ).astype(jnp.float32),
        lax.psum_scatter(
            gain_one_grad.astype(jnp.bfloat16), "fsdp", scatter_dimension=0, tiled=True
        ).astype(jnp.float32),
        lax.psum_scatter(
            gain_two_grad.astype(jnp.bfloat16), "fsdp", scatter_dimension=0, tiled=True
        ).astype(jnp.float32),
        lax.psum_scatter(
            bias_part.astype(jnp.bfloat16), "fsdp", scatter_dimension=0, tiled=True
        ).astype(jnp.float32),
    )
    summed = (
        lax.psum(owned[0].astype(jnp.bfloat16), "seq").astype(jnp.float32),
        lax.psum(owned[1].astype(jnp.bfloat16), "seq").astype(jnp.float32),
        lax.psum(owned[2].astype(jnp.bfloat16), "seq").astype(jnp.float32),
        lax.psum(owned[3].astype(jnp.bfloat16), "seq").astype(jnp.float32),
        lax.psum(owned[4].astype(jnp.bfloat16), "seq").astype(jnp.float32),
        lax.psum(owned[5].astype(jnp.bfloat16), "seq").astype(jnp.float32),
        lax.psum(owned[6].astype(jnp.bfloat16), "seq").astype(jnp.float32),
        lax.psum(owned[7].astype(jnp.bfloat16), "seq").astype(jnp.float32),
        lax.psum(owned[8].astype(jnp.bfloat16), "seq").astype(jnp.float32),
    )
    (
        query_grad,
        key_grad,
        value_grad,
        output_sum,
        expand_sum,
        contract_sum,
        gain_one_sum,
        gain_two_sum,
        bias_grad,
    ) = summed
    return (
        layer_output,
        input_grad,
        gain_one_sum,
        gain_two_sum,
        query_grad,
        key_grad,
        value_grad,
        output_sum,
        expand_sum,
        contract_sum,
        bias_grad,
    )


def solution(mesh):
    in_specs = (
        P("fsdp", "seq", None),
        P("fsdp", None),
        P("fsdp", None),
        P("fsdp", None),
        P("fsdp", None),
        P("fsdp", None),
        P("fsdp", None),
        P("fsdp"),
        P("fsdp"),
        P("fsdp", None),
        P("fsdp"),
        P("fsdp"),
        P("fsdp"),
        P("fsdp", "seq", None),
    )
    out_specs = (
        P("fsdp", "seq", None),
        P("fsdp", "seq", None),
        P("fsdp"),
        P("fsdp"),
        P("fsdp", None),
        P("fsdp", None),
        P("fsdp", None),
        P("fsdp", None),
        P("fsdp", None),
        P("fsdp", None),
        P("fsdp", None),
    )
    return jax.shard_map(local, mesh=mesh, in_specs=in_specs, out_specs=out_specs, check_vma=False)
```

profile of v0, /device:TPU:0, one launch (start us, length us, event | category | flops | bytes accessed | tf_op | source)
XLA Modules:
  0.0 935.6 jit_solution(2660350554029112692)
XLA Ops:
  8.0 0.7 all-gather.12.cloned.1.call-update
  9.5 1.3 fusion.92
  11.4 0.8 dynamic-update-slice
  12.3 0.8 dynamic-update-slice.1
  13.1 35.2 %all-reduce.6 = (bf16[768]{0:T(1024)(128)(2,1)S(1)}, bf16[768]{0:T(1024)(128)(2,1)S(1)}) all-reduce(bf16[768]{0:T(1024)(128)(2,1)S(1)} %dynamic-update-slice, bf16[768]{0:T(1024)(128)(2,1)S(1)} %dynamic-update-slice.1), channel_id=1, replica_groups=mesh['fsdp'=16,'seq'=2] {'fsdp'}, use_global_device_ids=true, to_apply=%add | all-reduce | flops 1536 | bytes 6144
  48.3 1.4 fusion.49
  49.7 1.8 all-gather.16.cloned.1.call-done
  51.5 3.2 convolution_convert_fusion.7
  54.8 36.2 %all-gather.12.cloned.1.call-done = bf16[768,768]{1,0:T(8,128)(2,1)} async-done(((bf16[48,768]{1,0:T(8,128)(2,1)}), bf16[768,768]{1,0:T(8,128)(2,1)}) %all-gather.12.cloned.1.call-update) | async-done | bytes 1179664 | tf_op jit(solution)/shard_map/all_gather | solution.py:156
  91.0 3.0 convolution_convert_fusion.9
  94.7 0.7 all-gather.20.cloned.1.call-update
  95.4 0.7 all-gather.22.cloned.1.call-update
  98.1 19.3 %all-gather.2 = bf16[16,2,12]{2,1,0:T(2,128)(2,1)S(1)} all-gather(bf16[1,2,12]{2,1,0:T(2,128)(2,1)S(1)} %bitcast.146), channel_id=1, replica_groups=mesh['fsdp'=16,'seq'=2] {'fsdp'}, dimensions={0}, use_global_device_ids=true | all-gather | bytes 816 | tf_op jit(solution)/shard_map/all_gather | solution.py:162
  117.9 2.1 fusion.26
  120.1 1.4 copy-done.3
  121.4 16.4 %fusion.1 = f32[512,1024,12]{1,2,0:T(8,128)} fusion(bf16[32,12,1]{1,0,2:T(8,128)(2,1)S(1)} %bitcast.145, s32[512,1024]{1,0:T(8,128)S(1)} %fusion.26), kind=kOutput, calls=%fused_computation.2 | convolution fusion | flops 419430400 | bytes 27263744 | tf_op jit(solution)/shard_map/ijb,bh->hij/dot_general | solution.py:81
  137.9 2.2 convolution_convert_fusion.8
  140.4 18.5 %all-gather.26.cloned.1.call-done = bf16[1024,768]{1,0:T(8,128)(2,1)} async-done(((bf16[512,768]{1,0:T(8,128)(2,1)}), bf16[1024,768]{1,0:T(8,128)(2,1)}) %all-gather.26.cloned.1.call-update) | async-done | bytes 1572880 | tf_op jit(solution)/shard_map/all_gather | solution.py:114
  158.9 2.7 copy.45
  161.5 26.5 %all-gather.24.cloned.1.call-done = bf16[1024,768]{1,0:T(8,128)(2,1)} async-done(((bf16[512,768]{1,0:T(8,128)(2,1)}), bf16[1024,768]{1,0:T(8,128)(2,1)}) %all-gather.24.cloned.1.call-update) | async-done | bytes 1572880 | tf_op jit(solution)/shard_map/all_gather | solution.py:115
  188.1 1.7 copy.43
  189.8 29.0 %fusion.93 = (f32[12,512]{1,0:T(8,128)S(1)}, f32[12,512,1024]{2,1,0:T(8,128)}) fusion(f32[512,1024,12]{1,2,0:T(8,128)} %fusion.1, bf16[512,12,64]{0,2,1:T(8,128)(2,1)S(1)} %bitcast.135, bf16[1024,12,64]{0,2,1:T(8,128)(2,1)} %bitcast.133, pred[512,1024]{1,0:T(8,128)(4,1)S(1)} %not_and_fusion), kind=kOutput, calls=%fused_computation.111 | convolution fusion | flops 824174592 | bytes 53239808 | tf_op jit(solution)/shard_map/rihe,rjhe->rhij/dot_general | solution.py:84
  218.8 11.4 %exponential_reduce_fusion = f32[12,512]{1,0:T(8,128)S(1)} fusion(f32[12,512,1024]{2,1,0:T(8,128)} %get-tuple-element.32, f32[12,512]{1,0:T(8,128)S(1)} %get-tuple-element.31), kind=kLoop, calls=%fused_computation.11 | loop fusion | flops 12576768 | bytes 25214976 | tf_op jit(solution)/shard_map/reduce_sum | solution.py:87
  230.2 11.4 %fusion.55 = bf16[12,64,512]{2,1,0:T(8,128)(2,1)} fusion(bf16[1024,12,64]{0,2,1:T(8,128)(2,1)S(1)} %bitcast.131, f32[12,512,1024]{2,1,0:T(8,128)} %get-tuple-element.32, f32[12,512]{1,0:T(8,128)S(1)} %log_add_fusion), kind=kOutput, calls=%fused_computation.81 | convolution fusion | flops 818282496 | bytes 27549696 | tf_op jit(solution)/shard_map/rhij,rjhe->rihe/dot_general | solution.py:122
  241.5 3.7 multiply_reduce_fusion.1
  245.2 38.0 %all-gather.20.cloned.1.call-done = bf16[768,3072]{1,0:T(8,128)(2,1)} async-done(((bf16[48,3072]{1,0:T(8,128)(2,1)}), bf16[768,3072]{1,0:T(8,128)(2,1)}) %all-gather.20.cloned.1.call-update) | async-done | bytes 4718608 | tf_op jit(solution)/shard_map/all_gather | solution.py:158
  283.3 8.2 fusion.84
  291.4 46.1 %all-gather.22.cloned.1.call-done = bf16[3072,768]{1,0:T(8,128)(2,1)} async-done(((bf16[192,768]{1,0:T(8,128)(2,1)}), bf16[3072,768]{1,0:T(8,128)(2,1)}) %all-gather.22.cloned.1.call-update) | async-done | bytes 4718608 | tf_op jit(solution)/shard_map/all_gather | solution.py:159
  337.5 8.7 fusion.13
  346.3 3.3 fusion.50
  350.2 1.1 copy-done
  351.3 1.7 convolution_convert_fusion.6
  353.0 2.3 copy.48
  355.3 12.0 %fusion.36 = bf16[12,64,1024]{2,1,0:T(8,128)(2,1)} fusion(bf16[512,12,64]{0,2,1:T(8,128)(2,1)} %bitcast.137, f32[12,512,1024]{2,1,0:T(8,128)} %get-tuple-element.32, f32[12,512]{1,0:T(8,128)S(1)} %log_add_fusion), kind=kOutput, calls=%fused_computation.51 | convolution fusion | flops 818675712 | bytes 27549696 | tf_op jit(solution)/shard_map/rhij,rihe->rjhe/dot_general | solution.py:236
  367.3 15.8 %multiply_reduce_fusion = (f32[12,512]{1,0:T(8,128)S(1)}, f32[12,512,1024]{2,1,0:T(8,128)}) fusion(f32[12,512,1024]{2,1,0:T(8,128)} %get-tuple-element.32, f32[12,512]{1,0:T(8,128)S(1)} %log_add_fusion, bf16[512,12,64]{0,2,1:T(8,128)(2,1)} %bitcast.138, bf16[1024,12,64]{0,2,1:T(8,128)(2,1)S(1)} %bitcast.132), kind=kOutput, calls=%fused_computation.9 | convolution fusion | flops 824174592 | bytes 52740096 | tf_op jit(solution)/shard_map/rihe,rjhe->rhij/dot_general | solution.py:222
  383.2 26.5 %subtract_multiply_fusion = f32[12,512,1024]{2,1,0:T(8,128)} fusion(f32[12,512,1024]{2,1,0:T(8,128)} %get-tuple-element.37, f32[12,512,1024]{2,1,0:T(8,128)} %get-tuple-element.32, f32[12,512]{1,0:T(8,128)S(1)} %get-tuple-element.36, f32[12,512]{1,0:T(8,128)S(1)} %log_add_fusion), kind=kLoop, calls=%fused_computation.8 | loop fusion | flops 18874368 | bytes 75546624 | tf_op jit(solution)/shard_map/mul | solution.py:226
  409.7 11.7 %fusion.39 = bf16[12,64,1024]{2,1,0:T(8,128)(2,1)} fusion(bf16[512,12,64]{0,2,1:T(8,128)(2,1)S(1)} %bitcast.136, f32[12,512,1024]{2,1,0:T(8,128)} %subtract_multiply_fusion), kind=kOutput, calls=%fused_computation.52 | convolution fusion | flops 812384256 | bytes 27525120 | tf_op jit(solution)/shard_map/rhij,rihe->rjhe/dot_general | solution.py:239
  421.5 3.0 convolution_convert_fusion.2
  424.6 13.5 %fusion.58 = bf16[12,64,512]{2,1,0:T(8,128)(2,1)} fusion(bf16[1024,12,64]{0,2,1:T(8,128)(2,1)S(1)} %bitcast.134, f32[12,512,1024]{2,1,0:T(8,128)} %subtract_multiply_fusion), kind=kOutput, calls=%fused_computation.82 | convolution fusion | flops 811991040 | bytes 27525120 | tf_op jit(solution)/shard_map/rhij,rjhe->rihe/dot_general | solution.py:234
  438.1 3.5 convolution_convert_fusion.5
  441.9 3.2 convolution_convert_fusion.3
  445.2 0.9 reduce-scatter.9.cloned.1.call-done
  446.1 3.1 convolution_convert_fusion.4
  449.3 8.2 convolution_convert_fusion
  457.6 7.3 convolution_convert_fusion.1
  466.6 3.4 fusion.94
  470.0 8.9 fusion.54
  478.9 47.0 %fusion.64 = bf16[32,12]{1,0:T(8,128)(2,1)} fusion(f32[12,512,1024]{2,1,0:T(8,128)} %subtract_multiply_fusion, s32[512,1024]{1,0:T(8,128)S(1)} %copy-done.4), kind=kOutput, calls=%fused_computation.84 | convolution fusion | flops 2432696832 | bytes 27263744 | tf_op jit(solution)/shard_map/hij,ijb->bh/dot_general | solution.py:227
  526.0 2.0 fusion.72
  528.0 40.5 %reduce-scatter.13.cloned.1.call-done = bf16[48,768]{1,0:T(8,128)(2,1)} async-done(((bf16[768,768]{1,0:T(8,128)(2,1)}), bf16[48,768]{1,0:T(8,128)(2,1)}) %reduce-scatter.13.cloned.1.call-update) | async-done | bytes 73744 | tf_op jit(solution)/shard_map/reduce_scatter | solution.py:269
  568.5 60.7 %reduce-scatter.17.cloned.1.call-done = bf16[48,768]{1,0:T(8,128)(2,1)} async-done(((bf16[768,768]{1,0:T(8,128)(2,1)}), bf16[48,768]{1,0:T(8,128)(2,1)}) %reduce-scatter.17.cloned.1.call-update) | async-done | bytes 73744 | tf_op jit(solution)/shard_map/reduce_scatter | solution.py:275
  629.2 60.6 %reduce-scatter.15.cloned.1.call-done = bf16[48,768]{1,0:T(8,128)(2,1)} async-done(((bf16[768,768]{1,0:T(8,128)(2,1)}), bf16[48,768]{1,0:T(8,128)(2,1)}) %reduce-scatter.15.cloned.1.call-update) | async-done | bytes 73744 | tf_op jit(solution)/shard_map/reduce_scatter | solution.py:272
  689.7 78.3 %reduce-scatter.23.cloned.1.call-done = bf16[192,768]{1,0:T(8,128)(2,1)} async-done(((bf16[3072,768]{1,0:T(8,128)(2,1)}), bf16[192,768]{1,0:T(8,128)(2,1)}) %reduce-scatter.23.cloned.1.call-update) | async-done | bytes 294928 | tf_op jit(solution)/shard_map/reduce_scatter | solution.py:284
  768.0 78.8 %reduce-scatter.21.cloned.1.call-done = bf16[48,3072]{1,0:T(8,128)(2,1)} async-done(((bf16[768,3072]{1,0:T(8,128)(2,1)}), bf16[48,3072]{1,0:T(8,128)(2,1)}) %reduce-scatter.21.cloned.1.call-update) | async-done | bytes 294928 | tf_op jit(solution)/shard_map/reduce_scatter | solution.py:281
  846.9 4.4 fusion.48
  851.3 58.0 %all-reduce.5 = (bf16[768]{0:T(1024)(128)(2,1)S(1)}, bf16[768]{0:T(1024)(128)(2,1)S(1)}, bf16[32,12]{1,0:T(8,128)(2,1)S(1)}) all-reduce(bf16[768]{0:T(1024)(128)(2,1)S(1)} %get-tuple-element.13, bf16[768]{0:T(1024)(128)(2,1)} %get-tuple-element.11, bf16[32,12]{1,0:T(8,128)(2,1)} %fusion.64), channel_id=6, replica_groups=mesh['fsdp'=16,'seq'=2] {'fsdp'}, use_global_device_ids=true, to_apply=%region_10.11.clone | all-reduce | flops 1920 | bytes 7680
  909.5 4.9 all-reduce.7
  916.0 2.7 fusion.47
  918.8 1.6 convert_element_type.329
  920.3 1.6 convert_element_type.331
  921.9 1.6 convert_element_type.333
  923.4 1.6 convert_element_type.335
  925.0 1.8 convert_element_type.337
  926.8 1.8 convert_element_type.339
  (93 shorter events, 6.3 us)
Async XLA Ops:
  7.2 44.3 %all-gather.16.cloned.1.call-start = ((), (), s32[]{:S(2)}) async-start(), calls=%async_computation.10 | async-start | bytes 1253376 | tf_op jit(solution)/shard_map/all_gather | solution.py:155
  7.9 83.1 %all-gather.12.cloned.1.call-start = ((), (), s32[]{:S(2)}) async-start(), calls=%async_computation.8 | async-start | bytes 1253376 | tf_op jit(solution)/shard_map/all_gather | solution.py:156
  8.7 129.2 %all-gather.14.cloned.1.call-start = ((), (), s32[]{:S(2)}) async-start(), calls=%async_computation.9 | async-start | bytes 1253376 | tf_op jit(solution)/shard_map/all_gather | solution.py:154
  9.4 149.5 %all-gather.26.cloned.1.call-start = ((), (), s32[]{:S(2)}) async-start(), calls=%async_computation.23 | async-start | bytes 2359296 | tf_op jit(solution)/shard_map/all_gather | solution.py:114
  49.7 41.4 %copy-start.5 = (bf16[1,512,768]{2,1,0:T(8,128)(2,1)S(1)}, bf16[1,512,768]{2,1,0:T(8,128)(2,1)}, u32[]{:S(2)}) copy-start(bf16[1,512,768]{2,1,0:T(8,128)(2,1)} %param.14) | copy-start | bytes 2359300
  54.8 43.4 %copy-start.14 = (bf16[2,12]{1,0:T(2,128)(2,1)S(1)}, bf16[2,12]{1,0:T(2,128)(2,1)}, u32[]{:S(2)}) copy-start(bf16[2,12]{1,0:T(2,128)(2,1)} %param.23) | copy-start | bytes 148
  54.8 133.3 %all-gather.24.cloned.1.call-start = ((), (), s32[]{:S(2)}) async-start(), calls=%async_computation.22 | async-start | bytes 2359296 | tf_op jit(solution)/shard_map/all_gather | solution.py:115
  94.0 147.5 %all-gather.18.cloned.1.call-start = ((), (), s32[]{:S(2)}) async-start(), calls=%async_computation.11 | async-start | bytes 1253376 | tf_op jit(solution)/shard_map/all_gather | solution.py:157
  94.6 188.6 %all-gather.20.cloned.1.call-start = ((), (), s32[]{:S(2)}) async-start(), calls=%async_computation.12 | async-start | bytes 5013504 | tf_op jit(solution)/shard_map/all_gather | solution.py:158
  95.4 242.1 %all-gather.22.cloned.1.call-start = ((), (), s32[]{:S(2)}) async-start(), calls=%async_computation.13 | async-start | bytes 5013504 | tf_op jit(solution)/shard_map/all_gather | solution.py:159
  96.1 345.7 %reduce-scatter.11.cloned.1.call-start = ((), (), s32[]{:S(2)}) async-start(), calls=%async_computation.15 | async-start | bytes 2359296 | tf_op jit(solution)/shard_map/reduce_scatter | solution.py:246
  120.1 1.4 copy-start.3
  337.5 8.8 copy-start.7
  337.5 8.8 copy-start.9
  346.3 3.4 copy-start.18
  346.3 3.4 copy-start.11
  349.7 1.6 copy-start.16
  350.1 1.1 copy-start
  383.1 63.0 %reduce-scatter.9.cloned.1.call-start = ((), (), s32[]{:S(2)}) async-start(), calls=%async_computation.14 | async-start | bytes 2359296 | tf_op jit(solution)/shard_map/reduce_scatter | solution.py:243
  409.7 11.8 %copy-start.1 = (f32[1,512,768]{2,1,0:T(8,128)S(1)}, f32[1,512,768]{2,1,0:T(8,128)}, u32[]{:S(2)}) copy-start(f32[1,512,768]{2,1,0:T(8,128)} %copy-done) | copy-start | bytes 4718596
  421.4 3.2 copy-start.2
  421.4 106.6 %reduce-scatter.19.cloned.1.call-start = ((), (), s32[]{:S(2)}) async-start(), calls=%async_computation.19 | async-start | bytes 1253376 | tf_op jit(solution)/shard_map/reduce_scatter | solution.py:278
  424.5 144.0 %reduce-scatter.13.cloned.1.call-start = ((), (), s32[]{:S(2)}) async-start(), calls=%async_computation.16 | async-start | bytes 1253376 | tf_op jit(solution)/shard_map/reduce_scatter | solution.py:269
  438.1 3.8 copy-start.6
  441.6 187.6 %reduce-scatter.17.cloned.1.call-start = ((), (), s32[]{:S(2)}) async-start(), calls=%async_computation.18 | async-start | bytes 1253376 | tf_op jit(solution)/shard_map/reduce_scatter | solution.py:275
  445.1 4.2 copy-start.12
  445.1 244.6 %reduce-scatter.15.cloned.1.call-start = ((), (), s32[]{:S(2)}) async-start(), calls=%async_computation.17 | async-start | bytes 1253376 | tf_op jit(solution)/shard_map/reduce_scatter | solution.py:272
  449.3 318.8 %reduce-scatter.23.cloned.1.call-start = ((), (), s32[]{:S(2)}) async-start(), calls=%async_computation.21 | async-start | bytes 5013504 | tf_op jit(solution)/shard_map/reduce_scatter | solution.py:284
  457.6 389.3 %reduce-scatter.21.cloned.1.call-start = ((), (), s32[]{:S(2)}) async-start(), calls=%async_computation.20 | async-start | bytes 5013504 | tf_op jit(solution)/shard_map/reduce_scatter | solution.py:281
  464.9 1.6 copy-start.13
  465.0 453.8 %all-reduce.11.cloned.1.call-start = ((), (), s32[]{:S(2)}) async-start(), calls=%async_computation.24 | async-start | bytes 1769472 | tf_op jit(solution)/shard_map/psum | solution.py:298
  466.6 3.4 copy-start.8
  470.0 8.9 copy-start.4
  478.9 47.1 %copy-start.15 = (bf16[768,768]{1,0:T(8,128)(2,1)S(1)}, bf16[768,768]{1,0:T(8,128)(2,1)}, u32[]{:S(2)}) copy-start(bf16[768,768]{1,0:T(8,128)(2,1)} %all-gather.16.cloned.1.call-done) | copy-start | bytes 3538948
  478.9 47.1 %copy-start.17 = (bf16[1,512,768]{1,2,0:T(8,128)(2,1)S(1)}, bf16[1,512,768]{1,2,0:T(8,128)(2,1)}, u32[]{:S(2)}) copy-start(bf16[1,512,768]{1,2,0:T(8,128)(2,1)} %reduce-scatter.9.cloned.1.call-done) | copy-start | bytes 2359300
  526.0 320.9 %copy-start.10 = (bf16[768,768]{1,0:T(8,128)(2,1)S(1)}, bf16[768,768]{1,0:T(8,128)(2,1)}, u32[]{:S(2)}) copy-start(bf16[768,768]{1,0:T(8,128)(2,1)} %all-gather.12.cloned.1.call-done) | copy-start | bytes 3538948
Sparse Core Ops, SparseCore 0:
  10.3 41.1 all-gather.15
  53.8 37.1 all-gather.11
  93.3 37.2 all-gather.13
  132.6 26.1 all-gather.25
  160.8 27.1 all-gather.23
  190.2 38.3 all-gather.17
  230.8 52.3 all-gather.19
  285.5 51.9 all-gather.21
  383.2 24.5 reduce-scatter.10
  421.5 24.5 reduce-scatter.8
  449.7 58.1 reduce-scatter.18
  511.4 57.0 reduce-scatter.12
  572.1 57.0 reduce-scatter.16
  632.7 57.0 reduce-scatter.14
  693.4 74.5 reduce-scatter.22
  772.2 74.5 reduce-scatter.20
  849.4 36.4 all-reduce.10
where the time goes:
time: 941 us; the launch traced here: 936 us
  waiting for transfers between devices  491 us (52%)
  matrix products  238 us (25%)
  blocking collectives  117 us (12%)
  other arithmetic  56.5 us (6%)
  between operations  18.6 us (2%)
  local copies, waits for them, and re-layouts  12.7 us (1%)
    unnamed x2, blocking collectives  93.2 us
    reduce_scatter x1, waiting for transfers between devices, local(): lax.psum_scatter(expand_grad.astype(jnp.bfloat16), 'fsdp', scatter_dimens...  78.8 us
    reduce_scatter x1, waiting for transfers between devices, local(): lax.psum_scatter(contract_grad.astype(jnp.bfloat16), 'fsdp', scatter_dime...  78.3 us
    reduce_scatter x1, waiting for transfers between devices, local(): lax.psum_scatter(value_part.astype(jnp.bfloat16), 'fsdp', scatter_dimensi...  60.7 us
    reduce_scatter x1, waiting for transfers between devices, local(): lax.psum_scatter(key_part.astype(jnp.bfloat16), 'fsdp', scatter_dimension...  60.6 us
    dot_general x1, matrix products, local(): jnp.einsum('hij,ijb->bh', jnp.sum(grad_scores, axis=0), onehot.astype(f32...  47 us
    all_gather x1, waiting for transfers between devices, local(): lax.all_gather(contract_weight, 'fsdp', axis=0, tiled=True)  46.1 us
    reduce_scatter x1, waiting for transfers between devices, local(): lax.psum_scatter(query_part.astype(jnp.bfloat16), 'fsdp', scatter_dimensi...  40.5 us
  transfers between devices with their start and end apart: 17, of which 12 were waited for; matrix products, arithmetic and copies ran while one was open for 27% of the time, Pallas kernels for 0%

commit v1 on v0

--- a/solution.py
+++ b/solution.py
@@ -1,13 +1,795 @@
+import functools
+
 import jax
 import jax.numpy as jnp
 from jax import lax
+from jax.experimental import pallas as pl
+from jax.experimental.pallas import tpu as pltpu
 from jax.sharding import PartitionSpec as P
 
+f32 = jnp.float32
+bf16 = jnp.bfloat16
 BUCKETS = 32
-
-
 EPS = 1e-06
 far_edges = (12, 16, 23, 32, 46, 64, 91)
+HIDDEN = -(2.0**30)
+VMEM = 56 * 1024 * 1024
+ANY = pl.BlockSpec(memory_space=pl.ANY)
+FULL = pl.BlockSpec(memory_space=pltpu.VMEM)
+SCALARS = pl.BlockSpec(memory_space=pltpu.SMEM)
+
+
+def dot(left, right, left_dim, right_dim):
+    return lax.dot_general(
+        left, right, (((left_dim,), (right_dim,)), ((), ())), preferred_element_type=f32
+    )
+
+
+def params():
+    return pltpu.CompilerParams(vmem_limit_bytes=VMEM)
+
+
+def cost(flops, byte_count, exps=0):
+    return pl.CostEstimate(flops=flops, bytes_accessed=byte_count, transcendentals=exps)
+
+
+def bucket_of(offset):
+    distance = jnp.abs(offset)
+    beyond = jnp.zeros_like(distance)
+    for far_edge in far_edges:
+        beyond = beyond + (distance >= far_edge).astype(jnp.int32)
+    nearby = jnp.where(distance < 8, distance, 8 + beyond)
+    return nearby + 16 * (offset > 0).astype(jnp.int32)
+
+
+def iota(shape, dim):
+    return lax.broadcasted_iota(jnp.int32, shape, dim)
+
+
+def place_blocks(place, near, far, dest, sems):
+    z, y, c = place[0], place[1], place[2]
+    copies = []
+    for turn in range(4):
+        for dy in range(2):
+            owner = ((jnp.bitwise_xor(z, turn) * 2) + jnp.bitwise_xor(y, dy)) * 2
+            for other, source in enumerate((near, far)):
+                row = pl.multiple_of((owner + jnp.bitwise_xor(c, other)) * 48, 16)
+                index = turn * 2 + dy
+                copy = pltpu.make_async_copy(
+                    source.at[index], dest.at[pl.ds(row, 48)], sems.at[len(copies)]
+                )
+                copy.start()
+                copies.append(copy)
+    return copies
+
+
+def place_tokens(x, near, far, dest, sems, count):
+    copies = []
+    for other, source in enumerate((near, far)):
+        row = pl.multiple_of(jnp.bitwise_xor(x, other) * count, count)
+        copy = pltpu.make_async_copy(source, dest.at[pl.ds(row, count)], sems.at[other])
+        copy.start()
+        copies.append(copy)
+    return copies
+
+
+def project_kernel(place, x_near, x_far, w_near, w_far, qkv, normed, small, xs, w, sems, xsems):
+    tokens = place_tokens(place[3], x_near, x_far, xs, xsems, 512)
+    blocks = place_blocks(place, w_near, w_far, w, sems)
+    for copy in tokens + blocks:
+        copy.wait()
+    side = w[:, 1152:1280].astype(f32).T
+    small[...] = side[:8]
+    gain = side[0:1]
+    for row in range(0, 1024, 256):
+        wide = xs[row : row + 256].astype(f32)
+        scale = lax.rsqrt(jnp.mean(wide * wide, axis=-1, keepdims=True) + EPS)
+        normed[row : row + 256] = (wide * scale * gain).astype(bf16)
+    for col in range(0, 1152, 384):
+        made = dot(w[:, col : col + 384], normed[...], 0, 1)
+        qkv[col : col + 384] = made.astype(bf16)
+
+
+def project(place, x_near, x_far, w_near, w_far):
+    return pl.pallas_call(
+        project_kernel,
+        out_shape=(
+            jax.ShapeDtypeStruct((1152, 1024), bf16),
+            jax.ShapeDtypeStruct((1024, 768), bf16),
+            jax.ShapeDtypeStruct((8, 768), f32),
+        ),
+        in_specs=[SCALARS, ANY, ANY, ANY, ANY],
+        out_specs=(FULL, FULL, FULL),
+        scratch_shapes=[
+            pltpu.VMEM((1024, 768), bf16),
+            pltpu.VMEM((768, 1280), bf16),
+            pltpu.SemaphoreType.DMA((16,)),
+            pltpu.SemaphoreType.DMA((2,)),
+        ],
+        compiler_params=params(),
+        cost_estimate=cost(2 * 1024 * 768 * 1152, 9_000_000),
+        name="project",
+    )(place, x_near, x_far, w_near, w_far)
+
+
+def attend_kernel(scal, table, q, k, v, out, kept, inverse, ka, kt, qt, vt, s0, s1, tile, which):
+    head = pl.program_id(0)
+    first, valid, instr, pair = scal[0], scal[1], scal[2], scal[3]
+
+    @pl.when(head == 0)
+    def _():
+        which[...] = bucket_of(iota((384, 128), 0) - 128 - iota((384, 128), 1))
+        kt[64:128] = jnp.zeros((64, 1024), bf16)
+        qt[64:128] = jnp.zeros((64, 512), bf16)
+        row = iota((16, 1024), 0)
+        key = iota((16, 1024), 1)
+        extra = jnp.where(row < 8, (key // 128 == row).astype(f32), 0.0)
+        extra = jnp.where(row == 8, jnp.where(key >= valid, HIDDEN, 0.0), extra)
+        extra = jnp.where(row == 9, (key >= instr).astype(f32), extra)
+        kt[64:80] = extra.astype(bf16)
+        vt[64:80] = jnp.where(row == 0, 1.0, 0.0).astype(bf16)
+
+    buckets = which[...]
+    bias = jnp.zeros((384, 128), f32)
+    for bucket in range(BUCKETS):
+        bias = jnp.where(buckets == bucket, table[head, bucket], bias)
+    tile[...] = bias
+    row = iota((16, 512), 0)
+    query = iota((16, 512), 1) + first
+    block = query // 128
+    extra = jnp.where(row <= block - 2, table[head, 15], 0.0)
+    extra = jnp.where(row >= block + 2, table[head, 31], extra)
+    extra = jnp.where(row == 8, 1.0, extra)
+    guarded = (query < instr) & (pair == 1)
+    extra = jnp.where(row == 9, jnp.where(guarded, HIDDEN, 0.0), extra)
+    extra = jnp.where(row > 9, 0.0, extra)
+    qt[64:80] = extra.astype(bf16)
+    qt[0:64] = q[...]
+    kt[0:64] = k[...]
+    vt[0:64] = v[...]
+    ka[...] = kt[...].T
+    for part, s in enumerate((s0, s1)):
+        lanes = slice(part * 256, part * 256 + 256)
+        s[128:1152] = dot(ka[...], qt[:, lanes], 1, 0)
+        for half in range(2):
+            base = pl.multiple_of(first + (part * 2 + half) * 128, 128)
+            cols = slice(half * 128, half * 128 + 128)
+            s[pl.ds(base, 384), cols] = s[pl.ds(base, 384), cols] + tile[...]
+        scores = s[128:1152]
+        peak = jnp.max(scores, axis=0, keepdims=True)
+        weights = jnp.exp(scores - peak).astype(bf16)
+        kept[0, :, lanes] = weights
+        summed = dot(vt[...], weights, 1, 0)
+        share = 1.0 / summed[64:65]
+        out[:, lanes] = (summed[0:64] * share).astype(bf16)
+        inverse[0, :, lanes] = share
+
+
+def attend(scal, table, qkv, half):
+    heads = 6
+    grid = pltpu.PrefetchScalarGridSpec(
+        num_scalar_prefetch=1,
+        grid=(heads,),
+        in_specs=[
+            SCALARS,
+            pl.BlockSpec((64, 512), lambda h, s: (h, s[0] // 512)),
+            pl.BlockSpec((64, 1024), lambda h, s: (6 + h, 0)),
+            pl.BlockSpec((64, 1024), lambda h, s: (12 + h, 0)),
+        ],
+        out_specs=(
+            pl.BlockSpec((64, 512), lambda h, s: (h, 0)),
+            pl.BlockSpec((1, 1024, 512), lambda h, s: (h, 0, 0)),
+            pl.BlockSpec((1, 1, 512), lambda h, s: (h, 0, 0)),
+        ),
+        scratch_shapes=[
+            pltpu.VMEM((1024, 128), bf16),
+            pltpu.VMEM((128, 1024), bf16),
+            pltpu.VMEM((128, 512), bf16),
+            pltpu.VMEM((80, 1024), bf16),
+            pltpu.VMEM((1280, 256), f32),
+            pltpu.VMEM((1280, 256), f32),
+            pltpu.VMEM((384, 128), f32),
+            pltpu.VMEM((384, 128), jnp.int32),
+        ],
+    )
+    return pl.pallas_call(
+        attend_kernel,
+        out_shape=(
+            jax.ShapeDtypeStruct((384, 512), bf16),
+            jax.ShapeDtypeStruct((heads, 1024, 512), bf16),
+            jax.ShapeDtypeStruct((heads, 1, 512), f32),
+        ),
+        grid_spec=grid,
+        compiler_params=params(),
+        cost_estimate=cost(heads * 1024 * 512 * 512, 10_000_000, heads * 1024 * 512),
+        name="attend_" + half,
+    )(scal, table, qkv, qkv, qkv)
+
+
+def attend_back_kernel(
+    carried, scal, grad, out, inverse, q, k, v, kept, *refs
+):
+    if carried:
+        dk_in, dv_in, band_in, far_in, *refs = refs
+    dq, dk, dv, band, far, va, vt, kt, gt, ds = refs
+    head = pl.program_id(0)
+    first = scal[0]
+
+    @pl.when(head == 0)
+    def _():
+        row = iota((16, 1024), 0)
+        key = iota((16, 1024), 1)
+        vt[64:128] = jnp.zeros((64, 1024), bf16)
+        vt[64:80] = jnp.where(row < 2, 1.0, 0.0).astype(bf16)
+        kt[64:80] = jnp.where(row < 8, (key // 128 == row).astype(f32), 0.0).astype(bf16)
+        gt[64:128] = jnp.zeros((64, 512), bf16)
+        ds[0:128] = jnp.zeros((128, 512), bf16)
+        ds[1152:1280] = jnp.zeros((128, 512), bf16)
+
+    share = inverse[0]
+    scaled = grad[...].astype(f32) * share
+    delta = jnp.sum(scaled * out[...].astype(f32), axis=0, keepdims=True)
+    high = delta.astype(bf16).astype(f32)
+    row = iota((16, 512), 0)
+    extra = jnp.where(row == 0, -high, jnp.where(row == 1, high - delta, 0.0))
+    gt[64:80] = extra.astype(bf16)
+    gt[0:64] = scaled.astype(bf16)
+    vt[0:64] = v[...]
+    kt[0:64] = k[...]
+    va[...] = vt[...].T
+    for row_at in range(0, 1024, 256):
+        rows = slice(row_at, row_at + 256)
+        pull = dot(va[rows], gt[...], 1, 0)
+        ds[128 + row_at : 384 + row_at] = (kept[0, rows] * pull).astype(bf16)
+    made = dot(kt[...], ds[128:1152], 1, 0)
+    dq[...] = made[0:64].astype(bf16)
+    block = (iota((8, 512), 1) + first) // 128
+    key_block = iota((8, 512), 0)
+    totals = made[64:72]
+    left = jnp.sum(jnp.where(key_block <= block - 2, totals, 0.0), axis=0, keepdims=True)
+    right = jnp.sum(jnp.where(key_block >= block + 2, totals, 0.0), axis=0, keepdims=True)
+    sides = jnp.concatenate([left, right, jnp.zeros((6, 512), f32)], axis=0)
+    far[0] = sides + far_in[0] if carried else sides
+    dv_made = dot(gt[0:64], kept[0], 1, 1)
+    dk_made = dot(q[...], ds[128:1152], 1, 1)
+    near = None
+    for part in range(4):
+        base = pl.multiple_of(first + part * 128, 128)
+        window = ds[pl.ds(base, 384), part * 128 : part * 128 + 128].astype(f32)
+        near = window if near is None else near + window
+    if carried:
+        dk[...] = (dk_made + dk_in[...]).astype(bf16)
+        dv[...] = (dv_made + dv_in[...]).astype(bf16)
+        band[0] = near + band_in[0]
+    else:
+        dk[...] = dk_made
+        dv[...] = dv_made
+        band[0] = near
+
+
+def attend_back(scal, grad, out, inverse, qkv, kept, carry, half):
+    heads = 6
+    rows512 = pl.BlockSpec((64, 512), lambda h, s: (h, 0))
+    rows1024 = pl.BlockSpec((64, 1024), lambda h, s: (h, 0))
+    band_spec = pl.BlockSpec((1, 384, 128), lambda h, s: (h, 0, 0))
+    in_specs = [
+        rows512,
+        rows512,
+        pl.BlockSpec((1, 1, 512), lambda h, s: (h, 0, 0)),
+        pl.BlockSpec((64, 512), lambda h, s: (h, s[0] // 512)),
+        pl.BlockSpec((64, 1024), lambda h, s: (6 + h, 0)),
+        pl.BlockSpec((64, 1024), lambda h, s: (12 + h, 0)),
+        pl.BlockSpec((1, 1024, 512), lambda h, s: (h, 0, 0)),
+    ]
+    far_spec = pl.BlockSpec((1, 8, 512), lambda h, s: (h, 0, 0))
+    if carry:
+        in_specs += [rows1024, rows1024, band_spec, far_spec]
+    wide = bf16 if carry else f32
+    grid = pltpu.PrefetchScalarGridSpec(
+        num_scalar_prefetch=1,
+        grid=(heads,),
+        in_specs=in_specs,
+        out_specs=(
+            rows512,
+            rows1024,
+            rows1024,
+            band_spec,
+            far_spec,
+        ),
+        scratch_shapes=[
+            pltpu.VMEM((1024, 128), bf16),
+            pltpu.VMEM((128, 1024), bf16),
+            pltpu.VMEM((80, 1024), bf16),
+            pltpu.VMEM((128, 512), bf16),
+            pltpu.VMEM((1280, 512), bf16),
+        ],
+    )
+    return pl.pallas_call(
+        functools.partial(attend_back_kernel, bool(carry)),
+        out_shape=(
+            jax.ShapeDtypeStruct((384, 512), bf16),
+            jax.ShapeDtypeStruct((384, 1024), wide),
+            jax.ShapeDtypeStruct((384, 1024), wide),
+            jax.ShapeDtypeStruct((heads, 384, 128), f32),
+            jax.ShapeDtypeStruct((heads, 8, 512), f32),
+        ),
+        grid_spec=grid,
+        compiler_params=params(),
+        cost_estimate=cost(heads * 1024 * 512 * 1024, 12_000_000),
+        name="attend_back_" + half,
+    )(scal, grad, out, inverse, qkv, qkv, qkv, kept, *carry)
+
+
+def gelu_both(wide):
+    square = wide * wide
+    inner = 0.7978845608 * wide * (1.0 + 0.044715 * square)
+    bend = jnp.tanh(inner)
+    half = 0.5 * (1.0 + bend)
+    slope = 0.7978845608 * (1.0 + 3 * 0.044715 * square)
+    return (wide * half, half + 0.5 * wide * (1.0 - bend * bend) * slope)
+
+
+def forward_kernel(
+    place, att_near, att_far, x, cot, small, near0, near1, far0, far1, nearx0, nearx1, farx0, farx1,
+    hidden_hbm, pre_hbm, contract_hbm, middle, normed, branch_low, middle_grad, att, near_grad,
+    far_grad, gain_grad,
+    w_out, w_up, w_down, hidden, pre, normed_grad, pulled, sems, att_sems, out_sems,
+):
+    z, y, c, xs = place[0], place[1], place[2], place[3]
+    att_copies = []
+    for other, source in enumerate((att_near, att_far)):
+        row = pl.multiple_of(jnp.bitwise_xor(xs, other) * 384, 128)
+        copy = pltpu.make_async_copy(source, att.at[pl.ds(row, 384)], att_sems.at[other])
+        copy.start()
+        att_copies.append(copy)
+    groups = ([], [], [])
+    for turn in range(4):
+        for dy in range(2):
+            owner = ((jnp.bitwise_xor(z, turn) * 2) + jnp.bitwise_xor(y, dy)) * 2
+            index = (turn % 2) * 2 + dy
+            for other in range(2):
+                main = ((near0, near1), (far0, far1))[other][turn // 2]
+                side = ((nearx0, nearx1), (farx0, farx1))[other][turn // 2]
+                who = owner + jnp.bitwise_xor(c, other)
+                row = pl.multiple_of(who * 48, 16)
+                pieces = (
+                    (0, main.at[index, 4], w_out.at[pl.ds(row, 48)]),
+                    (1, main.at[index, 0:4], w_up.at[:, pl.ds(row, 48)]),
+                    (2, main.at[index, 5:7], w_down.at[pl.ds(who * 4 + xs * 2, 2)]),
+                    (2, side.at[index], w_down.at[pl.ds(who * 4 + (1 - xs) * 2, 2)]),
+                )
+                for at, (group, source, dest) in enumerate(pieces):
+                    sem = sems.at[at, turn * 4 + dy * 2 + other]
+                    groups[group].append(pltpu.make_async_copy(source, dest, sem))
+    for group in groups:
+        for copy in group:
+            copy.start()
+    for copy in att_copies + groups[0]:
+        copy.wait()
+    gain = small[1:2]
+    wide = x[...].astype(f32) + dot(att[...], w_out[...], 0, 0)
+    middle[...] = wide
+    scale = lax.rsqrt(jnp.mean(wide * wide, axis=-1, keepdims=True) + EPS)
+    normed[...] = (wide * scale * gain).astype(bf16)
+    for group in groups[1:]:
+        for copy in group:
+            copy.wait()
+    keep = pltpu.make_async_copy(w_down, contract_hbm, out_sems.at[0])
+    keep.start()
+    normed_grad[...] = jnp.zeros_like(normed_grad)
+
+    def chunk(j, carry):
+        pulled[...] = dot(cot[...], w_down[pl.ds(j * 16, 16)].reshape(768, 768), 1, 1)
+        value, slope = gelu_both(dot(normed[...], w_up[j], 1, 0))
+        hidden[j] = value.astype(bf16)
+        low = (pulled[...] * slope).astype(bf16)
+        pre[j] = low
+        normed_grad[...] += dot(low, w_up[j], 1, 1)
+        return carry
+
+    lax.fori_loop(0, 4, chunk, 0)
+    first = pltpu.make_async_copy(hidden, hidden_hbm, out_sems.at[1])
+    second = pltpu.make_async_copy(pre, pre_hbm, out_sems.at[2])
+    first.start()
+    second.start()
+    wide = middle[...]
+    scale = lax.rsqrt(jnp.mean(wide * wide, axis=-1, keepdims=True) + EPS)
+    unit = wide * scale
+    incoming = normed_grad[...]
+    gain_grad[...] = jnp.sum(incoming * unit, axis=0, keepdims=True)
+    direct = incoming * gain
+    inward = scale * (direct - unit * jnp.mean(direct * unit, axis=-1, keepdims=True))
+    grad = cot[...].astype(f32) + inward
+    middle_grad[...] = grad
+    low = grad.astype(bf16)
+    branch_low[...] = low
+    for other, dest in enumerate((near_grad, far_grad)):
+        row = pl.multiple_of(jnp.bitwise_xor(xs, other) * 384, 128)
+        dest[...] = dot(w_out[pl.ds(row, 384)], low, 1, 1).astype(bf16)
+    keep.wait()
+    first.wait()
+    second.wait()
+
+
+def forward(place, att_near, att_far, x, cot, small, blocks):
+    tokens = jax.ShapeDtypeStruct((512, 768), bf16)
+    wide = jax.ShapeDtypeStruct((512, 768), f32)
+    half = jax.ShapeDtypeStruct((384, 512), bf16)
+    return pl.pallas_call(
+        forward_kernel,
+        out_shape=(
+            jax.ShapeDtypeStruct((4, 512, 768), bf16),
+            jax.ShapeDtypeStruct((4, 512, 768), bf16),
+            jax.ShapeDtypeStruct((64, 48, 768), bf16),
+            wide,
+            tokens,
+            tokens,
+            wide,
+            jax.ShapeDtypeStruct((768, 512), bf16),
+            half,
+            half,
+            jax.ShapeDtypeStruct((1, 768), f32),
+        ),
+        in_specs=[SCALARS, ANY, ANY, FULL, FULL, FULL] + [ANY] * 8,
+        out_specs=(ANY, ANY, ANY) + (FULL,) * 8,
+        scratch_shapes=[
+            pltpu.VMEM((768, 768), bf16),
+            pltpu.VMEM((4, 768, 768), bf16),
+            pltpu.VMEM((64, 48, 768), bf16),
+            pltpu.VMEM((4, 512, 768), bf16),
+            pltpu.VMEM((4, 512, 768), bf16),
+            pltpu.VMEM((512, 768), f32),
+            pltpu.VMEM((512, 768), f32),
+            pltpu.SemaphoreType.DMA((4, 16)),
+            pltpu.SemaphoreType.DMA((2,)),
+            pltpu.SemaphoreType.DMA((3,)),
+        ],
+        compiler_params=params(),
+        cost_estimate=cost(8_500_000_000, 20_000_000, 512 * 3072),
+        name="forward",
+    )(place, att_near, att_far, x, cot, small, *blocks)
+
+
+def pick(made, core, near, far, index):
+    first, second = made
+    near[index] = jnp.where(core == 0, first, second)
+    far[index] = jnp.where(core == 0, second, first)
+
+
+def contract_grad_kernel(place, hidden, cot, near, far):
+    made = dot(hidden[0], cot[...], 0, 0).astype(bf16).reshape(2, 4, 48, 768)
+    pick((made[0], made[1]), place[2], near, far, 0)
+
+
+def contract_weight_grad(place, hidden, cot):
+    shape = jax.ShapeDtypeStruct((8, 4, 48, 768), bf16)
+    spec = pl.BlockSpec((1, 4, 48, 768), lambda j: (j, 0, 0, 0))
+    return pl.pallas_call(
+        contract_grad_kernel,
+        out_shape=(shape, shape),
+        grid=(8,),
+        in_specs=[
+            SCALARS,
+            pl.BlockSpec((1, 512, 384), lambda j: (j // 2, 0, j % 2)),
+            pl.BlockSpec((512, 768), lambda j: (0, 0)),
+        ],
+        out_specs=(spec, spec),
+        compiler_params=params(),
+        cost_estimate=cost(2 * 512 * 3072 * 768, 9_000_000),
+        name="contract_weight_grad",
+    )(place, hidden, cot)
+
+
+def expand_grad_kernel(place, normed, pre, att, branch, hidden, contract, middle, near, far, result, total):
+    step = pl.program_id(0)
+
+    def store(made):
+        made = made.astype(bf16).reshape(8, 2, 48, 768)
+        near[:, 0] = jnp.where(place[2] == 0, made[:, 0], made[:, 1])
+        far[:, 0] = jnp.where(place[2] == 0, made[:, 1], made[:, 0])
+
+    @pl.when(step < 4)
+    def _():
+        store(dot(normed[...], pre[0], 0, 0))
+
+    @pl.when(step == 4)
+    def _():
+        store(dot(att[...], branch[...], 1, 0))
+
+    @pl.when(step == 0)
+    def _():
+        total[...] = middle[...]
+
+    @pl.when(step < 4)
+    def _():
+        total[...] += dot(hidden[0], contract[...].reshape(768, 768), 1, 0)
+
+    @pl.when(step == 4)
+    def _():
+        result[...] = total[...].astype(bf16)
+
+
+def expand_weight_grad(place, normed, pre, att, branch, hidden, contract, middle):
+    shape = jax.ShapeDtypeStruct((8, 5, 48, 768), bf16)
+    spec = pl.BlockSpec((8, 1, 48, 768), lambda j: (0, j, 0, 0))
+    chunk = pl.BlockSpec((1, 512, 768), lambda j: (jnp.minimum(j, 3), 0, 0))
+    whole = pl.BlockSpec((512, 768), lambda j: (0, 0))
+    return pl.pallas_call(
+        expand_grad_kernel,
+        out_shape=(shape, shape, jax.ShapeDtypeStruct((512, 768), bf16)),
+        grid=(5,),
+        in_specs=[
+            SCALARS,
+            whole,
+            chunk,
+            pl.BlockSpec((768, 512), lambda j: (0, 0)),
+            whole,
+            chunk,
+            pl.BlockSpec((16, 48, 768), lambda j: (jnp.minimum(j, 3), 0, 0)),
+            whole,
+        ],
+        out_specs=(spec, spec, whole),
+        scratch_shapes=[pltpu.VMEM((512, 768), f32)],
+        compiler_params=params(),
+        cost_estimate=cost(2 * 512 * 768 * (6144 + 768), 24_000_000),
+        name="expand_weight_grad",
+    )(place, normed, pre, att, branch, hidden, contract, middle)
+
+
+def project_back_kernel(
+    place, x_near, x_far, w_near, w_far, small, normed, dq_near, dq_far, dk, dv, band, far, gain_two,
+    g_near, g_far, part_near, part_far, xs, w, grad, gains, sems, xsems, qsems,
+):
+    x, core = place[3], place[2]
+    tokens = place_tokens(x, x_near, x_far, xs, xsems, 512)
+    blocks = place_blocks(place, w_near, w_far, w, sems)
+    moves = []
+    for other, source in enumerate((dq_near, dq_far)):
+        lane = pl.multiple_of(jnp.bitwise_xor(x, other) * 512, 128)
+        moves.append(pltpu.make_async_copy(source, grad.at[0:384, pl.ds(lane, 512)], qsems.at[other]))
+    moves.append(pltpu.make_async_copy(dk, grad.at[384:768], qsems.at[2]))
+    moves.append(pltpu.make_async_copy(dv, grad.at[768:1152], qsems.at[3]))
+    for copy in moves:
+        copy.start()
+    for copy in moves + blocks + tokens:
+        copy.wait()
+    gain_total = jnp.zeros((1, 768), f32)
+    for other, dest in ((1, part_far), (0, part_near)):
+        start = pl.multiple_of(jnp.bitwise_xor(x, other) * 512, 512)
+        part = dot(grad[:, pl.ds(start, 512)], w[:, 0:1152], 0, 1)
+        dest[...] = part.astype(bf16)
+        wide = xs[pl.ds(start, 512)].astype(f32)
+        scale = lax.rsqrt(jnp.mean(wide * wide, axis=-1, keepdims=True) + EPS)
+        gain_total = gain_total + jnp.sum(part * (wide * scale), axis=0, keepdims=True)
+    buckets = bucket_of(iota((384, 128), 0) - 128 - iota((384, 128), 1))
+    lane = iota((1, 128), 1)
+    rows = []
+    for head in range(6):
+        sums = jnp.zeros((1, 128), f32)
+        here = band[head]
+        for bucket in range(BUCKETS):
+            if bucket == 16:
+                continue
+            some = jnp.sum(jnp.where(buckets == bucket, here, 0.0))
+            if bucket in (15, 31):
+                some = some + jnp.sum(far[head, bucket // 16])
+            sums = jnp.where(lane == bucket, some, sums)
+        rows.append(sums)
+    bias = jnp.concatenate(rows + [jnp.zeros((2, 128), f32)], axis=0)
+    owner_row = iota((768, 128), 0)
+    spot = owner_row % 48
+    bucket_at = (owner_row // 48) * 2 + spot // 6
+    chosen = jnp.where((iota((768, 128), 1) == bucket_at) & (spot < 12), 1.0, 0.0)
+    per_head = lax.dot_general(
+        chosen, bias, (((1,), (1,)), ((), ())),
+        precision=lax.Precision.HIGHEST, preferred_element_type=f32,
+    )
+    pattern = (iota((768, 8), 1) == (iota((768, 8), 0) % 48) % 6).astype(f32)
+    bias_column = jnp.sum(per_head * pattern, axis=1, keepdims=True)
+    gains[...] = jnp.zeros((8, 768), f32)
+    gains[0:1] = gain_total
+    gains[1:2] = gain_two[...]
+    columns = jnp.concatenate([gains[...], jnp.zeros((120, 768), f32)], axis=0).T
+    side = jnp.where(iota((768, 128), 1) == 2, bias_column, columns)
+
+    def store(made, low, high):
+        made = made.astype(bf16).reshape(8, 2, 48, high - low)
+        g_near[:, :, low:high] = jnp.where(core == 0, made[:, 0], made[:, 1])
+        g_far[:, :, low:high] = jnp.where(core == 0, made[:, 1], made[:, 0])
+
+    for col in range(0, 1152, 384):
+        store(dot(normed[...], grad[col : col + 384], 0, 1), col, col + 384)
+    store(side, 1152, 1280)
+
+
+def project_back(place, x_near, x_far, w_near, w_far, small, normed, dq_near, dq_far, dk, dv, band, far, gain_two):
+    owned = jax.ShapeDtypeStruct((8, 48, 1280), bf16)
+    part = jax.ShapeDtypeStruct((512, 768), bf16)
+    return pl.pallas_call(
+        project_back_kernel,
+        out_shape=(owned, owned, part, part),
+        in_specs=[SCALARS, ANY, ANY, ANY, ANY, FULL, FULL, ANY, ANY, ANY, ANY, FULL, FULL, FULL],
+        out_specs=(FULL,) * 4,
+        scratch_shapes=[
+            pltpu.VMEM((1024, 768), bf16),
+            pltpu.VMEM((768, 1280), bf16),
+            pltpu.VMEM((1152, 1024), bf16),
+            pltpu.VMEM((8, 768), f32),
+            pltpu.SemaphoreType.DMA((16,)),
+            pltpu.SemaphoreType.DMA((2,)),
+            pltpu.SemaphoreType.DMA((4,)),
+        ],
+        compiler_params=params(),
+        cost_estimate=cost(4 * 1024 * 768 * 1152, 16_000_000),
+        name="project_back",
+    )(place, x_near, x_far, w_near, w_far, small, normed, dq_near, dq_far, dk, dv, band, far, gain_two)
+
+
+def input_grad_kernel(x, small, near, far, middle_grad, result):
+    for row in range(0, 512, 256):
+        rows = slice(row, row + 256)
+        wide = x[rows].astype(f32)
+        scale = lax.rsqrt(jnp.mean(wide * wide, axis=-1, keepdims=True) + EPS)
+        unit = wide * scale
+        direct = (near[rows].astype(f32) + far[rows].astype(f32)) * small[0:1]
+        inward = scale * (direct - unit * jnp.mean(direct * unit, axis=-1, keepdims=True))
+        result[rows] = (middle_grad[rows] + inward).astype(bf16)
+
+
+def input_grad(x, small, near, far, middle_grad):
+    return pl.pallas_call(
+        input_grad_kernel,
+        out_shape=jax.ShapeDtypeStruct((512, 768), bf16),
+        in_specs=[FULL] * 5,
+        out_specs=FULL,
+        compiler_params=params(),
+        cost_estimate=cost(512 * 768 * 20, 6_000_000),
+        name="input_grad",
+    )(x, small, near, far, middle_grad)
+
+
+def swap(array, axis, bit):
+    count = lax.axis_size(axis)
+    return lax.ppermute(array, axis, [(i, i ^ bit) for i in range(count)])
+
+
+CORE, Y, Z = 1, 2, 4
+
+
+def take(array, index, axis):
+    return lax.dynamic_index_in_dim(array, index, axis, keepdims=False)
+
+
+def added(parts):
+    total = parts[0].astype(f32)
+    for part in parts[1:]:
+        total = total + part.astype(f32)
+    return total
+
+
+def trade(parts, axis, index, mesh_axis, bit):
+    sent = added([take(part, 1 - index, axis) for part in parts]).astype(bf16)
+    return [take(part, index, axis) for part in parts] + [swap(sent, mesh_axis, bit)]
+
+
+def trade_z(parts, z):
+    got = []
+    for turn in range(1, 4):
+        sent = added([take(part, z ^ turn, 0) for part in parts]).astype(bf16)
+        got.append(swap(sent, "fsdp", Z * turn))
+    return added([take(part, z, 0) for part in parts] + got)
+
+
+def both(array):
+    low = lax.optimization_barrier(array.astype(bf16))
+    return low, swap(low, "seq", 1)
+
+
+def local_split(
+    layer_input, query_weight, key_weight, value_weight, output_weight, expand_weight,
+    contract_weight, attention_gain, feedforward_gain, bias_table, valid_len, instr_len, pair_flag,
+    cotangent,
+):
+    owner, x = lax.axis_index("fsdp"), lax.axis_index("seq")
+    z, y, c = owner // 4, (owner // 2) % 2, owner % 2
+    place = jnp.stack([z, y, c, x]).astype(jnp.int32)
+    tokens, cot = layer_input[0], cotangent[0]
+
+    def columns(weight):
+        return lax.dynamic_slice(weight, (0, 384 * x), (48, 384))
+
+    table_column = jnp.pad(bias_table.reshape(24, 1), ((0, 24), (0, 0)))
+    side = jnp.concatenate(
+        [attention_gain[:, None], feedforward_gain[:, None], table_column], axis=1
+    )
+    shard = jnp.concatenate(
+        [columns(query_weight), columns(key_weight), columns(value_weight), jnp.pad(side, ((0, 0), (0, 125)))],
+        axis=1,
+    )
+    x_far = swap(tokens, "seq", 1)
+    along = [shard] + [swap(shard, "fsdp", Z * turn) for turn in range(1, 4)]
+    across = [swap(block, "fsdp", Y) for block in along]
+    w_near = jnp.stack([block for pair in zip(along, across) for block in pair])
+    w_far = swap(w_near, "fsdp", CORE)
+
+    half = lax.dynamic_slice(contract_weight, (96 * x, 0), (96, 768)).reshape(2, 48, 768)
+    shard = jnp.concatenate(
+        [expand_weight.reshape(48, 4, 768).transpose(1, 0, 2), output_weight[None], half], axis=0
+    )
+    shard, _ = lax.optimization_barrier((shard, along[3]))
+    zs = [shard] + [swap(shard, "fsdp", Z * turn) for turn in range(1, 4)]
+    ys = [swap(block, "fsdp", Y) for block in zs]
+    near, near_x, far, far_x = [], [], [], []
+    for group in range(2):
+        at = 2 * group
+        blocks = jnp.stack([zs[at], ys[at], zs[at + 1], ys[at + 1]])
+        side_blocks = swap(blocks[:, 5:7], "seq", 1)
+        near.append(blocks)
+        near_x.append(side_blocks)
+        far.append(swap(blocks, "fsdp", CORE))
+        far_x.append(swap(side_blocks, "fsdp", CORE))
+
+    qkv, normed, small = project(place, tokens, x_far, w_near, w_far)
+    table = small[2].reshape(16, 48)[:, :24].reshape(32, 12).T
+    table = jnp.pad(lax.dynamic_slice(table, (6 * x, 0), (6, 32)), ((0, 2), (0, 0)))
+    lens = jnp.stack([valid_len[0], instr_len[0], pair_flag[0]])
+    mine = jnp.concatenate([(x * 512).astype(jnp.int32)[None], lens])
+    theirs = jnp.concatenate([((1 - x) * 512).astype(jnp.int32)[None], lens])
+    out_theirs, kept_theirs, inverse_theirs = attend(theirs, table, qkv, "theirs")
+    out_got = swap(out_theirs, "seq", 1)
+    out_mine, kept_mine, inverse_mine = attend(mine, table, qkv, "mine")
+
+    (
+        hidden, pre, contract, middle, normed_two, branch_low, middle_grad, att, grad_mine, grad_sent, gain_two,
+    ) = forward(place, out_mine, out_got, tokens, cot, small, near + far + near_x + far_x)
+    grad_theirs = swap(grad_sent, "seq", 1)
+
+    a_near, a_far = contract_weight_grad(place, hidden, cot)
+    a_parts = [part.reshape(4, 2, 2, 2, 48, 768) for part in (a_near, swap(a_far, "fsdp", CORE))]
+    b_near, b_far, layer_output = expand_weight_grad(
+        place, normed_two, pre, att, branch_low, hidden, contract, middle
+    )
+    b_parts = [part.reshape(4, 2, 5, 48, 768) for part in (b_near, swap(b_far, "fsdp", CORE))]
+
+    dq_mine, dk, dv, band, far_sum = attend_back(
+        mine, grad_mine, out_mine, inverse_mine, qkv, kept_mine, (), "mine"
+    )
+    a_parts = trade(a_parts, 2, x, "seq", 1)
+    b_parts = trade(b_parts, 1, y, "fsdp", Y)
+    dq_theirs, dk, dv, band, far_sum = attend_back(
+        theirs, grad_theirs, out_theirs, inverse_theirs, qkv, kept_theirs, (dk, dv, band, far_sum), "theirs"
+    )
+    a_parts = trade(a_parts, 1, y, "fsdp", Y)
+    g_near, g_far, part_near, part_far = project_back(
+        place, tokens, x_far, w_near, w_far, small, normed, dq_mine, dq_theirs, dk, dv, band, far_sum, gain_two
+    )
+    part_got = swap(part_far, "seq", 1)
+    g_parts = [part.reshape(4, 2, 48, 1280) for part in (g_near, swap(g_far, "fsdp", CORE))]
+    g_parts = trade(g_parts, 1, y, "fsdp", Y)
+
+    b_low, b_other = both(trade_z(b_parts, z))
+    b_sum = b_low.astype(f32) + b_other.astype(f32)
+    expand_sum = b_sum[:4].transpose(1, 0, 2).reshape(48, 3072)
+    output_sum = b_sum[4]
+    a_low, a_other = both(trade_z(a_parts, z))
+    first, second = jnp.where(x == 0, a_low, a_other), jnp.where(x == 0, a_other, a_low)
+    contract_sum = jnp.concatenate([first, second], axis=0).reshape(192, 768).astype(f32)
+
+    result = input_grad(tokens, small, part_near, part_got, middle_grad)
+    g_low, g_other = both(trade_z(g_parts, z))
+    first, second = jnp.where(x == 0, g_low, g_other), jnp.where(x == 0, g_other, g_low)
+    grads = [
+        jnp.concatenate([first[:, at : at + 384], second[:, at : at + 384]], axis=1).astype(f32)
+        for at in (0, 384, 768)
+    ]
+    gains = g_low[:, 1152:1154].astype(f32) + g_other[:, 1152:1154].astype(f32)
+    bias_grad = jnp.concatenate(
+        [first[:12, 1154].reshape(2, 6), second[:12, 1154].reshape(2, 6)], axis=1
+    ).astype(f32)
+    return (
+        layer_output[None], result[None], gains[:, 0], gains[:, 1], *grads,
+        output_sum, expand_sum, contract_sum, bias_grad,
+    )
 
 
 def bucket_table(query_pos, key_pos):
@@ -361,4 +1143,6 @@
         P("fsdp", None),
         P("fsdp", None),
     )
-    return jax.shard_map(local, mesh=mesh, in_specs=in_specs, out_specs=out_specs, check_vma=False)
+    split = mesh.shape["fsdp"] == 16 and mesh.shape["seq"] == 2
+    step = local_split if split else local
+    return jax.shard_map(step, mesh=mesh, in_specs=in_specs, out_specs=out_specs, check_vma=False)

time: 941 us -> 394 us (0.42)
  waiting for transfers between devices: 491 us -> 168 us
  matrix products: 238 us -> 0 us
  Pallas kernels: 0 us -> 130 us
  blocking collectives: 117 us -> 0 us
  starting transfers between devices: 1.15 us -> 44.2 us
  other arithmetic: 56.5 us -> 29 us
  between operations: 18.6 us -> 2.96 us
    reduce_scatter x8 -> x0, waiting for transfers between devices: 320 us -> none  [the longest x1 78.8 us: local(): lax.psum_scatter(expand_grad.astype(jnp.bfloat16), 'fsdp', scatter_dimens...]
    dot_general x26 -> x0, matrix products: 238 us -> none  [the longest x1 47 us: local(): jnp.einsum('hij,ijb->bh', jnp.sum(grad_scores, axis=0), onehot.astype(f32...]
    ppermute x0 -> x44, waiting for transfers between devices: none -> 168 us  [swap(): return lax.ppermute(array, axis, [(i, i ^ bit) for i in range(count)])]
    all_gather x8 -> x0, waiting for transfers between devices: 167 us -> none  [the longest x1 46.1 us: local(): lax.all_gather(contract_weight, 'fsdp', axis=0, tiled=True)]
    pallas_call x0 -> x10, Pallas kernels: none -> 130 us  [the longest x2 34.9 us: attend(): pl.pallas_call(attend_kernel, out_shape=(jax.ShapeDtypeStruct((384, 512),...]
    unnamed x2 -> x0, blocking collectives: 93.2 us -> none
    ppermute x0 -> x44, starting transfers between devices: none -> 44.2 us  [swap(): return lax.ppermute(array, axis, [(i, i ^ bit) for i in range(count)])]
    mul x1 -> x0, other arithmetic: 26.5 us -> none  [local(): grad_scores = probs * (grad_probs - row_delta[..., None])]
  transfers between devices with their start and end apart: 17 -> 44, of which waited for: 12 -> 20; matrix products, arithmetic and copies ran while one was open for 27% -> 10% of each run, Pallas kernels for 0% -> 27%
where the time goes in v1:
time: 394 us; the launch traced here: 391 us
  waiting for transfers between devices  168 us (43%)
  Pallas kernels  130 us (33%)
  starting transfers between devices  44.2 us (11%)
  other arithmetic  29 us (7%)
  local copies, waits for them, and re-layouts  16.6 us (4%)
    ppermute x44, waiting for transfers between devices, swap(): return lax.ppermute(array, axis, [(i, i ^ bit) for i in range(count)])  168 us
    ppermute x44, starting transfers between devices, swap(): return lax.ppermute(array, axis, [(i, i ^ bit) for i in range(count)])  44.2 us
    pallas_call x2, Pallas kernels, attend(): pl.pallas_call(attend_kernel, out_shape=(jax.ShapeDtypeStruct((384, 512),...  34.9 us
    pallas_call x2, Pallas kernels, attend_back(): pl.pallas_call(functools.partial(attend_back_kernel, bool(carry)), out_sh...  23.6 us
    pallas_call x1, Pallas kernels, forward(): pl.pallas_call(forward_kernel, out_shape=(jax.ShapeDtypeStruct((4, 512, 7...  23.4 us
    pallas_call x1, Pallas kernels, project_back(): pl.pallas_call(project_back_kernel, out_shape=(owned, owned, part, part),...  15.6 us
    pallas_call x1, Pallas kernels, expand_weight_grad(): pl.pallas_call(expand_grad_kernel, out_shape=(shape, shape, jax.ShapeDtyp...  13 us
    convert_element_type x4, other arithmetic, trade(): sent = added([take(part, 1 - index, axis) for part in parts]).astype(bf16)  9.22 us
  transfers between devices with their start and end apart: 44, of which 20 were waited for; matrix products, arithmetic and copies ran while one was open for 10% of the time, Pallas kernels for 27%

profile of v1, /device:TPU:0, one launch (start us, length us, event | category | flops | bytes accessed | tf_op | source)
XLA Modules:
  0.0 390.8 jit_solution(298209193806112643)
XLA Ops:
  0.7 0.8 reshape.207
  3.0 0.8 constant_dynamic-slice_fusion.2
  3.8 3.0 collective-permute-start.1
  6.9 1.6 collective-permute-start.2
  8.4 2.6 collective-permute-start.4
  11.2 1.5 collective-permute-start
  13.4 1.0 copy.47
  14.4 0.9 pad_maximum_fusion.2
  15.4 3.6 collective-permute-done.6
  18.9 4.4 %collective-permute-start.13 = (bf16[7,48,768]{2,1,0:T(8,128)(2,1)S(1)}, bf16[7,48,768]{2,1,0:T(8,128)(2,1)S(1)}, u32[]{:S(2)}, u32[]{:S(2)}) collective-permute-start(bf16[7,48,768]{2,1,0:T(8,128)(2,1)S(1)} %pad_maximum_fusion.2), channel_id=1, source_target_pairs={{0,16},{2,18},{4,20},{6,22},{8,24},{10,26},{12,28},{14,30},{16,0},... | collective-permute-start | bytes 1548296 | tf_op jit(solution)/shard_map/ppermute | solution.py:653
  23.4 1.4 collective-permute-start.15
  26.6 3.0 collective-permute-done.3
  31.4 3.8 collective-permute-done.5
  36.0 21.5 %collective-permute-done.13 = bf16[7,48,768]{2,1,0:T(8,128)(2,1)S(1)} collective-permute-done((bf16[7,48,768]{2,1,0:T(8,128)(2,1)S(1)}, bf16[7,48,768]{2,1,0:T(8,128)(2,1)S(1)}, u32[]{:S(2)}, u32[]{:S(2)}) %collective-permute-start.13) | collective-permute-done | bytes 516128 | tf_op jit(solution)/shard_map/ppermute | solution.py:653
  58.0 1.5 collective-permute-start.16
  61.4 10.8 %collective-permute-done.14 = bf16[7,48,768]{2,1,0:T(8,128)(2,1)S(1)} collective-permute-done((bf16[7,48,768]{2,1,0:T(8,128)(2,1)S(1)}, bf16[7,48,768]{2,1,0:T(8,128)(2,1)S(1)}, u32[]{:S(2)}, u32[]{:S(2)}) %collective-permute-start.14) | collective-permute-done | bytes 516128 | tf_op jit(solution)/shard_map/ppermute | solution.py:653
  72.7 10.6 %collective-permute-done.16 = bf16[7,48,768]{2,1,0:T(8,128)(2,1)S(1)} collective-permute-done((bf16[7,48,768]{2,1,0:T(8,128)(2,1)S(1)}, bf16[7,48,768]{2,1,0:T(8,128)(2,1)S(1)}, u32[]{:S(2)}, u32[]{:S(2)}) %collective-permute-start.16) | collective-permute-done | bytes 516128 | tf_op jit(solution)/shard_map/ppermute | solution.py:653
  83.6 8.6 %collective-permute-done.12 = bf16[7,48,768]{2,1,0:T(8,128)(2,1)S(1)} collective-permute-done((bf16[7,48,768]{2,1,0:T(8,128)(2,1)S(1)}, bf16[7,48,768]{2,1,0:T(8,128)(2,1)S(1)}, u32[]{:S(2)}, u32[]{:S(2)}) %collective-permute-start.12) | collective-permute-done | bytes 516128 | tf_op jit(solution)/shard_map/ppermute | solution.py:653
  92.2 1.6 pad_maximum_fusion.near0
  95.1 1.1 slice.73
  96.2 1.6 collective-permute-start.20
  101.5 6.7 %project.1 = (bf16[1152,1024]{1,0:T(8,128)(2,1)}, bf16[1024,768]{1,0:T(8,128)(2,1)}, f32[8,768]{1,0:T(8,128)}) custom-call(s32[4]{0:T(128)} %pad_add_fusion.place, bf16[512,768]{1,0:T(8,128)(2,1)} %bitcast.160, bf16[512,768]{1,0:T(8,128)(2,1)} %collective-permute-done.x_far, bf16[8,48,1280]{2,1,0:T(8,128)(2,1)} %bitcast_dynamic-update-slice_fusion.w_near, ...), custom_call_target="tpu_custom_call" | custom-call | flops 1811939328 | bytes 9000000 | tf_op jit(solution)/shard_map/project/pallas_call | solution.py:94
  109.1 3.5 collective-permute-done.20.nearx1
  112.6 11.7 %collective-permute-done.19.nearx0 = bf16[4,2,48,768]{3,2,1,0:T(8,128)(2,1)} collective-permute-done((bf16[4,2,48,768]{3,2,1,0:T(8,128)(2,1)S(1)}, bf16[4,2,48,768]{3,2,1,0:T(8,128)(2,1)}, u32[]{:S(2)}, u32[]{:S(2)}) %collective-permute-start.19) | collective-permute-done | bytes 589856 | tf_op jit(solution)/shard_map/ppermute | solution.py:653
  125.0 17.5 %attend_theirs.1 = (bf16[384,512]{1,0:T(8,128)(2,1)}, bf16[6,1024,512]{2,1,0:T(8,128)(2,1)}, f32[6,1,512]{2,1,0:T(1,128)}) custom-call(s32[4]{0:T(128)} %add_add_fusion.1.scal, f32[8,32]{1,0:T(8,128)} %pad.14.table, bf16[1152,1024]{1,0:T(8,128)(2,1)} %get-tuple-element.52.q.k.v, bf16[1152,1024]{1,0:T(8,128)(2,1)} %get-tuple-element.52.q.k.v, ...), custom_call_target="tpu_custom_call" | custom-call | flops 1610612736 | bytes 10000000 | tf_op jit(solution)/shard_map/attend_theirs/pallas_call | solution.py:195
  142.6 1.5 collective-permute-start.9
  144.7 17.4 %attend_mine.1 = (bf16[384,512]{1,0:T(8,128)(2,1)}, bf16[6,1024,512]{2,1,0:T(8,128)(2,1)}, f32[6,1,512]{2,1,0:T(1,128)}) custom-call(s32[4]{0:T(128)} %add_add_fusion.scal, f32[8,32]{1,0:T(8,128)} %pad.14.table, bf16[1152,1024]{1,0:T(8,128)(2,1)} %get-tuple-element.52.q.k.v, bf16[1152,1024]{1,0:T(8,128)(2,1)} %get-tuple-element.52.q.k.v, ...), custom_call_target="tpu_custom_call" | custom-call | flops 1610612736 | bytes 10000000 | tf_op jit(solution)/shard_map/attend_mine/pallas_call | solution.py:195
  163.1 23.4 %forward.1 = (bf16[4,512,768]{2,1,0:T(8,128)(2,1)}, bf16[4,512,768]{2,1,0:T(8,128)(2,1)}, bf16[64,48,768]{2,1,0:T(8,128)(2,1)}, f32[512,768]{1,0:T(8,128)}, bf16...) custom-call(s32[4]{0:T(128)} %pad_add_fusion.place, ...), custom_call_target="tpu_custom_call" | custom-call | flops 8499999744 | bytes 20000000 | tf_op jit(solution)/shard_map/forward/pallas_call | solution.py:418
  187.1 8.5 %contract_weight_grad.1 = (bf16[8,4,48,768]{3,2,1,0:T(8,128)(2,1)}, bf16[8,4,48,768]{3,2,1,0:T(8,128)(2,1)}) custom-call(s32[4]{0:T(128)} %pad_add_fusion.place, bf16[4,512,768]{2,1,0:T(8,128)(2,1)} %get-tuple-element.60.hidden, bf16[512,768]{1,0:T(8,128)(2,1)} %bitcast.181), custom_call_target="tpu_custom_call" | custom-call | flops 2415919104 | bytes 9000000 | tf_op jit(solution)/shard_map/contract_weight_grad/pallas_call | solution.py:467
  195.6 11.5 %attend_back_mine.1 = (bf16[384,512]{1,0:T(8,128)(2,1)}, f32[384,1024]{1,0:T(8,128)}, f32[384,1024]{1,0:T(8,128)}, f32[6,384,128]{2,1,0:T(8,128)}, f32[6,8,512]{2,1,0:T(8,128)}) custom-call(s32[4]{0:T(128)} %add_add_fusion.scal, bf16[384,512]{1,0:T(8,128)(2,1)} %get-tuple-element.65.grad, bf16[384,512]{1,0:T(8,128)(2,1)} %get-tuple-element.53.att_near.out, ...), custom_call_target="tpu_custom_call" | custom-call | flops 3221225472 | bytes 12000000 | tf_op jit(solution)/shard_map/attend_back_mine/pallas_call | solution.py:307
  207.9 12.0 %attend_back_theirs.1 = (bf16[384,512]{1,0:T(8,128)(2,1)}, bf16[384,1024]{1,0:T(8,128)(2,1)}, bf16[384,1024]{1,0:T(8,128)(2,1)}, f32[6,384,128]{2,1,0:T(8,128)}, f32[6,8,512]{2,1,0:T(8,128)}) custom-call(s32[4]{0:T(128)} %add_add_fusion.1.scal, bf16[384,512]{1,0:T(8,128)(2,1)} %copy-done.6, bf16[384,512]{1,0:T(8,128)(2,1)} %get-tuple-element.54.out, ...), custom_call_target="tpu_custom_call" | custom-call | flops 3221225472 | bytes 12000000 | tf_op jit(solution)/shard_map/attend_back_theirs/pallas_call | solution.py:307
  220.0 15.6 %project_back.1 = (bf16[8,48,1280]{2,1,0:T(8,128)(2,1)}, bf16[8,48,1280]{2,1,0:T(8,128)(2,1)}, bf16[512,768]{1,0:T(8,128)(2,1)}, bf16[512,768]{1,0:T(8,128)(2,1)}) custom-call(s32[4]{0:T(128)} %pad_add_fusion.place, bf16[512,768]{1,0:T(8,128)(2,1)} %bitcast.162, bf16[512,768]{1,0:T(8,128)(2,1)} %collective-permute-done.x_far, ...), custom_call_target="tpu_custom_call" | custom-call | flops 3623878656 | bytes 16000000 | tf_op jit(solution)/shard_map/project_back/pallas_call | solution.py:608
  236.1 13.0 %expand_weight_grad.1 = (bf16[8,5,48,768]{3,2,1,0:T(8,128)(2,1)}, bf16[8,5,48,768]{3,2,1,0:T(8,128)(2,1)}, bf16[512,768]{1,0:T(8,128)(2,1)}) custom-call(s32[4]{0:T(128)} %pad_add_fusion.place, bf16[512,768]{1,0:T(8,128)(2,1)} %get-tuple-element.56.normed, bf16[4,512,768]{2,1,0:T(8,128)(2,1)} %get-tuple-element.57.pre, ...), custom_call_target="tpu_custom_call" | custom-call | flops 5435817984 | bytes 24000000 | tf_op jit(solution)/shard_map/expand_weight_grad/pallas_call | solution.py:517
  249.2 2.1 fusion.10
  251.9 13.4 %collective-permute-done.26 = bf16[4,48,1280]{2,1,0:T(8,128)(2,1)} collective-permute-done((bf16[4,48,1280]{2,1,0:T(8,128)(2,1)}, bf16[4,48,1280]{2,1,0:T(8,128)(2,1)}, u32[]{:S(2)}, u32[]{:S(2)}) %collective-permute-start.26) | collective-permute-done | bytes 491552 | tf_op jit(solution)/shard_map/ppermute | solution.py:653
  265.2 2.0 fusion.20
  268.5 3.1 collective-permute-start.29
  271.6 1.6 collective-permute-done.27
  273.2 1.6 collective-permute-start.24
  274.8 5.2 %collective-permute-done.28 = bf16[48,1280]{1,0:T(8,128)(2,1)} collective-permute-done((bf16[48,1280]{1,0:T(8,128)(2,1)}, bf16[48,1280]{1,0:T(8,128)(2,1)}, u32[]{:S(2)}, u32[]{:S(2)}) %collective-permute-start.28) | collective-permute-done | bytes 122912 | tf_op jit(solution)/shard_map/ppermute | solution.py:653
  279.9 1.2 fusion.24
  281.2 1.6 collective-permute-start.30
  282.8 2.6 fusion.1
  285.8 8.1 %collective-permute-done.24.far = bf16[512,768]{1,0:T(8,128)(2,1)} collective-permute-done((bf16[512,768]{1,0:T(8,128)(2,1)}, bf16[512,768]{1,0:T(8,128)(2,1)}, u32[]{:S(2)}, u32[]{:S(2)}) %collective-permute-start.24) | collective-permute-done | bytes 786464 | tf_op jit(solution)/shard_map/ppermute | solution.py:653
  294.0 3.9 %input_grad.1 = bf16[512,768]{1,0:T(8,128)(2,1)} custom-call(bf16[512,768]{1,0:T(8,128)(2,1)} %bitcast.163, f32[8,768]{1,0:T(8,128)} %get-tuple-element.51.small, bf16[512,768]{1,0:T(8,128)(2,1)} %get-tuple-element.82.near, bf16[512,768]{1,0:T(8,128)(2,1)} %collective-permute-done.24.far, f32[512,768]{1,0:T(8,128)} %get-tuple-element.84.middle_grad), custom_call_target="tpu_custom_call" | custom-call | flops 7864320 | bytes 6000000 | tf_op jit(solution)/shard_map/input_grad/pallas_call | solution.py:640
  297.9 2.9 fusion
  302.1 16.3 %collective-permute-done.38 = bf16[4,2,2,48,768]{4,3,2,1,0:T(8,128)(2,1)} collective-permute-done((bf16[4,2,2,48,768]{4,3,2,1,0:T(8,128)(2,1)}, bf16[4,2,2,48,768]{4,3,2,1,0:T(8,128)(2,1)}, u32[]{:S(2)}, u32[]{:S(2)}) %collective-permute-start.38) | collective-permute-done | bytes 1179680 | tf_op jit(solution)/shard_map/ppermute | solution.py:653
  318.4 1.6 fusion.2
  323.5 17.5 %collective-permute-done.39 = bf16[4,2,48,768]{3,2,1,0:T(8,128)(2,1)S(1)} collective-permute-done((bf16[4,2,48,768]{3,2,1,0:T(8,128)(2,1)S(1)}, bf16[4,2,48,768]{3,2,1,0:T(8,128)(2,1)S(1)}, u32[]{:S(2)}, u32[]{:S(2)}) %collective-permute-start.39) | collective-permute-done | bytes 589856 | tf_op jit(solution)/shard_map/ppermute | solution.py:653
  341.0 2.3 fusion.13
  344.4 3.7 collective-permute-start.42
  348.1 1.9 fusion.5
  350.8 2.3 collective-permute-done.40
  353.1 1.4 collective-permute-start.35
  355.8 5.0 %collective-permute-done.41 = bf16[2,48,768]{2,1,0:T(8,128)(2,1)S(1)} collective-permute-done((bf16[2,48,768]{2,1,0:T(8,128)(2,1)}, bf16[2,48,768]{2,1,0:T(8,128)(2,1)S(1)}, u32[]{:S(2)}, u32[]{:S(2)}) %collective-permute-start.41) | collective-permute-done | bytes 147488 | tf_op jit(solution)/shard_map/ppermute | solution.py:653
  360.8 1.3 fusion.17
  362.1 1.3 collective-permute-start.43
  363.4 1.6 collective-permute-done.33
  365.0 15.1 %collective-permute-done.34 = bf16[5,48,768]{2,1,0:T(8,128)(2,1)S(1)} collective-permute-done((bf16[5,48,768]{2,1,0:T(8,128)(2,1)S(1)}, bf16[5,48,768]{2,1,0:T(8,128)(2,1)S(1)}, u32[]{:S(2)}, u32[]{:S(2)}) %collective-permute-start.34) | collective-permute-done | bytes 368672 | tf_op jit(solution)/shard_map/ppermute | solution.py:653
  380.2 1.4 fusion.9
  381.5 1.5 collective-permute-start.36
  383.1 0.9 bitcast_convert_fusion
  384.0 5.1 %collective-permute-done.36 = bf16[5,48,768]{2,1,0:T(8,128)(2,1)S(1)} collective-permute-done((bf16[5,48,768]{2,1,0:T(8,128)(2,1)S(1)}, bf16[5,48,768]{2,1,0:T(8,128)(2,1)S(1)}, u32[]{:S(2)}, u32[]{:S(2)}) %collective-permute-start.36) | collective-permute-done | bytes 368672 | tf_op jit(solution)/shard_map/ppermute | solution.py:653
  389.9 0.9 copy.45
  (116 shorter events, 29.3 us)
Async XLA Ops:
  0.6 13.7 %copy-start = (bf16[192,768]{1,0:T(8,128)(2,1)S(1)}, bf16[192,768]{1,0:T(8,128)(2,1)}, u32[]{:S(2)}) copy-start(bf16[192,768]{1,0:T(8,128)(2,1)} %param.20) | copy-start | bytes 884740
  3.8 19.5 %collective-permute-start.1 = (bf16[48,1280]{1,0:T(8,128)(2,1)S(1)}, bf16[48,1280]{1,0:T(8,128)(2,1)S(1)}, u32[]{:S(2)}, u32[]{:S(2)}) collective-permute-start(bf16[48,1280]{1,0:T(8,128)(2,1)S(1)} %fusion.26), channel_id=1, source_target_pairs={{0,4},{2,6},{4,0},{6,2},{8,12},{10,14},{12,8},{14,10},{16,20},{18,... | collective-permute-start | bytes 368648 | tf_op jit(solution)/shard_map/ppermute | solution.py:653
  6.9 17.9 %collective-permute-start.2 = (bf16[48,1280]{1,0:T(8,128)(2,1)S(1)}, bf16[48,1280]{1,0:T(8,128)(2,1)S(1)}, u32[]{:S(2)}, u32[]{:S(2)}) collective-permute-start(bf16[48,1280]{1,0:T(8,128)(2,1)S(1)} %fusion.26), channel_id=1, source_target_pairs={{0,8},{2,10},{4,12},{6,14},{8,0},{10,2},{12,4},{14,6},{16,24},{18,... | collective-permute-start | bytes 368648 | tf_op jit(solution)/shard_map/ppermute | solution.py:653
  8.4 18.1 %collective-permute-start.4 = (bf16[48,1280]{1,0:T(8,128)(2,1)S(1)}, bf16[48,1280]{1,0:T(8,128)(2,1)S(1)}, u32[]{:S(2)}, u32[]{:S(2)}) collective-permute-start(bf16[48,1280]{1,0:T(8,128)(2,1)S(1)} %fusion.26), channel_id=1, source_target_pairs={{0,16},{2,18},{4,20},{6,22},{8,24},{10,26},{12,28},{14,30},{16,0},... | collective-permute-start | bytes 368648 | tf_op jit(solution)/shard_map/ppermute | solution.py:653
  11.0 7.9 %collective-permute-start.6 = (bf16[48,1280]{1,0:T(8,128)(2,1)S(1)}, bf16[48,1280]{1,0:T(8,128)(2,1)S(1)}, u32[]{:S(2)}, u32[]{:S(2)}) collective-permute-start(bf16[48,1280]{1,0:T(8,128)(2,1)S(1)} %fusion.26), channel_id=1, source_target_pairs={{0,24},{2,26},{4,28},{6,30},{8,16},{10,18},{12,20},{14,22},{16,8},... | collective-permute-start | bytes 368648 | tf_op jit(solution)/shard_map/ppermute | solution.py:653
  11.2 86.5 %collective-permute-start = (bf16[512,768]{1,0:T(8,128)(2,1)}, bf16[512,768]{1,0:T(8,128)(2,1)}, u32[]{:S(2)}, u32[]{:S(2)}) collective-permute-start(bf16[512,768]{1,0:T(8,128)(2,1)} %bitcast.159), channel_id=1, source_target_pairs={{0,1},{1,0},{2,3},{3,2},{4,5},{5,4},{6,7},{7,6},{8,9},{9,8},{10,11... | collective-permute-start | bytes 2359304 | tf_op jit(solution)/shard_map/ppermute | solution.py:653
  18.9 38.6 %collective-permute-start.13 = (bf16[7,48,768]{2,1,0:T(8,128)(2,1)S(1)}, bf16[7,48,768]{2,1,0:T(8,128)(2,1)S(1)}, u32[]{:S(2)}, u32[]{:S(2)}) collective-permute-start(bf16[7,48,768]{2,1,0:T(8,128)(2,1)S(1)} %pad_maximum_fusion.2), channel_id=1, source_target_pairs={{0,16},{2,18},{4,20},{6,22},{8,24},{10,26},{12,28},{14,30},{16,0},... | collective-permute-start | bytes 1548296 | tf_op jit(solution)/shard_map/ppermute | solution.py:653
  23.4 34.7 %collective-permute-start.15 = (bf16[7,48,768]{2,1,0:T(8,128)(2,1)S(1)}, bf16[7,48,768]{2,1,0:T(8,128)(2,1)S(1)}, u32[]{:S(2)}, u32[]{:S(2)}) collective-permute-start(bf16[7,48,768]{2,1,0:T(8,128)(2,1)S(1)} %pad_maximum_fusion.2), channel_id=1, source_target_pairs={{0,24},{2,26},{4,28},{6,30},{8,16},{10,18},{12,20},{14,22},{16,8},... | collective-permute-start | bytes 1548296 | tf_op jit(solution)/shard_map/ppermute | solution.py:653
  24.7 4.9 %collective-permute-start.3 = (bf16[48,1280]{1,0:T(8,128)(2,1)S(1)}, bf16[48,1280]{1,0:T(8,128)(2,1)S(1)}, u32[]{:S(2)}, u32[]{:S(2)}) collective-permute-start(bf16[48,1280]{1,0:T(8,128)(2,1)S(1)} %collective-permute-done.2), channel_id=1, source_target_pairs={{0,4},{2,6},{4,0},{6,2},{8,12},{10,14},{12,8},{14,10},{16,20},{18,... | collective-permute-start | bytes 368648 | tf_op jit(solution)/shard_map/ppermute | solution.py:653
  26.6 33.6 %collective-permute-start.11 = (bf16[7,48,768]{2,1,0:T(8,128)(2,1)S(1)}, bf16[7,48,768]{2,1,0:T(8,128)(2,1)S(1)}, u32[]{:S(2)}, u32[]{:S(2)}) collective-permute-start(bf16[7,48,768]{2,1,0:T(8,128)(2,1)S(1)} %pad_maximum_fusion.2), channel_id=1, source_target_pairs={{0,8},{2,10},{4,12},{6,14},{8,0},{10,2},{12,4},{14,6},{16,24},{18,... | collective-permute-start | bytes 1548296 | tf_op jit(solution)/shard_map/ppermute | solution.py:653
  29.6 5.7 %collective-permute-start.5 = (bf16[48,1280]{1,0:T(8,128)(2,1)S(1)}, bf16[48,1280]{1,0:T(8,128)(2,1)S(1)}, u32[]{:S(2)}, u32[]{:S(2)}) collective-permute-start(bf16[48,1280]{1,0:T(8,128)(2,1)S(1)} %collective-permute-done.4), channel_id=1, source_target_pairs={{0,4},{2,6},{4,0},{6,2},{8,12},{10,14},{12,8},{14,10},{16,20},{18,... | collective-permute-start | bytes 368648 | tf_op jit(solution)/shard_map/ppermute | solution.py:653
  35.2 48.4 %collective-permute-start.10 = (bf16[7,48,768]{2,1,0:T(8,128)(2,1)S(1)}, bf16[7,48,768]{2,1,0:T(8,128)(2,1)S(1)}, u32[]{:S(2)}, u32[]{:S(2)}) collective-permute-start(bf16[7,48,768]{2,1,0:T(8,128)(2,1)S(1)} %pad_maximum_fusion.2), channel_id=1, source_target_pairs={{0,4},{2,6},{4,0},{6,2},{8,12},{10,14},{12,8},{14,10},{16,20},{18,... | collective-permute-start | bytes 1548296 | tf_op jit(solution)/shard_map/ppermute | solution.py:653
  57.5 14.7 %collective-permute-start.14 = (bf16[7,48,768]{2,1,0:T(8,128)(2,1)S(1)}, bf16[7,48,768]{2,1,0:T(8,128)(2,1)S(1)}, u32[]{:S(2)}, u32[]{:S(2)}) collective-permute-start(bf16[7,48,768]{2,1,0:T(8,128)(2,1)S(1)} %collective-permute-done.13), channel_id=1, source_target_pairs={{0,4},{2,6},{4,0},{6,2},{8,12},{10,14},{12,8},{14,10},{16,20},{18,... | collective-permute-start | bytes 1548296 | tf_op jit(solution)/shard_map/ppermute | solution.py:653
  58.0 25.2 %collective-permute-start.16 = (bf16[7,48,768]{2,1,0:T(8,128)(2,1)S(1)}, bf16[7,48,768]{2,1,0:T(8,128)(2,1)S(1)}, u32[]{:S(2)}, u32[]{:S(2)}) collective-permute-start(bf16[7,48,768]{2,1,0:T(8,128)(2,1)S(1)} %collective-permute-done.15), channel_id=1, source_target_pairs={{0,4},{2,6},{4,0},{6,2},{8,12},{10,14},{12,8},{14,10},{16,20},{18,... | collective-permute-start | bytes 1548296 | tf_op jit(solution)/shard_map/ppermute | solution.py:653
  60.2 32.1 %collective-permute-start.12 = (bf16[7,48,768]{2,1,0:T(8,128)(2,1)S(1)}, bf16[7,48,768]{2,1,0:T(8,128)(2,1)S(1)}, u32[]{:S(2)}, u32[]{:S(2)}) collective-permute-start(bf16[7,48,768]{2,1,0:T(8,128)(2,1)S(1)} %collective-permute-done.11), channel_id=1, source_target_pairs={{0,4},{2,6},{4,0},{6,2},{8,12},{10,14},{12,8},{14,10},{16,20},{18,... | collective-permute-start | bytes 1548296 | tf_op jit(solution)/shard_map/ppermute | solution.py:653
  72.2 21.7 %collective-permute-start.7 = (bf16[48,1280]{1,0:T(8,128)(2,1)S(1)}, bf16[48,1280]{1,0:T(8,128)(2,1)S(1)}, u32[]{:S(2)}, u32[]{:S(2)}) collective-permute-start(bf16[48,1280]{1,0:T(8,128)(2,1)S(1)} %collective-permute-done.6), channel_id=1, source_target_pairs={{0,4},{2,6},{4,0},{6,2},{8,12},{10,14},{12,8},{14,10},{16,20},{18,... | collective-permute-start | bytes 368648 | tf_op jit(solution)/shard_map/ppermute | solution.py:653
  83.5 11.6 %copy-start.2 = (bf16[4,7,48,768]{3,2,1,0:T(8,128)(2,1)}, bf16[4,7,48,768]{3,2,1,0:T(8,128)(2,1)S(1)}, u32[]{:S(2)}) copy-start(bf16[4,7,48,768]{3,2,1,0:T(8,128)(2,1)S(1)} %pad_maximum_fusion.1.near1) | copy-start | bytes 6193156
  83.5 78.7 %collective-permute-start.18 = (bf16[4,7,48,768]{3,2,1,0:T(8,128)(2,1)S(1)}, bf16[4,7,48,768]{3,2,1,0:T(8,128)(2,1)}, u32[]{:S(2)}, u32[]{:S(2)}) collective-permute-start(bf16[4,7,48,768]{3,2,1,0:T(8,128)(2,1)S(1)} %pad_maximum_fusion.1.near1), channel_id=1, source_target_pairs={{0,2},{2,0},{4,6},{6,4},{8,10},{10,8},{12,14},{14,12},{16,18},{18,... | collective-permute-start | bytes 6193160 | tf_op jit(solution)/shard_map/ppermute | solution.py:653
  93.9 68.3 %collective-permute-start.17 = (bf16[4,7,48,768]{3,2,1,0:T(8,128)(2,1)}, bf16[4,7,48,768]{3,2,1,0:T(8,128)(2,1)}, u32[]{:S(2)}, u32[]{:S(2)}) collective-permute-start(bf16[4,7,48,768]{3,2,1,0:T(8,128)(2,1)} %pad_maximum_fusion.near0), channel_id=1, source_target_pairs={{0,2},{2,0},{4,6},{6,4},{8,10},{10,8},{12,14},{14,12},{16,18},{18,... | collective-permute-start | bytes 6193160 | tf_op jit(solution)/shard_map/ppermute | solution.py:653
  94.6 6.9 %collective-permute-start.8 = (bf16[8,48,1280]{2,1,0:T(8,128)(2,1)}, bf16[8,48,1280]{2,1,0:T(8,128)(2,1)}, u32[]{:S(2)}, u32[]{:S(2)}) collective-permute-start(bf16[8,48,1280]{2,1,0:T(8,128)(2,1)} %bitcast_dynamic-update-slice_fusion.w_near), channel_id=1, source_target_pairs={{0,2},{2,0},{4,6},{6,4},{8,10},{10,8},{12,14},{14,12},{16,18},{18,... | collective-permute-start | bytes 2949128 | tf_op jit(solution)/shard_map/ppermute | solution.py:653
  96.2 16.4 %collective-permute-start.20 = (bf16[4,2,48,768]{3,2,1,0:T(8,128)(2,1)S(1)}, bf16[4,2,48,768]{3,2,1,0:T(8,128)(2,1)}, u32[]{:S(2)}, u32[]{:S(2)}) collective-permute-start(bf16[4,2,48,768]{3,2,1,0:T(8,128)(2,1)S(1)} %slice.74), channel_id=1, source_target_pairs={{0,1},{1,0},{2,3},{3,2},{4,5},{5,4},{6,7},{7,6},{8,9},{9,8},{10,11... | collective-permute-start | bytes 1769480 | tf_op jit(solution)/shard_map/ppermute | solution.py:653
  97.8 26.5 %collective-permute-start.19 = (bf16[4,2,48,768]{3,2,1,0:T(8,128)(2,1)S(1)}, bf16[4,2,48,768]{3,2,1,0:T(8,128)(2,1)}, u32[]{:S(2)}, u32[]{:S(2)}) collective-permute-start(bf16[4,2,48,768]{3,2,1,0:T(8,128)(2,1)S(1)} %slice.73), channel_id=1, source_target_pairs={{0,1},{1,0},{2,3},{3,2},{4,5},{5,4},{6,7},{7,6},{8,9},{9,8},{10,11... | collective-permute-start | bytes 1769480 | tf_op jit(solution)/shard_map/ppermute | solution.py:653
  112.6 49.6 %collective-permute-start.22 = (bf16[4,2,48,768]{3,2,1,0:T(8,128)(2,1)}, bf16[4,2,48,768]{3,2,1,0:T(8,128)(2,1)S(1)}, u32[]{:S(2)}, u32[]{:S(2)}) collective-permute-start(bf16[4,2,48,768]{3,2,1,0:T(8,128)(2,1)} %collective-permute-done.20.nearx1), channel_id=1, source_target_pairs={{0,2},{2,0},{4,6},{6,4},{8,10},{10,8},{12,14},{14,12},{16,18},{18,... | collective-permute-start | bytes 1769480 | tf_op jit(solution)/shard_map/ppermute | solution.py:653
  124.3 37.9 %collective-permute-start.21 = (bf16[4,2,48,768]{3,2,1,0:T(8,128)(2,1)}, bf16[4,2,48,768]{3,2,1,0:T(8,128)(2,1)}, u32[]{:S(2)}, u32[]{:S(2)}) collective-permute-start(bf16[4,2,48,768]{3,2,1,0:T(8,128)(2,1)} %collective-permute-done.19.nearx0), channel_id=1, source_target_pairs={{0,2},{2,0},{4,6},{6,4},{8,10},{10,8},{12,14},{14,12},{16,18},{18,... | collective-permute-start | bytes 1769480 | tf_op jit(solution)/shard_map/ppermute | solution.py:653
  142.6 19.6 %collective-permute-start.9 = (bf16[384,512]{1,0:T(8,128)(2,1)}, bf16[384,512]{1,0:T(8,128)(2,1)S(1)}, u32[]{:S(2)}, u32[]{:S(2)}) collective-permute-start(bf16[384,512]{1,0:T(8,128)(2,1)} %get-tuple-element.54.out), channel_id=1, source_target_pairs={{0,1},{1,0},{2,3},{3,2},{4,5},{5,4},{6,7},{7,6},{8,9},{9,8},{10,11... | collective-permute-start | bytes 1179656 | tf_op jit(solution)/shard_map/ppermute | solution.py:653
  162.1 0.7 copy-start.10
  162.2 0.9 copy-start.9
  186.5 20.7 %collective-permute-start.23 = (bf16[384,512]{1,0:T(8,128)(2,1)}, bf16[384,512]{1,0:T(8,128)(2,1)S(1)}, u32[]{:S(2)}, u32[]{:S(2)}) collective-permute-start(bf16[384,512]{1,0:T(8,128)(2,1)} %get-tuple-element.69), channel_id=1, source_target_pairs={{0,1},{1,0},{2,3},{3,2},{4,5},{5,4},{6,7},{7,6},{8,9},{9,8},{10,11... | collective-permute-start | bytes 1179656 | tf_op jit(solution)/shard_map/ppermute | solution.py:653
  195.6 87.2 %collective-permute-start.37 = (bf16[8,4,48,768]{3,2,1,0:T(8,128)(2,1)}, bf16[8,4,48,768]{3,2,1,0:T(8,128)(2,1)}, u32[]{:S(2)}, u32[]{:S(2)}) collective-permute-start(bf16[8,4,48,768]{3,2,1,0:T(8,128)(2,1)} %get-tuple-element.90), channel_id=1, source_target_pairs={{0,2},{2,0},{4,6},{6,4},{8,10},{10,8},{12,14},{14,12},{16,18},{18,... | collective-permute-start | bytes 7077896 | tf_op jit(solution)/shard_map/ppermute | solution.py:653
  207.2 0.7 copy-start.6
  235.6 13.7 %collective-permute-start.25 = (bf16[8,48,1280]{2,1,0:T(8,128)(2,1)}, bf16[8,48,1280]{2,1,0:T(8,128)(2,1)}, u32[]{:S(2)}, u32[]{:S(2)}) collective-permute-start(bf16[8,48,1280]{2,1,0:T(8,128)(2,1)} %get-tuple-element.86), channel_id=1, source_target_pairs={{0,2},{2,0},{4,6},{6,4},{8,10},{10,8},{12,14},{14,12},{16,18},{18,... | collective-permute-start | bytes 2949128 | tf_op jit(solution)/shard_map/ppermute | solution.py:653
  236.1 13.1 %copy-start.5 = (bf16[8,48,1280]{2,1,0:T(8,128)(2,1)S(1)}, bf16[8,48,1280]{2,1,0:T(8,128)(2,1)}, u32[]{:S(2)}) copy-start(bf16[8,48,1280]{2,1,0:T(8,128)(2,1)} %get-tuple-element.85) | copy-start | bytes 2949124
  249.1 33.7 %copy-start.4 = (bf16[8,4,48,768]{3,2,1,0:T(8,128)(2,1)S(1)}, bf16[8,4,48,768]{3,2,1,0:T(8,128)(2,1)}, u32[]{:S(2)}) copy-start(bf16[8,4,48,768]{3,2,1,0:T(8,128)(2,1)} %get-tuple-element.89) | copy-start | bytes 7077892
  249.1 48.8 %collective-permute-start.31 = (bf16[8,5,48,768]{3,2,1,0:T(8,128)(2,1)}, bf16[8,5,48,768]{3,2,1,0:T(8,128)(2,1)}, u32[]{:S(2)}, u32[]{:S(2)}) collective-permute-start(bf16[8,5,48,768]{3,2,1,0:T(8,128)(2,1)} %get-tuple-element.88), channel_id=1, source_target_pairs={{0,2},{2,0},{4,6},{6,4},{8,10},{10,8},{12,14},{14,12},{16,18},{18,... | collective-permute-start | bytes 8847368 | tf_op jit(solution)/shard_map/ppermute | solution.py:653
  251.3 13.9 %collective-permute-start.26 = (bf16[4,48,1280]{2,1,0:T(8,128)(2,1)}, bf16[4,48,1280]{2,1,0:T(8,128)(2,1)}, u32[]{:S(2)}, u32[]{:S(2)}) collective-permute-start(bf16[4,48,1280]{2,1,0:T(8,128)(2,1)} %fusion.10), channel_id=1, source_target_pairs={{0,4},{2,6},{4,0},{6,2},{8,12},{10,14},{12,8},{14,10},{16,20},{18,... | collective-permute-start | bytes 1474568 | tf_op jit(solution)/shard_map/ppermute | solution.py:653
  267.2 6.0 %collective-permute-start.27 = (bf16[48,1280]{1,0:T(8,128)(2,1)S(1)}, bf16[48,1280]{1,0:T(8,128)(2,1)}, u32[]{:S(2)}, u32[]{:S(2)}) collective-permute-start(bf16[48,1280]{1,0:T(8,128)(2,1)S(1)} %get-tuple-element.99), channel_id=1, source_target_pairs={{0,8},{2,10},{4,12},{6,14},{8,0},{10,2},{12,4},{14,6},{16,24},{18,... | collective-permute-start | bytes 368648 | tf_op jit(solution)/shard_map/ppermute | solution.py:653
  267.8 12.1 %collective-permute-start.28 = (bf16[48,1280]{1,0:T(8,128)(2,1)}, bf16[48,1280]{1,0:T(8,128)(2,1)}, u32[]{:S(2)}, u32[]{:S(2)}) collective-permute-start(bf16[48,1280]{1,0:T(8,128)(2,1)} %get-tuple-element.101), channel_id=1, source_target_pairs={{0,16},{2,18},{4,20},{6,22},{8,24},{10,26},{12,28},{14,30},{16,0},... | collective-permute-start | bytes 368648 | tf_op jit(solution)/shard_map/ppermute | solution.py:653
  268.5 11.4 %collective-permute-start.29 = (bf16[48,1280]{1,0:T(8,128)(2,1)S(1)}, bf16[48,1280]{1,0:T(8,128)(2,1)}, u32[]{:S(2)}, u32[]{:S(2)}) collective-permute-start(bf16[48,1280]{1,0:T(8,128)(2,1)S(1)} %get-tuple-element.100), channel_id=1, source_target_pairs={{0,24},{2,26},{4,28},{6,30},{8,16},{10,18},{12,20},{14,22},{16,8},... | collective-permute-start | bytes 368648 | tf_op jit(solution)/shard_map/ppermute | solution.py:653
  273.2 20.8 %collective-permute-start.24 = (bf16[512,768]{1,0:T(8,128)(2,1)}, bf16[512,768]{1,0:T(8,128)(2,1)}, u32[]{:S(2)}, u32[]{:S(2)}) collective-permute-start(bf16[512,768]{1,0:T(8,128)(2,1)} %get-tuple-element.83), channel_id=1, source_target_pairs={{0,1},{1,0},{2,3},{3,2},{4,5},{5,4},{6,7},{7,6},{8,9},{9,8},{10,11... | collective-permute-start | bytes 2359304 | tf_op jit(solution)/shard_map/ppermute | solution.py:653
  281.2 16.7 %collective-permute-start.30 = (bf16[48,1280]{1,0:T(8,128)(2,1)S(1)}, bf16[48,1280]{1,0:T(8,128)(2,1)S(1)}, u32[]{:S(2)}, u32[]{:S(2)}) collective-permute-start(bf16[48,1280]{1,0:T(8,128)(2,1)S(1)} %fusion.24), channel_id=1, source_target_pairs={{0,1},{1,0},{2,3},{3,2},{4,5},{5,4},{6,7},{7,6},{8,9},{9,8},{10,11... | collective-permute-start | bytes 368648 | tf_op jit(solution)/shard_map/ppermute | solution.py:653
  285.4 33.0 %collective-permute-start.38 = (bf16[4,2,2,48,768]{4,3,2,1,0:T(8,128)(2,1)}, bf16[4,2,2,48,768]{4,3,2,1,0:T(8,128)(2,1)}, u32[]{:S(2)}, u32[]{:S(2)}) collective-permute-start(bf16[4,2,2,48,768]{4,3,2,1,0:T(8,128)(2,1)} %fusion.1), channel_id=1, source_target_pairs={{0,1},{1,0},{2,3},{3,2},{4,5},{5,4},{6,7},{7,6},{8,9},{9,8},{10,11... | collective-permute-start | bytes 3538952 | tf_op jit(solution)/shard_map/ppermute | solution.py:653
  294.0 4.0 %copy-start.3 = (bf16[8,5,48,768]{3,2,1,0:T(8,128)(2,1)S(1)}, bf16[8,5,48,768]{3,2,1,0:T(8,128)(2,1)}, u32[]{:S(2)}) copy-start(bf16[8,5,48,768]{3,2,1,0:T(8,128)(2,1)} %get-tuple-element.87) | copy-start | bytes 8847364
  300.9 47.2 %collective-permute-start.32 = (bf16[4,5,48,768]{3,2,1,0:T(8,128)(2,1)}, bf16[4,5,48,768]{3,2,1,0:T(8,128)(2,1)}, u32[]{:S(2)}, u32[]{:S(2)}) collective-permute-start(bf16[4,5,48,768]{3,2,1,0:T(8,128)(2,1)} %fusion), channel_id=1, source_target_pairs={{0,4},{2,6},{4,0},{6,2},{8,12},{10,14},{12,8},{14,10},{16,20},{18,... | collective-permute-start | bytes 4423688 | tf_op jit(solution)/shard_map/ppermute | solution.py:653
  320.0 21.0 %collective-permute-start.39 = (bf16[4,2,48,768]{3,2,1,0:T(8,128)(2,1)S(1)}, bf16[4,2,48,768]{3,2,1,0:T(8,128)(2,1)S(1)}, u32[]{:S(2)}, u32[]{:S(2)}) collective-permute-start(bf16[4,2,48,768]{3,2,1,0:T(8,128)(2,1)S(1)} %fusion.2), channel_id=1, source_target_pairs={{0,4},{2,6},{4,0},{6,2},{8,12},{10,14},{12,8},{14,10},{16,20},{18,... | collective-permute-start | bytes 1769480 | tf_op jit(solution)/shard_map/ppermute | solution.py:653
  343.4 9.8 %collective-permute-start.40 = (bf16[2,48,768]{2,1,0:T(8,128)(2,1)}, bf16[2,48,768]{2,1,0:T(8,128)(2,1)}, u32[]{:S(2)}, u32[]{:S(2)}) collective-permute-start(bf16[2,48,768]{2,1,0:T(8,128)(2,1)} %get-tuple-element.96), channel_id=1, source_target_pairs={{0,8},{2,10},{4,12},{6,14},{8,0},{10,2},{12,4},{14,6},{16,24},{18,... | collective-permute-start | bytes 442376 | tf_op jit(solution)/shard_map/ppermute | solution.py:653
  343.9 16.9 %collective-permute-start.41 = (bf16[2,48,768]{2,1,0:T(8,128)(2,1)}, bf16[2,48,768]{2,1,0:T(8,128)(2,1)S(1)}, u32[]{:S(2)}, u32[]{:S(2)}) collective-permute-start(bf16[2,48,768]{2,1,0:T(8,128)(2,1)} %get-tuple-element.98), channel_id=1, source_target_pairs={{0,16},{2,18},{4,20},{6,22},{8,24},{10,26},{12,28},{14,30},{16,0},... | collective-permute-start | bytes 442376 | tf_op jit(solution)/shard_map/ppermute | solution.py:653
  344.4 10.7 %copy-start.7 = (bf16[48,384]{1,0:T(8,128)(2,1)S(1)}, bf16[48,384]{1,0:T(8,128)(2,1)}, u32[]{:S(2)}) copy-start(bf16[48,384]{1,0:T(8,128)(2,1)} %get-tuple-element.108) | copy-start | bytes 110596
  344.4 10.7 %copy-start.8 = (bf16[48,384]{1,0:T(8,128)(2,1)S(1)}, bf16[48,384]{1,0:T(8,128)(2,1)}, u32[]{:S(2)}) copy-start(bf16[48,384]{1,0:T(8,128)(2,1)} %get-tuple-element.111) | copy-start | bytes 110596
  344.4 16.4 %collective-permute-start.42 = (bf16[2,48,768]{2,1,0:T(8,128)(2,1)}, bf16[2,48,768]{2,1,0:T(8,128)(2,1)S(1)}, u32[]{:S(2)}, u32[]{:S(2)}) collective-permute-start(bf16[2,48,768]{2,1,0:T(8,128)(2,1)} %get-tuple-element.97), channel_id=1, source_target_pairs={{0,24},{2,26},{4,28},{6,30},{8,16},{10,18},{12,20},{14,22},{16,8},... | collective-permute-start | bytes 442376 | tf_op jit(solution)/shard_map/ppermute | solution.py:653
  350.1 15.0 %collective-permute-start.33 = (bf16[5,48,768]{2,1,0:T(8,128)(2,1)S(1)}, bf16[5,48,768]{2,1,0:T(8,128)(2,1)S(1)}, u32[]{:S(2)}, u32[]{:S(2)}) collective-permute-start(bf16[5,48,768]{2,1,0:T(8,128)(2,1)S(1)} %get-tuple-element.93), channel_id=1, source_target_pairs={{0,8},{2,10},{4,12},{6,14},{8,0},{10,2},{12,4},{14,6},{16,24},{18,... | collective-permute-start | bytes 1105928 | tf_op jit(solution)/shard_map/ppermute | solution.py:653
  350.1 30.0 %collective-permute-start.34 = (bf16[5,48,768]{2,1,0:T(8,128)(2,1)S(1)}, bf16[5,48,768]{2,1,0:T(8,128)(2,1)S(1)}, u32[]{:S(2)}, u32[]{:S(2)}) collective-permute-start(bf16[5,48,768]{2,1,0:T(8,128)(2,1)S(1)} %get-tuple-element.95), channel_id=1, source_target_pairs={{0,16},{2,18},{4,20},{6,22},{8,24},{10,26},{12,28},{14,30},{16,0},... | collective-permute-start | bytes 1105928 | tf_op jit(solution)/shard_map/ppermute | solution.py:653
  353.1 27.0 %collective-permute-start.35 = (bf16[5,48,768]{2,1,0:T(8,128)(2,1)S(1)}, bf16[5,48,768]{2,1,0:T(8,128)(2,1)S(1)}, u32[]{:S(2)}, u32[]{:S(2)}) collective-permute-start(bf16[5,48,768]{2,1,0:T(8,128)(2,1)S(1)} %get-tuple-element.94), channel_id=1, source_target_pairs={{0,24},{2,26},{4,28},{6,30},{8,16},{10,18},{12,20},{14,22},{16,8},... | collective-permute-start | bytes 1105928 | tf_op jit(solution)/shard_map/ppermute | solution.py:653
  362.1 20.9 %collective-permute-start.43 = (bf16[2,48,768]{2,1,0:T(8,128)(2,1)S(1)}, bf16[2,48,768]{2,1,0:T(8,128)(2,1)S(1)}, u32[]{:S(2)}, u32[]{:S(2)}) collective-permute-start(bf16[2,48,768]{2,1,0:T(8,128)(2,1)S(1)} %fusion.17), channel_id=1, source_target_pairs={{0,1},{1,0},{2,3},{3,2},{4,5},{5,4},{6,7},{7,6},{8,9},{9,8},{10,11... | collective-permute-start | bytes 442376 | tf_op jit(solution)/shard_map/ppermute | solution.py:653
  381.5 7.6 %collective-permute-start.36 = (bf16[5,48,768]{2,1,0:T(8,128)(2,1)S(1)}, bf16[5,48,768]{2,1,0:T(8,128)(2,1)S(1)}, u32[]{:S(2)}, u32[]{:S(2)}) collective-permute-start(bf16[5,48,768]{2,1,0:T(8,128)(2,1)S(1)} %fusion.9), channel_id=1, source_target_pairs={{0,1},{1,0},{2,3},{3,2},{4,5},{5,4},{6,7},{7,6},{8,9},{9,8},{10,11... | collective-permute-start | bytes 1105928 | tf_op jit(solution)/shard_map/ppermute | solution.py:653
  383.1 7.7 %copy-start.1 = (bf16[192,768]{1,0:T(8,128)(2,1)S(1)}, bf16[192,768]{1,0:T(8,128)(2,1)}, u32[]{:S(2)}) copy-start(bf16[192,768]{1,0:T(8,128)(2,1)} %param.20) | copy-start | bytes 884740

commit v2 on v1

--- a/solution.py
+++ b/solution.py
@@ -1,4 +1,6 @@
 import functools
+import itertools
+import math
 
 import jax
 import jax.numpy as jnp
@@ -30,7 +32,7 @@
 
 
 def cost(flops, byte_count, exps=0):
-    return pl.CostEstimate(flops=flops, bytes_accessed=byte_count, transcendentals=exps)
+    return pl.CostEstimate(flops=flops // 1000, bytes_accessed=byte_count // 1000, transcendentals=exps // 1000)
 
 
 def bucket_of(offset):
@@ -46,17 +48,86 @@
     return lax.broadcasted_iota(jnp.int32, shape, dim)
 
 
+def narrow_kernel(place, q, k, v, gain_one, gain_two, table, out, side, sems):
+    x = place[3]
+    column = pl.multiple_of(x * 384, 128)
+    copies = []
+    for at, weight in enumerate((q, k, v)):
+        source = weight.at[:, pl.ds(column, 384)]
+        copy = pltpu.make_async_copy(source, out.at[:, at * 384 : at * 384 + 384], sems.at[at])
+        copy.start()
+        copies.append(copy)
+    side[...] = jnp.zeros((8, 128), f32)
+    side[0:1, 0:48] = gain_one[...].astype(f32)
+    side[1:2, 0:48] = gain_two[...].astype(f32)
+    side[2:3, 0:12] = table[0:1].astype(f32)
+    side[2:3, 12:24] = table[1:2].astype(f32)
+    wide = jnp.concatenate([side[...], jnp.zeros((120, 128), f32)], axis=0).T
+    out[:, 1152:1280] = wide[0:48].astype(bf16)
+    for copy in copies:
+        copy.wait()
+
+
+def narrow_shard(place, q, k, v, gain_one, gain_two, table):
+    return pl.pallas_call(
+        narrow_kernel,
+        out_shape=jax.ShapeDtypeStruct((48, 1280), bf16),
+        in_specs=[SCALARS, ANY, ANY, ANY, FULL, FULL, FULL],
+        out_specs=FULL,
+        scratch_shapes=[pltpu.VMEM((8, 128), f32), pltpu.SemaphoreType.DMA((3,))],
+        compiler_params=params(),
+        cost_estimate=cost(1000, 250_000),
+        name="narrow_shard",
+    )(place, q, k, v, gain_one.reshape(1, 48), gain_two.reshape(1, 48), table)
+
+
+def wide_kernel(place, expand, output, contract, out, side, sems):
+    x = place[3]
+    pieces = [(expand.at[:, at * 768 : at * 768 + 768], out.at[at]) for at in range(4)]
+    pieces.append((output, out.at[4]))
+    for at in range(2):
+        row = pl.multiple_of(x * 96 + at * 48, 16)
+        pieces.append((contract.at[pl.ds(row, 48)], out.at[5 + at]))
+        row = pl.multiple_of((1 - x) * 96 + at * 48, 16)
+        pieces.append((contract.at[pl.ds(row, 48)], side.at[at]))
+    copies = [pltpu.make_async_copy(*piece, sems.at[at]) for at, piece in enumerate(pieces)]
+    for copy in copies:
+        copy.start()
+    for copy in copies:
+        copy.wait()
+
+
+def wide_shard(place, expand, output, contract):
+    return pl.pallas_call(
+        wide_kernel,
+        out_shape=(
+            jax.ShapeDtypeStruct((7, 48, 768), bf16), jax.ShapeDtypeStruct((2, 48, 768), bf16),
+        ),
+        in_specs=[SCALARS, ANY, ANY, ANY],
+        out_specs=(FULL, FULL),
+        scratch_shapes=[pltpu.SemaphoreType.DMA((9,))],
+        compiler_params=params(),
+        cost_estimate=cost(1000, 900_000),
+        name="wide_shard",
+    )(place, expand, output, contract)
+
+
+def eight(blocks):
+    own, across, along, both = blocks
+    return [own, across] + [ref.at[at] for at in range(3) for ref in (along, both)]
+
+
 def place_blocks(place, near, far, dest, sems):
     z, y, c = place[0], place[1], place[2]
     copies = []
+    near, far = eight(near), eight(far)
     for turn in range(4):
         for dy in range(2):
             owner = ((jnp.bitwise_xor(z, turn) * 2) + jnp.bitwise_xor(y, dy)) * 2
             for other, source in enumerate((near, far)):
                 row = pl.multiple_of((owner + jnp.bitwise_xor(c, other)) * 48, 16)
-                index = turn * 2 + dy
                 copy = pltpu.make_async_copy(
-                    source.at[index], dest.at[pl.ds(row, 48)], sems.at[len(copies)]
+                    source[turn * 2 + dy], dest.at[pl.ds(row, 48)], sems.at[len(copies)]
                 )
                 copy.start()
                 copies.append(copy)
@@ -73,7 +144,13 @@
     return copies
 
 
-def project_kernel(place, x_near, x_far, w_near, w_far, qkv, normed, small, xs, w, sems, xsems):
+def first_query(place, mine):
+    return (place[3] if mine else 1 - place[3]) * 512
+
+
+def project_kernel(place, x_near, x_far, *refs):
+    w_near, w_far, refs = refs[:4], refs[4:8], refs[8:]
+    qkv, normed, small, table, tiles, xs, w, sems, xsems = refs
     tokens = place_tokens(place[3], x_near, x_far, xs, xsems, 512)
     blocks = place_blocks(place, w_near, w_far, w, sems)
     for copy in tokens + blocks:
@@ -81,6 +158,24 @@
     side = w[:, 1152:1280].astype(f32).T
     small[...] = side[:8]
     gain = side[0:1]
+    row = iota((768, 128), 0)
+    spot = row % 48
+    bucket = (row // 48) * 2 + spot // 12
+    kept = (iota((768, 128), 1) == bucket) & (spot < 24)
+    values = jnp.where(kept, w[:, 1154:1155].astype(f32), 0.0).astype(bf16)
+    head = iota((8, 768), 0)
+    chosen = ((iota((8, 768), 1) % 48) % 12 == place[3] * 6 + head) & (head < 6)
+    made = dot(chosen.astype(bf16), values, 1, 0)
+    table[...] = made
+    lane = iota((128, 512), 1)
+    spread = (bucket_of(jnp.where(lane < 128, -128 - lane, 384 - lane)) == iota((128, 512), 0)).astype(bf16)
+    turned = dot(made.astype(bf16), spread, 1, 0)
+    for head in range(6):
+        for block, (low, high) in enumerate(((384, 0), (256, 384), (128, 256))):
+            parts = [turned[head : head + 1, at : at + 128] for at in (low, high)]
+            wide = jnp.broadcast_to(jnp.concatenate(parts, axis=1), (128, 256))
+            rolled = pltpu.roll(wide, 0, 1, stride=1, stride_axis=0)
+            tiles[head, block * 128 : block * 128 + 128] = rolled[:, 128:256]
     for row in range(0, 1024, 256):
         wide = xs[row : row + 256].astype(f32)
         scale = lax.rsqrt(jnp.mean(wide * wide, axis=-1, keepdims=True) + EPS)
@@ -97,9 +192,11 @@
             jax.ShapeDtypeStruct((1152, 1024), bf16),
             jax.ShapeDtypeStruct((1024, 768), bf16),
             jax.ShapeDtypeStruct((8, 768), f32),
+            jax.ShapeDtypeStruct((8, 128), f32),
+            jax.ShapeDtypeStruct((6, 384, 128), f32),
         ),
-        in_specs=[SCALARS, ANY, ANY, ANY, ANY],
-        out_specs=(FULL, FULL, FULL),
+        in_specs=[SCALARS] + [ANY] * 10,
+        out_specs=(FULL,) * 5,
         scratch_shapes=[
             pltpu.VMEM((1024, 768), bf16),
             pltpu.VMEM((768, 1280), bf16),
@@ -109,16 +206,15 @@
         compiler_params=params(),
         cost_estimate=cost(2 * 1024 * 768 * 1152, 9_000_000),
         name="project",
-    )(place, x_near, x_far, w_near, w_far)
-
-
-def attend_kernel(scal, table, q, k, v, out, kept, inverse, ka, kt, qt, vt, s0, s1, tile, which):
+    )(place, x_near, x_far, *w_near, *w_far)
+
+
+def attend_kernel(mine, place, table, tile, q, k, v, out, kept, inverse, ka, kt, qt, vt, s):
     head = pl.program_id(0)
-    first, valid, instr, pair = scal[0], scal[1], scal[2], scal[3]
+    first, valid, instr, pair = first_query(place, mine), place[4], place[5], place[6]
 
     @pl.when(head == 0)
     def _():
-        which[...] = bucket_of(iota((384, 128), 0) - 128 - iota((384, 128), 1))
         kt[64:128] = jnp.zeros((64, 1024), bf16)
         qt[64:128] = jnp.zeros((64, 512), bf16)
         row = iota((16, 1024), 0)
@@ -129,11 +225,6 @@
         kt[64:80] = extra.astype(bf16)
         vt[64:80] = jnp.where(row == 0, 1.0, 0.0).astype(bf16)
 
-    buckets = which[...]
-    bias = jnp.zeros((384, 128), f32)
-    for bucket in range(BUCKETS):
-        bias = jnp.where(buckets == bucket, table[head, bucket], bias)
-    tile[...] = bias
     row = iota((16, 512), 0)
     query = iota((16, 512), 1) + first
     block = query // 128
@@ -148,31 +239,30 @@
     kt[0:64] = k[...]
     vt[0:64] = v[...]
     ka[...] = kt[...].T
-    for part, s in enumerate((s0, s1)):
-        lanes = slice(part * 256, part * 256 + 256)
-        s[128:1152] = dot(ka[...], qt[:, lanes], 1, 0)
-        for half in range(2):
-            base = pl.multiple_of(first + (part * 2 + half) * 128, 128)
-            cols = slice(half * 128, half * 128 + 128)
-            s[pl.ds(base, 384), cols] = s[pl.ds(base, 384), cols] + tile[...]
-        scores = s[128:1152]
-        peak = jnp.max(scores, axis=0, keepdims=True)
-        weights = jnp.exp(scores - peak).astype(bf16)
-        kept[0, :, lanes] = weights
-        summed = dot(vt[...], weights, 1, 0)
-        share = 1.0 / summed[64:65]
-        out[:, lanes] = (summed[0:64] * share).astype(bf16)
-        inverse[0, :, lanes] = share
-
-
-def attend(scal, table, qkv, half):
-    heads = 6
+    s[128:1152] = dot(ka[...], qt[...], 1, 0)
+    for part in range(4):
+        base = pl.multiple_of(first + part * 128, 128)
+        cols = slice(part * 128, part * 128 + 128)
+        s[pl.ds(base, 384), cols] = s[pl.ds(base, 384), cols] + tile[0]
+    scores = s[128:1152]
+    peak = jnp.max(scores, axis=0, keepdims=True)
+    weights = jnp.exp(scores - peak).astype(bf16)
+    kept[0] = weights
+    summed = dot(vt[...], weights, 1, 0)
+    share = 1.0 / summed[64:65]
+    out[...] = (summed[0:64] * share).astype(bf16)
+    inverse[0] = share
+
+
+def attend(place, table, tiles, qkv, mine):
+    half = (lambda s: s[3]) if mine else (lambda s: 1 - s[3])
     grid = pltpu.PrefetchScalarGridSpec(
         num_scalar_prefetch=1,
-        grid=(heads,),
+        grid=(6,),
         in_specs=[
             SCALARS,
-            pl.BlockSpec((64, 512), lambda h, s: (h, s[0] // 512)),
+            pl.BlockSpec((1, 384, 128), lambda h, s: (h, 0, 0)),
+            pl.BlockSpec((64, 512), lambda h, s: (h, half(s))),
             pl.BlockSpec((64, 1024), lambda h, s: (6 + h, 0)),
             pl.BlockSpec((64, 1024), lambda h, s: (12 + h, 0)),
         ],
@@ -186,36 +276,30 @@
             pltpu.VMEM((128, 1024), bf16),
             pltpu.VMEM((128, 512), bf16),
             pltpu.VMEM((80, 1024), bf16),
-            pltpu.VMEM((1280, 256), f32),
-            pltpu.VMEM((1280, 256), f32),
-            pltpu.VMEM((384, 128), f32),
-            pltpu.VMEM((384, 128), jnp.int32),
+            pltpu.VMEM((1280, 512), f32),
         ],
     )
     return pl.pallas_call(
-        attend_kernel,
+        functools.partial(attend_kernel, mine),
         out_shape=(
             jax.ShapeDtypeStruct((384, 512), bf16),
-            jax.ShapeDtypeStruct((heads, 1024, 512), bf16),
-            jax.ShapeDtypeStruct((heads, 1, 512), f32),
+            jax.ShapeDtypeStruct((6, 1024, 512), bf16),
+            jax.ShapeDtypeStruct((6, 1, 512), f32),
         ),
         grid_spec=grid,
         compiler_params=params(),
-        cost_estimate=cost(heads * 1024 * 512 * 512, 10_000_000, heads * 1024 * 512),
-        name="attend_" + half,
-    )(scal, table, qkv, qkv, qkv)
-
-
-def attend_back_kernel(
-    carried, scal, grad, out, inverse, q, k, v, kept, *refs
-):
+        cost_estimate=cost(6 * 1024 * 512 * 512, 10_000_000, 6 * 1024 * 512),
+        name="attend_mine" if mine else "attend_theirs",
+    )(place, table, tiles, qkv, qkv, qkv)
+
+
+def attend_back_kernel(carried, mine, place, grad, out, inverse, q, k, v, kept, *refs):
     if carried:
         dk_in, dv_in, band_in, far_in, *refs = refs
     dq, dk, dv, band, far, va, vt, kt, gt, ds = refs
-    head = pl.program_id(0)
-    first = scal[0]
-
-    @pl.when(head == 0)
+    first = first_query(place, mine)
+
+    @pl.when(pl.program_id(0) == 0)
     def _():
         row = iota((16, 1024), 0)
         key = iota((16, 1024), 1)
@@ -267,35 +351,30 @@
         band[0] = near
 
 
-def attend_back(scal, grad, out, inverse, qkv, kept, carry, half):
-    heads = 6
-    rows512 = pl.BlockSpec((64, 512), lambda h, s: (h, 0))
+def attend_back(place, grad, out, inverse, qkv, kept, carry, mine, start, count):
+    half = (lambda s: s[3]) if mine else (lambda s: 1 - s[3])
+    whole = lambda h, s: (start + h, 0)
+    whole3 = lambda h, s: (start + h, 0, 0)
     rows1024 = pl.BlockSpec((64, 1024), lambda h, s: (h, 0))
     band_spec = pl.BlockSpec((1, 384, 128), lambda h, s: (h, 0, 0))
+    far_spec = pl.BlockSpec((1, 8, 512), lambda h, s: (h, 0, 0))
     in_specs = [
-        rows512,
-        rows512,
-        pl.BlockSpec((1, 1, 512), lambda h, s: (h, 0, 0)),
-        pl.BlockSpec((64, 512), lambda h, s: (h, s[0] // 512)),
-        pl.BlockSpec((64, 1024), lambda h, s: (6 + h, 0)),
-        pl.BlockSpec((64, 1024), lambda h, s: (12 + h, 0)),
-        pl.BlockSpec((1, 1024, 512), lambda h, s: (h, 0, 0)),
+        pl.BlockSpec((64, 512), whole),
+        pl.BlockSpec((64, 512), whole),
+        pl.BlockSpec((1, 1, 512), whole3),
+        pl.BlockSpec((64, 512), lambda h, s: (start + h, half(s))),
+        pl.BlockSpec((64, 1024), lambda h, s: (start + 6 + h, 0)),
+        pl.BlockSpec((64, 1024), lambda h, s: (start + 12 + h, 0)),
+        pl.BlockSpec((1, 1024, 512), whole3),
     ]
-    far_spec = pl.BlockSpec((1, 8, 512), lambda h, s: (h, 0, 0))
     if carry:
         in_specs += [rows1024, rows1024, band_spec, far_spec]
     wide = bf16 if carry else f32
     grid = pltpu.PrefetchScalarGridSpec(
         num_scalar_prefetch=1,
-        grid=(heads,),
+        grid=(count,),
         in_specs=in_specs,
-        out_specs=(
-            rows512,
-            rows1024,
-            rows1024,
-            band_spec,
-            far_spec,
-        ),
+        out_specs=(pl.BlockSpec((64, 512), lambda h, s: (h, 0)), rows1024, rows1024, band_spec, far_spec),
         scratch_shapes=[
             pltpu.VMEM((1024, 128), bf16),
             pltpu.VMEM((128, 1024), bf16),
@@ -305,19 +384,19 @@
         ],
     )
     return pl.pallas_call(
-        functools.partial(attend_back_kernel, bool(carry)),
+        functools.partial(attend_back_kernel, bool(carry), mine),
         out_shape=(
-            jax.ShapeDtypeStruct((384, 512), bf16),
-            jax.ShapeDtypeStruct((384, 1024), wide),
-            jax.ShapeDtypeStruct((384, 1024), wide),
-            jax.ShapeDtypeStruct((heads, 384, 128), f32),
-            jax.ShapeDtypeStruct((heads, 8, 512), f32),
+            jax.ShapeDtypeStruct((64 * count, 512), bf16),
+            jax.ShapeDtypeStruct((64 * count, 1024), wide),
+            jax.ShapeDtypeStruct((64 * count, 1024), wide),
+            jax.ShapeDtypeStruct((count, 384, 128), f32),
+            jax.ShapeDtypeStruct((count, 8, 512), f32),
         ),
         grid_spec=grid,
         compiler_params=params(),
-        cost_estimate=cost(heads * 1024 * 512 * 1024, 12_000_000),
-        name="attend_back_" + half,
-    )(scal, grad, out, inverse, qkv, qkv, qkv, kept, *carry)
+        cost_estimate=cost(count * 1024 * 512 * 1024, 6_000_000),
+        name=("attend_back_mine_" if mine else "attend_back_theirs_") + str(start),
+    )(place, grad, out, inverse, qkv, qkv, qkv, kept, *carry)
 
 
 def gelu_both(wide):
@@ -329,12 +408,26 @@
     return (wide * half, half + 0.5 * wide * (1.0 - bend * bend) * slope)
 
 
+BLOCKS = (
+    lambda s: s[0], lambda s: s[1], lambda s: s[2].at[0], lambda s: s[3].at[0],
+    lambda s: s[2].at[1], lambda s: s[3].at[1], lambda s: s[4], lambda s: s[5],
+)
+SIDES = (
+    lambda s: s[0], lambda s: s[1].at[2], lambda s: s[1].at[0], lambda s: s[3].at[0],
+    lambda s: s[1].at[1], lambda s: s[3].at[1], lambda s: s[2], lambda s: s[4],
+)
+
+
 def forward_kernel(
-    place, att_near, att_far, x, cot, small, near0, near1, far0, far1, nearx0, nearx1, farx0, farx1,
-    hidden_hbm, pre_hbm, contract_hbm, middle, normed, branch_low, middle_grad, att, near_grad,
-    far_grad, gain_grad,
-    w_out, w_up, w_down, hidden, pre, normed_grad, pulled, sems, att_sems, out_sems,
+    place, att_near, att_far, x, cot, small, *refs
 ):
+    nears, fars, near_sides, far_sides, refs = refs[:6], refs[6:12], refs[12:17], refs[17:22], refs[22:]
+    nears, fars = ([get(blocks) for get in BLOCKS] for blocks in (nears, fars))
+    near_sides, far_sides = ([get(sides) for get in SIDES] for sides in (near_sides, far_sides))
+    (
+        hidden_hbm, pre_hbm, result, normed, branch_low, middle_grad, att, near_grad, far_grad,
+        w_out, w_up, w_down, hidden, pre, normed_grad, pulled, middle, total, sems, att_sems, out_sems,
+    ) = refs
     z, y, c, xs = place[0], place[1], place[2], place[3]
     att_copies = []
     for other, source in enumerate((att_near, att_far)):
@@ -346,17 +439,16 @@
     for turn in range(4):
         for dy in range(2):
             owner = ((jnp.bitwise_xor(z, turn) * 2) + jnp.bitwise_xor(y, dy)) * 2
-            index = (turn % 2) * 2 + dy
             for other in range(2):
-                main = ((near0, near1), (far0, far1))[other][turn // 2]
-                side = ((nearx0, nearx1), (farx0, farx1))[other][turn // 2]
+                main = (nears, fars)[other][turn * 2 + dy]
+                side = (near_sides, far_sides)[other][turn * 2 + dy]
                 who = owner + jnp.bitwise_xor(c, other)
                 row = pl.multiple_of(who * 48, 16)
                 pieces = (
-                    (0, main.at[index, 4], w_out.at[pl.ds(row, 48)]),
-                    (1, main.at[index, 0:4], w_up.at[:, pl.ds(row, 48)]),
-                    (2, main.at[index, 5:7], w_down.at[pl.ds(who * 4 + xs * 2, 2)]),
-                    (2, side.at[index], w_down.at[pl.ds(who * 4 + (1 - xs) * 2, 2)]),
+                    (0, main.at[4], w_out.at[pl.ds(row, 48)]),
+                    (1, main.at[0:4], w_up.at[:, pl.ds(row, 48)]),
+                    (2, main.at[5:7], w_down.at[pl.ds(who * 4 + xs * 2, 2)]),
+                    (2, side, w_down.at[pl.ds(who * 4 + (1 - xs) * 2, 2)]),
                 )
                 for at, (group, source, dest) in enumerate(pieces):
                     sem = sems.at[at, turn * 4 + dy * 2 + other]
@@ -374,14 +466,15 @@
     for group in groups[1:]:
         for copy in group:
             copy.wait()
-    keep = pltpu.make_async_copy(w_down, contract_hbm, out_sems.at[0])
-    keep.start()
+    total[...] = wide
     normed_grad[...] = jnp.zeros_like(normed_grad)
 
     def chunk(j, carry):
-        pulled[...] = dot(cot[...], w_down[pl.ds(j * 16, 16)].reshape(768, 768), 1, 1)
+        down = w_down[pl.ds(j * 16, 16)].reshape(768, 768)
+        pulled[...] = dot(cot[...], down, 1, 1)
         value, slope = gelu_both(dot(normed[...], w_up[j], 1, 0))
         hidden[j] = value.astype(bf16)
+        total[...] += dot(hidden[j], down, 1, 0)
         low = (pulled[...] * slope).astype(bf16)
         pre[j] = low
         normed_grad[...] += dot(low, w_up[j], 1, 1)
@@ -396,7 +489,6 @@
     scale = lax.rsqrt(jnp.mean(wide * wide, axis=-1, keepdims=True) + EPS)
     unit = wide * scale
     incoming = normed_grad[...]
-    gain_grad[...] = jnp.sum(incoming * unit, axis=0, keepdims=True)
     direct = incoming * gain
     inward = scale * (direct - unit * jnp.mean(direct * unit, axis=-1, keepdims=True))
     grad = cot[...].astype(f32) + inward
@@ -406,12 +498,12 @@
     for other, dest in enumerate((near_grad, far_grad)):
         row = pl.multiple_of(jnp.bitwise_xor(xs, other) * 384, 128)
         dest[...] = dot(w_out[pl.ds(row, 384)], low, 1, 1).astype(bf16)
-    keep.wait()
+    result[...] = total[...].astype(bf16)
     first.wait()
     second.wait()
 
 
-def forward(place, att_near, att_far, x, cot, small, blocks):
+def forward(place, att_near, att_far, x, cot, small, blocks, sides):
     tokens = jax.ShapeDtypeStruct((512, 768), bf16)
     wide = jax.ShapeDtypeStruct((512, 768), f32)
     half = jax.ShapeDtypeStruct((384, 512), bf16)
@@ -420,24 +512,24 @@
         out_shape=(
             jax.ShapeDtypeStruct((4, 512, 768), bf16),
             jax.ShapeDtypeStruct((4, 512, 768), bf16),
-            jax.ShapeDtypeStruct((64, 48, 768), bf16),
-            wide,
+            tokens,
             tokens,
             tokens,
             wide,
             jax.ShapeDtypeStruct((768, 512), bf16),
             half,
             half,
-            jax.ShapeDtypeStruct((1, 768), f32),
         ),
-        in_specs=[SCALARS, ANY, ANY, FULL, FULL, FULL] + [ANY] * 8,
-        out_specs=(ANY, ANY, ANY) + (FULL,) * 8,
+        in_specs=[SCALARS, ANY, ANY, FULL, FULL, FULL] + [ANY] * 22,
+        out_specs=(ANY, ANY) + (FULL,) * 7,
         scratch_shapes=[
             pltpu.VMEM((768, 768), bf16),
             pltpu.VMEM((4, 768, 768), bf16),
             pltpu.VMEM((64, 48, 768), bf16),
             pltpu.VMEM((4, 512, 768), bf16),
             pltpu.VMEM((4, 512, 768), bf16),
+            pltpu.VMEM((512, 768), f32),
+            pltpu.VMEM((512, 768), f32),
             pltpu.VMEM((512, 768), f32),
             pltpu.VMEM((512, 768), f32),
             pltpu.SemaphoreType.DMA((4, 16)),
@@ -447,30 +539,25 @@
         compiler_params=params(),
         cost_estimate=cost(8_500_000_000, 20_000_000, 512 * 3072),
         name="forward",
-    )(place, att_near, att_far, x, cot, small, *blocks)
-
-
-def pick(made, core, near, far, index):
-    first, second = made
-    near[index] = jnp.where(core == 0, first, second)
-    far[index] = jnp.where(core == 0, second, first)
+    )(place, att_near, att_far, x, cot, small, *blocks, *sides)
 
 
 def contract_grad_kernel(place, hidden, cot, near, far):
-    made = dot(hidden[0], cot[...], 0, 0).astype(bf16).reshape(2, 4, 48, 768)
-    pick((made[0], made[1]), place[2], near, far, 0)
+    made = dot(hidden[0], cot[...], 0, 0).astype(bf16).reshape(2, 2, 4, 48, 768)
+    near[...] = jnp.where(place[2] == 0, made[:, 0], made[:, 1])
+    far[...] = jnp.where(place[2] == 0, made[:, 1], made[:, 0])
 
 
 def contract_weight_grad(place, hidden, cot):
     shape = jax.ShapeDtypeStruct((8, 4, 48, 768), bf16)
-    spec = pl.BlockSpec((1, 4, 48, 768), lambda j: (j, 0, 0, 0))
+    spec = pl.BlockSpec((2, 4, 48, 768), lambda j: (j, 0, 0, 0))
     return pl.pallas_call(
         contract_grad_kernel,
         out_shape=(shape, shape),
-        grid=(8,),
+        grid=(4,),
         in_specs=[
             SCALARS,
-            pl.BlockSpec((1, 512, 384), lambda j: (j // 2, 0, j % 2)),
+            pl.BlockSpec((1, 512, 768), lambda j: (j, 0, 0)),
             pl.BlockSpec((512, 768), lambda j: (0, 0)),
         ],
         out_specs=(spec, spec),
@@ -480,7 +567,7 @@
     )(place, hidden, cot)
 
 
-def expand_grad_kernel(place, normed, pre, att, branch, hidden, contract, middle, near, far, result, total):
+def expand_grad_kernel(place, normed, pre, att, branch, near, far):
     step = pl.program_id(0)
 
     def store(made):
@@ -496,136 +583,236 @@
     def _():
         store(dot(att[...], branch[...], 1, 0))
 
-    @pl.when(step == 0)
-    def _():
-        total[...] = middle[...]
-
-    @pl.when(step < 4)
-    def _():
-        total[...] += dot(hidden[0], contract[...].reshape(768, 768), 1, 0)
-
-    @pl.when(step == 4)
-    def _():
-        result[...] = total[...].astype(bf16)
-
-
-def expand_weight_grad(place, normed, pre, att, branch, hidden, contract, middle):
+
+def expand_weight_grad(place, normed, pre, att, branch):
     shape = jax.ShapeDtypeStruct((8, 5, 48, 768), bf16)
     spec = pl.BlockSpec((8, 1, 48, 768), lambda j: (0, j, 0, 0))
-    chunk = pl.BlockSpec((1, 512, 768), lambda j: (jnp.minimum(j, 3), 0, 0))
     whole = pl.BlockSpec((512, 768), lambda j: (0, 0))
     return pl.pallas_call(
         expand_grad_kernel,
-        out_shape=(shape, shape, jax.ShapeDtypeStruct((512, 768), bf16)),
+        out_shape=(shape, shape),
         grid=(5,),
         in_specs=[
             SCALARS,
             whole,
-            chunk,
+            pl.BlockSpec((1, 512, 768), lambda j: (jnp.minimum(j, 3), 0, 0)),
             pl.BlockSpec((768, 512), lambda j: (0, 0)),
             whole,
-            chunk,
-            pl.BlockSpec((16, 48, 768), lambda j: (jnp.minimum(j, 3), 0, 0)),
-            whole,
         ],
-        out_specs=(spec, spec, whole),
-        scratch_shapes=[pltpu.VMEM((512, 768), f32)],
+        out_specs=(spec, spec),
         compiler_params=params(),
-        cost_estimate=cost(2 * 512 * 768 * (6144 + 768), 24_000_000),
+        cost_estimate=cost(2 * 512 * 768 * 3840, 12_000_000),
         name="expand_weight_grad",
-    )(place, normed, pre, att, branch, hidden, contract, middle)
-
-
-def project_back_kernel(
-    place, x_near, x_far, w_near, w_far, small, normed, dq_near, dq_far, dk, dv, band, far, gain_two,
-    g_near, g_far, part_near, part_far, xs, w, grad, gains, sems, xsems, qsems,
-):
-    x, core = place[3], place[2]
-    tokens = place_tokens(x, x_near, x_far, xs, xsems, 512)
-    blocks = place_blocks(place, w_near, w_far, w, sems)
+    )(place, normed, pre, att, branch)
+
+
+GROUPS = ((0, 4), (4, 2))
+
+
+def place_grads(x, group, pieces, grad, rows, sems):
+    dq_near, dq_far, dk, dv = pieces
+    size = 64 * GROUPS[group][1]
     moves = []
     for other, source in enumerate((dq_near, dq_far)):
         lane = pl.multiple_of(jnp.bitwise_xor(x, other) * 512, 128)
-        moves.append(pltpu.make_async_copy(source, grad.at[0:384, pl.ds(lane, 512)], qsems.at[other]))
-    moves.append(pltpu.make_async_copy(dk, grad.at[384:768], qsems.at[2]))
-    moves.append(pltpu.make_async_copy(dv, grad.at[768:1152], qsems.at[3]))
-    for copy in moves:
+        moves.append((source, grad.at[rows[0] : rows[0] + size, pl.ds(lane, 512)]))
+    moves.append((dk, grad.at[rows[1] : rows[1] + size]))
+    moves.append((dv, grad.at[rows[2] : rows[2] + size]))
+    copies = [pltpu.make_async_copy(*move, sems.at[group, at]) for at, move in enumerate(moves)]
+    for copy in copies:
         copy.start()
-    for copy in moves + blocks + tokens:
+    return copies
+
+
+def bias_sums(band, far):
+    flip = (iota((128, 128), 0) + iota((128, 128), 1) == 127).astype(f32)
+    total = None
+    heads = band.shape[0]
+    for block in range(3):
+        rows = []
+        for head in range(heads):
+            here = lax.dot_general(
+                flip, band[head, block * 128 : block * 128 + 128], (((1,), (0,)), ((), ())),
+                precision=lax.Precision.HIGHEST, preferred_element_type=f32,
+            )
+            wide = jnp.concatenate([here, jnp.zeros((128, 128), f32)], axis=1)
+            rolled = pltpu.roll(wide, 0, 1, stride=1, stride_axis=0)
+            rows.append(jnp.sum(rolled, axis=0, keepdims=True))
+        diagonals = jnp.concatenate(rows + [jnp.zeros((8 - heads, 256), f32)], axis=0)
+        offset = block * 128 - 1 - iota((256, 128), 0)
+        spread = (bucket_of(offset) == iota((256, 128), 1)).astype(f32)
+        made = lax.dot_general(
+            diagonals, spread, (((1,), (0,)), ((), ())),
+            precision=lax.Precision.HIGHEST, preferred_element_type=f32,
+        )
+        total = made if total is None else total + made
+    lane = iota((1, 128), 1)
+    rows = []
+    for head in range(heads):
+        sums = jnp.sum(far[head], axis=1, keepdims=True)
+        rows.append(jnp.where(lane == 15, sums[0:1], jnp.where(lane == 31, sums[1:2], 0.0)))
+    return total + jnp.concatenate(rows + [jnp.zeros((8 - heads, 128), f32)], axis=0)
+
+
+def weight_grad_kernel(group, place, normed, *refs):
+    pieces, (band, far_sum), refs = refs[:4], refs[4:6], refs[6:]
+    if group == 1:
+        bias, near, far, grad, sems = refs
+    else:
+        near, far, bias, grad, sems = refs
+    core = place[2]
+    size = 64 * GROUPS[group][1]
+    copies = place_grads(place[3], group, pieces, grad, (0, size, 2 * size), sems)
+
+    def store(made, low, high):
+        made = made.astype(bf16).reshape(8, 2, 48, high - low)
+        near[:, :, low:high] = jnp.where(core == 0, made[:, 0], made[:, 1])
+        far[:, :, low:high] = jnp.where(core == 0, made[:, 1], made[:, 0])
+
+    sums = bias_sums(band, far_sum)
+    if group == 0:
+        bias[...] = sums
+    else:
+        whole = jnp.concatenate([bias[0:4], sums[0:4]], axis=0)
+        spot = iota((768, 128), 0) % 48
+        bucket = (iota((768, 128), 0) // 48) * 2 + spot // 6
+        chosen = jnp.where((iota((768, 128), 1) == bucket) & (spot < 12), 1.0, 0.0)
+        per_head = lax.dot_general(
+            chosen, whole, (((1,), (1,)), ((), ())),
+            precision=lax.Precision.HIGHEST, preferred_element_type=f32,
+        )
+        pattern = (iota((768, 8), 1) == (iota((768, 8), 0) % 48) % 6).astype(f32)
+        column = jnp.sum(per_head * pattern, axis=1, keepdims=True)
+        store(jnp.where(iota((768, 128), 1) == 0, column, 0.0), 3 * size, 3 * size + 128)
+    for copy in copies:
         copy.wait()
-    gain_total = jnp.zeros((1, 768), f32)
+    store(dot(normed[...], grad[...], 0, 1), 0, 3 * size)
+
+
+def weight_grad(place, normed, group, pieces, rest):
+    columns = 192 * GROUPS[group][1]
+    owned = jax.ShapeDtypeStruct((8, 48, columns + 128 * group), bf16)
+    out_shape = (owned, owned) + ((jax.ShapeDtypeStruct((8, 128), f32),) if group == 0 else ())
+    return pl.pallas_call(
+        functools.partial(weight_grad_kernel, group),
+        out_shape=out_shape,
+        in_specs=[SCALARS, FULL] + [ANY] * 4 + [FULL] * len(rest),
+        out_specs=(FULL,) * len(out_shape),
+        scratch_shapes=[pltpu.VMEM((columns, 1024), bf16), pltpu.SemaphoreType.DMA((2, 4))],
+        compiler_params=params(),
+        cost_estimate=cost(2 * 1024 * 768 * columns, 6_000_000),
+        name="weight_grad_" + str(group),
+    )(place, normed, *pieces, *rest)
+
+
+def project_back_kernel(place, *refs):
+    w_near, w_far, refs = refs[:4], refs[4:8], refs[8:]
+    pieces, refs = (refs[0:4], refs[4:8]), refs[8:]
+    part_near, part_far, w, grad, sems, qsems = refs
+    x = place[3]
+    copies = place_blocks(place, w_near, w_far, w, sems)
+    for group, (start, _) in enumerate(GROUPS):
+        rows = [start * 64 + at for at in (0, 384, 768)]
+        copies += place_grads(x, group, pieces[group], grad, rows, qsems)
+    for copy in copies:
+        copy.wait()
     for other, dest in ((1, part_far), (0, part_near)):
         start = pl.multiple_of(jnp.bitwise_xor(x, other) * 512, 512)
-        part = dot(grad[:, pl.ds(start, 512)], w[:, 0:1152], 0, 1)
-        dest[...] = part.astype(bf16)
-        wide = xs[pl.ds(start, 512)].astype(f32)
-        scale = lax.rsqrt(jnp.mean(wide * wide, axis=-1, keepdims=True) + EPS)
-        gain_total = gain_total + jnp.sum(part * (wide * scale), axis=0, keepdims=True)
-    buckets = bucket_of(iota((384, 128), 0) - 128 - iota((384, 128), 1))
-    lane = iota((1, 128), 1)
-    rows = []
-    for head in range(6):
-        sums = jnp.zeros((1, 128), f32)
-        here = band[head]
-        for bucket in range(BUCKETS):
-            if bucket == 16:
-                continue
-            some = jnp.sum(jnp.where(buckets == bucket, here, 0.0))
-            if bucket in (15, 31):
-                some = some + jnp.sum(far[head, bucket // 16])
-            sums = jnp.where(lane == bucket, some, sums)
-        rows.append(sums)
-    bias = jnp.concatenate(rows + [jnp.zeros((2, 128), f32)], axis=0)
-    owner_row = iota((768, 128), 0)
-    spot = owner_row % 48
-    bucket_at = (owner_row // 48) * 2 + spot // 6
-    chosen = jnp.where((iota((768, 128), 1) == bucket_at) & (spot < 12), 1.0, 0.0)
-    per_head = lax.dot_general(
-        chosen, bias, (((1,), (1,)), ((), ())),
-        precision=lax.Precision.HIGHEST, preferred_element_type=f32,
-    )
-    pattern = (iota((768, 8), 1) == (iota((768, 8), 0) % 48) % 6).astype(f32)
-    bias_column = jnp.sum(per_head * pattern, axis=1, keepdims=True)
-    gains[...] = jnp.zeros((8, 768), f32)
-    gains[0:1] = gain_total
-    gains[1:2] = gain_two[...]
-    columns = jnp.concatenate([gains[...], jnp.zeros((120, 768), f32)], axis=0).T
-    side = jnp.where(iota((768, 128), 1) == 2, bias_column, columns)
-
-    def store(made, low, high):
-        made = made.astype(bf16).reshape(8, 2, 48, high - low)
-        g_near[:, :, low:high] = jnp.where(core == 0, made[:, 0], made[:, 1])
-        g_far[:, :, low:high] = jnp.where(core == 0, made[:, 1], made[:, 0])
-
-    for col in range(0, 1152, 384):
-        store(dot(normed[...], grad[col : col + 384], 0, 1), col, col + 384)
-    store(side, 1152, 1280)
-
-
-def project_back(place, x_near, x_far, w_near, w_far, small, normed, dq_near, dq_far, dk, dv, band, far, gain_two):
-    owned = jax.ShapeDtypeStruct((8, 48, 1280), bf16)
+        dest[...] = dot(grad[:, pl.ds(start, 512)], w[:, 0:1152], 0, 1).astype(bf16)
+
+
+def project_back(place, w_near, w_far, pieces):
     part = jax.ShapeDtypeStruct((512, 768), bf16)
     return pl.pallas_call(
         project_back_kernel,
-        out_shape=(owned, owned, part, part),
-        in_specs=[SCALARS, ANY, ANY, ANY, ANY, FULL, FULL, ANY, ANY, ANY, ANY, FULL, FULL, FULL],
-        out_specs=(FULL,) * 4,
+        out_shape=(part, part),
+        in_specs=[SCALARS] + [ANY] * 16,
+        out_specs=(FULL,) * 2,
         scratch_shapes=[
-            pltpu.VMEM((1024, 768), bf16),
             pltpu.VMEM((768, 1280), bf16),
             pltpu.VMEM((1152, 1024), bf16),
-            pltpu.VMEM((8, 768), f32),
             pltpu.SemaphoreType.DMA((16,)),
-            pltpu.SemaphoreType.DMA((2,)),
-            pltpu.SemaphoreType.DMA((4,)),
+            pltpu.SemaphoreType.DMA((2, 4)),
         ],
         compiler_params=params(),
-        cost_estimate=cost(4 * 1024 * 768 * 1152, 16_000_000),
+        cost_estimate=cost(2 * 1024 * 768 * 1152, 10_000_000),
         name="project_back",
-    )(place, x_near, x_far, w_near, w_far, small, normed, dq_near, dq_far, dk, dv, band, far, gain_two)
-
-
-def input_grad_kernel(x, small, near, far, middle_grad, result):
+    )(place, *w_near, *w_far, *pieces[0], *pieces[1])
+
+
+def finish_kernel(place, near, far, g0_near, g0_far, g1_near, g1_far, qw, kw, vw, gain, contract, q, k, v, gain_grad, bias):
+    swapped = place[3] == 1
+
+    def ordered(near, far):
+        near, far = near[...].astype(f32), far[...].astype(f32)
+        return jnp.where(swapped, far, near), jnp.where(swapped, near, far)
+
+    for half, wide in enumerate(ordered(near, far)):
+        for at in range(2):
+            row = half * 96 + at * 48
+            contract[row : row + 48] = wide[at]
+    (a0, b0), (a1, b1) = ordered(g0_near, g0_far), ordered(g1_near, g1_far)
+    for at, dest in enumerate((q, k, v)):
+        for half, (wide, thin) in enumerate(((a0, a1), (b0, b1))):
+            dest[:, half * 384 : half * 384 + 256] = wide[:, at * 256 : at * 256 + 256]
+            dest[:, half * 384 + 256 : half * 384 + 384] = thin[:, at * 128 : at * 128 + 128]
+    joint = q[...] * qw[...].astype(f32) + k[...] * kw[...].astype(f32) + v[...] * vw[...].astype(f32)
+    summed = jnp.broadcast_to(jnp.sum(joint, axis=1, keepdims=True), (48, 128))
+    blank = jnp.zeros((80, 128), f32)
+    turned = jnp.concatenate([summed, blank], axis=0).T
+    gain_grad[...] = turned[0:1, 0:48] / gain[...].astype(f32)
+    first = jnp.concatenate([a1[:, 384:512], blank], axis=0).T
+    second = jnp.concatenate([b1[:, 384:512], blank], axis=0).T
+    for row in range(2):
+        cols = slice(row * 6, row * 6 + 6)
+        bias[row : row + 1, 0:6] = first[0:1, cols]
+        bias[row : row + 1, 6:12] = second[0:1, cols]
+
+
+def finish(place, near, far, g0_near, g0_far, g1_near, g1_far, qw, kw, vw, gain):
+    full = jax.ShapeDtypeStruct((48, 768), f32)
+    return pl.pallas_call(
+        finish_kernel,
+        out_shape=(
+            jax.ShapeDtypeStruct((192, 768), f32),
+            full, full, full, jax.ShapeDtypeStruct((1, 48), f32), jax.ShapeDtypeStruct((2, 12), f32),
+        ),
+        in_specs=[SCALARS] + [FULL] * 10,
+        out_specs=(FULL,) * 6,
+        compiler_params=params(),
+        cost_estimate=cost(1000, 1_000_000),
+        name="finish",
+    )(place, near, far, g0_near, g0_far, g1_near, g1_far, qw, kw, vw, gain.reshape(1, 48))
+
+
+def finish_wide_kernel(place, near, far, up, gain, expand, output, gain_grad):
+    summed = near[...].astype(f32) + far[...].astype(f32)
+    joint = jnp.zeros((48, 768), f32)
+    for at in range(4):
+        cols = slice(at * 768, at * 768 + 768)
+        expand[:, cols] = summed[at]
+        joint = joint + summed[at] * up[:, cols].astype(f32)
+    output[...] = summed[4]
+    column = jnp.broadcast_to(jnp.sum(joint, axis=1, keepdims=True), (48, 128))
+    turned = jnp.concatenate([column, jnp.zeros((80, 128), f32)], axis=0).T
+    gain_grad[...] = turned[0:1, 0:48] / gain[...].astype(f32)
+
+
+def finish_wide(place, near, far, up, gain):
+    return pl.pallas_call(
+        finish_wide_kernel,
+        out_shape=(
+            jax.ShapeDtypeStruct((48, 3072), f32), jax.ShapeDtypeStruct((48, 768), f32), jax.ShapeDtypeStruct((1, 48), f32),
+        ),
+        in_specs=[SCALARS] + [FULL] * 4,
+        out_specs=(FULL,) * 3,
+        compiler_params=params(),
+        cost_estimate=cost(1000, 2_000_000),
+        name="finish_wide",
+    )(place, near, far, up, gain.reshape(1, 48))
+
+
+def input_grad_kernel(place, x, small, near, far, middle_grad, result):
     for row in range(0, 512, 256):
         rows = slice(row, row + 256)
         wide = x[rows].astype(f32)
@@ -636,16 +823,16 @@
         result[rows] = (middle_grad[rows] + inward).astype(bf16)
 
 
-def input_grad(x, small, near, far, middle_grad):
+def input_grad(place, x, small, near, far, middle_grad):
     return pl.pallas_call(
         input_grad_kernel,
         out_shape=jax.ShapeDtypeStruct((512, 768), bf16),
-        in_specs=[FULL] * 5,
+        in_specs=[SCALARS] + [FULL] * 5,
         out_specs=FULL,
         compiler_params=params(),
         cost_estimate=cost(512 * 768 * 20, 6_000_000),
         name="input_grad",
-    )(x, small, near, far, middle_grad)
+    )(place, x, small, near, far, middle_grad)
 
 
 def swap(array, axis, bit):
@@ -653,36 +840,56 @@
     return lax.ppermute(array, axis, [(i, i ^ bit) for i in range(count)])
 
 
+def swap_both(array):
+    pairs = [(i * 2 + j, (i ^ Y) * 2 + 1 - j) for i in range(lax.axis_size("fsdp")) for j in range(2)]
+    return lax.ppermute(array, ("fsdp", "seq"), pairs)
+
+
 CORE, Y, Z = 1, 2, 4
 
 
-def take(array, index, axis):
-    return lax.dynamic_index_in_dim(array, index, axis, keepdims=False)
-
-
-def added(parts):
-    total = parts[0].astype(f32)
-    for part in parts[1:]:
-        total = total + part.astype(f32)
-    return total
-
-
-def trade(parts, axis, index, mesh_axis, bit):
-    sent = added([take(part, 1 - index, axis) for part in parts]).astype(bf16)
-    return [take(part, index, axis) for part in parts] + [swap(sent, mesh_axis, bit)]
-
-
-def trade_z(parts, z):
-    got = []
-    for turn in range(1, 4):
-        sent = added([take(part, z ^ turn, 0) for part in parts]).astype(bf16)
-        got.append(swap(sent, "fsdp", Z * turn))
-    return added([take(part, z, 0) for part in parts] + got)
-
-
-def both(array):
-    low = lax.optimization_barrier(array.astype(bf16))
-    return low, swap(low, "seq", 1)
+def after(value, *others):
+    return lax.optimization_barrier((value, *others))[0]
+
+
+class Line:
+    def __init__(self, place):
+        self.place = place
+
+    def wait(self, *arrays):
+        self.place = after(self.place, *arrays)
+
+    def run(self, kernel, *args):
+        made = kernel(self.place, *args)
+        self.wait(jax.tree.leaves(made)[0])
+        return made
+
+
+def gather_part(part, own, now):
+    array, dims, gone = part
+    for axis in reversed(range(len(dims))):
+        if dims[axis] == now:
+            array = lax.dynamic_index_in_dim(array, 1 - own[now], axis, keepdims=False)
+        elif dims[axis] in gone:
+            array = lax.dynamic_index_in_dim(array, own[dims[axis]], axis, keepdims=False)
+    return array.astype(f32)
+
+
+def total(line, parts, own, now=None):
+    arrays = after([array for array, _, _ in parts], line.place)
+    made = None
+    for array, (_, dims, gone) in zip(arrays, parts):
+        term = gather_part((array, dims, gone), own, now)
+        made = term if made is None else made + term
+    made = lax.optimization_barrier(made.astype(bf16))
+    line.wait(made)
+    return made
+
+
+def keep(parts, now, got):
+    _, dims, gone = parts[0]
+    left = tuple(dim for dim in dims if dim not in gone and dim != now)
+    return [(a, d, g + (now,)) for a, d, g in parts] + [(got, left, ())]
 
 
 def local_split(
@@ -692,102 +899,144 @@
 ):
     owner, x = lax.axis_index("fsdp"), lax.axis_index("seq")
     z, y, c = owner // 4, (owner // 2) % 2, owner % 2
-    place = jnp.stack([z, y, c, x]).astype(jnp.int32)
+    place = jnp.stack([z, y, c, x, valid_len[0], instr_len[0], pair_flag[0]]).astype(jnp.int32)
+    line = Line(place)
     tokens, cot = layer_input[0], cotangent[0]
 
-    def columns(weight):
-        return lax.dynamic_slice(weight, (0, 384 * x), (48, 384))
-
-    table_column = jnp.pad(bias_table.reshape(24, 1), ((0, 24), (0, 0)))
-    side = jnp.concatenate(
-        [attention_gain[:, None], feedforward_gain[:, None], table_column], axis=1
-    )
-    shard = jnp.concatenate(
-        [columns(query_weight), columns(key_weight), columns(value_weight), jnp.pad(side, ((0, 0), (0, 125)))],
-        axis=1,
-    )
-    x_far = swap(tokens, "seq", 1)
-    along = [shard] + [swap(shard, "fsdp", Z * turn) for turn in range(1, 4)]
-    across = [swap(block, "fsdp", Y) for block in along]
-    w_near = jnp.stack([block for pair in zip(along, across) for block in pair])
-    w_far = swap(w_near, "fsdp", CORE)
-
-    half = lax.dynamic_slice(contract_weight, (96 * x, 0), (96, 768)).reshape(2, 48, 768)
-    shard = jnp.concatenate(
-        [expand_weight.reshape(48, 4, 768).transpose(1, 0, 2), output_weight[None], half], axis=0
-    )
-    shard, _ = lax.optimization_barrier((shard, along[3]))
-    zs = [shard] + [swap(shard, "fsdp", Z * turn) for turn in range(1, 4)]
-    ys = [swap(block, "fsdp", Y) for block in zs]
-    near, near_x, far, far_x = [], [], [], []
-    for group in range(2):
-        at = 2 * group
-        blocks = jnp.stack([zs[at], ys[at], zs[at + 1], ys[at + 1]])
-        side_blocks = swap(blocks[:, 5:7], "seq", 1)
-        near.append(blocks)
-        near_x.append(side_blocks)
-        far.append(swap(blocks, "fsdp", CORE))
-        far_x.append(swap(side_blocks, "fsdp", CORE))
-
-    qkv, normed, small = project(place, tokens, x_far, w_near, w_far)
-    table = small[2].reshape(16, 48)[:, :24].reshape(32, 12).T
-    table = jnp.pad(lax.dynamic_slice(table, (6 * x, 0), (6, 32)), ((0, 2), (0, 0)))
-    lens = jnp.stack([valid_len[0], instr_len[0], pair_flag[0]])
-    mine = jnp.concatenate([(x * 512).astype(jnp.int32)[None], lens])
-    theirs = jnp.concatenate([((1 - x) * 512).astype(jnp.int32)[None], lens])
-    out_theirs, kept_theirs, inverse_theirs = attend(theirs, table, qkv, "theirs")
-    out_got = swap(out_theirs, "seq", 1)
-    out_mine, kept_mine, inverse_mine = attend(mine, table, qkv, "mine")
-
+    def by_z(array):
+        return swap(array, "fsdp", Z)
+
+    def by_zz(array):
+        return swap(array, "fsdp", 2 * Z)
+
+    def by_y(array):
+        return swap(array, "fsdp", Y)
+
+    def by_core(array):
+        return swap(array, "fsdp", CORE)
+
+    def by_x(array):
+        return swap(array, "seq", 1)
+
+    shard = line.run(
+        narrow_shard, query_weight, key_weight, value_weight, attention_gain, feedforward_gain, bias_table
+    )
+    a2, a3, a1, b0 = by_zz(shard), swap(shard, "fsdp", 3 * Z), by_z(shard), by_y(shard)
+    x_far = by_x(tokens)
+    rest, own_side = line.run(wide_shard, expand_weight, output_weight, contract_weight)
+    a1, a2, a3, rest = lax.optimization_barrier((a1, a2, a3, rest))
+    along = jnp.stack([a1, a2, a3])
+    across = by_y(along)
+    z2, z1 = by_zz(rest), by_z(rest)
+    w_near = [shard, b0, along, across]
+    x_far, across, rest = lax.optimization_barrier((x_far, across, rest))
+    y0 = by_y(rest)
+    w_far = [by_core(block) for block in w_near]
+
+    qkv, normed, small, table, tiles = line.run(project, tokens, x_far, w_near, w_far)
+    line.place, z1, z2, y0 = lax.optimization_barrier((line.place, z1, z2, y0))
+    z12 = jnp.stack([z1, z2])
+    z3, y12 = by_z(z2), by_y(z12)
+    sides = jnp.stack([z1[5:], z2[5:], y0[5:]])
+    sides_a = by_x(sides)
+    line.wait(sides, z12)
+    out_theirs, kept_theirs, inverse_theirs = line.run(attend, table, tiles, qkv, False)
+    line.place, z3, sides_a, out_theirs = lax.optimization_barrier((line.place, z3, sides_a, out_theirs))
+    y3 = by_y(z3)
+    out_got = by_x(out_theirs)
+    sides_b = by_x(z3[5:])
+    out_mine, kept_mine, inverse_mine = line.run(attend, table, tiles, qkv, True)
+    out_mine, y12, out_got, sides_b, rest, own_side, y0, z12, z3, sides_a = lax.optimization_barrier(
+        (out_mine, y12, out_got, sides_b, rest, own_side, y0, z12, z3, sides_a)
+    )
+    sides_c = by_x(y12[:, 5:])
+    far = [by_core(block) for block in (rest, y0, z12, z3, y12)]
+    far[3], far[4] = far[4], far[3]
+    y3, sides_c = lax.optimization_barrier((y3, sides_c))
+    sides_d = by_x(y3[5:])
+    near, near_sides = [rest, y0, z12, y12, z3, y3], [own_side, sides_a, sides_b, sides_c, sides_d]
+    far, far_sides = far + [by_core(y3)], [by_core(side) for side in near_sides]
     (
-        hidden, pre, contract, middle, normed_two, branch_low, middle_grad, att, grad_mine, grad_sent, gain_two,
-    ) = forward(place, out_mine, out_got, tokens, cot, small, near + far + near_x + far_x)
-    grad_theirs = swap(grad_sent, "seq", 1)
-
-    a_near, a_far = contract_weight_grad(place, hidden, cot)
-    a_parts = [part.reshape(4, 2, 2, 2, 48, 768) for part in (a_near, swap(a_far, "fsdp", CORE))]
-    b_near, b_far, layer_output = expand_weight_grad(
-        place, normed_two, pre, att, branch_low, hidden, contract, middle
-    )
-    b_parts = [part.reshape(4, 2, 5, 48, 768) for part in (b_near, swap(b_far, "fsdp", CORE))]
-
-    dq_mine, dk, dv, band, far_sum = attend_back(
-        mine, grad_mine, out_mine, inverse_mine, qkv, kept_mine, (), "mine"
-    )
-    a_parts = trade(a_parts, 2, x, "seq", 1)
-    b_parts = trade(b_parts, 1, y, "fsdp", Y)
-    dq_theirs, dk, dv, band, far_sum = attend_back(
-        theirs, grad_theirs, out_theirs, inverse_theirs, qkv, kept_theirs, (dk, dv, band, far_sum), "theirs"
-    )
-    a_parts = trade(a_parts, 1, y, "fsdp", Y)
-    g_near, g_far, part_near, part_far = project_back(
-        place, tokens, x_far, w_near, w_far, small, normed, dq_mine, dq_theirs, dk, dv, band, far_sum, gain_two
-    )
-    part_got = swap(part_far, "seq", 1)
-    g_parts = [part.reshape(4, 2, 48, 1280) for part in (g_near, swap(g_far, "fsdp", CORE))]
-    g_parts = trade(g_parts, 1, y, "fsdp", Y)
-
-    b_low, b_other = both(trade_z(b_parts, z))
-    b_sum = b_low.astype(f32) + b_other.astype(f32)
-    expand_sum = b_sum[:4].transpose(1, 0, 2).reshape(48, 3072)
-    output_sum = b_sum[4]
-    a_low, a_other = both(trade_z(a_parts, z))
-    first, second = jnp.where(x == 0, a_low, a_other), jnp.where(x == 0, a_other, a_low)
-    contract_sum = jnp.concatenate([first, second], axis=0).reshape(192, 768).astype(f32)
-
-    result = input_grad(tokens, small, part_near, part_got, middle_grad)
-    g_low, g_other = both(trade_z(g_parts, z))
-    first, second = jnp.where(x == 0, g_low, g_other), jnp.where(x == 0, g_other, g_low)
-    grads = [
-        jnp.concatenate([first[:, at : at + 384], second[:, at : at + 384]], axis=1).astype(f32)
-        for at in (0, 384, 768)
-    ]
-    gains = g_low[:, 1152:1154].astype(f32) + g_other[:, 1152:1154].astype(f32)
-    bias_grad = jnp.concatenate(
-        [first[:12, 1154].reshape(2, 6), second[:12, 1154].reshape(2, 6)], axis=1
-    ).astype(f32)
+        hidden, pre, layer_output, normed_two, branch_low, middle_grad, att, grad_mine, grad_sent,
+    ) = line.run(forward, out_mine, out_got, tokens, cot, small, near + far, near_sides + far_sides)
+    grad_theirs = by_x(grad_sent)
+
+    def parts(near, far_got, *left):
+        dims = ("high", "low", "y") + left
+        sizes = {"high": 2, "low": 2, "y": 2, "x": 2}
+        rest = near.size // (8 * 48 * near.shape[-1] * (2 if "x" in left else 1))
+        shape = tuple(sizes.get(dim, rest) for dim in dims) + (48, near.shape[-1])
+        return [(near.reshape(shape), dims, ()), (far_got.reshape(shape), dims, ())]
+
+    own = {"high": z // 2, "low": z % 2, "y": y, "x": x}
+    b_near, b_far = line.run(expand_weight_grad, normed_two, pre, att, branch_low)
+    b_parts = parts(b_near, by_core(b_far), "n")
+    a_near, a_far = line.run(contract_weight_grad, hidden, cot)
+    a_parts = parts(a_near, by_core(a_far), "x", "n")
+
+    def back_mine(place, group):
+        return attend_back(place, grad_mine, out_mine, inverse_mine, qkv, kept_mine, (), True, *GROUPS[group])
+
+    def back_theirs(place, group, carry):
+        return attend_back(
+            place, grad_theirs, out_theirs, inverse_theirs, qkv, kept_theirs, carry[1:], False, *GROUPS[group]
+        )
+
+    mine0 = line.run(back_mine, 0)
+    line.wait(grad_theirs)
+    b_parts = keep(b_parts, "y", by_y(total(line, b_parts, own, "y")))
+    a_parts = keep(a_parts, "x", by_x(total(line, a_parts, own, "x")))
+    theirs0 = line.run(back_theirs, 0, mine0)
+    pieces0 = (mine0[0], *theirs0[:3])
+    g_near, g_far, bias0 = line.run(weight_grad, normed, 0, pieces0, theirs0[3:])
+    g_parts = parts(g_near, by_core(g_far))
+    mine1 = line.run(back_mine, 1)
+    b_parts = keep(b_parts, "low", by_z(total(line, b_parts, own, "low")))
+    a_parts = keep(a_parts, "y", by_y(total(line, a_parts, own, "y")))
+    g_parts = keep(g_parts, "y", by_y(total(line, g_parts, own, "y")))
+    theirs1 = line.run(back_theirs, 1, mine1)
+    pieces1 = (mine1[0], *theirs1[:3])
+    h_near, h_far = line.run(weight_grad, normed, 1, pieces1, (*theirs1[3:], bias0))
+    h_parts = parts(h_near, by_core(h_far))
+    b_parts = keep(b_parts, "high", by_zz(total(line, b_parts, own, "high")))
+    part_near, part_far = line.run(project_back, w_near, w_far, (pieces0, pieces1))
+    part_got = by_x(part_far)
+    arrays = after([array.reshape(4, 2, 48, 512) for array, _, _ in h_parts], line.place)
+
+    def for_owner(turn, dy):
+        terms = []
+        for array in arrays:
+            along_z = lax.dynamic_index_in_dim(array, z ^ turn, 0, keepdims=False)
+            terms.append(lax.dynamic_index_in_dim(along_z, y ^ dy, 0, keepdims=False).astype(f32))
+        return terms[0] + terms[1]
+
+    turns = [(turn, dy) for turn in range(4) for dy in range(2)][1:]
+    sends = lax.optimization_barrier([for_owner(*turn).astype(bf16) for turn in turns])
+    line.wait(*sends)
+    h_got = [swap(sent, "fsdp", Z * turn + Y * dy) for (turn, dy), sent in zip(turns, sends)]
+    a_parts = keep(a_parts, "low", by_z(total(line, a_parts, own, "low")))
+    g_parts = keep(g_parts, "low", by_z(total(line, g_parts, own, "low")))
+    b_low = total(line, b_parts, own)
+    b_other = by_x(b_low)
+    line.wait(*h_got)
+    arrays, h_got = lax.optimization_barrier((arrays, h_got))
+    made = for_owner(0, 0)
+    for got in h_got:
+        made = made + got.astype(f32)
+    h_low = lax.optimization_barrier(made.astype(bf16))
+    line.wait(h_low)
+    h_other = by_x(h_low)
+    a_parts = keep(a_parts, "high", by_zz(total(line, a_parts, own, "high")))
+    g_parts = keep(g_parts, "high", by_zz(total(line, g_parts, own, "high")))
+    result = line.run(input_grad, tokens, small, part_near, part_got, middle_grad)
+    a_low, g_low = total(line, a_parts, own), total(line, g_parts, own)
+    a_other, g_other = by_x(a_low), by_x(g_low)
+    expand_sum, output_sum, gain_two = line.run(finish_wide, b_low, b_other, expand_weight, feedforward_gain)
+    contract_sum, *grads, gain_one, bias_grad = line.run(
+        finish, a_low, a_other, g_low, g_other, h_low, h_other, query_weight, key_weight, value_weight, attention_gain
+    )
     return (
-        layer_output[None], result[None], gains[:, 0], gains[:, 1], *grads,
+        layer_output[None], result[None], gain_one[0], gain_two[0], *grads,
         output_sum, expand_sum, contract_sum, bias_grad,
     )
 

time: 394 us -> 275 us (0.70)
  waiting for transfers between devices: 168 us -> 52.6 us
  starting transfers between devices: 44.2 us -> 59.3 us
  local copies, waits for them, and re-layouts: 16.6 us -> 6.03 us
  other arithmetic: 29 us -> 24.5 us
    ppermute x44 -> x59, waiting for transfers between devices: 168 us -> 52.6 us  [swap(): return lax.ppermute(array, axis, [(i, i ^ bit) for i in range(count)])]
    ppermute x44 -> x59, starting transfers between devices: 44.2 us -> 59.3 us  [swap(): return lax.ppermute(array, axis, [(i, i ^ bit) for i in range(count)])]
    slice x8 -> x3, local copies, waits for them, and re-layouts: 4.21 us -> 0.04 us  [the longest x1 0.02 us: local_split(): sides_c = by_x(y12[:, 5:])]
    pallas_call x7 -> x15, Pallas kernels: 95.6 us -> 93.1 us  [the longest x4 29 us: attend_back(): pl.pallas_call(functools.partial(attend_back_kernel, bool(carry), mine),...]
  transfers between devices with their start and end apart: 44 -> 59, of which waited for: 20 -> 20; matrix products, arithmetic and copies ran while one was open for 10% -> 9% of each run, Pallas kernels for 27% -> 34%
where the time goes in v2:
time: 275 us; the launch traced here: 273 us
  Pallas kernels  127 us (46%)
  starting transfers between devices  59.3 us (22%)
  waiting for transfers between devices  52.6 us (19%)
  other arithmetic  24.5 us (9%)
  local copies, waits for them, and re-layouts  6.03 us (2%)
  between operations  3.54 us (1%)
    ppermute x59, starting transfers between devices, swap(): return lax.ppermute(array, axis, [(i, i ^ bit) for i in range(count)])  59.3 us
    ppermute x59, waiting for transfers between devices, swap(): return lax.ppermute(array, axis, [(i, i ^ bit) for i in range(count)])  52.6 us
    pallas_call x4, Pallas kernels, attend_back(): pl.pallas_call(functools.partial(attend_back_kernel, bool(carry), mine),...  29 us
    pallas_call x1, Pallas kernels, forward(): pl.pallas_call(forward_kernel, out_shape=(jax.ShapeDtypeStruct((4, 512, 7...  22.9 us
    convert_element_type x13, other arithmetic, total(): made = lax.optimization_barrier(made.astype(bf16))  22.3 us
    pallas_call x2, Pallas kernels, attend(): pl.pallas_call(functools.partial(attend_kernel, mine), out_shape=(jax.Sha...  21 us
    pallas_call x2, Pallas kernels, weight_grad(): pl.pallas_call(functools.partial(weight_grad_kernel, group), out_shape=ou...  12.5 us
    pallas_call x1, Pallas kernels, expand_weight_grad(): pl.pallas_call(expand_grad_kernel, out_shape=(shape, shape), grid=(5,), i...  8.05 us
  transfers between devices with their start and end apart: 59, of which 20 were waited for; matrix products, arithmetic and copies ran while one was open for 9% of the time, Pallas kernels for 34%

profile of v2, /device:TPU:0, one launch (start us, length us, event | category | flops | bytes accessed | tf_op | source)
XLA Modules:
  0.0 273.1 jit_solution(7350769234939597264)
XLA Ops:
  0.6 3.0 %collective-permute-start = (bf16[512,768]{1,0:T(8,128)(2,1)}, bf16[512,768]{1,0:T(8,128)(2,1)S(1)}, u32[]{:S(2)}, u32[]{:S(2)}) collective-permute-start(bf16[512,768]{1,0:T(8,128)(2,1)} %bitcast.144), channel_id=1, source_target_pairs={{0,1},{1,0},{2,3},{3,2},{4,5},{5,4},{6,7},{7,6},{8,9},{9,8},{10,11... | collective-permute-start | bytes 2359304 | tf_op jit(solution)/shard_map/ppermute | solution.py:840
  6.2 2.3 narrow_shard.1.refs_0_
  8.5 1.6 collective-permute-start.1
  10.2 2.6 collective-permute-start.2
  13.0 2.7 %wide_shard.1 = (bf16[7,48,768]{2,1,0:T(8,128)(2,1)}, bf16[2,48,768]{2,1,0:T(8,128)(2,1)}) custom-call(s32[7]{0:T(128)} %stack.52.place, bf16[48,3072]{1,0:T(8,128)(2,1)} %up.1, bf16[48,768]{1,0:T(8,128)(2,1)} %output.1, bf16[192,768]{1,0:T(8,128)(2,1)} %contract.1), custom_call_target="tpu_custom_call" | custom-call | flops 1 | bytes 900 | tf_op jit(solution)/shard_map/wide_shard/pallas_call | solution.py:101
  15.7 6.7 %collective-permute-done.2 = bf16[48,1280]{1,0:T(8,128)(2,1)S(1)} collective-permute-done((bf16[48,1280]{1,0:T(8,128)(2,1)}, bf16[48,1280]{1,0:T(8,128)(2,1)S(1)}, u32[]{:S(2)}, u32[]{:S(2)}) %collective-permute-start.2) | collective-permute-done | bytes 122912 | tf_op jit(solution)/shard_map/ppermute | solution.py:840
  22.5 1.6 collective-permute-start.4
  24.6 1.9 collective-permute-start.10
  26.4 1.1 collective-permute-start.11
  27.6 6.1 %collective-permute-done.4.refs_3_ = bf16[3,48,1280]{2,1,0:T(8,128)(2,1)S(1)} collective-permute-done((bf16[3,48,1280]{2,1,0:T(8,128)(2,1)S(1)}, bf16[3,48,1280]{2,1,0:T(8,128)(2,1)S(1)}, u32[]{:S(2)}, u32[]{:S(2)}) %collective-permute-start.4) | collective-permute-done | bytes 368672 | tf_op jit(solution)/shard_map/ppermute | solution.py:840
  33.7 1.6 collective-permute-start.12
  35.2 1.0 collective-permute-done.5.refs_1_
  40.1 7.3 %project.1 = (bf16[1152,1024]{1,0:T(8,128)(2,1)}, bf16[1024,768]{1,0:T(8,128)(2,1)}, f32[8,768]{1,0:T(8,128)}, f32[8,128]{1,0:T(8,128)}, f32[6,384,128]{2,1,0:T(8,128)}) custom-call(s32[7]{0:T(128)} %stack.52.place, bf16[512,768]{1,0:T(8,128)(2,1)} %bitcast.145, bf16[512,768]{1,0:T(8,128)(2,1)} %copy-done.15, bf16[48,1280]{1,0:T(8,128)(2,1)} %narrow_shard.1.refs_0_, ...), custom_call_target="tpu_custom_call" | custom-call | flops 1811939 | bytes 9000 | tf_op jit(solution)/shard_map/project/pallas_call | solution.py:189
  47.7 2.6 collective-permute-done.11
  50.8 1.6 collective-permute-start.15
  53.1 10.6 %attend_theirs.1 = (bf16[384,512]{1,0:T(8,128)(2,1)}, bf16[6,1024,512]{2,1,0:T(8,128)(2,1)}, f32[6,1,512]{2,1,0:T(1,128)}) custom-call(s32[7]{0:T(128)} %stack.52.place, f32[8,128]{1,0:T(8,128)} %get-tuple-element.216.table, f32[6,384,128]{2,1,0:T(8,128)} %get-tuple-element.217.tile, bf16[1152,1024]{1,0:T(8,128)(2,1)} %get-tuple-element.208.q.k.v, ...), custom_call_target="tpu_custom_call" | custom-call | flops 1610612 | bytes 10000 | tf_op jit(solution)/shard_map/attend_theirs/pallas_call | solution.py:282
  63.7 1.6 collective-permute-start.16
  66.5 10.5 %attend_mine.1 = (bf16[384,512]{1,0:T(8,128)(2,1)}, bf16[6,1024,512]{2,1,0:T(8,128)(2,1)}, f32[6,1,512]{2,1,0:T(1,128)}) custom-call(s32[7]{0:T(128)} %stack.52.place, f32[8,128]{1,0:T(8,128)} %get-tuple-element.216.table, f32[6,384,128]{2,1,0:T(8,128)} %get-tuple-element.217.tile, bf16[1152,1024]{1,0:T(8,128)(2,1)} %get-tuple-element.208.q.k.v, ...), custom_call_target="tpu_custom_call" | custom-call | flops 1610612 | bytes 10000 | tf_op jit(solution)/shard_map/attend_mine/pallas_call | solution.py:282
  77.0 1.5 collective-permute-start.19
  79.0 6.2 %collective-permute-done.18.refs_5_ = bf16[7,48,768]{2,1,0:T(8,128)(2,1)S(1)} collective-permute-done((bf16[7,48,768]{2,1,0:T(8,128)(2,1)S(1)}, bf16[7,48,768]{2,1,0:T(8,128)(2,1)S(1)}, u32[]{:S(2)}, u32[]{:S(2)}) %collective-permute-start.18) | collective-permute-done | bytes 516128 | tf_op jit(solution)/shard_map/ppermute | solution.py:840
  87.0 5.3 %collective-permute-done.26.refs_16_ = bf16[2,48,768]{2,1,0:T(8,128)(2,1)S(1)} collective-permute-done((bf16[2,48,768]{2,1,0:T(8,128)(2,1)S(1)}, bf16[2,48,768]{2,1,0:T(8,128)(2,1)S(1)}, u32[]{:S(2)}, u32[]{:S(2)}) %collective-permute-start.26) | collective-permute-done | bytes 147488 | tf_op jit(solution)/shard_map/ppermute | solution.py:840
  93.0 1.3 collective-permute-done.21.refs_7_
  95.1 1.0 collective-permute-done.30.refs_20_
  97.8 22.9 %forward.1 = (bf16[4,512,768]{2,1,0:T(8,128)(2,1)}, bf16[4,512,768]{2,1,0:T(8,128)(2,1)}, bf16[512,768]{1,0:T(8,128)(2,1)}, bf16[512,768]{1,0:T(8,128)(2,1)}, bf...) custom-call(s32[7]{0:T(128)} %stack.52.place, ...), custom_call_target="tpu_custom_call" | custom-call | flops 8500000 | bytes 20000 | tf_op jit(solution)/shard_map/forward/pallas_call | solution.py:510
  120.8 8.0 %expand_weight_grad.1 = (bf16[8,5,48,768]{3,2,1,0:T(8,128)(2,1)}, bf16[8,5,48,768]{3,2,1,0:T(8,128)(2,1)}) custom-call(s32[7]{0:T(128)} %stack.52.place, bf16[512,768]{1,0:T(8,128)(2,1)} %get-tuple-element.243.normed, bf16[4,512,768]{2,1,0:T(8,128)(2,1)} %get-tuple-element.244.pre, bf16[768,512]{1,0:T(8,128)(2,1)} %get-tuple-element.245.att, ...), custom_call_target="tpu_custom_call" | custom-call | flops 3019898 | bytes 12000 | tf_op jit(solution)/shard_map/expand_weight_grad/pallas_call | solution.py:591
  129.0 6.6 %contract_weight_grad.1 = (bf16[8,4,48,768]{3,2,1,0:T(8,128)(2,1)}, bf16[8,4,48,768]{3,2,1,0:T(8,128)(2,1)}) custom-call(s32[7]{0:T(128)} %stack.52.place, bf16[4,512,768]{2,1,0:T(8,128)(2,1)} %get-tuple-element.241.hidden, bf16[512,768]{1,0:T(8,128)(2,1)} %bitcast.149), custom_call_target="tpu_custom_call" | custom-call | flops 2415919 | bytes 9000 | tf_op jit(solution)/shard_map/contract_weight_grad/pallas_call | solution.py:554
  136.5 8.9 %attend_back_mine_0.1 = (bf16[256,512]{1,0:T(8,128)(2,1)}, f32[256,1024]{1,0:T(8,128)}, f32[256,1024]{1,0:T(8,128)}, f32[4,384,128]{2,1,0:T(8,128)}, f32[4,8,512]{2,1,0:T(8,128)}) custom-call(s32[7]{0:T(128)} %stack.52.place, bf16[384,512]{1,0:T(8,128)(2,1)} %get-tuple-element.251.grad, bf16[384,512]{1,0:T(8,128)(2,1)} %get-tuple-element.227.att_near.out, ...), custom_call_target="tpu_custom_call" | custom-call | flops 2147483 | bytes 6000 | tf_op jit(solution)/shard_map/attend_back_mine_0/pallas_call | solution.py:386
  145.4 1.9 collective-permute-done.32.grad
  147.3 3.0 %fusion = bf16[2,2,5,48,768]{4,3,2,1,0:T(8,128)(2,1)} fusion(bf16[2,2,2,5,48,768]{5,4,3,2,1,0:T(8,128)(2,1)} %bitcast.18, s32[]{:T(128)S(6)} %select_n.217, bf16[2,2,2,5,48,768]{5,4,3,2,1,0:T(8,128)(2,1)S(1)} %bitcast.150), kind=kLoop, calls=%fused_computation.2 | loop fusion | flops 2949120 | bytes 4423684 | tf_op jit(solution)/shard_map/convert_element_type | solution.py:884
  150.4 1.5 collective-permute-start.35
  151.9 2.9 %fusion.2 = bf16[2,2,2,2,48,768]{5,4,3,2,1,0:T(8,128)(2,1)} fusion(bf16[2,2,2,2,2,48,768]{6,5,4,3,2,1,0:T(8,128)(2,1)} %bitcast.21, s32[]{:T(128)S(6)} %select_n.218, bf16[2,2,2,2,2,48,768]{6,5,4,3,2,1,0:T(8,128)(2,1)} %bitcast.154), kind=kLoop, calls=%fused_computation.5 | loop fusion | flops 2359296 | bytes 3538948 | tf_op jit(solution)/shard_map/convert_element_type | solution.py:884
  155.4 8.7 %attend_back_theirs_0.1 = (bf16[256,512]{1,0:T(8,128)(2,1)}, bf16[256,1024]{1,0:T(8,128)(2,1)}, bf16[256,1024]{1,0:T(8,128)(2,1)}, f32[4,384,128]{2,1,0:T(8,128)}, f32[4,8,512]{2,1,0:T(8,128)}) custom-call(s32[7]{0:T(128)} %stack.52.place, bf16[384,512]{1,0:T(8,128)(2,1)} %copy-done.4, bf16[384,512]{1,0:T(8,128)(2,1)} %get-tuple-element.223.out, ...), custom_call_target="tpu_custom_call" | custom-call | flops 2147483 | bytes 6000 | tf_op jit(solution)/shard_map/attend_back_theirs_0/pallas_call | solution.py:386
  164.1 6.7 %weight_grad_0.1 = (bf16[8,48,768]{2,1,0:T(8,128)(2,1)}, bf16[8,48,768]{2,1,0:T(8,128)(2,1)}, f32[8,128]{1,0:T(8,128)}) custom-call(s32[7]{0:T(128)} %stack.52.place, bf16[1024,768]{1,0:T(8,128)(2,1)} %get-tuple-element.274.normed, bf16[256,512]{1,0:T(8,128)(2,1)} %get-tuple-element.254.refs_0_.refs_8_, bf16[256,512]{1,0:T(8,128)(2,1)} %get-tuple-element.272.refs_1_.refs_9_, ...), custom_call_target="tpu_custom_call" | custom-call | flops 1207959 | bytes 6000 | tf_op jit(solution)/shard_map/weight_grad_0/pallas_call | solution.py:696
  170.8 5.7 %attend_back_mine_4.1 = (bf16[128,512]{1,0:T(8,128)(2,1)}, f32[128,1024]{1,0:T(8,128)}, f32[128,1024]{1,0:T(8,128)}, f32[2,384,128]{2,1,0:T(8,128)}, f32[2,8,512]{2,1,0:T(8,128)}) custom-call(s32[7]{0:T(128)} %stack.52.place, bf16[384,512]{1,0:T(8,128)(2,1)} %get-tuple-element.251.grad, bf16[384,512]{1,0:T(8,128)(2,1)} %get-tuple-element.227.att_near.out, ...), custom_call_target="tpu_custom_call" | custom-call | flops 1073741 | bytes 6000 | tf_op jit(solution)/shard_map/attend_back_mine_4/pallas_call | solution.py:386
  176.5 7.7 %collective-permute-done.35 = bf16[2,2,5,48,768]{4,3,2,1,0:T(8,128)(2,1)} collective-permute-done((bf16[2,2,5,48,768]{4,3,2,1,0:T(8,128)(2,1)}, bf16[2,2,5,48,768]{4,3,2,1,0:T(8,128)(2,1)}, u32[]{:S(2)}, u32[]{:S(2)}) %collective-permute-start.35) | collective-permute-done | bytes 1474592 | tf_op jit(solution)/shard_map/ppermute | solution.py:840
  184.2 2.5 fusion.1
  187.0 2.4 fusion.3
  189.5 1.5 collective-permute-start.40
  191.0 1.8 fusion.8
  192.7 5.7 %attend_back_theirs_4.1 = (bf16[128,512]{1,0:T(8,128)(2,1)}, bf16[128,1024]{1,0:T(8,128)(2,1)}, bf16[128,1024]{1,0:T(8,128)(2,1)}, f32[2,384,128]{2,1,0:T(8,128)}, f32[2,8,512]{2,1,0:T(8,128)}) custom-call(s32[7]{0:T(128)} %stack.52.place, bf16[384,512]{1,0:T(8,128)(2,1)} %copy-done.4, bf16[384,512]{1,0:T(8,128)(2,1)} %get-tuple-element.223.out, ...), custom_call_target="tpu_custom_call" | custom-call | flops 1073741 | bytes 6000 | tf_op jit(solution)/shard_map/attend_back_theirs_4/pallas_call | solution.py:386
  198.5 5.8 %weight_grad_1.1 = (bf16[8,48,512]{2,1,0:T(8,128)(2,1)}, bf16[8,48,512]{2,1,0:T(8,128)(2,1)}) custom-call(s32[7]{0:T(128)} %stack.52.place, bf16[1024,768]{1,0:T(8,128)(2,1)} %get-tuple-element.274.normed, bf16[128,512]{1,0:T(8,128)(2,1)} %get-tuple-element.281.refs_0_.refs_12_, bf16[128,512]{1,0:T(8,128)(2,1)} %get-tuple-element.299.refs_1_.refs_13_, ...), custom_call_target="tpu_custom_call" | custom-call | flops 603979 | bytes 6000 | tf_op jit(solution)/shard_map/weight_grad_1/pallas_call | solution.py:696
  205.0 1.4 fusion.6
  206.5 6.5 %project_back.1 = (bf16[512,768]{1,0:T(8,128)(2,1)}, bf16[512,768]{1,0:T(8,128)(2,1)}) custom-call(s32[7]{0:T(128)} %stack.52.place, bf16[48,1280]{1,0:T(8,128)(2,1)} %narrow_shard.1.refs_0_, bf16[48,1280]{1,0:T(8,128)(2,1)} %copy-done.23, bf16[3,48,1280]{2,1,0:T(8,128)(2,1)} %copy-done.1, bf16[3,48,1280]{2,1,0:T(8,128)(2,1)} %copy-done.6, ...), custom_call_target="tpu_custom_call" | custom-call | flops 1811939 | bytes 10000 | tf_op jit(solution)/shard_map/project_back/pallas_call | solution.py:726
  213.0 1.1 fusion.29
  214.1 1.6 collective-permute-start.43
  215.7 1.7 collective-permute-start.44
  217.6 2.7 collective-permute-start.46
  220.4 1.4 fusion.7
  221.7 1.2 collective-permute-start.47
  223.0 2.5 collective-permute-start.48
  225.4 1.3 collective-permute-start.49
  229.2 6.6 %collective-permute-start.50 = (bf16[2,2,48,768]{3,2,1,0:T(8,128)(2,1)S(1)}, bf16[2,2,48,768]{3,2,1,0:T(8,128)(2,1)S(1)}, u32[]{:S(2)}, u32[]{:S(2)}) collective-permute-start(bf16[2,2,48,768]{3,2,1,0:T(8,128)(2,1)S(1)} %fusion.7), channel_id=1, source_target_pairs={{0,8},{2,10},{4,12},{6,14},{8,0},{10,2},{12,4},{14,6},{16,24},{18,... | collective-permute-start | bytes 884744 | tf_op jit(solution)/shard_map/ppermute | solution.py:840
  235.8 3.3 %collective-permute-start.51 = (bf16[2,48,768]{2,1,0:T(8,128)(2,1)S(1)}, bf16[2,48,768]{2,1,0:T(8,128)(2,1)S(1)}, u32[]{:S(2)}, u32[]{:S(2)}) collective-permute-start(bf16[2,48,768]{2,1,0:T(8,128)(2,1)S(1)} %fusion.12), channel_id=1, source_target_pairs={{0,8},{2,10},{4,12},{6,14},{8,0},{10,2},{12,4},{14,6},{16,24},{18,... | collective-permute-start | bytes 442376 | tf_op jit(solution)/shard_map/ppermute | solution.py:840
  240.0 7.2 %collective-permute-done.42 = bf16[5,48,768]{2,1,0:T(8,128)(2,1)S(1)} collective-permute-done((bf16[5,48,768]{2,1,0:T(8,128)(2,1)S(1)}, bf16[5,48,768]{2,1,0:T(8,128)(2,1)S(1)}, u32[]{:S(2)}, u32[]{:S(2)}) %collective-permute-start.42) | collective-permute-done | bytes 368672 | tf_op jit(solution)/shard_map/ppermute | solution.py:840
  247.2 1.4 fusion.5.near
  248.6 1.4 fusion.11
  251.0 3.0 %collective-permute-start.54 = (bf16[48,768]{1,0:T(8,128)(2,1)S(1)}, bf16[48,768]{1,0:T(8,128)(2,1)S(1)}, u32[]{:S(2)}, u32[]{:S(2)}) collective-permute-start(bf16[48,768]{1,0:T(8,128)(2,1)S(1)} %fusion.15), channel_id=1, source_target_pairs={{0,16},{2,18},{4,20},{6,22},{8,24},{10,26},{12,28},{14,30},{16,0},... | collective-permute-start | bytes 221192 | tf_op jit(solution)/shard_map/ppermute | solution.py:840
  255.5 3.8 %input_grad.1 = bf16[512,768]{1,0:T(8,128)(2,1)} custom-call(s32[7]{0:T(128)} %stack.52.place, bf16[512,768]{1,0:T(8,128)(2,1)} %bitcast.147, f32[8,768]{1,0:T(8,128)} %get-tuple-element.229.small, bf16[512,768]{1,0:T(8,128)(2,1)} %get-tuple-element.313.near, bf16[512,768]{1,0:T(8,128)(2,1)} %copy-done.14, f32[512,768]{1,0:T(8,128)} %get-tuple-element.364.middle_grad), custom_call_target="tpu_custom_call" | custom-call | flops 7864 | bytes 6000 | tf_op jit(solution)/shard_map/input_grad/pallas_call | solution.py:827
  259.8 1.2 fusion.10.near
  261.0 1.0 collective-permute-start.56
  263.0 1.1 collective-permute-start.57
  265.9 2.2 finish_wide.1
  268.0 1.3 collective-permute-done.58.g1_far
  270.6 2.3 finish.1
  (184 shorter events, 26.5 us)
Async XLA Ops:
  0.6 33.0 %collective-permute-start = (bf16[512,768]{1,0:T(8,128)(2,1)}, bf16[512,768]{1,0:T(8,128)(2,1)S(1)}, u32[]{:S(2)}, u32[]{:S(2)}) collective-permute-start(bf16[512,768]{1,0:T(8,128)(2,1)} %bitcast.144), channel_id=1, source_target_pairs={{0,1},{1,0},{2,3},{3,2},{4,5},{5,4},{6,7},{7,6},{8,9},{9,8},{10,11... | collective-permute-start | bytes 2359304 | tf_op jit(solution)/shard_map/ppermute | solution.py:840
  8.5 7.2 %collective-permute-start.1 = (bf16[48,1280]{1,0:T(8,128)(2,1)}, bf16[48,1280]{1,0:T(8,128)(2,1)S(1)}, u32[]{:S(2)}, u32[]{:S(2)}) collective-permute-start(bf16[48,1280]{1,0:T(8,128)(2,1)} %narrow_shard.1.refs_0_), channel_id=1, source_target_pairs={{0,8},{2,10},{4,12},{6,14},{8,0},{10,2},{12,4},{14,6},{16,24},{18,... | collective-permute-start | bytes 368648 | tf_op jit(solution)/shard_map/ppermute | solution.py:840
  10.2 12.3 %collective-permute-start.2 = (bf16[48,1280]{1,0:T(8,128)(2,1)}, bf16[48,1280]{1,0:T(8,128)(2,1)S(1)}, u32[]{:S(2)}, u32[]{:S(2)}) collective-permute-start(bf16[48,1280]{1,0:T(8,128)(2,1)} %narrow_shard.1.refs_0_), channel_id=1, source_target_pairs={{0,16},{2,18},{4,20},{6,22},{8,24},{10,26},{12,28},{14,30},{16,0},... | collective-permute-start | bytes 368648 | tf_op jit(solution)/shard_map/ppermute | solution.py:840
  12.7 9.7 %collective-permute-start.3 = (bf16[48,1280]{1,0:T(8,128)(2,1)}, bf16[48,1280]{1,0:T(8,128)(2,1)S(1)}, u32[]{:S(2)}, u32[]{:S(2)}) collective-permute-start(bf16[48,1280]{1,0:T(8,128)(2,1)} %narrow_shard.1.refs_0_), channel_id=1, source_target_pairs={{0,24},{2,26},{4,28},{6,30},{8,16},{10,18},{12,20},{14,22},{16,8},... | collective-permute-start | bytes 368648 | tf_op jit(solution)/shard_map/ppermute | solution.py:840
  22.5 11.2 %collective-permute-start.4 = (bf16[3,48,1280]{2,1,0:T(8,128)(2,1)S(1)}, bf16[3,48,1280]{2,1,0:T(8,128)(2,1)S(1)}, u32[]{:S(2)}, u32[]{:S(2)}) collective-permute-start(bf16[3,48,1280]{2,1,0:T(8,128)(2,1)S(1)} %pad_maximum_fusion.2.refs_2_), channel_id=1, source_target_pairs={{0,4},{2,6},{4,0},{6,2},{8,12},{10,14},{12,8},{14,10},{16,20},{18,... | collective-permute-start | bytes 1105928 | tf_op jit(solution)/shard_map/ppermute | solution.py:840
  24.1 12.2 %collective-permute-start.5 = (bf16[48,1280]{1,0:T(8,128)(2,1)}, bf16[48,1280]{1,0:T(8,128)(2,1)S(1)}, u32[]{:S(2)}, u32[]{:S(2)}) collective-permute-start(bf16[48,1280]{1,0:T(8,128)(2,1)} %narrow_shard.1.refs_0_), channel_id=1, source_target_pairs={{0,4},{2,6},{4,0},{6,2},{8,12},{10,14},{12,8},{14,10},{16,20},{18,... | collective-permute-start | bytes 368648 | tf_op jit(solution)/shard_map/ppermute | solution.py:840
  24.6 23.1 %collective-permute-start.10 = (bf16[7,48,768]{2,1,0:T(8,128)(2,1)}, bf16[7,48,768]{2,1,0:T(8,128)(2,1)S(1)}, u32[]{:S(2)}, u32[]{:S(2)}) collective-permute-start(bf16[7,48,768]{2,1,0:T(8,128)(2,1)} %get-tuple-element.230.refs_0_), channel_id=1, source_target_pairs={{0,8},{2,10},{4,12},{6,14},{8,0},{10,2},{12,4},{14,6},{16,24},{18,... | collective-permute-start | bytes 1548296 | tf_op jit(solution)/shard_map/ppermute | solution.py:840
  26.4 23.8 %collective-permute-start.11 = (bf16[7,48,768]{2,1,0:T(8,128)(2,1)}, bf16[7,48,768]{2,1,0:T(8,128)(2,1)S(1)}, u32[]{:S(2)}, u32[]{:S(2)}) collective-permute-start(bf16[7,48,768]{2,1,0:T(8,128)(2,1)} %get-tuple-element.230.refs_0_), channel_id=1, source_target_pairs={{0,16},{2,18},{4,20},{6,22},{8,24},{10,26},{12,28},{14,30},{16,0},... | collective-permute-start | bytes 1548296 | tf_op jit(solution)/shard_map/ppermute | solution.py:840
  33.7 16.6 %collective-permute-start.12 = (bf16[7,48,768]{2,1,0:T(8,128)(2,1)}, bf16[7,48,768]{2,1,0:T(8,128)(2,1)S(1)}, u32[]{:S(2)}, u32[]{:S(2)}) collective-permute-start(bf16[7,48,768]{2,1,0:T(8,128)(2,1)} %get-tuple-element.230.refs_0_), channel_id=1, source_target_pairs={{0,4},{2,6},{4,0},{6,2},{8,12},{10,14},{12,8},{14,10},{16,20},{18,... | collective-permute-start | bytes 1548296 | tf_op jit(solution)/shard_map/ppermute | solution.py:840
  35.2 1.5 collective-permute-start.6
  36.3 1.3 collective-permute-start.7
  36.8 1.7 collective-permute-start.8
  37.6 1.7 collective-permute-start.9
  50.2 42.1 %copy-start.11 = (bf16[7,48,768]{2,1,0:T(8,128)(2,1)}, bf16[7,48,768]{2,1,0:T(8,128)(2,1)S(1)}, u32[]{:S(2)}) copy-start(bf16[7,48,768]{2,1,0:T(8,128)(2,1)S(1)} %collective-permute-done.12.refs_1_) | copy-start | bytes 1548292
  50.3 13.5 %collective-permute-start.13 = (bf16[7,48,768]{2,1,0:T(8,128)(2,1)S(1)}, bf16[7,48,768]{2,1,0:T(8,128)(2,1)S(1)}, u32[]{:S(2)}, u32[]{:S(2)}) collective-permute-start(bf16[7,48,768]{2,1,0:T(8,128)(2,1)S(1)} %collective-permute-done.11), channel_id=1, source_target_pairs={{0,8},{2,10},{4,12},{6,14},{8,0},{10,2},{12,4},{14,6},{16,24},{18,... | collective-permute-start | bytes 1548296 | tf_op jit(solution)/shard_map/ppermute | solution.py:840
  50.8 34.4 %copy-start = (bf16[2,7,48,768]{3,2,1,0:T(8,128)(2,1)}, bf16[2,7,48,768]{3,2,1,0:T(8,128)(2,1)S(1)}, u32[]{:S(2)}) copy-start(bf16[2,7,48,768]{3,2,1,0:T(8,128)(2,1)S(1)} %pad_maximum_fusion.refs_2_) | copy-start | bytes 3096580
  50.8 26.1 %collective-permute-start.15 = (bf16[2,7,48,768]{3,2,1,0:T(8,128)(2,1)S(1)}, bf16[2,7,48,768]{3,2,1,0:T(8,128)(2,1)S(1)}, u32[]{:S(2)}, u32[]{:S(2)}) collective-permute-start(bf16[2,7,48,768]{3,2,1,0:T(8,128)(2,1)S(1)} %pad_maximum_fusion.refs_2_), channel_id=1, source_target_pairs={{0,4},{2,6},{4,0},{6,2},{8,12},{10,14},{12,8},{14,10},{16,20},{18,... | collective-permute-start | bytes 3096584 | tf_op jit(solution)/shard_map/ppermute | solution.py:840
  52.5 11.2 %collective-permute-start.14 = (bf16[3,2,48,768]{3,2,1,0:T(8,128)(2,1)S(1)}, bf16[3,2,48,768]{3,2,1,0:T(8,128)(2,1)S(1)}, u32[]{:S(2)}, u32[]{:S(2)}) collective-permute-start(bf16[3,2,48,768]{3,2,1,0:T(8,128)(2,1)S(1)} %pad_maximum_fusion.1), channel_id=1, source_target_pairs={{0,1},{1,0},{2,3},{3,2},{4,5},{5,4},{6,7},{7,6},{8,9},{9,8},{10,11... | collective-permute-start | bytes 1327112 | tf_op jit(solution)/shard_map/ppermute | solution.py:840
  63.7 28.6 %copy-start.12 = (bf16[7,48,768]{2,1,0:T(8,128)(2,1)}, bf16[7,48,768]{2,1,0:T(8,128)(2,1)S(1)}, u32[]{:S(2)}) copy-start(bf16[7,48,768]{2,1,0:T(8,128)(2,1)S(1)} %collective-permute-done.13.refs_4_) | copy-start | bytes 1548292
  63.7 13.2 %collective-permute-start.16 = (bf16[384,512]{1,0:T(8,128)(2,1)}, bf16[384,512]{1,0:T(8,128)(2,1)S(1)}, u32[]{:S(2)}, u32[]{:S(2)}) collective-permute-start(bf16[384,512]{1,0:T(8,128)(2,1)} %get-tuple-element.223.out), channel_id=1, source_target_pairs={{0,1},{1,0},{2,3},{3,2},{4,5},{5,4},{6,7},{7,6},{8,9},{9,8},{10,11... | collective-permute-start | bytes 1179656 | tf_op jit(solution)/shard_map/ppermute | solution.py:840
  65.3 19.9 %collective-permute-start.18 = (bf16[7,48,768]{2,1,0:T(8,128)(2,1)S(1)}, bf16[7,48,768]{2,1,0:T(8,128)(2,1)S(1)}, u32[]{:S(2)}, u32[]{:S(2)}) collective-permute-start(bf16[7,48,768]{2,1,0:T(8,128)(2,1)S(1)} %collective-permute-done.13.refs_4_), channel_id=1, source_target_pairs={{0,4},{2,6},{4,0},{6,2},{8,12},{10,14},{12,8},{14,10},{16,20},{18,... | collective-permute-start | bytes 1548296 | tf_op jit(solution)/shard_map/ppermute | solution.py:840
  65.8 11.1 %collective-permute-start.17 = (bf16[2,48,768]{2,1,0:T(8,128)(2,1)S(1)}, bf16[2,48,768]{2,1,0:T(8,128)(2,1)S(1)}, u32[]{:S(2)}, u32[]{:S(2)}) collective-permute-start(bf16[2,48,768]{2,1,0:T(8,128)(2,1)S(1)} %slice.21), channel_id=1, source_target_pairs={{0,1},{1,0},{2,3},{3,2},{4,5},{5,4},{6,7},{7,6},{8,9},{9,8},{10,11... | collective-permute-start | bytes 442376 | tf_op jit(solution)/shard_map/ppermute | solution.py:840
  77.0 19.5 %copy-start.3 = (bf16[2,7,48,768]{3,2,1,0:T(8,128)(2,1)}, bf16[2,7,48,768]{3,2,1,0:T(8,128)(2,1)S(1)}, u32[]{:S(2)}) copy-start(bf16[2,7,48,768]{3,2,1,0:T(8,128)(2,1)S(1)} %collective-permute-done.15.refs_3_) | copy-start | bytes 3096580
  77.0 8.8 %collective-permute-start.19 = (bf16[2,2,48,768]{3,2,1,0:T(8,128)(2,1)S(1)}, bf16[2,2,48,768]{3,2,1,0:T(8,128)(2,1)S(1)}, u32[]{:S(2)}, u32[]{:S(2)}) collective-permute-start(bf16[2,2,48,768]{3,2,1,0:T(8,128)(2,1)S(1)} %slice.22), channel_id=1, source_target_pairs={{0,1},{1,0},{2,3},{3,2},{4,5},{5,4},{6,7},{7,6},{8,9},{9,8},{10,11... | collective-permute-start | bytes 884744 | tf_op jit(solution)/shard_map/ppermute | solution.py:840
  78.5 6.7 %collective-permute-start.27 = (bf16[2,48,768]{2,1,0:T(8,128)(2,1)S(1)}, bf16[2,48,768]{2,1,0:T(8,128)(2,1)S(1)}, u32[]{:S(2)}, u32[]{:S(2)}) collective-permute-start(bf16[2,48,768]{2,1,0:T(8,128)(2,1)S(1)} %copy-done.35), channel_id=1, source_target_pairs={{0,2},{2,0},{4,6},{6,4},{8,10},{10,8},{12,14},{14,12},{16,18},{18,... | collective-permute-start | bytes 442376 | tf_op jit(solution)/shard_map/ppermute | solution.py:840
  78.5 7.9 %collective-permute-start.29 = (bf16[2,48,768]{2,1,0:T(8,128)(2,1)S(1)}, bf16[2,48,768]{2,1,0:T(8,128)(2,1)S(1)}, u32[]{:S(2)}, u32[]{:S(2)}) collective-permute-start(bf16[2,48,768]{2,1,0:T(8,128)(2,1)S(1)} %collective-permute-done.17.refs_14_), channel_id=1, source_target_pairs={{0,2},{2,0},{4,6},{6,4},{8,10},{10,8},{12,14},{14,12},{16,18},{18,... | collective-permute-start | bytes 442376 | tf_op jit(solution)/shard_map/ppermute | solution.py:840
  79.0 13.3 %collective-permute-start.28 = (bf16[3,2,48,768]{3,2,1,0:T(8,128)(2,1)S(1)}, bf16[3,2,48,768]{3,2,1,0:T(8,128)(2,1)}, u32[]{:S(2)}, u32[]{:S(2)}) collective-permute-start(bf16[3,2,48,768]{3,2,1,0:T(8,128)(2,1)S(1)} %collective-permute-done.14.refs_13_), channel_id=1, source_target_pairs={{0,2},{2,0},{4,6},{6,4},{8,10},{10,8},{12,14},{14,12},{16,18},{18,... | collective-permute-start | bytes 1327112 | tf_op jit(solution)/shard_map/ppermute | solution.py:840
  85.2 7.6 %collective-permute-start.20 = (bf16[7,48,768]{2,1,0:T(8,128)(2,1)S(1)}, bf16[7,48,768]{2,1,0:T(8,128)(2,1)S(1)}, u32[]{:S(2)}, u32[]{:S(2)}) collective-permute-start(bf16[7,48,768]{2,1,0:T(8,128)(2,1)S(1)} %copy-done.18), channel_id=1, source_target_pairs={{0,2},{2,0},{4,6},{6,4},{8,10},{10,8},{12,14},{14,12},{16,18},{18,... | collective-permute-start | bytes 1548296 | tf_op jit(solution)/shard_map/ppermute | solution.py:840
  85.3 11.1 %collective-permute-start.22 = (bf16[2,7,48,768]{3,2,1,0:T(8,128)(2,1)S(1)}, bf16[2,7,48,768]{3,2,1,0:T(8,128)(2,1)S(1)}, u32[]{:S(2)}, u32[]{:S(2)}) collective-permute-start(bf16[2,7,48,768]{3,2,1,0:T(8,128)(2,1)S(1)} %pad_maximum_fusion.refs_2_), channel_id=1, source_target_pairs={{0,2},{2,0},{4,6},{6,4},{8,10},{10,8},{12,14},{14,12},{16,18},{18,... | collective-permute-start | bytes 3096584 | tf_op jit(solution)/shard_map/ppermute | solution.py:840
  86.0 10.4 %collective-permute-start.23 = (bf16[2,7,48,768]{3,2,1,0:T(8,128)(2,1)S(1)}, bf16[2,7,48,768]{3,2,1,0:T(8,128)(2,1)S(1)}, u32[]{:S(2)}, u32[]{:S(2)}) collective-permute-start(bf16[2,7,48,768]{3,2,1,0:T(8,128)(2,1)S(1)} %collective-permute-done.15.refs_3_), channel_id=1, source_target_pairs={{0,2},{2,0},{4,6},{6,4},{8,10},{10,8},{12,14},{14,12},{16,18},{18,... | collective-permute-start | bytes 3096584 | tf_op jit(solution)/shard_map/ppermute | solution.py:840
  86.4 5.9 %collective-permute-start.26 = (bf16[2,48,768]{2,1,0:T(8,128)(2,1)S(1)}, bf16[2,48,768]{2,1,0:T(8,128)(2,1)S(1)}, u32[]{:S(2)}, u32[]{:S(2)}) collective-permute-start(bf16[2,48,768]{2,1,0:T(8,128)(2,1)S(1)} %slice.23), channel_id=1, source_target_pairs={{0,1},{1,0},{2,3},{3,2},{4,5},{5,4},{6,7},{7,6},{8,9},{9,8},{10,11... | collective-permute-start | bytes 442376 | tf_op jit(solution)/shard_map/ppermute | solution.py:840
  92.3 1.9 collective-permute-start.21
  92.4 2.6 collective-permute-start.24
  92.9 3.5 %collective-permute-start.25 = (bf16[7,48,768]{2,1,0:T(8,128)(2,1)S(1)}, bf16[7,48,768]{2,1,0:T(8,128)(2,1)S(1)}, u32[]{:S(2)}, u32[]{:S(2)}) collective-permute-start(bf16[7,48,768]{2,1,0:T(8,128)(2,1)S(1)} %collective-permute-done.18.refs_5_), channel_id=1, source_target_pairs={{0,2},{2,0},{4,6},{6,4},{8,10},{10,8},{12,14},{14,12},{16,18},{18,... | collective-permute-start | bytes 1548296 | tf_op jit(solution)/shard_map/ppermute | solution.py:840
  94.2 1.9 collective-permute-start.30
  95.0 1.4 collective-permute-start.31
  128.8 18.5 %collective-permute-start.33 = (bf16[8,5,48,768]{3,2,1,0:T(8,128)(2,1)}, bf16[8,5,48,768]{3,2,1,0:T(8,128)(2,1)}, u32[]{:S(2)}, u32[]{:S(2)}) collective-permute-start(bf16[8,5,48,768]{3,2,1,0:T(8,128)(2,1)} %get-tuple-element.258), channel_id=1, source_target_pairs={{0,2},{2,0},{4,6},{6,4},{8,10},{10,8},{12,14},{14,12},{16,18},{18,... | collective-permute-start | bytes 8847368 | tf_op jit(solution)/shard_map/ppermute | solution.py:840
  135.6 16.3 %collective-permute-start.34 = (bf16[8,4,48,768]{3,2,1,0:T(8,128)(2,1)}, bf16[8,4,48,768]{3,2,1,0:T(8,128)(2,1)}, u32[]{:S(2)}, u32[]{:S(2)}) collective-permute-start(bf16[8,4,48,768]{3,2,1,0:T(8,128)(2,1)} %get-tuple-element.262), channel_id=1, source_target_pairs={{0,2},{2,0},{4,6},{6,4},{8,10},{10,8},{12,14},{14,12},{16,18},{18,... | collective-permute-start | bytes 7077896 | tf_op jit(solution)/shard_map/ppermute | solution.py:840
  136.0 11.4 %collective-permute-start.32 = (bf16[384,512]{1,0:T(8,128)(2,1)}, bf16[384,512]{1,0:T(8,128)(2,1)S(1)}, u32[]{:S(2)}, u32[]{:S(2)}) collective-permute-start(bf16[384,512]{1,0:T(8,128)(2,1)} %get-tuple-element.256), channel_id=1, source_target_pairs={{0,1},{1,0},{2,3},{3,2},{4,5},{5,4},{6,7},{7,6},{8,9},{9,8},{10,11... | collective-permute-start | bytes 1179656 | tf_op jit(solution)/shard_map/ppermute | solution.py:840
  150.4 33.8 %collective-permute-start.35 = (bf16[2,2,5,48,768]{4,3,2,1,0:T(8,128)(2,1)}, bf16[2,2,5,48,768]{4,3,2,1,0:T(8,128)(2,1)}, u32[]{:S(2)}, u32[]{:S(2)}) collective-permute-start(bf16[2,2,5,48,768]{4,3,2,1,0:T(8,128)(2,1)} %fusion), channel_id=1, source_target_pairs={{0,4},{2,6},{4,0},{6,2},{8,12},{10,14},{12,8},{14,10},{16,20},{18,... | collective-permute-start | bytes 4423688 | tf_op jit(solution)/shard_map/ppermute | solution.py:840
  154.8 32.2 %collective-permute-start.36 = (bf16[2,2,2,2,48,768]{5,4,3,2,1,0:T(8,128)(2,1)}, bf16[2,2,2,2,48,768]{5,4,3,2,1,0:T(8,128)(2,1)}, u32[]{:S(2)}, u32[]{:S(2)}) collective-permute-start(bf16[2,2,2,2,48,768]{5,4,3,2,1,0:T(8,128)(2,1)} %fusion.2), channel_id=1, source_target_pairs={{0,1},{1,0},{2,3},{3,2},{4,5},{5,4},{6,7},{7,6},{8,9},{9,8},{10,11... | collective-permute-start | bytes 3538952 | tf_op jit(solution)/shard_map/ppermute | solution.py:840
  176.4 14.5 %collective-permute-start.37 = (bf16[8,48,768]{2,1,0:T(8,128)(2,1)}, bf16[8,48,768]{2,1,0:T(8,128)(2,1)}, u32[]{:S(2)}, u32[]{:S(2)}) collective-permute-start(bf16[8,48,768]{2,1,0:T(8,128)(2,1)} %get-tuple-element.291), channel_id=1, source_target_pairs={{0,2},{2,0},{4,6},{6,4},{8,10},{10,8},{12,14},{14,12},{16,18},{18,... | collective-permute-start | bytes 1769480 | tf_op jit(solution)/shard_map/ppermute | solution.py:840
  186.7 18.4 %collective-permute-start.38 = (bf16[2,5,48,768]{3,2,1,0:T(8,128)(2,1)}, bf16[2,5,48,768]{3,2,1,0:T(8,128)(2,1)}, u32[]{:S(2)}, u32[]{:S(2)}) collective-permute-start(bf16[2,5,48,768]{3,2,1,0:T(8,128)(2,1)} %fusion.1), channel_id=1, source_target_pairs={{0,8},{2,10},{4,12},{6,14},{8,0},{10,2},{12,4},{14,6},{16,24},{18,... | collective-permute-start | bytes 2211848 | tf_op jit(solution)/shard_map/ppermute | solution.py:840
  189.5 28.2 %collective-permute-start.40 = (bf16[2,2,2,48,768]{4,3,2,1,0:T(8,128)(2,1)}, bf16[2,2,2,48,768]{4,3,2,1,0:T(8,128)(2,1)}, u32[]{:S(2)}, u32[]{:S(2)}) collective-permute-start(bf16[2,2,2,48,768]{4,3,2,1,0:T(8,128)(2,1)} %fusion.3), channel_id=1, source_target_pairs={{0,4},{2,6},{4,0},{6,2},{8,12},{10,14},{12,8},{14,10},{16,20},{18,... | collective-permute-start | bytes 1769480 | tf_op jit(solution)/shard_map/ppermute | solution.py:840
  204.3 8.7 %collective-permute-start.39 = (bf16[8,48,512]{2,1,0:T(8,128)(2,1)}, bf16[8,48,512]{2,1,0:T(8,128)(2,1)}, u32[]{:S(2)}, u32[]{:S(2)}) collective-permute-start(bf16[8,48,512]{2,1,0:T(8,128)(2,1)} %get-tuple-element.315), channel_id=1, source_target_pairs={{0,2},{2,0},{4,6},{6,4},{8,10},{10,8},{12,14},{14,12},{16,18},{18,... | collective-permute-start | bytes 1179656 | tf_op jit(solution)/shard_map/ppermute | solution.py:840
  204.5 17.3 %collective-permute-start.41 = (bf16[2,2,48,768]{3,2,1,0:T(8,128)(2,1)}, bf16[2,2,48,768]{3,2,1,0:T(8,128)(2,1)S(1)}, u32[]{:S(2)}, u32[]{:S(2)}) collective-permute-start(bf16[2,2,48,768]{3,2,1,0:T(8,128)(2,1)} %fusion.8), channel_id=1, source_target_pairs={{0,4},{2,6},{4,0},{6,2},{8,12},{10,14},{12,8},{14,10},{16,20},{18,... | collective-permute-start | bytes 884744 | tf_op jit(solution)/shard_map/ppermute | solution.py:840
  214.1 8.9 %collective-permute-start.43 = (bf16[48,512]{1,0:T(8,128)(2,1)S(1)}, bf16[48,512]{1,0:T(8,128)(2,1)S(1)}, u32[]{:S(2)}, u32[]{:S(2)}) collective-permute-start(bf16[48,512]{1,0:T(8,128)(2,1)S(1)} %get-tuple-element.318), channel_id=1, source_target_pairs={{0,4},{2,6},{4,0},{6,2},{8,12},{10,14},{12,8},{14,10},{16,20},{18,... | collective-permute-start | bytes 147464 | tf_op jit(solution)/shard_map/ppermute | solution.py:840
  215.7 9.8 %collective-permute-start.44 = (bf16[48,512]{1,0:T(8,128)(2,1)S(1)}, bf16[48,512]{1,0:T(8,128)(2,1)S(1)}, u32[]{:S(2)}, u32[]{:S(2)}) collective-permute-start(bf16[48,512]{1,0:T(8,128)(2,1)S(1)} %get-tuple-element.319), channel_id=1, source_target_pairs={{0,8},{2,10},{4,12},{6,14},{8,0},{10,2},{12,4},{14,6},{16,24},{18,... | collective-permute-start | bytes 147464 | tf_op jit(solution)/shard_map/ppermute | solution.py:840
  217.4 9.4 %collective-permute-start.45 = (bf16[48,512]{1,0:T(8,128)(2,1)S(1)}, bf16[48,512]{1,0:T(8,128)(2,1)S(1)}, u32[]{:S(2)}, u32[]{:S(2)}) collective-permute-start(bf16[48,512]{1,0:T(8,128)(2,1)S(1)} %get-tuple-element.320), channel_id=1, source_target_pairs={{0,12},{2,14},{4,8},{6,10},{8,4},{10,6},{12,0},{14,2},{16,28},{18,... | collective-permute-start | bytes 147464 | tf_op jit(solution)/shard_map/ppermute | solution.py:840
  217.6 10.0 %collective-permute-start.46 = (bf16[48,512]{1,0:T(8,128)(2,1)S(1)}, bf16[48,512]{1,0:T(8,128)(2,1)S(1)}, u32[]{:S(2)}, u32[]{:S(2)}) collective-permute-start(bf16[48,512]{1,0:T(8,128)(2,1)S(1)} %get-tuple-element.321), channel_id=1, source_target_pairs={{0,16},{2,18},{4,20},{6,22},{8,24},{10,26},{12,28},{14,30},{16,0},... | collective-permute-start | bytes 147464 | tf_op jit(solution)/shard_map/ppermute | solution.py:840
  221.7 7.5 %collective-permute-start.47 = (bf16[48,512]{1,0:T(8,128)(2,1)S(1)}, bf16[48,512]{1,0:T(8,128)(2,1)S(1)}, u32[]{:S(2)}, u32[]{:S(2)}) collective-permute-start(bf16[48,512]{1,0:T(8,128)(2,1)S(1)} %get-tuple-element.322), channel_id=1, source_target_pairs={{0,20},{2,22},{4,16},{6,18},{8,28},{10,30},{12,24},{14,26},{16,4},... | collective-permute-start | bytes 147464 | tf_op jit(solution)/shard_map/ppermute | solution.py:840
  223.0 12.9 %collective-permute-start.48 = (bf16[48,512]{1,0:T(8,128)(2,1)S(1)}, bf16[48,512]{1,0:T(8,128)(2,1)S(1)}, u32[]{:S(2)}, u32[]{:S(2)}) collective-permute-start(bf16[48,512]{1,0:T(8,128)(2,1)S(1)} %get-tuple-element.323), channel_id=1, source_target_pairs={{0,24},{2,26},{4,28},{6,30},{8,16},{10,18},{12,20},{14,22},{16,8},... | collective-permute-start | bytes 147464 | tf_op jit(solution)/shard_map/ppermute | solution.py:840
  225.4 13.7 %collective-permute-start.49 = (bf16[48,512]{1,0:T(8,128)(2,1)S(1)}, bf16[48,512]{1,0:T(8,128)(2,1)S(1)}, u32[]{:S(2)}, u32[]{:S(2)}) collective-permute-start(bf16[48,512]{1,0:T(8,128)(2,1)S(1)} %get-tuple-element.324), channel_id=1, source_target_pairs={{0,28},{2,30},{4,24},{6,26},{8,20},{10,22},{12,16},{14,18},{16,12}... | collective-permute-start | bytes 147464 | tf_op jit(solution)/shard_map/ppermute | solution.py:840
  226.8 20.4 %collective-permute-start.42 = (bf16[5,48,768]{2,1,0:T(8,128)(2,1)S(1)}, bf16[5,48,768]{2,1,0:T(8,128)(2,1)S(1)}, u32[]{:S(2)}, u32[]{:S(2)}) collective-permute-start(bf16[5,48,768]{2,1,0:T(8,128)(2,1)S(1)} %fusion.6), channel_id=1, source_target_pairs={{0,16},{2,18},{4,20},{6,22},{8,24},{10,26},{12,28},{14,30},{16,0},... | collective-permute-start | bytes 1105928 | tf_op jit(solution)/shard_map/ppermute | solution.py:840
  227.7 26.9 %collective-permute-start.52 = (bf16[512,768]{1,0:T(8,128)(2,1)S(1)}, bf16[512,768]{1,0:T(8,128)(2,1)S(1)}, u32[]{:S(2)}, u32[]{:S(2)}) collective-permute-start(bf16[512,768]{1,0:T(8,128)(2,1)S(1)} %copy-done.43), channel_id=1, source_target_pairs={{0,1},{1,0},{2,3},{3,2},{4,5},{5,4},{6,7},{7,6},{8,9},{9,8},{10,11... | collective-permute-start | bytes 2359304 | tf_op jit(solution)/shard_map/ppermute | solution.py:840
  229.2 19.4 %collective-permute-start.50 = (bf16[2,2,48,768]{3,2,1,0:T(8,128)(2,1)S(1)}, bf16[2,2,48,768]{3,2,1,0:T(8,128)(2,1)S(1)}, u32[]{:S(2)}, u32[]{:S(2)}) collective-permute-start(bf16[2,2,48,768]{3,2,1,0:T(8,128)(2,1)S(1)} %fusion.7), channel_id=1, source_target_pairs={{0,8},{2,10},{4,12},{6,14},{8,0},{10,2},{12,4},{14,6},{16,24},{18,... | collective-permute-start | bytes 884744 | tf_op jit(solution)/shard_map/ppermute | solution.py:840
  235.8 14.2 %collective-permute-start.51 = (bf16[2,48,768]{2,1,0:T(8,128)(2,1)S(1)}, bf16[2,48,768]{2,1,0:T(8,128)(2,1)S(1)}, u32[]{:S(2)}, u32[]{:S(2)}) collective-permute-start(bf16[2,48,768]{2,1,0:T(8,128)(2,1)S(1)} %fusion.12), channel_id=1, source_target_pairs={{0,8},{2,10},{4,12},{6,14},{8,0},{10,2},{12,4},{14,6},{16,24},{18,... | collective-permute-start | bytes 442376 | tf_op jit(solution)/shard_map/ppermute | solution.py:840
  240.0 24.1 %copy-start.33 = (bf16[48,512]{1,0:T(8,128)(2,1)}, bf16[48,512]{1,0:T(8,128)(2,1)S(1)}, u32[]{:S(2)}) copy-start(bf16[48,512]{1,0:T(8,128)(2,1)S(1)} %fusion.22.g1_near) | copy-start | bytes 147460
  250.0 9.8 %collective-permute-start.53 = (bf16[2,48,768]{2,1,0:T(8,128)(2,1)S(1)}, bf16[2,48,768]{2,1,0:T(8,128)(2,1)S(1)}, u32[]{:S(2)}, u32[]{:S(2)}) collective-permute-start(bf16[2,48,768]{2,1,0:T(8,128)(2,1)S(1)} %fusion.11), channel_id=1, source_target_pairs={{0,16},{2,18},{4,20},{6,22},{8,24},{10,26},{12,28},{14,30},{16,0},... | collective-permute-start | bytes 442376 | tf_op jit(solution)/shard_map/ppermute | solution.py:840
  251.0 11.0 %collective-permute-start.54 = (bf16[48,768]{1,0:T(8,128)(2,1)S(1)}, bf16[48,768]{1,0:T(8,128)(2,1)S(1)}, u32[]{:S(2)}, u32[]{:S(2)}) collective-permute-start(bf16[48,768]{1,0:T(8,128)(2,1)S(1)} %fusion.15), channel_id=1, source_target_pairs={{0,16},{2,18},{4,20},{6,22},{8,24},{10,26},{12,28},{14,30},{16,0},... | collective-permute-start | bytes 221192 | tf_op jit(solution)/shard_map/ppermute | solution.py:840
  254.0 11.1 %collective-permute-start.55 = (bf16[5,48,768]{2,1,0:T(8,128)(2,1)S(1)}, bf16[5,48,768]{2,1,0:T(8,128)(2,1)S(1)}, u32[]{:S(2)}, u32[]{:S(2)}) collective-permute-start(bf16[5,48,768]{2,1,0:T(8,128)(2,1)S(1)} %fusion.5.near), channel_id=1, source_target_pairs={{0,1},{1,0},{2,3},{3,2},{4,5},{5,4},{6,7},{7,6},{8,9},{9,8},{10,11... | collective-permute-start | bytes 1105928 | tf_op jit(solution)/shard_map/ppermute | solution.py:840
  261.0 8.3 %collective-permute-start.56 = (bf16[2,48,768]{2,1,0:T(8,128)(2,1)S(1)}, bf16[2,48,768]{2,1,0:T(8,128)(2,1)S(1)}, u32[]{:S(2)}, u32[]{:S(2)}) collective-permute-start(bf16[2,48,768]{2,1,0:T(8,128)(2,1)S(1)} %fusion.10.near), channel_id=1, source_target_pairs={{0,1},{1,0},{2,3},{3,2},{4,5},{5,4},{6,7},{7,6},{8,9},{9,8},{10,11... | collective-permute-start | bytes 442376 | tf_op jit(solution)/shard_map/ppermute | solution.py:840
  263.0 6.4 %collective-permute-start.57 = (bf16[48,768]{1,0:T(8,128)(2,1)S(1)}, bf16[48,768]{1,0:T(8,128)(2,1)S(1)}, u32[]{:S(2)}, u32[]{:S(2)}) collective-permute-start(bf16[48,768]{1,0:T(8,128)(2,1)S(1)} %fusion.14.g0_near), channel_id=1, source_target_pairs={{0,1},{1,0},{2,3},{3,2},{4,5},{5,4},{6,7},{7,6},{8,9},{9,8},{10,11... | collective-permute-start | bytes 221192 | tf_op jit(solution)/shard_map/ppermute | solution.py:840
  264.1 5.2 %collective-permute-start.58 = (bf16[48,512]{1,0:T(8,128)(2,1)S(1)}, bf16[48,512]{1,0:T(8,128)(2,1)S(1)}, u32[]{:S(2)}, u32[]{:S(2)}) collective-permute-start(bf16[48,512]{1,0:T(8,128)(2,1)S(1)} %fusion.22.g1_near), channel_id=1, source_target_pairs={{0,1},{1,0},{2,3},{3,2},{4,5},{5,4},{6,7},{7,6},{8,9},{9,8},{10,11... | collective-permute-start | bytes 147464 | tf_op jit(solution)/shard_map/ppermute | solution.py:840
  (39 other events, 213.8 us)

commit v3 on v2

--- a/solution.py
+++ b/solution.py
@@ -35,6 +35,10 @@
     return pl.CostEstimate(flops=flops // 1000, bytes_accessed=byte_count // 1000, transcendentals=exps // 1000)
 
 
+def small_cost():
+    return pl.CostEstimate(flops=1000, bytes_accessed=1000, transcendentals=0)
+
+
 def bucket_of(offset):
     distance = jnp.abs(offset)
     beyond = jnp.zeros_like(distance)
@@ -48,15 +52,12 @@
     return lax.broadcasted_iota(jnp.int32, shape, dim)
 
 
-def narrow_kernel(place, q, k, v, gain_one, gain_two, table, out, side, sems):
-    x = place[3]
-    column = pl.multiple_of(x * 384, 128)
-    copies = []
-    for at, weight in enumerate((q, k, v)):
-        source = weight.at[:, pl.ds(column, 384)]
-        copy = pltpu.make_async_copy(source, out.at[:, at * 384 : at * 384 + 384], sems.at[at])
-        copy.start()
-        copies.append(copy)
+def narrow_kernel(place, q, k, v, gain_one, gain_two, table, out, side):
+    column = pl.multiple_of(place[3] * 384, 128)
+    pieces = [weight[:, pl.ds(column, 384)] for weight in (q, k, v)]
+    for pair in range(3):
+        parts = [piece[:, at : at + 64] for at in (pair * 128, pair * 128 + 64) for piece in pieces]
+        out[:, pair * 384 : pair * 384 + 384] = jnp.concatenate(parts, axis=1)
     side[...] = jnp.zeros((8, 128), f32)
     side[0:1, 0:48] = gain_one[...].astype(f32)
     side[1:2, 0:48] = gain_two[...].astype(f32)
@@ -64,24 +65,22 @@
     side[2:3, 12:24] = table[1:2].astype(f32)
     wide = jnp.concatenate([side[...], jnp.zeros((120, 128), f32)], axis=0).T
     out[:, 1152:1280] = wide[0:48].astype(bf16)
-    for copy in copies:
-        copy.wait()
 
 
 def narrow_shard(place, q, k, v, gain_one, gain_two, table):
     return pl.pallas_call(
         narrow_kernel,
         out_shape=jax.ShapeDtypeStruct((48, 1280), bf16),
-        in_specs=[SCALARS, ANY, ANY, ANY, FULL, FULL, FULL],
+        in_specs=[SCALARS] + [FULL] * 6,
         out_specs=FULL,
-        scratch_shapes=[pltpu.VMEM((8, 128), f32), pltpu.SemaphoreType.DMA((3,))],
+        scratch_shapes=[pltpu.VMEM((8, 128), f32)],
         compiler_params=params(),
-        cost_estimate=cost(1000, 250_000),
+        cost_estimate=small_cost(),
         name="narrow_shard",
     )(place, q, k, v, gain_one.reshape(1, 48), gain_two.reshape(1, 48), table)
 
 
-def wide_kernel(place, expand, output, contract, out, side, sems):
+def wide_kernel(place, expand, output, contract, out, full, sems):
     x = place[3]
     pieces = [(expand.at[:, at * 768 : at * 768 + 768], out.at[at]) for at in range(4)]
     pieces.append((output, out.at[4]))
@@ -89,38 +88,40 @@
         row = pl.multiple_of(x * 96 + at * 48, 16)
         pieces.append((contract.at[pl.ds(row, 48)], out.at[5 + at]))
         row = pl.multiple_of((1 - x) * 96 + at * 48, 16)
-        pieces.append((contract.at[pl.ds(row, 48)], side.at[at]))
+        pieces.append((contract.at[pl.ds(row, 48)], full.at[7 + at]))
     copies = [pltpu.make_async_copy(*piece, sems.at[at]) for at, piece in enumerate(pieces)]
     for copy in copies:
         copy.start()
     for copy in copies:
         copy.wait()
+    full[0:7] = out[...]
 
 
 def wide_shard(place, expand, output, contract):
     return pl.pallas_call(
         wide_kernel,
         out_shape=(
-            jax.ShapeDtypeStruct((7, 48, 768), bf16), jax.ShapeDtypeStruct((2, 48, 768), bf16),
+            jax.ShapeDtypeStruct((7, 48, 768), bf16), jax.ShapeDtypeStruct((9, 48, 768), bf16),
         ),
         in_specs=[SCALARS, ANY, ANY, ANY],
         out_specs=(FULL, FULL),
         scratch_shapes=[pltpu.SemaphoreType.DMA((9,))],
         compiler_params=params(),
-        cost_estimate=cost(1000, 900_000),
+        cost_estimate=small_cost(),
         name="wide_shard",
     )(place, expand, output, contract)
 
 
-def eight(blocks):
-    own, across, along, both = blocks
-    return [own, across] + [ref.at[at] for at in range(3) for ref in (along, both)]
+def narrow_blocks(refs):
+    shard, b0, a1, a2, turned, b2, b3, four, three, last = refs
+    near = [shard, b0, a1, turned.at[1], a2, b2, turned.at[0], b3]
+    far = [four.at[0], four.at[1], four.at[2], three.at[1], four.at[3], three.at[2], three.at[0], last]
+    return near, far
 
 
 def place_blocks(place, near, far, dest, sems):
     z, y, c = place[0], place[1], place[2]
     copies = []
-    near, far = eight(near), eight(far)
     for turn in range(4):
         for dy in range(2):
             owner = ((jnp.bitwise_xor(z, turn) * 2) + jnp.bitwise_xor(y, dy)) * 2
@@ -149,8 +150,8 @@
 
 
 def project_kernel(place, x_near, x_far, *refs):
-    w_near, w_far, refs = refs[:4], refs[4:8], refs[8:]
-    qkv, normed, small, table, tiles, xs, w, sems, xsems = refs
+    (w_near, w_far), refs = narrow_blocks(refs[:10]), refs[10:]
+    qkv, kept, sent, small, table, tiles, normed, xs, w, sems, xsems = refs
     tokens = place_tokens(place[3], x_near, x_far, xs, xsems, 512)
     blocks = place_blocks(place, w_near, w_far, w, sems)
     for copy in tokens + blocks:
@@ -161,8 +162,8 @@
     row = iota((768, 128), 0)
     spot = row % 48
     bucket = (row // 48) * 2 + spot // 12
-    kept = (iota((768, 128), 1) == bucket) & (spot < 24)
-    values = jnp.where(kept, w[:, 1154:1155].astype(f32), 0.0).astype(bf16)
+    match = (iota((768, 128), 1) == bucket) & (spot < 24)
+    values = jnp.where(match, w[:, 1154:1155].astype(f32), 0.0).astype(bf16)
     head = iota((8, 768), 0)
     chosen = ((iota((8, 768), 1) % 48) % 12 == place[3] * 6 + head) & (head < 6)
     made = dot(chosen.astype(bf16), values, 1, 0)
@@ -183,30 +184,35 @@
     for col in range(0, 1152, 384):
         made = dot(w[:, col : col + 384], normed[...], 0, 1)
         qkv[col : col + 384] = made.astype(bf16)
-
-
-def project(place, x_near, x_far, w_near, w_far):
+    turned = normed[...].T.reshape(8, 2, 48, 1024)
+    kept[...] = jnp.where(place[2] == 0, turned[:, 0], turned[:, 1])
+    sent[...] = jnp.where(place[2] == 0, turned[:, 1], turned[:, 0])
+
+
+def project(place, x_near, x_far, blocks):
     return pl.pallas_call(
         project_kernel,
         out_shape=(
             jax.ShapeDtypeStruct((1152, 1024), bf16),
-            jax.ShapeDtypeStruct((1024, 768), bf16),
+            jax.ShapeDtypeStruct((8, 48, 1024), bf16),
+            jax.ShapeDtypeStruct((8, 48, 1024), bf16),
             jax.ShapeDtypeStruct((8, 768), f32),
             jax.ShapeDtypeStruct((8, 128), f32),
             jax.ShapeDtypeStruct((6, 384, 128), f32),
         ),
-        in_specs=[SCALARS] + [ANY] * 10,
-        out_specs=(FULL,) * 5,
+        in_specs=[SCALARS] + [ANY] * 12,
+        out_specs=(FULL,) * 6,
         scratch_shapes=[
+            pltpu.VMEM((1024, 768), bf16),
             pltpu.VMEM((1024, 768), bf16),
             pltpu.VMEM((768, 1280), bf16),
             pltpu.SemaphoreType.DMA((16,)),
             pltpu.SemaphoreType.DMA((2,)),
         ],
         compiler_params=params(),
-        cost_estimate=cost(2 * 1024 * 768 * 1152, 9_000_000),
+        cost_estimate=small_cost(),
         name="project",
-    )(place, x_near, x_far, *w_near, *w_far)
+    )(place, x_near, x_far, *blocks)
 
 
 def attend_kernel(mine, place, table, tile, q, k, v, out, kept, inverse, ka, kt, qt, vt, s):
@@ -262,9 +268,9 @@
         in_specs=[
             SCALARS,
             pl.BlockSpec((1, 384, 128), lambda h, s: (h, 0, 0)),
-            pl.BlockSpec((64, 512), lambda h, s: (h, half(s))),
-            pl.BlockSpec((64, 1024), lambda h, s: (6 + h, 0)),
-            pl.BlockSpec((64, 1024), lambda h, s: (12 + h, 0)),
+            pl.BlockSpec((64, 512), lambda h, s: (3 * h, half(s))),
+            pl.BlockSpec((64, 1024), lambda h, s: (3 * h + 1, 0)),
+            pl.BlockSpec((64, 1024), lambda h, s: (3 * h + 2, 0)),
         ],
         out_specs=(
             pl.BlockSpec((64, 512), lambda h, s: (h, 0)),
@@ -288,15 +294,43 @@
         ),
         grid_spec=grid,
         compiler_params=params(),
-        cost_estimate=cost(6 * 1024 * 512 * 512, 10_000_000, 6 * 1024 * 512),
+        cost_estimate=small_cost(),
         name="attend_mine" if mine else "attend_theirs",
     )(place, table, tiles, qkv, qkv, qkv)
 
 
+def diagonal_sums(band):
+    flip = (iota((128, 128), 0) + iota((128, 128), 1) == 127).astype(f32)
+    rows = []
+    for block in range(3):
+        here = lax.dot_general(
+            flip, band[block * 128 : block * 128 + 128], (((1,), (0,)), ((), ())),
+            precision=lax.Precision.HIGHEST, preferred_element_type=f32,
+        )
+        wide = jnp.concatenate([here, jnp.zeros((128, 128), f32)], axis=1)
+        rolled = pltpu.roll(wide, 0, 1, stride=1, stride_axis=0)
+        rows.append(jnp.sum(rolled, axis=0, keepdims=True))
+    return rows
+
+
+def bucket_sums(diagonals, sides):
+    total = sides
+    for block in range(3):
+        offset = block * 128 - 1 - iota((256, 128), 0)
+        spread = (bucket_of(offset) == iota((256, 128), 1)).astype(f32)
+        total = total + lax.dot_general(
+            diagonals[block], spread, (((1,), (0,)), ((), ())),
+            precision=lax.Precision.HIGHEST, preferred_element_type=f32,
+        )
+    return total
+
+
 def attend_back_kernel(carried, mine, place, grad, out, inverse, q, k, v, kept, *refs):
     if carried:
-        dk_in, dv_in, band_in, far_in, *refs = refs
-    dq, dk, dv, band, far, va, vt, kt, gt, ds = refs
+        dq_in, dk_in, dv_in, band_in, far_in, whole, diagonals, sides, *refs = refs
+    else:
+        dq, dk, dv, band, far, *refs = refs
+    va, vt, kt, gt, ds = refs
     first = first_query(place, mine)
 
     @pl.when(pl.program_id(0) == 0)
@@ -305,6 +339,9 @@
         key = iota((16, 1024), 1)
         vt[64:128] = jnp.zeros((64, 1024), bf16)
         vt[64:80] = jnp.where(row < 2, 1.0, 0.0).astype(bf16)
+        if carried:
+            diagonals[...] = jnp.zeros_like(diagonals)
+            sides[...] = jnp.zeros_like(sides)
         kt[64:80] = jnp.where(row < 8, (key // 128 == row).astype(f32), 0.0).astype(bf16)
         gt[64:128] = jnp.zeros((64, 512), bf16)
         ds[0:128] = jnp.zeros((128, 512), bf16)
@@ -326,14 +363,11 @@
         pull = dot(va[rows], gt[...], 1, 0)
         ds[128 + row_at : 384 + row_at] = (kept[0, rows] * pull).astype(bf16)
     made = dot(kt[...], ds[128:1152], 1, 0)
-    dq[...] = made[0:64].astype(bf16)
     block = (iota((8, 512), 1) + first) // 128
     key_block = iota((8, 512), 0)
     totals = made[64:72]
     left = jnp.sum(jnp.where(key_block <= block - 2, totals, 0.0), axis=0, keepdims=True)
     right = jnp.sum(jnp.where(key_block >= block + 2, totals, 0.0), axis=0, keepdims=True)
-    sides = jnp.concatenate([left, right, jnp.zeros((6, 512), f32)], axis=0)
-    far[0] = sides + far_in[0] if carried else sides
     dv_made = dot(gt[0:64], kept[0], 1, 1)
     dk_made = dot(q[...], ds[128:1152], 1, 1)
     near = None
@@ -342,40 +376,70 @@
         window = ds[pl.ds(base, 384), part * 128 : part * 128 + 128].astype(f32)
         near = window if near is None else near + window
     if carried:
-        dk[...] = (dk_made + dk_in[...]).astype(bf16)
-        dv[...] = (dv_made + dv_in[...]).astype(bf16)
-        band[0] = near + band_in[0]
+        whole[0, 0:64, pl.ds(pl.multiple_of(first, 512), 512)] = made[0:64].astype(bf16)
+        whole[0, 0:64, pl.ds(pl.multiple_of(512 - first, 512), 512)] = dq_in[...]
+        whole[0, 64:128] = (dk_made + dk_in[...]).astype(bf16)
+        whole[0, 128:192] = (dv_made + dv_in[...]).astype(bf16)
+        head = pl.program_id(0)
+        for at, row in enumerate(diagonal_sums(near + band_in[0])):
+            diagonals[at, pl.ds(head, 1)] = row
+        lane = iota((1, 128), 1)
+        left, right = (
+            jnp.sum(side, axis=1, keepdims=True) for side in (left + far_in[0, 0:1], right + far_in[0, 1:2])
+        )
+        sides[pl.ds(head, 1)] = jnp.where(lane == 15, left, jnp.where(lane == 31, right, 0.0))
+        whole[0, 192:208] = jnp.zeros((16, 1024), bf16)
+
+        @pl.when(head == 5)
+        def _():
+            bias = bucket_sums([diagonals[at] for at in range(3)], sides[...])
+            whole[0, 192:208, 0:128] = jnp.concatenate([bias, jnp.zeros((8, 128), f32)], axis=0).astype(bf16)
+
     else:
+        dq[...] = made[0:64].astype(bf16)
         dk[...] = dk_made
         dv[...] = dv_made
         band[0] = near
-
-
-def attend_back(place, grad, out, inverse, qkv, kept, carry, mine, start, count):
+        far[0] = jnp.concatenate([left, right, jnp.zeros((6, 512), f32)], axis=0)
+
+
+def attend_back(place, grad, out, inverse, qkv, kept, carry, mine):
+    count = 6
     half = (lambda s: s[3]) if mine else (lambda s: 1 - s[3])
-    whole = lambda h, s: (start + h, 0)
-    whole3 = lambda h, s: (start + h, 0, 0)
+    rows512 = pl.BlockSpec((64, 512), lambda h, s: (h, 0))
     rows1024 = pl.BlockSpec((64, 1024), lambda h, s: (h, 0))
     band_spec = pl.BlockSpec((1, 384, 128), lambda h, s: (h, 0, 0))
     far_spec = pl.BlockSpec((1, 8, 512), lambda h, s: (h, 0, 0))
+    carry_specs = (rows512, rows1024, rows1024, band_spec, far_spec)
     in_specs = [
-        pl.BlockSpec((64, 512), whole),
-        pl.BlockSpec((64, 512), whole),
-        pl.BlockSpec((1, 1, 512), whole3),
-        pl.BlockSpec((64, 512), lambda h, s: (start + h, half(s))),
-        pl.BlockSpec((64, 1024), lambda h, s: (start + 6 + h, 0)),
-        pl.BlockSpec((64, 1024), lambda h, s: (start + 12 + h, 0)),
-        pl.BlockSpec((1, 1024, 512), whole3),
+        rows512,
+        rows512,
+        pl.BlockSpec((1, 1, 512), lambda h, s: (h, 0, 0)),
+        pl.BlockSpec((64, 512), lambda h, s: (3 * h, half(s))),
+        pl.BlockSpec((64, 1024), lambda h, s: (3 * h + 1, 0)),
+        pl.BlockSpec((64, 1024), lambda h, s: (3 * h + 2, 0)),
+        pl.BlockSpec((1, 1024, 512), lambda h, s: (h, 0, 0)),
     ]
     if carry:
-        in_specs += [rows1024, rows1024, band_spec, far_spec]
-    wide = bf16 if carry else f32
+        out_shape = jax.ShapeDtypeStruct((count, 208, 1024), bf16)
+        out_specs = pl.BlockSpec((1, 208, 1024), lambda h, s: (h, 0, 0))
+        in_specs += carry_specs
+    else:
+        out_shape = (
+            jax.ShapeDtypeStruct((64 * count, 512), bf16),
+            jax.ShapeDtypeStruct((64 * count, 1024), f32),
+            jax.ShapeDtypeStruct((64 * count, 1024), f32),
+            jax.ShapeDtypeStruct((count, 384, 128), f32),
+            jax.ShapeDtypeStruct((count, 8, 512), f32),
+        )
+        out_specs = carry_specs
     grid = pltpu.PrefetchScalarGridSpec(
         num_scalar_prefetch=1,
         grid=(count,),
         in_specs=in_specs,
-        out_specs=(pl.BlockSpec((64, 512), lambda h, s: (h, 0)), rows1024, rows1024, band_spec, far_spec),
-        scratch_shapes=[
+        out_specs=out_specs,
+        scratch_shapes=([pltpu.VMEM((3, 8, 256), f32), pltpu.VMEM((8, 128), f32)] if carry else [])
+        + [
             pltpu.VMEM((1024, 128), bf16),
             pltpu.VMEM((128, 1024), bf16),
             pltpu.VMEM((80, 1024), bf16),
@@ -385,17 +449,11 @@
     )
     return pl.pallas_call(
         functools.partial(attend_back_kernel, bool(carry), mine),
-        out_shape=(
-            jax.ShapeDtypeStruct((64 * count, 512), bf16),
-            jax.ShapeDtypeStruct((64 * count, 1024), wide),
-            jax.ShapeDtypeStruct((64 * count, 1024), wide),
-            jax.ShapeDtypeStruct((count, 384, 128), f32),
-            jax.ShapeDtypeStruct((count, 8, 512), f32),
-        ),
+        out_shape=out_shape,
         grid_spec=grid,
         compiler_params=params(),
         cost_estimate=cost(count * 1024 * 512 * 1024, 6_000_000),
-        name=("attend_back_mine_" if mine else "attend_back_theirs_") + str(start),
+        name="attend_back_mine" if mine else "attend_back_theirs",
     )(place, grad, out, inverse, qkv, qkv, qkv, kept, *carry)
 
 
@@ -408,25 +466,27 @@
     return (wide * half, half + 0.5 * wide * (1.0 - bend * bend) * slope)
 
 
-BLOCKS = (
-    lambda s: s[0], lambda s: s[1], lambda s: s[2].at[0], lambda s: s[3].at[0],
-    lambda s: s[2].at[1], lambda s: s[3].at[1], lambda s: s[4], lambda s: s[5],
-)
-SIDES = (
-    lambda s: s[0], lambda s: s[1].at[2], lambda s: s[1].at[0], lambda s: s[3].at[0],
-    lambda s: s[1].at[1], lambda s: s[3].at[1], lambda s: s[2], lambda s: s[4],
-)
+def all_blocks(full, three, two, y1, y3, side_a, side_b, side_c):
+    blocks = [full, three[0], three[1], y1, three[2], two[1], two[0], y3]
+    sides = [
+        full.at[7:9], side_a.at[2], side_a.at[0], y1.at[7:9], side_a.at[1], side_b.at[1], side_b.at[0], side_c,
+    ]
+    return blocks, sides
 
 
 def forward_kernel(
     place, att_near, att_far, x, cot, small, *refs
 ):
-    nears, fars, near_sides, far_sides, refs = refs[:6], refs[6:12], refs[12:17], refs[17:22], refs[22:]
-    nears, fars = ([get(blocks) for get in BLOCKS] for blocks in (nears, fars))
-    near_sides, far_sides = ([get(sides) for get in SIDES] for sides in (near_sides, far_sides))
+    full, y0, z1, z2, z3, y2, y1, y3, side_a, side_b, side_c = refs[:11]
+    nears, near_sides = all_blocks(full, (y0, z1, z2), (z3, y2), y1, y3, side_a, side_b, side_c)
+    full, three, two, y1, y3, side_a, side_b, side_c = refs[11:19]
+    three, two = [three.at[at] for at in range(3)], [two.at[at] for at in range(2)]
+    fars, far_sides = all_blocks(full, three, two, y1, y3, side_a, side_b, side_c)
+    refs = refs[19:]
     (
-        hidden_hbm, pre_hbm, result, normed, branch_low, middle_grad, att, near_grad, far_grad,
-        w_out, w_up, w_down, hidden, pre, normed_grad, pulled, middle, total, sems, att_sems, out_sems,
+        hid_keep_hbm, hid_send_hbm, pre_hbm, turned_keep, turned_send, result, middle_grad, near_grad, far_grad,
+        w_out, w_up, w_down, hid_keep, hid_send, pre, normed_grad, pulled, middle, total, normed, att,
+        sems, att_sems, out_sems,
     ) = refs
     z, y, c, xs = place[0], place[1], place[2], place[3]
     att_copies = []
@@ -473,18 +533,29 @@
         down = w_down[pl.ds(j * 16, 16)].reshape(768, 768)
         pulled[...] = dot(cot[...], down, 1, 1)
         value, slope = gelu_both(dot(normed[...], w_up[j], 1, 0))
-        hidden[j] = value.astype(bf16)
-        total[...] += dot(hidden[j], down, 1, 0)
+        value = value.astype(bf16)
+        total[...] += dot(value, down, 1, 0)
+        even = jnp.concatenate([value[:, 0:192], value[:, 384:576]], axis=1)
+        odd = jnp.concatenate([value[:, 192:384], value[:, 576:768]], axis=1)
+        hid_keep[j] = jnp.where(c == 0, even, odd)
+        hid_send[j] = jnp.where(c == 0, odd, even)
         low = (pulled[...] * slope).astype(bf16)
         pre[j] = low
         normed_grad[...] += dot(low, w_up[j], 1, 1)
         return carry
 
     lax.fori_loop(0, 4, chunk, 0)
-    first = pltpu.make_async_copy(hidden, hidden_hbm, out_sems.at[1])
-    second = pltpu.make_async_copy(pre, pre_hbm, out_sems.at[2])
-    first.start()
-    second.start()
+    outs = [
+        pltpu.make_async_copy(hid_send, hid_send_hbm, out_sems.at[0]),
+        pltpu.make_async_copy(hid_keep, hid_keep_hbm, out_sems.at[1]),
+        pltpu.make_async_copy(pre.at[0:4], pre_hbm.at[0:4], out_sems.at[2]),
+    ]
+    for copy in outs:
+        copy.start()
+    for at, whole in enumerate((normed[...].T, att[...])):
+        rows = whole.reshape(8, 2, 48, 512)
+        turned_keep[at] = jnp.where(c == 0, rows[:, 0], rows[:, 1])
+        turned_send[at] = jnp.where(c == 0, rows[:, 1], rows[:, 0])
     wide = middle[...]
     scale = lax.rsqrt(jnp.mean(wide * wide, axis=-1, keepdims=True) + EPS)
     unit = wide * scale
@@ -494,226 +565,178 @@
     grad = cot[...].astype(f32) + inward
     middle_grad[...] = grad
     low = grad.astype(bf16)
-    branch_low[...] = low
+    pre[4] = low
+    outs.append(pltpu.make_async_copy(pre.at[4], pre_hbm.at[4], out_sems.at[3]))
+    outs[3].start()
     for other, dest in enumerate((near_grad, far_grad)):
         row = pl.multiple_of(jnp.bitwise_xor(xs, other) * 384, 128)
         dest[...] = dot(w_out[pl.ds(row, 384)], low, 1, 1).astype(bf16)
     result[...] = total[...].astype(bf16)
-    first.wait()
-    second.wait()
-
-
-def forward(place, att_near, att_far, x, cot, small, blocks, sides):
-    tokens = jax.ShapeDtypeStruct((512, 768), bf16)
+    for copy in outs:
+        copy.wait()
+
+
+def forward(place, att_near, att_far, x, cot, small, near, far):
     wide = jax.ShapeDtypeStruct((512, 768), f32)
     half = jax.ShapeDtypeStruct((384, 512), bf16)
+    hidden = jax.ShapeDtypeStruct((4, 512, 384), bf16)
+    turned = jax.ShapeDtypeStruct((2, 8, 48, 512), bf16)
     return pl.pallas_call(
         forward_kernel,
         out_shape=(
-            jax.ShapeDtypeStruct((4, 512, 768), bf16),
-            jax.ShapeDtypeStruct((4, 512, 768), bf16),
-            tokens,
-            tokens,
-            tokens,
-            wide,
-            jax.ShapeDtypeStruct((768, 512), bf16),
-            half,
-            half,
+            hidden, hidden, jax.ShapeDtypeStruct((5, 512, 768), bf16), turned, turned,
+            jax.ShapeDtypeStruct((512, 768), bf16), wide, half, half,
         ),
-        in_specs=[SCALARS, ANY, ANY, FULL, FULL, FULL] + [ANY] * 22,
-        out_specs=(ANY, ANY) + (FULL,) * 7,
+        in_specs=[SCALARS, ANY, ANY, FULL, FULL, FULL] + [ANY] * 19,
+        out_specs=(ANY, ANY, ANY) + (FULL,) * 6,
         scratch_shapes=[
             pltpu.VMEM((768, 768), bf16),
             pltpu.VMEM((4, 768, 768), bf16),
             pltpu.VMEM((64, 48, 768), bf16),
-            pltpu.VMEM((4, 512, 768), bf16),
-            pltpu.VMEM((4, 512, 768), bf16),
+            pltpu.VMEM((4, 512, 384), bf16),
+            pltpu.VMEM((4, 512, 384), bf16),
+            pltpu.VMEM((5, 512, 768), bf16),
             pltpu.VMEM((512, 768), f32),
             pltpu.VMEM((512, 768), f32),
             pltpu.VMEM((512, 768), f32),
             pltpu.VMEM((512, 768), f32),
+            pltpu.VMEM((512, 768), bf16),
+            pltpu.VMEM((768, 512), bf16),
             pltpu.SemaphoreType.DMA((4, 16)),
             pltpu.SemaphoreType.DMA((2,)),
-            pltpu.SemaphoreType.DMA((3,)),
+            pltpu.SemaphoreType.DMA((4,)),
         ],
         compiler_params=params(),
         cost_estimate=cost(8_500_000_000, 20_000_000, 512 * 3072),
         name="forward",
-    )(place, att_near, att_far, x, cot, small, *blocks, *sides)
-
-
-def contract_grad_kernel(place, hidden, cot, near, far):
-    made = dot(hidden[0], cot[...], 0, 0).astype(bf16).reshape(2, 2, 4, 48, 768)
-    near[...] = jnp.where(place[2] == 0, made[:, 0], made[:, 1])
-    far[...] = jnp.where(place[2] == 0, made[:, 1], made[:, 0])
-
-
-def contract_weight_grad(place, hidden, cot):
-    shape = jax.ShapeDtypeStruct((8, 4, 48, 768), bf16)
-    spec = pl.BlockSpec((2, 4, 48, 768), lambda j: (j, 0, 0, 0))
+    )(place, att_near, att_far, x, cot, small, *near, *far)
+
+
+def contract_grad_kernel(place, hid, hid_far, cot, cot_far, send, keep):
+    made = dot(hid[0], cot[...], 0, 0) + dot(hid_far[0], cot_far[...], 0, 0)
+    made = made.astype(bf16).reshape(2, 2, 2, 48, 768)
+    send[...] = jnp.where(place[3] == 0, made[:, 1], made[:, 0])
+    keep[...] = jnp.where(place[3] == 0, made[:, 0], made[:, 1])
+
+
+def contract_weight_grad(place, hid, hid_far, cot, cot_far):
+    shape = jax.ShapeDtypeStruct((8, 2, 48, 768), bf16)
+    spec = pl.BlockSpec((2, 2, 48, 768), lambda j: (j, 0, 0, 0))
+    chunk = pl.BlockSpec((1, 512, 384), lambda j: (j, 0, 0))
+    whole = pl.BlockSpec((512, 768), lambda j: (0, 0))
     return pl.pallas_call(
         contract_grad_kernel,
         out_shape=(shape, shape),
         grid=(4,),
-        in_specs=[
-            SCALARS,
-            pl.BlockSpec((1, 512, 768), lambda j: (j, 0, 0)),
-            pl.BlockSpec((512, 768), lambda j: (0, 0)),
-        ],
+        in_specs=[SCALARS, chunk, chunk, whole, whole],
         out_specs=(spec, spec),
         compiler_params=params(),
         cost_estimate=cost(2 * 512 * 3072 * 768, 9_000_000),
         name="contract_weight_grad",
-    )(place, hidden, cot)
-
-
-def expand_grad_kernel(place, normed, pre, att, branch, near, far):
+    )(place, hid, hid_far, cot, cot_far)
+
+
+def expand_grad_kernel(place, turned, turned_far, pre, pre_far, b_send, b_keep, c_send, c_keep):
     step = pl.program_id(0)
 
-    def store(made):
-        made = made.astype(bf16).reshape(8, 2, 48, 768)
-        near[:, 0] = jnp.where(place[2] == 0, made[:, 0], made[:, 1])
-        far[:, 0] = jnp.where(place[2] == 0, made[:, 1], made[:, 0])
-
-    @pl.when(step < 4)
+    def made(at):
+        near = dot(turned[at].reshape(384, 512), pre[0], 1, 0)
+        return (near + dot(turned_far[at].reshape(384, 512), pre_far[0], 1, 0)).astype(bf16)
+
+    @pl.when(step < 3)
     def _():
-        store(dot(normed[...], pre[0], 0, 0))
+        rows = made(0).reshape(4, 2, 48, 768)
+        b_send[:, 0] = jnp.where(place[1] == 0, rows[:, 1], rows[:, 0])
+        b_keep[:, 0] = jnp.where(place[1] == 0, rows[:, 0], rows[:, 1])
+
+    def by_low(rows):
+        rows = rows.reshape(2, 2, 2, 48, 768)
+        low = place[0] % 2
+        c_send[:, :, 0] = jnp.where(low == 0, rows[:, 1], rows[:, 0])
+        c_keep[:, :, 0] = jnp.where(low == 0, rows[:, 0], rows[:, 1])
+
+    @pl.when(step == 3)
+    def _():
+        by_low(made(0))
 
     @pl.when(step == 4)
     def _():
-        store(dot(att[...], branch[...], 1, 0))
-
-
-def expand_weight_grad(place, normed, pre, att, branch):
-    shape = jax.ShapeDtypeStruct((8, 5, 48, 768), bf16)
-    spec = pl.BlockSpec((8, 1, 48, 768), lambda j: (0, j, 0, 0))
-    whole = pl.BlockSpec((512, 768), lambda j: (0, 0))
+        by_low(made(1))
+
+
+def expand_weight_grad(place, turned, turned_far, pre, pre_far):
+    first = jax.ShapeDtypeStruct((4, 3, 48, 768), bf16)
+    second = jax.ShapeDtypeStruct((2, 2, 2, 48, 768), bf16)
+    first_spec = pl.BlockSpec((4, 1, 48, 768), lambda j: (0, jnp.minimum(j, 2), 0, 0))
+    second_spec = pl.BlockSpec((2, 2, 1, 48, 768), lambda j: (0, 0, jnp.maximum(j - 3, 0), 0, 0))
+    whole = pl.BlockSpec((2, 8, 48, 512), lambda j: (0, 0, 0, 0))
+    chunk = pl.BlockSpec((1, 512, 768), lambda j: (j, 0, 0))
     return pl.pallas_call(
         expand_grad_kernel,
-        out_shape=(shape, shape),
+        out_shape=(first, first, second, second),
         grid=(5,),
-        in_specs=[
-            SCALARS,
-            whole,
-            pl.BlockSpec((1, 512, 768), lambda j: (jnp.minimum(j, 3), 0, 0)),
-            pl.BlockSpec((768, 512), lambda j: (0, 0)),
-            whole,
-        ],
-        out_specs=(spec, spec),
+        in_specs=[SCALARS, whole, whole, chunk, chunk],
+        out_specs=(first_spec, first_spec, second_spec, second_spec),
         compiler_params=params(),
         cost_estimate=cost(2 * 512 * 768 * 3840, 12_000_000),
         name="expand_weight_grad",
-    )(place, normed, pre, att, branch)
-
-
-GROUPS = ((0, 4), (4, 2))
-
-
-def place_grads(x, group, pieces, grad, rows, sems):
-    dq_near, dq_far, dk, dv = pieces
-    size = 64 * GROUPS[group][1]
-    moves = []
-    for other, source in enumerate((dq_near, dq_far)):
-        lane = pl.multiple_of(jnp.bitwise_xor(x, other) * 512, 128)
-        moves.append((source, grad.at[rows[0] : rows[0] + size, pl.ds(lane, 512)]))
-    moves.append((dk, grad.at[rows[1] : rows[1] + size]))
-    moves.append((dv, grad.at[rows[2] : rows[2] + size]))
-    copies = [pltpu.make_async_copy(*move, sems.at[group, at]) for at, move in enumerate(moves)]
-    for copy in copies:
-        copy.start()
+    )(place, turned, turned_far, pre, pre_far)
+
+
+def place_grads(whole, grad, sems):
+    copies = []
+    for head in range(6):
+        dest = grad.at[head * 192 : head * 192 + 192]
+        copies.append(pltpu.make_async_copy(whole.at[head, 0:192], dest, sems.at[head]))
+        copies[-1].start()
     return copies
 
 
-def bias_sums(band, far):
-    flip = (iota((128, 128), 0) + iota((128, 128), 1) == 127).astype(f32)
-    total = None
-    heads = band.shape[0]
-    for block in range(3):
-        rows = []
-        for head in range(heads):
-            here = lax.dot_general(
-                flip, band[head, block * 128 : block * 128 + 128], (((1,), (0,)), ((), ())),
-                precision=lax.Precision.HIGHEST, preferred_element_type=f32,
-            )
-            wide = jnp.concatenate([here, jnp.zeros((128, 128), f32)], axis=1)
-            rolled = pltpu.roll(wide, 0, 1, stride=1, stride_axis=0)
-            rows.append(jnp.sum(rolled, axis=0, keepdims=True))
-        diagonals = jnp.concatenate(rows + [jnp.zeros((8 - heads, 256), f32)], axis=0)
-        offset = block * 128 - 1 - iota((256, 128), 0)
-        spread = (bucket_of(offset) == iota((256, 128), 1)).astype(f32)
-        made = lax.dot_general(
-            diagonals, spread, (((1,), (0,)), ((), ())),
-            precision=lax.Precision.HIGHEST, preferred_element_type=f32,
-        )
-        total = made if total is None else total + made
-    lane = iota((1, 128), 1)
-    rows = []
-    for head in range(heads):
-        sums = jnp.sum(far[head], axis=1, keepdims=True)
-        rows.append(jnp.where(lane == 15, sums[0:1], jnp.where(lane == 31, sums[1:2], 0.0)))
-    return total + jnp.concatenate(rows + [jnp.zeros((8 - heads, 128), f32)], axis=0)
-
-
-def weight_grad_kernel(group, place, normed, *refs):
-    pieces, (band, far_sum), refs = refs[:4], refs[4:6], refs[6:]
-    if group == 1:
-        bias, near, far, grad, sems = refs
-    else:
-        near, far, bias, grad, sems = refs
-    core = place[2]
-    size = 64 * GROUPS[group][1]
-    copies = place_grads(place[3], group, pieces, grad, (0, size, 2 * size), sems)
-
-    def store(made, low, high):
-        made = made.astype(bf16).reshape(8, 2, 48, high - low)
-        near[:, :, low:high] = jnp.where(core == 0, made[:, 0], made[:, 1])
-        far[:, :, low:high] = jnp.where(core == 0, made[:, 1], made[:, 0])
-
-    sums = bias_sums(band, far_sum)
-    if group == 0:
-        bias[...] = sums
-    else:
-        whole = jnp.concatenate([bias[0:4], sums[0:4]], axis=0)
-        spot = iota((768, 128), 0) % 48
-        bucket = (iota((768, 128), 0) // 48) * 2 + spot // 6
-        chosen = jnp.where((iota((768, 128), 1) == bucket) & (spot < 12), 1.0, 0.0)
-        per_head = lax.dot_general(
-            chosen, whole, (((1,), (1,)), ((), ())),
-            precision=lax.Precision.HIGHEST, preferred_element_type=f32,
-        )
-        pattern = (iota((768, 8), 1) == (iota((768, 8), 0) % 48) % 6).astype(f32)
-        column = jnp.sum(per_head * pattern, axis=1, keepdims=True)
-        store(jnp.where(iota((768, 128), 1) == 0, column, 0.0), 3 * size, 3 * size + 128)
+def weight_grad_kernel(place, mine, other, whole, near, far, grad, bias, sems, bias_sem):
+    copies = place_grads(whole, grad, sems)
+    copies.append(pltpu.make_async_copy(whole.at[5, 192:208, 0:128], bias, bias_sem))
+    copies[-1].start()
     for copy in copies:
         copy.wait()
-    store(dot(normed[...], grad[...], 0, 1), 0, 3 * size)
-
-
-def weight_grad(place, normed, group, pieces, rest):
-    columns = 192 * GROUPS[group][1]
-    owned = jax.ShapeDtypeStruct((8, 48, columns + 128 * group), bf16)
-    out_shape = (owned, owned) + ((jax.ShapeDtypeStruct((8, 128), f32),) if group == 0 else ())
+    for kind, rows, dest in ((place[2], mine, near), (1 - place[2], other, far)):
+        spot = iota((384, 128), 0) % 48
+        bucket = ((iota((384, 128), 0) // 48) * 2 + kind) * 2 + spot // 6
+        chosen = jnp.where((iota((384, 128), 1) == bucket) & (spot < 12), 1.0, 0.0)
+        per_head = dot(chosen.astype(bf16), bias[0:8], 1, 1)
+        pattern = (iota((384, 8), 1) == (iota((384, 8), 0) % 48) % 6).astype(f32)
+        column = jnp.sum(per_head * pattern, axis=1, keepdims=True)
+        side = jnp.where(iota((384, 128), 1) == 0, column, 0.0)
+        dest[:, :, 1152:1280] = side.astype(bf16).reshape(8, 48, 128)
+        left = rows[...].reshape(384, 1024)
+        for col in range(0, 1152, 384):
+            made = dot(left, grad[col : col + 384], 1, 1)
+            dest[:, :, col : col + 384] = made.astype(bf16).reshape(8, 48, 384)
+
+
+def weight_grad(place, mine, other, whole):
+    owned = jax.ShapeDtypeStruct((8, 48, 1280), bf16)
     return pl.pallas_call(
-        functools.partial(weight_grad_kernel, group),
-        out_shape=out_shape,
-        in_specs=[SCALARS, FULL] + [ANY] * 4 + [FULL] * len(rest),
-        out_specs=(FULL,) * len(out_shape),
-        scratch_shapes=[pltpu.VMEM((columns, 1024), bf16), pltpu.SemaphoreType.DMA((2, 4))],
+        weight_grad_kernel,
+        out_shape=(owned, owned),
+        in_specs=[SCALARS, FULL, FULL, ANY],
+        out_specs=(FULL,) * 2,
+        scratch_shapes=[
+            pltpu.VMEM((1152, 1024), bf16),
+            pltpu.VMEM((16, 128), bf16),
+            pltpu.SemaphoreType.DMA((6,)),
+            pltpu.SemaphoreType.DMA,
+        ],
         compiler_params=params(),
-        cost_estimate=cost(2 * 1024 * 768 * columns, 6_000_000),
-        name="weight_grad_" + str(group),
-    )(place, normed, *pieces, *rest)
+        cost_estimate=cost(2 * 1024 * 768 * 1152, 6_000_000),
+        name="weight_grad",
+    )(place, mine, other, whole)
 
 
 def project_back_kernel(place, *refs):
-    w_near, w_far, refs = refs[:4], refs[4:8], refs[8:]
-    pieces, refs = (refs[0:4], refs[4:8]), refs[8:]
+    (w_near, w_far), whole, refs = narrow_blocks(refs[:10]), refs[10], refs[11:]
     part_near, part_far, w, grad, sems, qsems = refs
     x = place[3]
-    copies = place_blocks(place, w_near, w_far, w, sems)
-    for group, (start, _) in enumerate(GROUPS):
-        rows = [start * 64 + at for at in (0, 384, 768)]
-        copies += place_grads(x, group, pieces[group], grad, rows, qsems)
+    copies = place_blocks(place, w_near, w_far, w, sems) + place_grads(whole, grad, qsems)
     for copy in copies:
         copy.wait()
     for other, dest in ((1, part_far), (0, part_near)):
@@ -721,55 +744,57 @@
         dest[...] = dot(grad[:, pl.ds(start, 512)], w[:, 0:1152], 0, 1).astype(bf16)
 
 
-def project_back(place, w_near, w_far, pieces):
+def project_back(place, blocks, whole):
     part = jax.ShapeDtypeStruct((512, 768), bf16)
     return pl.pallas_call(
         project_back_kernel,
         out_shape=(part, part),
-        in_specs=[SCALARS] + [ANY] * 16,
+        in_specs=[SCALARS] + [ANY] * 11,
         out_specs=(FULL,) * 2,
         scratch_shapes=[
             pltpu.VMEM((768, 1280), bf16),
             pltpu.VMEM((1152, 1024), bf16),
             pltpu.SemaphoreType.DMA((16,)),
-            pltpu.SemaphoreType.DMA((2, 4)),
+            pltpu.SemaphoreType.DMA((6,)),
         ],
         compiler_params=params(),
         cost_estimate=cost(2 * 1024 * 768 * 1152, 10_000_000),
         name="project_back",
-    )(place, *w_near, *w_far, *pieces[0], *pieces[1])
-
-
-def finish_kernel(place, near, far, g0_near, g0_far, g1_near, g1_far, qw, kw, vw, gain, contract, q, k, v, gain_grad, bias):
+    )(place, *blocks, whole)
+
+
+def finish_kernel(place, a_near, a_far, g_near, g_far, qw, kw, vw, gain, contract, q, k, v, gain_grad, bias):
     swapped = place[3] == 1
 
     def ordered(near, far):
         near, far = near[...].astype(f32), far[...].astype(f32)
         return jnp.where(swapped, far, near), jnp.where(swapped, near, far)
 
-    for half, wide in enumerate(ordered(near, far)):
+    for half, wide in enumerate(ordered(a_near, a_far)):
         for at in range(2):
             row = half * 96 + at * 48
             contract[row : row + 48] = wide[at]
-    (a0, b0), (a1, b1) = ordered(g0_near, g0_far), ordered(g1_near, g1_far)
+    first, second = ordered(g_near, g_far)
     for at, dest in enumerate((q, k, v)):
-        for half, (wide, thin) in enumerate(((a0, a1), (b0, b1))):
-            dest[:, half * 384 : half * 384 + 256] = wide[:, at * 256 : at * 256 + 256]
-            dest[:, half * 384 + 256 : half * 384 + 384] = thin[:, at * 128 : at * 128 + 128]
+        for half, wide in enumerate((first, second)):
+            for head in range(6):
+                column = head * 192 + at * 64
+                spot = half * 384 + head * 64
+                dest[:, spot : spot + 64] = wide[:, column : column + 64]
     joint = q[...] * qw[...].astype(f32) + k[...] * kw[...].astype(f32) + v[...] * vw[...].astype(f32)
     summed = jnp.broadcast_to(jnp.sum(joint, axis=1, keepdims=True), (48, 128))
     blank = jnp.zeros((80, 128), f32)
     turned = jnp.concatenate([summed, blank], axis=0).T
     gain_grad[...] = turned[0:1, 0:48] / gain[...].astype(f32)
-    first = jnp.concatenate([a1[:, 384:512], blank], axis=0).T
-    second = jnp.concatenate([b1[:, 384:512], blank], axis=0).T
+    first = jnp.concatenate([first[:, 1152:1280], blank], axis=0).T
+    second = jnp.concatenate([second[:, 1152:1280], blank], axis=0).T
     for row in range(2):
         cols = slice(row * 6, row * 6 + 6)
         bias[row : row + 1, 0:6] = first[0:1, cols]
         bias[row : row + 1, 6:12] = second[0:1, cols]
 
 
-def finish(place, near, far, g0_near, g0_far, g1_near, g1_far, qw, kw, vw, gain):
+def finish(place, a_near, a_far, g_near, g_far, qw, kw, vw, gain):
     full = jax.ShapeDtypeStruct((48, 768), f32)
     return pl.pallas_call(
         finish_kernel,
@@ -777,12 +802,12 @@
             jax.ShapeDtypeStruct((192, 768), f32),
             full, full, full, jax.ShapeDtypeStruct((1, 48), f32), jax.ShapeDtypeStruct((2, 12), f32),
         ),
-        in_specs=[SCALARS] + [FULL] * 10,
+        in_specs=[SCALARS] + [FULL] * 8,
         out_specs=(FULL,) * 6,
         compiler_params=params(),
         cost_estimate=cost(1000, 1_000_000),
         name="finish",
-    )(place, near, far, g0_near, g0_far, g1_near, g1_far, qw, kw, vw, gain.reshape(1, 48))
+    )(place, a_near, a_far, g_near, g_far, qw, kw, vw, gain.reshape(1, 48))
 
 
 def finish_wide_kernel(place, near, far, up, gain, expand, output, gain_grad):
@@ -865,8 +890,8 @@
         return made
 
 
-def gather_part(part, own, now):
-    array, dims, gone = part
+def gather_part(array, part, own, now):
+    _, dims, gone = part
     for axis in reversed(range(len(dims))):
         if dims[axis] == now:
             array = lax.dynamic_index_in_dim(array, 1 - own[now], axis, keepdims=False)
@@ -876,10 +901,10 @@
 
 
 def total(line, parts, own, now=None):
-    arrays = after([array for array, _, _ in parts], line.place)
+    arrays = after([part[0] for part in parts], line.place)
     made = None
-    for array, (_, dims, gone) in zip(arrays, parts):
-        term = gather_part((array, dims, gone), own, now)
+    for array, part in zip(arrays, parts):
+        term = gather_part(array, part, own, now)
         made = term if made is None else made + term
     made = lax.optimization_barrier(made.astype(bf16))
     line.wait(made)
@@ -899,8 +924,8 @@
 ):
     owner, x = lax.axis_index("fsdp"), lax.axis_index("seq")
     z, y, c = owner // 4, (owner // 2) % 2, owner % 2
-    place = jnp.stack([z, y, c, x, valid_len[0], instr_len[0], pair_flag[0]]).astype(jnp.int32)
-    line = Line(place)
+    where = jnp.stack([z, y, c, x]).astype(jnp.int32)
+    line = Line(where)
     tokens, cot = layer_input[0], cotangent[0]
 
     def by_z(array):
@@ -921,119 +946,99 @@
     shard = line.run(
         narrow_shard, query_weight, key_weight, value_weight, attention_gain, feedforward_gain, bias_table
     )
-    a2, a3, a1, b0 = by_zz(shard), swap(shard, "fsdp", 3 * Z), by_z(shard), by_y(shard)
-    x_far = by_x(tokens)
-    rest, own_side = line.run(wide_shard, expand_weight, output_weight, contract_weight)
-    a1, a2, a3, rest = lax.optimization_barrier((a1, a2, a3, rest))
-    along = jnp.stack([a1, a2, a3])
-    across = by_y(along)
+    a2, a1, b0 = by_zz(shard), by_z(shard), by_y(shard)
+    x_far, cot_far = by_x(tokens), by_core(cot)
+    rest, full = line.run(wide_shard, expand_weight, output_weight, contract_weight)
+    a2, a1, b0, rest, cot_far = lax.optimization_barrier((a2, a1, b0, rest, cot_far))
+    turned, b2 = by_z(jnp.stack([a2, b0])), by_y(a2)
+    four = by_core(jnp.stack([shard, b0, a1, a2]))
     z2, z1 = by_zz(rest), by_z(rest)
-    w_near = [shard, b0, along, across]
-    x_far, across, rest = lax.optimization_barrier((x_far, across, rest))
+    turned, b2, rest, x_far = lax.optimization_barrier((turned, b2, rest, x_far))
+    b3 = by_y(turned[0])
+    three = by_core(jnp.stack([turned[0], turned[1], b2]))
+    b3, rest, three = lax.optimization_barrier((b3, rest, three))
     y0 = by_y(rest)
-    w_far = [by_core(block) for block in w_near]
-
-    qkv, normed, small, table, tiles = line.run(project, tokens, x_far, w_near, w_far)
+    narrow = [shard, b0, a1, a2, turned, b2, b3, four, three, by_core(b3)]
+
+    lens = jnp.stack([valid_len[0], instr_len[0], pair_flag[0]])
+    line.place = jnp.concatenate([line.place, lens])
+    qkv, normed_kept, normed_sent, small, table, tiles = line.run(project, tokens, x_far, narrow)
     line.place, z1, z2, y0 = lax.optimization_barrier((line.place, z1, z2, y0))
-    z12 = jnp.stack([z1, z2])
-    z3, y12 = by_z(z2), by_y(z12)
-    sides = jnp.stack([z1[5:], z2[5:], y0[5:]])
-    sides_a = by_x(sides)
-    line.wait(sides, z12)
+    z3, y2 = by_z(z2), by_y(z2)
+    sides, trio = jnp.stack([z1[5:], z2[5:], y0[5:]]), jnp.stack([y0, z1, z2])
+    sides_a, far_full, far_three = by_x(sides), by_core(full), by_core(trio)
+    line.wait(sides, trio)
     out_theirs, kept_theirs, inverse_theirs = line.run(attend, table, tiles, qkv, False)
-    line.place, z3, sides_a, out_theirs = lax.optimization_barrier((line.place, z3, sides_a, out_theirs))
+    line.place, z3, y2, sides_a, out_theirs, far_full, far_three = lax.optimization_barrier(
+        (line.place, z3, y2, sides_a, out_theirs, far_full, far_three)
+    )
+    out_got = by_x(out_theirs)
     y3 = by_y(z3)
-    out_got = by_x(out_theirs)
-    sides_b = by_x(z3[5:])
+    y1 = jnp.concatenate([y0, sides_a[2]], axis=0)
+    sides, two = jnp.stack([z3[5:], y2[5:]]), jnp.stack([z3, y2])
+    line.wait(y1, sides, two)
+    y1, sides_b, far_two = by_z(y1), by_x(sides), by_core(two)
     out_mine, kept_mine, inverse_mine = line.run(attend, table, tiles, qkv, True)
-    out_mine, y12, out_got, sides_b, rest, own_side, y0, z12, z3, sides_a = lax.optimization_barrier(
-        (out_mine, y12, out_got, sides_b, rest, own_side, y0, z12, z3, sides_a)
-    )
-    sides_c = by_x(y12[:, 5:])
-    far = [by_core(block) for block in (rest, y0, z12, z3, y12)]
-    far[3], far[4] = far[4], far[3]
-    y3, sides_c = lax.optimization_barrier((y3, sides_c))
-    sides_d = by_x(y3[5:])
-    near, near_sides = [rest, y0, z12, y12, z3, y3], [own_side, sides_a, sides_b, sides_c, sides_d]
-    far, far_sides = far + [by_core(y3)], [by_core(side) for side in near_sides]
-    (
-        hidden, pre, layer_output, normed_two, branch_low, middle_grad, att, grad_mine, grad_sent,
-    ) = line.run(forward, out_mine, out_got, tokens, cot, small, near + far, near_sides + far_sides)
-    grad_theirs = by_x(grad_sent)
-
-    def parts(near, far_got, *left):
-        dims = ("high", "low", "y") + left
-        sizes = {"high": 2, "low": 2, "y": 2, "x": 2}
-        rest = near.size // (8 * 48 * near.shape[-1] * (2 if "x" in left else 1))
-        shape = tuple(sizes.get(dim, rest) for dim in dims) + (48, near.shape[-1])
-        return [(near.reshape(shape), dims, ()), (far_got.reshape(shape), dims, ())]
+    out_mine, out_got, sides_a, y3, sides_b, far_two, y1 = lax.optimization_barrier(
+        (out_mine, out_got, sides_a, y3, sides_b, far_two, y1)
+    )
+    sides_c = by_x(y3[5:])
+    near = [full, y0, z1, z2, z3, y2, y1, y3, sides_a, sides_b, sides_c]
+    far = [far_full, far_three, far_two] + [by_core(block) for block in (y1, y3, sides_a, sides_b, sides_c)]
+    hid, hid_sent, pre, turned, turned_sent, layer_output, middle_grad, grad_mine, grad_sent = line.run(
+        forward, out_mine, out_got, tokens, cot, small, near, far
+    )
+    hid_far, grad_theirs, pre_far, turned_far = by_core(hid_sent), by_x(grad_sent), by_core(pre), by_core(turned_sent)
 
     own = {"high": z // 2, "low": z % 2, "y": y, "x": x}
-    b_near, b_far = line.run(expand_weight_grad, normed_two, pre, att, branch_low)
-    b_parts = parts(b_near, by_core(b_far), "n")
-    a_near, a_far = line.run(contract_weight_grad, hidden, cot)
-    a_parts = parts(a_near, by_core(a_far), "x", "n")
-
-    def back_mine(place, group):
-        return attend_back(place, grad_mine, out_mine, inverse_mine, qkv, kept_mine, (), True, *GROUPS[group])
-
-    def back_theirs(place, group, carry):
-        return attend_back(
-            place, grad_theirs, out_theirs, inverse_theirs, qkv, kept_theirs, carry[1:], False, *GROUPS[group]
+
+    def parts(kept, got, *dims):
+        lead = tuple({"high": 2, "low": 2, "y": 2}[dim] for dim in dims if dim != "n")
+        shape = lead + kept.shape[-3:] if "n" in dims else lead + kept.shape[-2:]
+        return [(array.reshape(shape), dims, ()) for array in (kept, got)]
+
+    carry = line.run(
+        lambda place: attend_back(place, grad_mine, out_mine, inverse_mine, qkv, kept_mine, (), True)
+    )
+    line.wait(grad_theirs)
+    sent, kept = line.run(contract_weight_grad, hid, hid_far, cot, cot_far)
+    a_parts = parts(kept, by_x(sent), "high", "low", "y", "n")
+    b_sent, b_kept, c_sent, c_kept = line.run(expand_weight_grad, turned, turned_far, pre, pre_far)
+    b_parts = parts(b_kept, by_y(b_sent), "high", "low", "n")
+    c_got = by_z(c_sent)
+    c_parts = parts(c_kept, c_got, "high", "y", "n")
+    whole = line.run(
+        lambda place: attend_back(
+            place, grad_theirs, out_theirs, inverse_theirs, qkv, kept_theirs, carry, False
         )
-
-    mine0 = line.run(back_mine, 0)
-    line.wait(grad_theirs)
-    b_parts = keep(b_parts, "y", by_y(total(line, b_parts, own, "y")))
-    a_parts = keep(a_parts, "x", by_x(total(line, a_parts, own, "x")))
-    theirs0 = line.run(back_theirs, 0, mine0)
-    pieces0 = (mine0[0], *theirs0[:3])
-    g_near, g_far, bias0 = line.run(weight_grad, normed, 0, pieces0, theirs0[3:])
-    g_parts = parts(g_near, by_core(g_far))
-    mine1 = line.run(back_mine, 1)
+    )
+    line.wait(c_got)
+    g_near, g_far = line.run(weight_grad, normed_kept, normed_sent, whole)
+    g_parts = parts(g_near, by_core(g_far), "high", "low", "y")
     b_parts = keep(b_parts, "low", by_z(total(line, b_parts, own, "low")))
+    c_parts = keep(c_parts, "y", by_y(total(line, c_parts, own, "y")))
+    part_near, part_far = line.run(project_back, narrow, whole)
+    part_got = by_x(part_far)
     a_parts = keep(a_parts, "y", by_y(total(line, a_parts, own, "y")))
+    g_parts = keep(g_parts, "low", by_z(total(line, g_parts, own, "low")))
+    b_parts = keep(b_parts, "high", by_zz(total(line, b_parts, own, "high")))
+    c_parts = keep(c_parts, "high", by_zz(total(line, c_parts, own, "high")))
     g_parts = keep(g_parts, "y", by_y(total(line, g_parts, own, "y")))
-    theirs1 = line.run(back_theirs, 1, mine1)
-    pieces1 = (mine1[0], *theirs1[:3])
-    h_near, h_far = line.run(weight_grad, normed, 1, pieces1, (*theirs1[3:], bias0))
-    h_parts = parts(h_near, by_core(h_far))
-    b_parts = keep(b_parts, "high", by_zz(total(line, b_parts, own, "high")))
-    part_near, part_far = line.run(project_back, w_near, w_far, (pieces0, pieces1))
-    part_got = by_x(part_far)
-    arrays = after([array.reshape(4, 2, 48, 512) for array, _, _ in h_parts], line.place)
-
-    def for_owner(turn, dy):
-        terms = []
-        for array in arrays:
-            along_z = lax.dynamic_index_in_dim(array, z ^ turn, 0, keepdims=False)
-            terms.append(lax.dynamic_index_in_dim(along_z, y ^ dy, 0, keepdims=False).astype(f32))
-        return terms[0] + terms[1]
-
-    turns = [(turn, dy) for turn in range(4) for dy in range(2)][1:]
-    sends = lax.optimization_barrier([for_owner(*turn).astype(bf16) for turn in turns])
-    line.wait(*sends)
-    h_got = [swap(sent, "fsdp", Z * turn + Y * dy) for (turn, dy), sent in zip(turns, sends)]
     a_parts = keep(a_parts, "low", by_z(total(line, a_parts, own, "low")))
-    g_parts = keep(g_parts, "low", by_z(total(line, g_parts, own, "low")))
-    b_low = total(line, b_parts, own)
+    b_low = jnp.concatenate([total(line, b_parts, own), total(line, c_parts, own)], axis=0)
+    b_low = lax.optimization_barrier(b_low)
     b_other = by_x(b_low)
-    line.wait(*h_got)
-    arrays, h_got = lax.optimization_barrier((arrays, h_got))
-    made = for_owner(0, 0)
-    for got in h_got:
-        made = made + got.astype(f32)
-    h_low = lax.optimization_barrier(made.astype(bf16))
-    line.wait(h_low)
-    h_other = by_x(h_low)
+    line.wait(b_low)
+    result = line.run(input_grad, tokens, small, part_near, part_got, middle_grad)
+    g_parts = keep(g_parts, "high", by_zz(total(line, g_parts, own, "high")))
     a_parts = keep(a_parts, "high", by_zz(total(line, a_parts, own, "high")))
-    g_parts = keep(g_parts, "high", by_zz(total(line, g_parts, own, "high")))
-    result = line.run(input_grad, tokens, small, part_near, part_got, middle_grad)
-    a_low, g_low = total(line, a_parts, own), total(line, g_parts, own)
-    a_other, g_other = by_x(a_low), by_x(g_low)
     expand_sum, output_sum, gain_two = line.run(finish_wide, b_low, b_other, expand_weight, feedforward_gain)
+    g_low = total(line, g_parts, own)
+    g_other = by_x(g_low)
+    a_low = total(line, a_parts, own)
+    a_other = by_x(a_low)
     contract_sum, *grads, gain_one, bias_grad = line.run(
-        finish, a_low, a_other, g_low, g_other, h_low, h_other, query_weight, key_weight, value_weight, attention_gain
+        finish, a_low, a_other, g_low, g_other, query_weight, key_weight, value_weight, attention_gain
     )
     return (
         layer_output[None], result[None], gain_one[0], gain_two[0], *grads,

time: 275 us -> 249 us (0.905)
  Pallas kernels: 127 us -> 117 us
  other arithmetic: 24.5 us -> 15.5 us
  starting transfers between devices: 59.3 us -> 52.1 us
  local copies, waits for them, and re-layouts: 6.03 us -> 11.9 us
  waiting for transfers between devices: 52.6 us -> 46.8 us
    convert_element_type x13 -> x14, other arithmetic: 22.3 us -> 13.8 us  [total(): made = lax.optimization_barrier(made.astype(bf16))]
    ppermute x59 -> x52, starting transfers between devices: 59.3 us -> 52.1 us  [swap(): return lax.ppermute(array, axis, [(i, i ^ bit) for i in range(count)])]
    unnamed x88 -> x102, local copies, waits for them, and re-layouts: 5.33 us -> 11.8 us
    ppermute x59 -> x52, waiting for transfers between devices: 52.6 us -> 46.8 us  [swap(): return lax.ppermute(array, axis, [(i, i ^ bit) for i in range(count)])]
    pallas_call x4 -> x3, Pallas kernels: 43.5 us -> 38.5 us  [the longest x1 23.1 us: forward(): pl.pallas_call(forward_kernel, out_shape=(hidden, hidden, jax.ShapeDtypeS...]
    pallas_call x4 -> x2, Pallas kernels: 29 us -> 24.4 us  [attend_back(): pl.pallas_call(functools.partial(attend_back_kernel, bool(carry), mine),...]
  transfers between devices with their start and end apart: 59 -> 52, of which waited for: 20 -> 18; matrix products, arithmetic and copies ran while one was open for 9% -> 6% of each run, Pallas kernels for 34% -> 34%
where the time goes in v3:
time: 249 us; the launch traced here: 247 us
  Pallas kernels  117 us (47%)
  starting transfers between devices  52.1 us (21%)
  waiting for transfers between devices  46.8 us (19%)
  other arithmetic  15.5 us (6%)
  local copies, waits for them, and re-layouts  11.9 us (5%)
  between operations  3.38 us (1%)
    ppermute x52, starting transfers between devices, swap(): return lax.ppermute(array, axis, [(i, i ^ bit) for i in range(count)])  52.1 us
    ppermute x52, waiting for transfers between devices, swap(): return lax.ppermute(array, axis, [(i, i ^ bit) for i in range(count)])  46.8 us
    pallas_call x2, Pallas kernels, attend_back(): pl.pallas_call(functools.partial(attend_back_kernel, bool(carry), mine),...  24.4 us
    pallas_call x1, Pallas kernels, forward(): pl.pallas_call(forward_kernel, out_shape=(hidden, hidden, jax.ShapeDtypeS...  23.1 us
    pallas_call x2, Pallas kernels, attend(): pl.pallas_call(functools.partial(attend_kernel, mine), out_shape=(jax.Sha...  21 us
    convert_element_type x14, other arithmetic, total(): made = lax.optimization_barrier(made.astype(bf16))  13.8 us
    unnamed x102, local copies, waits for them, and re-layouts  11.8 us
    pallas_call x1, Pallas kernels, expand_weight_grad(): pl.pallas_call(expand_grad_kernel, out_shape=(first, first, second, secon...  8.34 us
  transfers between devices with their start and end apart: 52, of which 18 were waited for; matrix products, arithmetic and copies ran while one was open for 6% of the time, Pallas kernels for 34%

profile of v3, /device:TPU:0, one launch (start us, length us, event | category | flops | bytes accessed | tf_op | source)
XLA Modules:
  0.0 247.2 jit_solution(4837154743023250039)
XLA Ops:
  1.2 2.6 %collective-permute-start.6 = (bf16[512,768]{1,0:T(8,128)(2,1)}, bf16[512,768]{1,0:T(8,128)(2,1)S(1)}, u32[]{:S(2)}, u32[]{:S(2)}) collective-permute-start(bf16[512,768]{1,0:T(8,128)(2,1)} %bitcast.112), channel_id=1, source_target_pairs={{0,1},{1,0},{2,3},{3,2},{4,5},{5,4},{6,7},{7,6},{8,9},{9,8},{10,11... | collective-permute-start | bytes 2359304 | tf_op jit(solution)/shard_map/ppermute | solution.py:865
  4.3 1.8 narrow_shard.1.refs_0_
  6.1 2.6 %collective-permute-start = (bf16[48,1280]{1,0:T(8,128)(2,1)}, bf16[48,1280]{1,0:T(8,128)(2,1)S(1)}, u32[]{:S(2)}, u32[]{:S(2)}) collective-permute-start(bf16[48,1280]{1,0:T(8,128)(2,1)} %narrow_shard.1.refs_0_), channel_id=1, source_target_pairs={{0,16},{2,18},{4,20},{6,22},{8,24},{10,26},{12,28},{14,30},{16,0},... | collective-permute-start | bytes 368648 | tf_op jit(solution)/shard_map/ppermute | solution.py:865
  8.7 1.6 collective-permute-start.1
  10.3 1.5 collective-permute-start.2
  11.8 2.9 %wide_shard.1 = (bf16[7,48,768]{2,1,0:T(8,128)(2,1)}, bf16[9,48,768]{2,1,0:T(8,128)(2,1)}) custom-call(s32[4]{0:T(128)} %pad_add_fusion.place, bf16[48,3072]{1,0:T(8,128)(2,1)} %up.1, bf16[48,768]{1,0:T(8,128)(2,1)} %output.1, bf16[192,768]{1,0:T(8,128)(2,1)} %contract.1), custom_call_target="tpu_custom_call" | custom-call | flops 1000 | bytes 1000 | tf_op jit(solution)/shard_map/wide_shard/pallas_call | solution.py:101
  15.6 1.5 collective-permute-start.4
  17.1 1.5 collective-permute-start.5
  18.6 3.5 %collective-permute-done.6.x_far = bf16[512,768]{1,0:T(8,128)(2,1)S(1)} collective-permute-done((bf16[512,768]{1,0:T(8,128)(2,1)}, bf16[512,768]{1,0:T(8,128)(2,1)S(1)}, u32[]{:S(2)}, u32[]{:S(2)}) %collective-permute-start.6) | collective-permute-done | bytes 786464 | tf_op jit(solution)/shard_map/ppermute | solution.py:865
  22.8 1.6 collective-permute-start.7
  24.3 1.7 collective-permute-start.11
  26.0 3.1 %collective-permute-start.12 = (bf16[7,48,768]{2,1,0:T(8,128)(2,1)}, bf16[7,48,768]{2,1,0:T(8,128)(2,1)S(1)}, u32[]{:S(2)}, u32[]{:S(2)}) collective-permute-start(bf16[7,48,768]{2,1,0:T(8,128)(2,1)} %get-tuple-element.182), channel_id=1, source_target_pairs={{0,16},{2,18},{4,20},{6,22},{8,24},{10,26},{12,28},{14,30},{16,0},... | collective-permute-start | bytes 1548296 | tf_op jit(solution)/shard_map/ppermute | solution.py:865
  29.1 1.0 collective-permute-start.13
  34.8 7.7 %project.1 = (bf16[1152,1024]{1,0:T(8,128)(2,1)}, bf16[8,48,1024]{2,1,0:T(8,128)(2,1)}, bf16[8,48,1024]{2,1,0:T(8,128)(2,1)}, f32[8,768]{1,0:T(8,128)}, f32[8,128]{1,0:T(8,128)}, /*index=5*/f32[6,384,128]{2,1,0:T(8,128)}) custom-call(s32[7]{0:T(128)} %pad_add_fusion.1.place, bf16[512,768]{1,0:T(8,128)(2,1)} %bitcast.113, bf16[512,768]{1,0:T(8,128)(2,1)} %copy-done.27, ...), custom_call_target="tpu_custom_call" | custom-call | flops 1000 | bytes 1000 | tf_op jit(solution)/shard_map/project/pallas_call | solution.py:193
  42.5 6.7 %collective-permute-done.11.refs_2_ = bf16[7,48,768]{2,1,0:T(8,128)(2,1)S(1)} collective-permute-done((bf16[7,48,768]{2,1,0:T(8,128)(2,1)}, bf16[7,48,768]{2,1,0:T(8,128)(2,1)S(1)}, u32[]{:S(2)}, u32[]{:S(2)}) %collective-permute-start.11) | collective-permute-done | bytes 516128 | tf_op jit(solution)/shard_map/ppermute | solution.py:865
  49.2 3.0 %collective-permute-done.12.refs_3_ = bf16[7,48,768]{2,1,0:T(8,128)(2,1)S(1)} collective-permute-done((bf16[7,48,768]{2,1,0:T(8,128)(2,1)}, bf16[7,48,768]{2,1,0:T(8,128)(2,1)S(1)}, u32[]{:S(2)}, u32[]{:S(2)}) %collective-permute-start.12) | collective-permute-done | bytes 516128 | tf_op jit(solution)/shard_map/ppermute | solution.py:865
  52.5 1.2 copy-done.28
  55.6 10.6 %attend_theirs.1 = (bf16[384,512]{1,0:T(8,128)(2,1)}, bf16[6,1024,512]{2,1,0:T(8,128)(2,1)}, f32[6,1,512]{2,1,0:T(1,128)}) custom-call(s32[7]{0:T(128)} %pad_add_fusion.1.place, f32[8,128]{1,0:T(8,128)} %get-tuple-element.188.table, f32[6,384,128]{2,1,0:T(8,128)} %get-tuple-element.189.tile, bf16[1152,1024]{1,0:T(8,128)(2,1)} %get-tuple-element.180.q.k.v, ...), custom_call_target="tpu_custom_call" | custom-call | flops 1000 | bytes 1000 | tf_op jit(solution)/shard_map/attend_theirs/pallas_call | solution.py:288
  66.9 1.1 collective-permute-done.14.refs_4_
  68.4 1.2 copy-done.12
  69.6 1.5 collective-permute-start.23
  72.8 1.3 collective-permute-start.21
  74.1 10.4 %attend_mine.1 = (bf16[384,512]{1,0:T(8,128)(2,1)}, bf16[6,1024,512]{2,1,0:T(8,128)(2,1)}, f32[6,1,512]{2,1,0:T(1,128)}) custom-call(s32[7]{0:T(128)} %pad_add_fusion.1.place, f32[8,128]{1,0:T(8,128)} %get-tuple-element.188.table, f32[6,384,128]{2,1,0:T(8,128)} %get-tuple-element.189.tile, bf16[1152,1024]{1,0:T(8,128)(2,1)} %get-tuple-element.180.q.k.v, ...), custom_call_target="tpu_custom_call" | custom-call | flops 1000 | bytes 1000 | tf_op jit(solution)/shard_map/attend_mine/pallas_call | solution.py:288
  84.5 3.6 %collective-permute-done.21.refs_9_ = bf16[2,2,48,768]{3,2,1,0:T(8,128)(2,1)S(1)} collective-permute-done((bf16[2,2,48,768]{3,2,1,0:T(8,128)(2,1)S(1)}, bf16[2,2,48,768]{3,2,1,0:T(8,128)(2,1)S(1)}, u32[]{:S(2)}, u32[]{:S(2)}) %collective-permute-start.21) | collective-permute-done | bytes 294944 | tf_op jit(solution)/shard_map/ppermute | solution.py:865
  88.8 1.0 collective-permute-start.24
  90.0 5.1 %collective-permute-done.24.refs_10_ = bf16[2,48,768]{2,1,0:T(8,128)(2,1)S(1)} collective-permute-done((bf16[2,48,768]{2,1,0:T(8,128)(2,1)S(1)}, bf16[2,48,768]{2,1,0:T(8,128)(2,1)S(1)}, u32[]{:S(2)}, u32[]{:S(2)}) %collective-permute-start.24) | collective-permute-done | bytes 147488 | tf_op jit(solution)/shard_map/ppermute | solution.py:865
  95.1 1.4 collective-permute-done.29.refs_18_
  97.8 23.1 %forward.1 = (bf16[4,512,384]{2,1,0:T(8,128)(2,1)}, bf16[4,512,384]{2,1,0:T(8,128)(2,1)}, bf16[5,512,768]{2,1,0:T(8,128)(2,1)}, bf16[2,8,48,512]{3,2,1,0:T(8,128...) custom-call(s32[7]{0:T(128)} %pad_add_fusion.1.place, ...), custom_call_target="tpu_custom_call" | custom-call | flops 8500000 | bytes 20000 | tf_op jit(solution)/shard_map/forward/pallas_call | solution.py:584
  121.6 1.0 collective-permute-start.30
  122.5 11.5 %attend_back_mine.1 = (bf16[384,512]{1,0:T(8,128)(2,1)}, f32[384,1024]{1,0:T(8,128)}, f32[384,1024]{1,0:T(8,128)}, f32[6,384,128]{2,1,0:T(8,128)}, f32[6,8,512]{2,1,0:T(8,128)}) custom-call(s32[7]{0:T(128)} %pad_add_fusion.1.place, bf16[384,512]{1,0:T(8,128)(2,1)} %get-tuple-element.214.grad, bf16[384,512]{1,0:T(8,128)(2,1)} %get-tuple-element.201.att_near.out, ...), custom_call_target="tpu_custom_call" | custom-call | flops 3221225 | bytes 6000 | tf_op jit(solution)/shard_map/attend_back_mine/pallas_call | solution.py:450
  134.0 1.2 copy-done.11
  135.3 6.3 %contract_weight_grad.1 = (bf16[8,2,48,768]{3,2,1,0:T(8,128)(2,1)}, bf16[8,2,48,768]{3,2,1,0:T(8,128)(2,1)}) custom-call(s32[7]{0:T(128)} %pad_add_fusion.1.place, bf16[4,512,384]{2,1,0:T(8,128)(2,1)} %get-tuple-element.212.hid, bf16[4,512,384]{2,1,0:T(8,128)(2,1)} %copy-done.11, bf16[512,768]{1,0:T(8,128)(2,1)} %bitcast.119, bf16[512,768]{1,0:T(8,128)(2,1)} %copy-done.23), custom_call_target="tpu_custom_call" | custom-call | flops 2415919 | bytes 9000 | tf_op jit(solution)/shard_map/contract_weight_grad/pallas_call | solution.py:627
  142.5 1.3 copy-done.1
  143.8 8.3 %expand_weight_grad.1 = (bf16[4,3,48,768]{3,2,1,0:T(8,128)(2,1)}, bf16[4,3,48,768]{3,2,1,0:T(8,128)(2,1)}, bf16[2,2,2,48,768]{4,3,2,1,0:T(8,128)(2,1)}, bf16[2,2,2,48,768]{4,3,2,1,0:T(8,128)(2,1)}) custom-call(s32[7]{0:T(128)} %pad_add_fusion.1.place, bf16[2,8,48,512]{3,2,1,0:T(8,128)(2,1)} %get-tuple-element.225.turned, bf16[2,8,48,512]{3,2,1,0:T(8,128)(2,1)} %copy-done.25, ...), custom_call_target="tpu_custom_call" | custom-call | flops 3019898 | bytes 12000 | tf_op jit(solution)/shard_map/expand_weight_grad/pallas_call | solution.py:674
  152.6 1.2 collective-permute-start.36
  153.8 1.5 collective-permute-start.35
  155.3 13.0 %attend_back_theirs.1.whole.refs_10_ = bf16[6,208,1024]{2,1,0:T(8,128)(2,1)} custom-call(s32[7]{0:T(128)} %pad_add_fusion.1.place, bf16[384,512]{1,0:T(8,128)(2,1)} %copy-done.42, bf16[384,512]{1,0:T(8,128)(2,1)} %get-tuple-element.200.out, f32[6,1,512]{2,1,0:T(1,128)} %get-tuple-element.230.inverse, bf16[1152,1024]{1,0:T(8,128)(2,1)} %get-tuple-element.180.q.k.v, ...), custom_call_target="tpu_custom_call" | custom-call | flops 3221225 | bytes 6000 | tf_op jit(solution)/shard_map/attend_back_theirs/pallas_call | solution.py:450
  168.3 7.1 %weight_grad.1 = (bf16[8,48,1280]{2,1,0:T(8,128)(2,1)}, bf16[8,48,1280]{2,1,0:T(8,128)(2,1)}) custom-call(s32[7]{0:T(128)} %pad_add_fusion.1.place, bf16[8,48,1024]{2,1,0:T(8,128)(2,1)} %get-tuple-element.239.mine, bf16[8,48,1024]{2,1,0:T(8,128)(2,1)} %get-tuple-element.240.other, bf16[6,208,1024]{2,1,0:T(8,128)(2,1)} %attend_back_theirs.1.whole.refs_10_), custom_call_target="tpu_custom_call" | custom-call | flops 1811939 | bytes 6000 | tf_op jit(solution)/shard_map/weight_grad/pallas_call | solution.py:718
  176.5 1.5 collective-permute-start.38
  178.0 1.7 fusion.8
  179.7 6.4 %project_back.1 = (bf16[512,768]{1,0:T(8,128)(2,1)}, bf16[512,768]{1,0:T(8,128)(2,1)}) custom-call(s32[7]{0:T(128)} %pad_add_fusion.1.place, bf16[48,1280]{1,0:T(8,128)(2,1)} %narrow_shard.1.refs_0_, bf16[48,1280]{1,0:T(8,128)(2,1)} %copy-done.10, bf16[48,1280]{1,0:T(8,128)(2,1)} %copy-done.16, bf16[48,1280]{1,0:T(8,128)(2,1)} %copy-done.9, ...), custom_call_target="tpu_custom_call" | custom-call | flops 1811939 | bytes 10000 | tf_op jit(solution)/shard_map/project_back/pallas_call | solution.py:749
  186.2 1.0 fusion
  187.6 1.9 fusion.2
  190.0 1.1 collective-permute-start.39
  192.8 1.2 fusion.7
  194.0 2.5 %collective-permute-start.42 = (bf16[3,48,768]{2,1,0:T(8,128)(2,1)S(1)}, bf16[3,48,768]{2,1,0:T(8,128)(2,1)S(1)}, u32[]{:S(2)}, u32[]{:S(2)}) collective-permute-start(bf16[3,48,768]{2,1,0:T(8,128)(2,1)S(1)} %fusion.7), channel_id=1, source_target_pairs={{0,16},{2,18},{4,20},{6,22},{8,24},{10,26},{12,28},{14,30},{16,0},... | collective-permute-start | bytes 663560 | tf_op jit(solution)/shard_map/ppermute | solution.py:865
  196.6 3.7 %collective-permute-done.39 = bf16[2,2,48,768]{3,2,1,0:T(8,128)(2,1)} collective-permute-done((bf16[2,2,48,768]{3,2,1,0:T(8,128)(2,1)}, bf16[2,2,48,768]{3,2,1,0:T(8,128)(2,1)}, u32[]{:S(2)}, u32[]{:S(2)}) %collective-permute-start.39) | collective-permute-done | bytes 294944 | tf_op jit(solution)/shard_map/ppermute | solution.py:865
  200.2 1.1 fusion.14
  201.3 2.4 collective-permute-start.43
  203.8 5.4 %collective-permute-done.40 = bf16[2,2,48,1280]{3,2,1,0:T(8,128)(2,1)} collective-permute-done((bf16[2,2,48,1280]{3,2,1,0:T(8,128)(2,1)}, bf16[2,2,48,1280]{3,2,1,0:T(8,128)(2,1)}, u32[]{:S(2)}, u32[]{:S(2)}) %collective-permute-start.40) | collective-permute-done | bytes 491552 | tf_op jit(solution)/shard_map/ppermute | solution.py:865
  209.2 1.2 fusion.3
  211.8 2.6 %collective-permute-start.46 = (bf16[2,2,48,768]{3,2,1,0:T(8,128)(2,1)S(1)}, bf16[2,2,48,768]{3,2,1,0:T(8,128)(2,1)S(1)}, u32[]{:S(2)}, u32[]{:S(2)}) collective-permute-start(bf16[2,2,48,768]{3,2,1,0:T(8,128)(2,1)S(1)} %fusion.1), channel_id=1, source_target_pairs={{0,8},{2,10},{4,12},{6,14},{8,0},{10,2},{12,4},{14,6},{16,24},{18,... | collective-permute-start | bytes 884744 | tf_op jit(solution)/shard_map/ppermute | solution.py:865
  214.4 1.3 fusion.6
  215.7 1.1 fusion.13
  218.6 3.8 %input_grad.1 = bf16[512,768]{1,0:T(8,128)(2,1)} custom-call(s32[7]{0:T(128)} %pad_add_fusion.1.place, bf16[512,768]{1,0:T(8,128)(2,1)} %bitcast.115, f32[8,768]{1,0:T(8,128)} %get-tuple-element.203.small, bf16[512,768]{1,0:T(8,128)(2,1)} %get-tuple-element.251.near, bf16[512,768]{1,0:T(8,128)(2,1)} %copy-done.24, f32[512,768]{1,0:T(8,128)} %get-tuple-element.289.middle_grad), custom_call_target="tpu_custom_call" | custom-call | flops 7864 | bytes 6000 | tf_op jit(solution)/shard_map/input_grad/pallas_call | solution.py:852
  222.4 1.0 fusion.17
  223.4 1.1 collective-permute-start.48
  224.6 1.9 collective-permute-start.49
  227.3 2.2 finish_wide.1
  229.4 4.7 %collective-permute-done.48 = bf16[48,1280]{1,0:T(8,128)(2,1)S(1)} collective-permute-done((bf16[48,1280]{1,0:T(8,128)(2,1)S(1)}, bf16[48,1280]{1,0:T(8,128)(2,1)S(1)}, u32[]{:S(2)}, u32[]{:S(2)}) %collective-permute-start.48) | collective-permute-done | bytes 122912 | tf_op jit(solution)/shard_map/ppermute | solution.py:865
  234.1 1.0 fusion.16.g_near
  236.2 1.3 collective-permute-start.50
  238.3 5.2 %collective-permute-done.51.g_far = bf16[48,1280]{1,0:T(8,128)(2,1)S(1)} collective-permute-done((bf16[48,1280]{1,0:T(8,128)(2,1)S(1)}, bf16[48,1280]{1,0:T(8,128)(2,1)S(1)}, u32[]{:S(2)}, u32[]{:S(2)}) %collective-permute-start.51) | collective-permute-done | bytes 122912 | tf_op jit(solution)/shard_map/ppermute | solution.py:865
  244.8 2.4 finish.1
  (189 shorter events, 24.7 us)
Async XLA Ops:
  0.6 14.9 %collective-permute-start.3 = (bf16[512,768]{1,0:T(8,128)(2,1)}, bf16[512,768]{1,0:T(8,128)(2,1)S(1)}, u32[]{:S(2)}, u32[]{:S(2)}) collective-permute-start(bf16[512,768]{1,0:T(8,128)(2,1)} %bitcast.117), channel_id=1, source_target_pairs={{0,2},{2,0},{4,6},{6,4},{8,10},{10,8},{12,14},{14,12},{16,18},{18,... | collective-permute-start | bytes 2359304 | tf_op jit(solution)/shard_map/ppermute | solution.py:865
  1.2 20.9 %collective-permute-start.6 = (bf16[512,768]{1,0:T(8,128)(2,1)}, bf16[512,768]{1,0:T(8,128)(2,1)S(1)}, u32[]{:S(2)}, u32[]{:S(2)}) collective-permute-start(bf16[512,768]{1,0:T(8,128)(2,1)} %bitcast.112), channel_id=1, source_target_pairs={{0,1},{1,0},{2,3},{3,2},{4,5},{5,4},{6,7},{7,6},{8,9},{9,8},{10,11... | collective-permute-start | bytes 2359304 | tf_op jit(solution)/shard_map/ppermute | solution.py:865
  6.1 24.0 %copy-start.8 = (bf16[48,1280]{1,0:T(8,128)(2,1)S(1)}, bf16[48,1280]{1,0:T(8,128)(2,1)}, u32[]{:S(2)}) copy-start(bf16[48,1280]{1,0:T(8,128)(2,1)} %narrow_shard.1.refs_0_) | copy-start | bytes 368644
  6.1 26.6 %copy-start.50 = (s32[4]{0:T(128)S(1)}, s32[4]{0:T(128)}, u32[]{:S(2)}) copy-start(s32[4]{0:T(128)} %pad_add_fusion.place) | copy-start | bytes 52
  6.1 9.3 %collective-permute-start = (bf16[48,1280]{1,0:T(8,128)(2,1)}, bf16[48,1280]{1,0:T(8,128)(2,1)S(1)}, u32[]{:S(2)}, u32[]{:S(2)}) collective-permute-start(bf16[48,1280]{1,0:T(8,128)(2,1)} %narrow_shard.1.refs_0_), channel_id=1, source_target_pairs={{0,16},{2,18},{4,20},{6,22},{8,24},{10,26},{12,28},{14,30},{16,0},... | collective-permute-start | bytes 368648 | tf_op jit(solution)/shard_map/ppermute | solution.py:865
  8.7 6.8 %collective-permute-start.1 = (bf16[48,1280]{1,0:T(8,128)(2,1)}, bf16[48,1280]{1,0:T(8,128)(2,1)S(1)}, u32[]{:S(2)}, u32[]{:S(2)}) collective-permute-start(bf16[48,1280]{1,0:T(8,128)(2,1)} %narrow_shard.1.refs_0_), channel_id=1, source_target_pairs={{0,8},{2,10},{4,12},{6,14},{8,0},{10,2},{12,4},{14,6},{16,24},{18,... | collective-permute-start | bytes 368648 | tf_op jit(solution)/shard_map/ppermute | solution.py:865
  10.3 5.3 %collective-permute-start.2 = (bf16[48,1280]{1,0:T(8,128)(2,1)}, bf16[48,1280]{1,0:T(8,128)(2,1)S(1)}, u32[]{:S(2)}, u32[]{:S(2)}) collective-permute-start(bf16[48,1280]{1,0:T(8,128)(2,1)} %narrow_shard.1.refs_0_), channel_id=1, source_target_pairs={{0,4},{2,6},{4,0},{6,2},{8,12},{10,14},{12,8},{14,10},{16,20},{18,... | collective-permute-start | bytes 368648 | tf_op jit(solution)/shard_map/ppermute | solution.py:865
  15.4 18.0 %copy-start.9 = (bf16[48,1280]{1,0:T(8,128)(2,1)}, bf16[48,1280]{1,0:T(8,128)(2,1)S(1)}, u32[]{:S(2)}) copy-start(bf16[48,1280]{1,0:T(8,128)(2,1)S(1)} %collective-permute-done.refs_3_) | copy-start | bytes 368644
  15.5 17.8 %copy-start.16 = (bf16[48,1280]{1,0:T(8,128)(2,1)}, bf16[48,1280]{1,0:T(8,128)(2,1)S(1)}, u32[]{:S(2)}) copy-start(bf16[48,1280]{1,0:T(8,128)(2,1)S(1)} %collective-permute-done.1.refs_2_) | copy-start | bytes 368644
  15.5 17.8 %copy-start.10 = (bf16[48,1280]{1,0:T(8,128)(2,1)}, bf16[48,1280]{1,0:T(8,128)(2,1)S(1)}, u32[]{:S(2)}) copy-start(bf16[48,1280]{1,0:T(8,128)(2,1)S(1)} %collective-permute-done.2.refs_1_) | copy-start | bytes 368644
  15.6 26.9 %copy-start.23 = (bf16[512,768]{1,0:T(8,128)(2,1)}, bf16[512,768]{1,0:T(8,128)(2,1)S(1)}, u32[]{:S(2)}) copy-start(bf16[512,768]{1,0:T(8,128)(2,1)S(1)} %collective-permute-done.3.cot_far) | copy-start | bytes 2359300
  15.6 7.0 %collective-permute-start.4 = (bf16[2,48,1280]{2,1,0:T(8,128)(2,1)S(1)}, bf16[2,48,1280]{2,1,0:T(8,128)(2,1)S(1)}, u32[]{:S(2)}, u32[]{:S(2)}) collective-permute-start(bf16[2,48,1280]{2,1,0:T(8,128)(2,1)S(1)} %pad_maximum_fusion.8), channel_id=1, source_target_pairs={{0,8},{2,10},{4,12},{6,14},{8,0},{10,2},{12,4},{14,6},{16,24},{18,... | collective-permute-start | bytes 737288 | tf_op jit(solution)/shard_map/ppermute | solution.py:865
  17.1 5.0 %collective-permute-start.5 = (bf16[48,1280]{1,0:T(8,128)(2,1)S(1)}, bf16[48,1280]{1,0:T(8,128)(2,1)S(1)}, u32[]{:S(2)}, u32[]{:S(2)}) collective-permute-start(bf16[48,1280]{1,0:T(8,128)(2,1)S(1)} %collective-permute-done.refs_3_), channel_id=1, source_target_pairs={{0,4},{2,6},{4,0},{6,2},{8,12},{10,14},{12,8},{14,10},{16,20},{18,... | collective-permute-start | bytes 368648 | tf_op jit(solution)/shard_map/ppermute | solution.py:865
  22.1 11.3 %copy-start.27 = (bf16[512,768]{1,0:T(8,128)(2,1)}, bf16[512,768]{1,0:T(8,128)(2,1)S(1)}, u32[]{:S(2)}) copy-start(bf16[512,768]{1,0:T(8,128)(2,1)S(1)} %collective-permute-done.6.x_far) | copy-start | bytes 2359300
  22.1 11.3 %copy-start.17 = (bf16[48,1280]{1,0:T(8,128)(2,1)}, bf16[48,1280]{1,0:T(8,128)(2,1)S(1)}, u32[]{:S(2)}) copy-start(bf16[48,1280]{1,0:T(8,128)(2,1)S(1)} %collective-permute-done.5.refs_5_) | copy-start | bytes 368644
  22.6 10.8 %copy-start.2 = (bf16[2,48,1280]{2,1,0:T(8,128)(2,1)}, bf16[2,48,1280]{2,1,0:T(8,128)(2,1)S(1)}, u32[]{:S(2)}) copy-start(bf16[2,48,1280]{2,1,0:T(8,128)(2,1)S(1)} %collective-permute-done.4.refs_4_) | copy-start | bytes 737284
  22.7 6.4 %collective-permute-start.8 = (bf16[3,48,1280]{2,1,0:T(8,128)(2,1)S(1)}, bf16[3,48,1280]{2,1,0:T(8,128)(2,1)S(1)}, u32[]{:S(2)}, u32[]{:S(2)}) collective-permute-start(bf16[3,48,1280]{2,1,0:T(8,128)(2,1)S(1)} %pad_maximum_fusion.5), channel_id=1, source_target_pairs={{0,2},{2,0},{4,6},{6,4},{8,10},{10,8},{12,14},{14,12},{16,18},{18,... | collective-permute-start | bytes 1105928 | tf_op jit(solution)/shard_map/ppermute | solution.py:865
  22.8 6.3 %collective-permute-start.7 = (bf16[48,1280]{1,0:T(8,128)(2,1)S(1)}, bf16[48,1280]{1,0:T(8,128)(2,1)S(1)}, u32[]{:S(2)}, u32[]{:S(2)}) collective-permute-start(bf16[48,1280]{1,0:T(8,128)(2,1)S(1)} %slice_bitcast_fusion.6), channel_id=1, source_target_pairs={{0,4},{2,6},{4,0},{6,2},{8,12},{10,14},{12,8},{14,10},{16,20},{18,... | collective-permute-start | bytes 368648 | tf_op jit(solution)/shard_map/ppermute | solution.py:865
  24.3 24.9 %collective-permute-start.11 = (bf16[7,48,768]{2,1,0:T(8,128)(2,1)}, bf16[7,48,768]{2,1,0:T(8,128)(2,1)S(1)}, u32[]{:S(2)}, u32[]{:S(2)}) collective-permute-start(bf16[7,48,768]{2,1,0:T(8,128)(2,1)} %get-tuple-element.182), channel_id=1, source_target_pairs={{0,8},{2,10},{4,12},{6,14},{8,0},{10,2},{12,4},{14,6},{16,24},{18,... | collective-permute-start | bytes 1548296 | tf_op jit(solution)/shard_map/ppermute | solution.py:865
  26.0 26.2 %collective-permute-start.12 = (bf16[7,48,768]{2,1,0:T(8,128)(2,1)}, bf16[7,48,768]{2,1,0:T(8,128)(2,1)S(1)}, u32[]{:S(2)}, u32[]{:S(2)}) collective-permute-start(bf16[7,48,768]{2,1,0:T(8,128)(2,1)} %get-tuple-element.182), channel_id=1, source_target_pairs={{0,16},{2,18},{4,20},{6,22},{8,24},{10,26},{12,28},{14,30},{16,0},... | collective-permute-start | bytes 1548296 | tf_op jit(solution)/shard_map/ppermute | solution.py:865
  29.1 23.2 %collective-permute-start.13 = (bf16[7,48,768]{2,1,0:T(8,128)(2,1)}, bf16[7,48,768]{2,1,0:T(8,128)(2,1)S(1)}, u32[]{:S(2)}, u32[]{:S(2)}) collective-permute-start(bf16[7,48,768]{2,1,0:T(8,128)(2,1)} %get-tuple-element.182), channel_id=1, source_target_pairs={{0,4},{2,6},{4,0},{6,2},{8,12},{10,14},{12,8},{14,10},{16,20},{18,... | collective-permute-start | bytes 1548296 | tf_op jit(solution)/shard_map/ppermute | solution.py:865
  30.2 3.1 %collective-permute-start.9 = (bf16[4,48,1280]{2,1,0:T(8,128)(2,1)S(1)}, bf16[4,48,1280]{2,1,0:T(8,128)(2,1)S(1)}, u32[]{:S(2)}, u32[]{:S(2)}) collective-permute-start(bf16[4,48,1280]{2,1,0:T(8,128)(2,1)S(1)} %pad_maximum_fusion.3), channel_id=1, source_target_pairs={{0,2},{2,0},{4,6},{6,4},{8,10},{10,8},{12,14},{14,12},{16,18},{18,... | collective-permute-start | bytes 1474568 | tf_op jit(solution)/shard_map/ppermute | solution.py:865
  30.3 3.1 %collective-permute-start.10 = (bf16[48,1280]{1,0:T(8,128)(2,1)S(1)}, bf16[48,1280]{1,0:T(8,128)(2,1)S(1)}, u32[]{:S(2)}, u32[]{:S(2)}) collective-permute-start(bf16[48,1280]{1,0:T(8,128)(2,1)S(1)} %collective-permute-done.7.refs_6_), channel_id=1, source_target_pairs={{0,2},{2,0},{4,6},{6,4},{8,10},{10,8},{12,14},{14,12},{16,18},{18,... | collective-permute-start | bytes 368648 | tf_op jit(solution)/shard_map/ppermute | solution.py:865
  52.3 16.1 %copy-start = (bf16[7,48,768]{2,1,0:T(8,128)(2,1)}, bf16[7,48,768]{2,1,0:T(8,128)(2,1)S(1)}, u32[]{:S(2)}) copy-start(bf16[7,48,768]{2,1,0:T(8,128)(2,1)S(1)} %collective-permute-done.13.refs_1_) | copy-start | bytes 1548292
  52.4 15.7 %collective-permute-start.18 = (bf16[3,7,48,768]{3,2,1,0:T(8,128)(2,1)S(1)}, bf16[3,7,48,768]{3,2,1,0:T(8,128)(2,1)S(1)}, u32[]{:S(2)}, u32[]{:S(2)}) collective-permute-start(bf16[3,7,48,768]{3,2,1,0:T(8,128)(2,1)S(1)} %pad_maximum_fusion), channel_id=1, source_target_pairs={{0,2},{2,0},{4,6},{6,4},{8,10},{10,8},{12,14},{14,12},{16,18},{18,... | collective-permute-start | bytes 4644872 | tf_op jit(solution)/shard_map/ppermute | solution.py:865
  53.7 12.5 %collective-permute-start.17 = (bf16[9,48,768]{2,1,0:T(8,128)(2,1)S(1)}, bf16[9,48,768]{2,1,0:T(8,128)(2,1)S(1)}, u32[]{:S(2)}, u32[]{:S(2)}) collective-permute-start(bf16[9,48,768]{2,1,0:T(8,128)(2,1)S(1)} %copy-done.28), channel_id=1, source_target_pairs={{0,2},{2,0},{4,6},{6,4},{8,10},{10,8},{12,14},{14,12},{16,18},{18,... | collective-permute-start | bytes 1990664 | tf_op jit(solution)/shard_map/ppermute | solution.py:865
  53.8 14.2 %collective-permute-start.14 = (bf16[7,48,768]{2,1,0:T(8,128)(2,1)S(1)}, bf16[7,48,768]{2,1,0:T(8,128)(2,1)S(1)}, u32[]{:S(2)}, u32[]{:S(2)}) collective-permute-start(bf16[7,48,768]{2,1,0:T(8,128)(2,1)S(1)} %collective-permute-done.12.refs_3_), channel_id=1, source_target_pairs={{0,8},{2,10},{4,12},{6,14},{8,0},{10,2},{12,4},{14,6},{16,24},{18,... | collective-permute-start | bytes 1548296 | tf_op jit(solution)/shard_map/ppermute | solution.py:865
  54.2 13.9 %collective-permute-start.15 = (bf16[7,48,768]{2,1,0:T(8,128)(2,1)S(1)}, bf16[7,48,768]{2,1,0:T(8,128)(2,1)S(1)}, u32[]{:S(2)}, u32[]{:S(2)}) collective-permute-start(bf16[7,48,768]{2,1,0:T(8,128)(2,1)S(1)} %collective-permute-done.12.refs_3_), channel_id=1, source_target_pairs={{0,4},{2,6},{4,0},{6,2},{8,12},{10,14},{12,8},{14,10},{16,20},{18,... | collective-permute-start | bytes 1548296 | tf_op jit(solution)/shard_map/ppermute | solution.py:865
  54.7 12.1 %collective-permute-start.16 = (bf16[3,2,48,768]{3,2,1,0:T(8,128)(2,1)S(1)}, bf16[3,2,48,768]{3,2,1,0:T(8,128)(2,1)S(1)}, u32[]{:S(2)}, u32[]{:S(2)}) collective-permute-start(bf16[3,2,48,768]{3,2,1,0:T(8,128)(2,1)S(1)} %pad_maximum_fusion.4), channel_id=1, source_target_pairs={{0,1},{1,0},{2,3},{3,2},{4,5},{5,4},{6,7},{7,6},{8,9},{9,8},{10,11... | collective-permute-start | bytes 1327112 | tf_op jit(solution)/shard_map/ppermute | solution.py:865
  66.9 21.9 %copy-start.26 = (bf16[3,2,48,768]{3,2,1,0:T(8,128)(2,1)}, bf16[3,2,48,768]{3,2,1,0:T(8,128)(2,1)S(1)}, u32[]{:S(2)}) copy-start(bf16[3,2,48,768]{3,2,1,0:T(8,128)(2,1)S(1)} %collective-permute-done.16.refs_8_) | copy-start | bytes 1327108
  68.2 19.9 %collective-permute-start.22 = (bf16[2,7,48,768]{3,2,1,0:T(8,128)(2,1)S(1)}, bf16[2,7,48,768]{3,2,1,0:T(8,128)(2,1)S(1)}, u32[]{:S(2)}, u32[]{:S(2)}) collective-permute-start(bf16[2,7,48,768]{3,2,1,0:T(8,128)(2,1)S(1)} %pad_maximum_fusion.1), channel_id=1, source_target_pairs={{0,2},{2,0},{4,6},{6,4},{8,10},{10,8},{12,14},{14,12},{16,18},{18,... | collective-permute-start | bytes 3096584 | tf_op jit(solution)/shard_map/ppermute | solution.py:865
  69.6 18.5 %collective-permute-start.23 = (bf16[9,48,768]{2,1,0:T(8,128)(2,1)S(1)}, bf16[9,48,768]{2,1,0:T(8,128)(2,1)S(1)}, u32[]{:S(2)}, u32[]{:S(2)}) collective-permute-start(bf16[9,48,768]{2,1,0:T(8,128)(2,1)S(1)} %pad_maximum_fusion.2), channel_id=1, source_target_pairs={{0,8},{2,10},{4,12},{6,14},{8,0},{10,2},{12,4},{14,6},{16,24},{18,... | collective-permute-start | bytes 1990664 | tf_op jit(solution)/shard_map/ppermute | solution.py:865
  71.1 17.0 %collective-permute-start.20 = (bf16[7,48,768]{2,1,0:T(8,128)(2,1)S(1)}, bf16[7,48,768]{2,1,0:T(8,128)(2,1)S(1)}, u32[]{:S(2)}, u32[]{:S(2)}) collective-permute-start(bf16[7,48,768]{2,1,0:T(8,128)(2,1)S(1)} %collective-permute-done.14.refs_4_), channel_id=1, source_target_pairs={{0,4},{2,6},{4,0},{6,2},{8,12},{10,14},{12,8},{14,10},{16,20},{18,... | collective-permute-start | bytes 1548296 | tf_op jit(solution)/shard_map/ppermute | solution.py:865
  71.9 16.2 %collective-permute-start.19 = (bf16[384,512]{1,0:T(8,128)(2,1)S(1)}, bf16[384,512]{1,0:T(8,128)(2,1)S(1)}, u32[]{:S(2)}, u32[]{:S(2)}) collective-permute-start(bf16[384,512]{1,0:T(8,128)(2,1)S(1)} %copy-done.41), channel_id=1, source_target_pairs={{0,1},{1,0},{2,3},{3,2},{4,5},{5,4},{6,7},{7,6},{8,9},{9,8},{10,11... | collective-permute-start | bytes 1179656 | tf_op jit(solution)/shard_map/ppermute | solution.py:865
  72.8 15.3 %collective-permute-start.21 = (bf16[2,2,48,768]{3,2,1,0:T(8,128)(2,1)S(1)}, bf16[2,2,48,768]{3,2,1,0:T(8,128)(2,1)S(1)}, u32[]{:S(2)}, u32[]{:S(2)}) collective-permute-start(bf16[2,2,48,768]{3,2,1,0:T(8,128)(2,1)S(1)} %pad_maximum_fusion.7), channel_id=1, source_target_pairs={{0,1},{1,0},{2,3},{3,2},{4,5},{5,4},{6,7},{7,6},{8,9},{9,8},{10,11... | collective-permute-start | bytes 884744 | tf_op jit(solution)/shard_map/ppermute | solution.py:865
  88.2 8.4 %collective-permute-start.25 = (bf16[9,48,768]{2,1,0:T(8,128)(2,1)S(1)}, bf16[9,48,768]{2,1,0:T(8,128)(2,1)S(1)}, u32[]{:S(2)}, u32[]{:S(2)}) collective-permute-start(bf16[9,48,768]{2,1,0:T(8,128)(2,1)S(1)} %collective-permute-done.23.refs_6_), channel_id=1, source_target_pairs={{0,2},{2,0},{4,6},{6,4},{8,10},{10,8},{12,14},{14,12},{16,18},{18,... | collective-permute-start | bytes 1990664 | tf_op jit(solution)/shard_map/ppermute | solution.py:865
  88.2 8.3 %collective-permute-start.26 = (bf16[7,48,768]{2,1,0:T(8,128)(2,1)S(1)}, bf16[7,48,768]{2,1,0:T(8,128)(2,1)S(1)}, u32[]{:S(2)}, u32[]{:S(2)}) collective-permute-start(bf16[7,48,768]{2,1,0:T(8,128)(2,1)S(1)} %collective-permute-done.20.refs_7_), channel_id=1, source_target_pairs={{0,2},{2,0},{4,6},{6,4},{8,10},{10,8},{12,14},{14,12},{16,18},{18,... | collective-permute-start | bytes 1548296 | tf_op jit(solution)/shard_map/ppermute | solution.py:865
  88.7 7.7 %collective-permute-start.27 = (bf16[3,2,48,768]{3,2,1,0:T(8,128)(2,1)S(1)}, bf16[3,2,48,768]{3,2,1,0:T(8,128)(2,1)S(1)}, u32[]{:S(2)}, u32[]{:S(2)}) collective-permute-start(bf16[3,2,48,768]{3,2,1,0:T(8,128)(2,1)S(1)} %collective-permute-done.16.refs_8_), channel_id=1, source_target_pairs={{0,2},{2,0},{4,6},{6,4},{8,10},{10,8},{12,14},{14,12},{16,18},{18,... | collective-permute-start | bytes 1327112 | tf_op jit(solution)/shard_map/ppermute | solution.py:865
  88.8 6.3 %collective-permute-start.24 = (bf16[2,48,768]{2,1,0:T(8,128)(2,1)S(1)}, bf16[2,48,768]{2,1,0:T(8,128)(2,1)S(1)}, u32[]{:S(2)}, u32[]{:S(2)}) collective-permute-start(bf16[2,48,768]{2,1,0:T(8,128)(2,1)S(1)} %slice.34), channel_id=1, source_target_pairs={{0,1},{1,0},{2,3},{3,2},{4,5},{5,4},{6,7},{7,6},{8,9},{9,8},{10,11... | collective-permute-start | bytes 442376 | tf_op jit(solution)/shard_map/ppermute | solution.py:865
  89.8 6.6 %collective-permute-start.28 = (bf16[2,2,48,768]{3,2,1,0:T(8,128)(2,1)S(1)}, bf16[2,2,48,768]{3,2,1,0:T(8,128)(2,1)S(1)}, u32[]{:S(2)}, u32[]{:S(2)}) collective-permute-start(bf16[2,2,48,768]{3,2,1,0:T(8,128)(2,1)S(1)} %collective-permute-done.21.refs_9_), channel_id=1, source_target_pairs={{0,2},{2,0},{4,6},{6,4},{8,10},{10,8},{12,14},{14,12},{16,18},{18,... | collective-permute-start | bytes 884744 | tf_op jit(solution)/shard_map/ppermute | solution.py:865
  95.1 1.4 collective-permute-start.29
  120.8 20.8 %collective-permute-start.33 = (bf16[5,512,768]{2,1,0:T(8,128)(2,1)}, bf16[5,512,768]{2,1,0:T(8,128)(2,1)S(1)}, u32[]{:S(2)}, u32[]{:S(2)}) collective-permute-start(bf16[5,512,768]{2,1,0:T(8,128)(2,1)} %get-tuple-element.227.pre), channel_id=1, source_target_pairs={{0,2},{2,0},{4,6},{6,4},{8,10},{10,8},{12,14},{14,12},{16,18},{18,... | collective-permute-start | bytes 11796488 | tf_op jit(solution)/shard_map/ppermute | solution.py:865
  121.1 13.0 %collective-permute-start.31 = (bf16[4,512,384]{2,1,0:T(8,128)(2,1)}, bf16[4,512,384]{2,1,0:T(8,128)(2,1)S(1)}, u32[]{:S(2)}, u32[]{:S(2)}) collective-permute-start(bf16[4,512,384]{2,1,0:T(8,128)(2,1)} %get-tuple-element.221), channel_id=1, source_target_pairs={{0,2},{2,0},{4,6},{6,4},{8,10},{10,8},{12,14},{14,12},{16,18},{18,... | collective-permute-start | bytes 4718600 | tf_op jit(solution)/shard_map/ppermute | solution.py:865
  121.4 20.2 %collective-permute-start.32 = (bf16[2,8,48,512]{3,2,1,0:T(8,128)(2,1)}, bf16[2,8,48,512]{3,2,1,0:T(8,128)(2,1)S(1)}, u32[]{:S(2)}, u32[]{:S(2)}) collective-permute-start(bf16[2,8,48,512]{3,2,1,0:T(8,128)(2,1)} %get-tuple-element.226), channel_id=1, source_target_pairs={{0,2},{2,0},{4,6},{6,4},{8,10},{10,8},{12,14},{14,12},{16,18},{18,... | collective-permute-start | bytes 2359304 | tf_op jit(solution)/shard_map/ppermute | solution.py:865
  121.6 12.4 %collective-permute-start.30 = (bf16[384,512]{1,0:T(8,128)(2,1)}, bf16[384,512]{1,0:T(8,128)(2,1)S(1)}, u32[]{:S(2)}, u32[]{:S(2)}) collective-permute-start(bf16[384,512]{1,0:T(8,128)(2,1)} %get-tuple-element.219), channel_id=1, source_target_pairs={{0,1},{1,0},{2,3},{3,2},{4,5},{5,4},{6,7},{7,6},{8,9},{9,8},{10,11... | collective-permute-start | bytes 1179656 | tf_op jit(solution)/shard_map/ppermute | solution.py:865
  134.0 18.1 %copy-start.42 = (bf16[384,512]{1,0:T(8,128)(2,1)}, bf16[384,512]{1,0:T(8,128)(2,1)S(1)}, u32[]{:S(2)}) copy-start(bf16[384,512]{1,0:T(8,128)(2,1)S(1)} %collective-permute-done.30.grad) | copy-start | bytes 1179652
  152.1 16.2 %collective-permute-start.34 = (bf16[2,2,2,48,768]{4,3,2,1,0:T(8,128)(2,1)}, bf16[2,2,2,48,768]{4,3,2,1,0:T(8,128)(2,1)S(1)}, u32[]{:S(2)}, u32[]{:S(2)}) collective-permute-start(bf16[2,2,2,48,768]{4,3,2,1,0:T(8,128)(2,1)} %get-tuple-element.237), channel_id=1, source_target_pairs={{0,8},{2,10},{4,12},{6,14},{8,0},{10,2},{12,4},{14,6},{16,24},{18,... | collective-permute-start | bytes 1769480 | tf_op jit(solution)/shard_map/ppermute | solution.py:865
  152.6 33.6 %collective-permute-start.36 = (bf16[8,2,48,768]{3,2,1,0:T(8,128)(2,1)}, bf16[8,2,48,768]{3,2,1,0:T(8,128)(2,1)S(1)}, u32[]{:S(2)}, u32[]{:S(2)}) collective-permute-start(bf16[8,2,48,768]{3,2,1,0:T(8,128)(2,1)} %get-tuple-element.223), channel_id=1, source_target_pairs={{0,1},{1,0},{2,3},{3,2},{4,5},{5,4},{6,7},{7,6},{8,9},{9,8},{10,11... | collective-permute-start | bytes 3538952 | tf_op jit(solution)/shard_map/ppermute | solution.py:865
  153.8 21.7 %collective-permute-start.35 = (bf16[4,3,48,768]{3,2,1,0:T(8,128)(2,1)}, bf16[4,3,48,768]{3,2,1,0:T(8,128)(2,1)S(1)}, u32[]{:S(2)}, u32[]{:S(2)}) collective-permute-start(bf16[4,3,48,768]{3,2,1,0:T(8,128)(2,1)} %get-tuple-element.228), channel_id=1, source_target_pairs={{0,4},{2,6},{4,0},{6,2},{8,12},{10,14},{12,8},{14,10},{16,20},{18,... | collective-permute-start | bytes 2654216 | tf_op jit(solution)/shard_map/ppermute | solution.py:865
  175.4 11.7 %collective-permute-start.37 = (bf16[8,48,1280]{2,1,0:T(8,128)(2,1)}, bf16[8,48,1280]{2,1,0:T(8,128)(2,1)}, u32[]{:S(2)}, u32[]{:S(2)}) collective-permute-start(bf16[8,48,1280]{2,1,0:T(8,128)(2,1)} %get-tuple-element.257), channel_id=1, source_target_pairs={{0,2},{2,0},{4,6},{6,4},{8,10},{10,8},{12,14},{14,12},{16,18},{18,... | collective-permute-start | bytes 2949128 | tf_op jit(solution)/shard_map/ppermute | solution.py:865
  176.5 16.3 %collective-permute-start.38 = (bf16[2,3,48,768]{3,2,1,0:T(8,128)(2,1)}, bf16[2,3,48,768]{3,2,1,0:T(8,128)(2,1)}, u32[]{:S(2)}, u32[]{:S(2)}) collective-permute-start(bf16[2,3,48,768]{3,2,1,0:T(8,128)(2,1)} %fusion.4), channel_id=1, source_target_pairs={{0,8},{2,10},{4,12},{6,14},{8,0},{10,2},{12,4},{14,6},{16,24},{18,... | collective-permute-start | bytes 1327112 | tf_op jit(solution)/shard_map/ppermute | solution.py:865
  189.5 19.7 %collective-permute-start.40 = (bf16[2,2,48,1280]{3,2,1,0:T(8,128)(2,1)}, bf16[2,2,48,1280]{3,2,1,0:T(8,128)(2,1)}, u32[]{:S(2)}, u32[]{:S(2)}) collective-permute-start(bf16[2,2,48,1280]{3,2,1,0:T(8,128)(2,1)} %fusion.2), channel_id=1, source_target_pairs={{0,8},{2,10},{4,12},{6,14},{8,0},{10,2},{12,4},{14,6},{16,24},{18,... | collective-permute-start | bytes 1474568 | tf_op jit(solution)/shard_map/ppermute | solution.py:865
  190.0 10.2 %collective-permute-start.39 = (bf16[2,2,48,768]{3,2,1,0:T(8,128)(2,1)}, bf16[2,2,48,768]{3,2,1,0:T(8,128)(2,1)}, u32[]{:S(2)}, u32[]{:S(2)}) collective-permute-start(bf16[2,2,48,768]{3,2,1,0:T(8,128)(2,1)} %fusion.8), channel_id=1, source_target_pairs={{0,4},{2,6},{4,0},{6,2},{8,12},{10,14},{12,8},{14,10},{16,20},{18,... | collective-permute-start | bytes 884744 | tf_op jit(solution)/shard_map/ppermute | solution.py:865
  191.1 20.6 %collective-permute-start.41 = (bf16[2,2,2,48,768]{4,3,2,1,0:T(8,128)(2,1)}, bf16[2,2,2,48,768]{4,3,2,1,0:T(8,128)(2,1)S(1)}, u32[]{:S(2)}, u32[]{:S(2)}) collective-permute-start(bf16[2,2,2,48,768]{4,3,2,1,0:T(8,128)(2,1)} %fusion), channel_id=1, source_target_pairs={{0,4},{2,6},{4,0},{6,2},{8,12},{10,14},{12,8},{14,10},{16,20},{18,... | collective-permute-start | bytes 1769480 | tf_op jit(solution)/shard_map/ppermute | solution.py:865
  192.1 25.6 %collective-permute-start.44 = (bf16[512,768]{1,0:T(8,128)(2,1)}, bf16[512,768]{1,0:T(8,128)(2,1)S(1)}, u32[]{:S(2)}, u32[]{:S(2)}) collective-permute-start(bf16[512,768]{1,0:T(8,128)(2,1)} %get-tuple-element.288), channel_id=1, source_target_pairs={{0,1},{1,0},{2,3},{3,2},{4,5},{5,4},{6,7},{7,6},{8,9},{9,8},{10,11... | collective-permute-start | bytes 2359304 | tf_op jit(solution)/shard_map/ppermute | solution.py:865
  194.0 20.4 %collective-permute-start.42 = (bf16[3,48,768]{2,1,0:T(8,128)(2,1)S(1)}, bf16[3,48,768]{2,1,0:T(8,128)(2,1)S(1)}, u32[]{:S(2)}, u32[]{:S(2)}) collective-permute-start(bf16[3,48,768]{2,1,0:T(8,128)(2,1)S(1)} %fusion.7), channel_id=1, source_target_pairs={{0,16},{2,18},{4,20},{6,22},{8,24},{10,26},{12,28},{14,30},{16,0},... | collective-permute-start | bytes 663560 | tf_op jit(solution)/shard_map/ppermute | solution.py:865
  201.3 14.4 %collective-permute-start.43 = (bf16[2,48,768]{2,1,0:T(8,128)(2,1)S(1)}, bf16[2,48,768]{2,1,0:T(8,128)(2,1)S(1)}, u32[]{:S(2)}, u32[]{:S(2)}) collective-permute-start(bf16[2,48,768]{2,1,0:T(8,128)(2,1)S(1)} %fusion.14), channel_id=1, source_target_pairs={{0,16},{2,18},{4,20},{6,22},{8,24},{10,26},{12,28},{14,30},{16,0},... | collective-permute-start | bytes 442376 | tf_op jit(solution)/shard_map/ppermute | solution.py:865
  210.3 12.0 %collective-permute-start.45 = (bf16[2,48,1280]{2,1,0:T(8,128)(2,1)S(1)}, bf16[2,48,1280]{2,1,0:T(8,128)(2,1)S(1)}, u32[]{:S(2)}, u32[]{:S(2)}) collective-permute-start(bf16[2,48,1280]{2,1,0:T(8,128)(2,1)S(1)} %fusion.3), channel_id=1, source_target_pairs={{0,4},{2,6},{4,0},{6,2},{8,12},{10,14},{12,8},{14,10},{16,20},{18,... | collective-permute-start | bytes 737288 | tf_op jit(solution)/shard_map/ppermute | solution.py:865
  211.8 12.7 %collective-permute-start.46 = (bf16[2,2,48,768]{3,2,1,0:T(8,128)(2,1)S(1)}, bf16[2,2,48,768]{3,2,1,0:T(8,128)(2,1)S(1)}, u32[]{:S(2)}, u32[]{:S(2)}) collective-permute-start(bf16[2,2,48,768]{3,2,1,0:T(8,128)(2,1)S(1)} %fusion.1), channel_id=1, source_target_pairs={{0,8},{2,10},{4,12},{6,14},{8,0},{10,2},{12,4},{14,6},{16,24},{18,... | collective-permute-start | bytes 884744 | tf_op jit(solution)/shard_map/ppermute | solution.py:865
  216.9 9.6 %collective-permute-start.47 = (bf16[5,48,768]{2,1,0:T(8,128)(2,1)S(1)}, bf16[5,48,768]{2,1,0:T(8,128)(2,1)S(1)}, u32[]{:S(2)}, u32[]{:S(2)}) collective-permute-start(bf16[5,48,768]{2,1,0:T(8,128)(2,1)S(1)} %pad_maximum_fusion.6.near), channel_id=1, source_target_pairs={{0,1},{1,0},{2,3},{3,2},{4,5},{5,4},{6,7},{7,6},{8,9},{9,8},{10,11... | collective-permute-start | bytes 1105928 | tf_op jit(solution)/shard_map/ppermute | solution.py:865
  223.4 10.7 %collective-permute-start.48 = (bf16[48,1280]{1,0:T(8,128)(2,1)S(1)}, bf16[48,1280]{1,0:T(8,128)(2,1)S(1)}, u32[]{:S(2)}, u32[]{:S(2)}) collective-permute-start(bf16[48,1280]{1,0:T(8,128)(2,1)S(1)} %fusion.17), channel_id=1, source_target_pairs={{0,16},{2,18},{4,20},{6,22},{8,24},{10,26},{12,28},{14,30},{16,0},... | collective-permute-start | bytes 368648 | tf_op jit(solution)/shard_map/ppermute | solution.py:865
  224.6 11.4 %collective-permute-start.49 = (bf16[2,48,768]{2,1,0:T(8,128)(2,1)S(1)}, bf16[2,48,768]{2,1,0:T(8,128)(2,1)S(1)}, u32[]{:S(2)}, u32[]{:S(2)}) collective-permute-start(bf16[2,48,768]{2,1,0:T(8,128)(2,1)S(1)} %fusion.11), channel_id=1, source_target_pairs={{0,16},{2,18},{4,20},{6,22},{8,24},{10,26},{12,28},{14,30},{16,0},... | collective-permute-start | bytes 442376 | tf_op jit(solution)/shard_map/ppermute | solution.py:865
  236.2 7.3 %collective-permute-start.50 = (bf16[2,48,768]{2,1,0:T(8,128)(2,1)S(1)}, bf16[2,48,768]{2,1,0:T(8,128)(2,1)S(1)}, u32[]{:S(2)}, u32[]{:S(2)}) collective-permute-start(bf16[2,48,768]{2,1,0:T(8,128)(2,1)S(1)} %fusion.10.a_near), channel_id=1, source_target_pairs={{0,1},{1,0},{2,3},{3,2},{4,5},{5,4},{6,7},{7,6},{8,9},{9,8},{10,11... | collective-permute-start | bytes 442376 | tf_op jit(solution)/shard_map/ppermute | solution.py:865
  237.5 6.0 %collective-permute-start.51 = (bf16[48,1280]{1,0:T(8,128)(2,1)S(1)}, bf16[48,1280]{1,0:T(8,128)(2,1)S(1)}, u32[]{:S(2)}, u32[]{:S(2)}) collective-permute-start(bf16[48,1280]{1,0:T(8,128)(2,1)S(1)} %fusion.16.g_near), channel_id=1, source_target_pairs={{0,1},{1,0},{2,3},{3,2},{4,5},{5,4},{6,7},{7,6},{8,9},{9,8},{10,11... | collective-permute-start | bytes 368648 | tf_op jit(solution)/shard_map/ppermute | solution.py:865
  (39 other events, 136.1 us)

commit v4 on v3

--- a/solution.py
+++ b/solution.py
@@ -758,7 +758,7 @@
             pltpu.SemaphoreType.DMA((6,)),
         ],
         compiler_params=params(),
-        cost_estimate=cost(2 * 1024 * 768 * 1152, 10_000_000),
+        cost_estimate=pl.CostEstimate(flops=20_000_000_000, bytes_accessed=10_000_000, transcendentals=0),
         name="project_back",
     )(place, *blocks, whole)
 
@@ -810,8 +810,11 @@
     )(place, a_near, a_far, g_near, g_far, qw, kw, vw, gain.reshape(1, 48))
 
 
-def finish_wide_kernel(place, near, far, up, gain, expand, output, gain_grad):
-    summed = near[...].astype(f32) + far[...].astype(f32)
+def finish_wide_kernel(
+    place, x, small, near, far, middle_grad, b_near, b_far, up, gain, result, expand, output, gain_grad
+):
+    input_grad_kernel(place, x, small, near, far, middle_grad, result)
+    summed = b_near[...].astype(f32) + b_far[...].astype(f32)
     joint = jnp.zeros((48, 768), f32)
     for at in range(4):
         cols = slice(at * 768, at * 768 + 768)
@@ -823,18 +826,19 @@
     gain_grad[...] = turned[0:1, 0:48] / gain[...].astype(f32)
 
 
-def finish_wide(place, near, far, up, gain):
+def finish_wide(place, x, small, near, far, middle_grad, b_near, b_far, up, gain):
     return pl.pallas_call(
         finish_wide_kernel,
         out_shape=(
-            jax.ShapeDtypeStruct((48, 3072), f32), jax.ShapeDtypeStruct((48, 768), f32), jax.ShapeDtypeStruct((1, 48), f32),
+            jax.ShapeDtypeStruct((512, 768), bf16), jax.ShapeDtypeStruct((48, 3072), f32),
+            jax.ShapeDtypeStruct((48, 768), f32), jax.ShapeDtypeStruct((1, 48), f32),
         ),
-        in_specs=[SCALARS] + [FULL] * 4,
-        out_specs=(FULL,) * 3,
+        in_specs=[SCALARS] + [FULL] * 9,
+        out_specs=(FULL,) * 4,
         compiler_params=params(),
         cost_estimate=cost(1000, 2_000_000),
         name="finish_wide",
-    )(place, near, far, up, gain.reshape(1, 48))
+    )(place, x, small, near, far, middle_grad, b_near, b_far, up, gain.reshape(1, 48))
 
 
 def input_grad_kernel(place, x, small, near, far, middle_grad, result):
@@ -846,18 +850,6 @@
         direct = (near[rows].astype(f32) + far[rows].astype(f32)) * small[0:1]
         inward = scale * (direct - unit * jnp.mean(direct * unit, axis=-1, keepdims=True))
         result[rows] = (middle_grad[rows] + inward).astype(bf16)
-
-
-def input_grad(place, x, small, near, far, middle_grad):
-    return pl.pallas_call(
-        input_grad_kernel,
-        out_shape=jax.ShapeDtypeStruct((512, 768), bf16),
-        in_specs=[SCALARS] + [FULL] * 5,
-        out_specs=FULL,
-        compiler_params=params(),
-        cost_estimate=cost(512 * 768 * 20, 6_000_000),
-        name="input_grad",
-    )(place, x, small, near, far, middle_grad)
 
 
 def swap(array, axis, bit):
@@ -952,37 +944,38 @@
     a2, a1, b0, rest, cot_far = lax.optimization_barrier((a2, a1, b0, rest, cot_far))
     turned, b2 = by_z(jnp.stack([a2, b0])), by_y(a2)
     four = by_core(jnp.stack([shard, b0, a1, a2]))
-    z2, z1 = by_zz(rest), by_z(rest)
-    turned, b2, rest, x_far = lax.optimization_barrier((turned, b2, rest, x_far))
+    z2, z1, y0 = by_zz(rest), by_z(rest), by_y(rest)
+    lens = jnp.stack([valid_len[0], instr_len[0], pair_flag[0]])
+    place = jnp.concatenate([where, lens])
+    turned, b2, x_far, line.place = lax.optimization_barrier((turned, b2, x_far, place))
     b3 = by_y(turned[0])
     three = by_core(jnp.stack([turned[0], turned[1], b2]))
-    b3, rest, three = lax.optimization_barrier((b3, rest, three))
-    y0 = by_y(rest)
-    narrow = [shard, b0, a1, a2, turned, b2, b3, four, three, by_core(b3)]
-
-    lens = jnp.stack([valid_len[0], instr_len[0], pair_flag[0]])
-    line.place = jnp.concatenate([line.place, lens])
+    last = by_core(b3)
+    z1, z2, y0, last, three = lax.optimization_barrier((z1, z2, y0, last, three))
+    z3, y2 = by_z(z2), by_y(z2)
+    sides = jnp.stack([z1[5:], z2[5:], y0[5:]])
+    sides_a = by_x(sides)
+    narrow = [shard, b0, a1, a2, turned, b2, b3, four, three, last]
+
+    line.wait(sides)
     qkv, normed_kept, normed_sent, small, table, tiles = line.run(project, tokens, x_far, narrow)
-    line.place, z1, z2, y0 = lax.optimization_barrier((line.place, z1, z2, y0))
-    z3, y2 = by_z(z2), by_y(z2)
-    sides, trio = jnp.stack([z1[5:], z2[5:], y0[5:]]), jnp.stack([y0, z1, z2])
-    sides_a, far_full, far_three = by_x(sides), by_core(full), by_core(trio)
-    line.wait(sides, trio)
-    out_theirs, kept_theirs, inverse_theirs = line.run(attend, table, tiles, qkv, False)
-    line.place, z3, y2, sides_a, out_theirs, far_full, far_three = lax.optimization_barrier(
-        (line.place, z3, y2, sides_a, out_theirs, far_full, far_three)
-    )
-    out_got = by_x(out_theirs)
+    line.place, z3, y2, sides_a = lax.optimization_barrier((line.place, z3, y2, sides_a))
     y3 = by_y(z3)
     y1 = jnp.concatenate([y0, sides_a[2]], axis=0)
-    sides, two = jnp.stack([z3[5:], y2[5:]]), jnp.stack([z3, y2])
-    line.wait(y1, sides, two)
-    y1, sides_b, far_two = by_z(y1), by_x(sides), by_core(two)
+    sides, trio = jnp.stack([z3[5:], y2[5:]]), jnp.stack([y0, z1, z2])
+    line.wait(y1, sides, trio)
+    y1, sides_b, far_full, far_three = by_z(y1), by_x(sides), by_core(full), by_core(trio)
+    out_theirs, kept_theirs, inverse_theirs = line.run(attend, table, tiles, qkv, False)
+    line.place, y3, sides_b, far_full, far_three, out_theirs = lax.optimization_barrier(
+        (line.place, y3, sides_b, far_full, far_three, out_theirs)
+    )
+    two = jnp.stack([z3, y2])
+    line.wait(two)
+    out_got, sides_c, far_two = by_x(out_theirs), by_x(y3[5:]), by_core(two)
     out_mine, kept_mine, inverse_mine = line.run(attend, table, tiles, qkv, True)
-    out_mine, out_got, sides_a, y3, sides_b, far_two, y1 = lax.optimization_barrier(
-        (out_mine, out_got, sides_a, y3, sides_b, far_two, y1)
-    )
-    sides_c = by_x(y3[5:])
+    out_mine, y1, out_got, sides_c, far_two, y3, sides_a, sides_b = lax.optimization_barrier(
+        (out_mine, y1, out_got, sides_c, far_two, y3, sides_a, sides_b)
+    )
     near = [full, y0, z1, z2, z3, y2, y1, y3, sides_a, sides_b, sides_c]
     far = [far_full, far_three, far_two] + [by_core(block) for block in (y1, y3, sides_a, sides_b, sides_c)]
     hid, hid_sent, pre, turned, turned_sent, layer_output, middle_grad, grad_mine, grad_sent = line.run(
@@ -1001,42 +994,46 @@
         lambda place: attend_back(place, grad_mine, out_mine, inverse_mine, qkv, kept_mine, (), True)
     )
     line.wait(grad_theirs)
+    b_sent, b_kept, c_sent, c_kept = line.run(expand_weight_grad, turned, turned_far, pre, pre_far)
+    b_got, c_got = by_y(b_sent), by_z(c_sent)
+    b_parts = parts(b_kept, b_got, "high", "low", "n")
+    c_parts = parts(c_kept, c_got, "high", "y", "n")
     sent, kept = line.run(contract_weight_grad, hid, hid_far, cot, cot_far)
-    a_parts = parts(kept, by_x(sent), "high", "low", "y", "n")
-    b_sent, b_kept, c_sent, c_kept = line.run(expand_weight_grad, turned, turned_far, pre, pre_far)
-    b_parts = parts(b_kept, by_y(b_sent), "high", "low", "n")
-    c_got = by_z(c_sent)
-    c_parts = parts(c_kept, c_got, "high", "y", "n")
+    a_got = by_x(sent)
+    a_parts = parts(kept, a_got, "high", "low", "y", "n")
     whole = line.run(
         lambda place: attend_back(
             place, grad_theirs, out_theirs, inverse_theirs, qkv, kept_theirs, carry, False
         )
     )
-    line.wait(c_got)
+    b_got = by_z(total(line, b_parts, own, "low"))
+    b_parts = keep(b_parts, "low", b_got)
+    c_got = by_y(total(line, c_parts, own, "y"))
+    c_parts = keep(c_parts, "y", c_got)
     g_near, g_far = line.run(weight_grad, normed_kept, normed_sent, whole)
     g_parts = parts(g_near, by_core(g_far), "high", "low", "y")
-    b_parts = keep(b_parts, "low", by_z(total(line, b_parts, own, "low")))
-    c_parts = keep(c_parts, "y", by_y(total(line, c_parts, own, "y")))
+    line.wait(a_got, b_got, c_got)
     part_near, part_far = line.run(project_back, narrow, whole)
     part_got = by_x(part_far)
+    g_parts = keep(g_parts, "low", by_z(total(line, g_parts, own, "low")))
     a_parts = keep(a_parts, "y", by_y(total(line, a_parts, own, "y")))
-    g_parts = keep(g_parts, "low", by_z(total(line, g_parts, own, "low")))
     b_parts = keep(b_parts, "high", by_zz(total(line, b_parts, own, "high")))
     c_parts = keep(c_parts, "high", by_zz(total(line, c_parts, own, "high")))
+    a_parts = keep(a_parts, "low", by_z(total(line, a_parts, own, "low")))
     g_parts = keep(g_parts, "y", by_y(total(line, g_parts, own, "y")))
-    a_parts = keep(a_parts, "low", by_z(total(line, a_parts, own, "low")))
     b_low = jnp.concatenate([total(line, b_parts, own), total(line, c_parts, own)], axis=0)
     b_low = lax.optimization_barrier(b_low)
     b_other = by_x(b_low)
     line.wait(b_low)
-    result = line.run(input_grad, tokens, small, part_near, part_got, middle_grad)
+    a_parts = keep(a_parts, "high", by_zz(total(line, a_parts, own, "high")))
     g_parts = keep(g_parts, "high", by_zz(total(line, g_parts, own, "high")))
-    a_parts = keep(a_parts, "high", by_zz(total(line, a_parts, own, "high")))
-    expand_sum, output_sum, gain_two = line.run(finish_wide, b_low, b_other, expand_weight, feedforward_gain)
+    result, expand_sum, output_sum, gain_two = line.run(
+        finish_wide, tokens, small, part_near, part_got, middle_grad, b_low, b_other, expand_weight, feedforward_gain
+    )
+    a_low = total(line, a_parts, own)
+    a_other = by_x(a_low)
     g_low = total(line, g_parts, own)
     g_other = by_x(g_low)
-    a_low = total(line, a_parts, own)
-    a_other = by_x(a_low)
     contract_sum, *grads, gain_one, bias_grad = line.run(
         finish, a_low, a_other, g_low, g_other, query_weight, key_weight, value_weight, attention_gain
     )

time: 249 us -> 242 us (0.972)
  waiting for transfers between devices: 46.8 us -> 35.8 us
  starting transfers between devices: 52.1 us -> 60.4 us
  local copies, waits for them, and re-layouts: 11.9 us -> 9.14 us
    ppermute x52, waiting for transfers between devices: 46.8 us -> 35.8 us  [swap(): return lax.ppermute(array, axis, [(i, i ^ bit) for i in range(count)])]
    ppermute x52, starting transfers between devices: 52.1 us -> 60.4 us  [swap(): return lax.ppermute(array, axis, [(i, i ^ bit) for i in range(count)])]
    unnamed x102 -> x98, local copies, waits for them, and re-layouts: 11.8 us -> 8.43 us
    pallas_call x2 -> x1, Pallas kernels: 5.95 us -> 4.2 us  [finish_wide(): pl.pallas_call(finish_wide_kernel, out_shape=(jax.ShapeDtypeStruct((512,...]
  transfers between devices with their start and end apart: 52 -> 52, of which waited for: 18 -> 15; matrix products, arithmetic and copies ran while one was open for 6% -> 6% of each run, Pallas kernels for 34% -> 38%
where the time goes in v4:
time: 242 us; the launch traced here: 240 us
  Pallas kernels  116 us (48%)
  starting transfers between devices  60.4 us (25%)
  waiting for transfers between devices  35.8 us (15%)
  other arithmetic  15.7 us (6%)
  local copies, waits for them, and re-layouts  9.14 us (4%)
  between operations  3.39 us (1%)
    ppermute x52, starting transfers between devices, swap(): return lax.ppermute(array, axis, [(i, i ^ bit) for i in range(count)])  60.4 us
    ppermute x52, waiting for transfers between devices, swap(): return lax.ppermute(array, axis, [(i, i ^ bit) for i in range(count)])  35.8 us
    pallas_call x2, Pallas kernels, attend_back(): pl.pallas_call(functools.partial(attend_back_kernel, bool(carry), mine),...  24.6 us
    pallas_call x1, Pallas kernels, forward(): pl.pallas_call(forward_kernel, out_shape=(hidden, hidden, jax.ShapeDtypeS...  23.1 us
    pallas_call x2, Pallas kernels, attend(): pl.pallas_call(functools.partial(attend_kernel, mine), out_shape=(jax.Sha...  21 us
    convert_element_type x14, other arithmetic, total(): made = lax.optimization_barrier(made.astype(bf16))  13.7 us
    unnamed x98, local copies, waits for them, and re-layouts  8.43 us
    pallas_call x1, Pallas kernels, expand_weight_grad(): pl.pallas_call(expand_grad_kernel, out_shape=(first, first, second, secon...  8.34 us
  transfers between devices with their start and end apart: 52, of which 15 were waited for; matrix products, arithmetic and copies ran while one was open for 6% of the time, Pallas kernels for 38%

profile of v4, /device:TPU:0, one launch (start us, length us, event | category | flops | bytes accessed | tf_op | source)
XLA Modules:
  0.0 240.1 jit_solution(13988098457584917449)
XLA Ops:
  1.2 2.6 %collective-permute-start.6 = (bf16[512,768]{1,0:T(8,128)(2,1)}, bf16[512,768]{1,0:T(8,128)(2,1)S(1)}, u32[]{:S(2)}, u32[]{:S(2)}) collective-permute-start(bf16[512,768]{1,0:T(8,128)(2,1)} %bitcast.112), channel_id=1, source_target_pairs={{0,1},{1,0},{2,3},{3,2},{4,5},{5,4},{6,7},{7,6},{8,9},{9,8},{10,11... | collective-permute-start | bytes 2359304 | tf_op jit(solution)/shard_map/ppermute | solution.py:857
  4.3 1.8 narrow_shard.1.refs_0_
  6.1 2.6 %collective-permute-start = (bf16[48,1280]{1,0:T(8,128)(2,1)}, bf16[48,1280]{1,0:T(8,128)(2,1)S(1)}, u32[]{:S(2)}, u32[]{:S(2)}) collective-permute-start(bf16[48,1280]{1,0:T(8,128)(2,1)} %narrow_shard.1.refs_0_), channel_id=1, source_target_pairs={{0,16},{2,18},{4,20},{6,22},{8,24},{10,26},{12,28},{14,30},{16,0},... | collective-permute-start | bytes 368648 | tf_op jit(solution)/shard_map/ppermute | solution.py:857
  8.7 1.6 collective-permute-start.1
  10.3 1.5 collective-permute-start.2
  11.8 2.9 %wide_shard.1 = (bf16[7,48,768]{2,1,0:T(8,128)(2,1)}, bf16[9,48,768]{2,1,0:T(8,128)(2,1)}) custom-call(s32[4]{0:T(128)} %pad_add_fusion.place, bf16[48,3072]{1,0:T(8,128)(2,1)} %up.1, bf16[48,768]{1,0:T(8,128)(2,1)} %output.1, bf16[192,768]{1,0:T(8,128)(2,1)} %contract.1), custom_call_target="tpu_custom_call" | custom-call | flops 1000 | bytes 1000 | tf_op jit(solution)/shard_map/wide_shard/pallas_call | solution.py:101
  15.6 1.5 collective-permute-start.4
  17.1 1.5 collective-permute-start.5
  21.8 1.8 collective-permute-start.8
  24.3 12.0 %collective-permute-start.10 = (bf16[48,1280]{1,0:T(8,128)(2,1)S(1)}, bf16[48,1280]{1,0:T(8,128)(2,1)S(1)}, u32[]{:S(2)}, u32[]{:S(2)}) collective-permute-start(bf16[48,1280]{1,0:T(8,128)(2,1)S(1)} %slice_bitcast_fusion.6), channel_id=1, source_target_pairs={{0,4},{2,6},{4,0},{6,2},{8,12},{10,14},{12,8},{14,10},{16,20},{18,... | collective-permute-start | bytes 368648 | tf_op jit(solution)/shard_map/ppermute | solution.py:857
  36.2 4.0 %collective-permute-done.10.refs_6_ = bf16[48,1280]{1,0:T(8,128)(2,1)S(1)} collective-permute-done((bf16[48,1280]{1,0:T(8,128)(2,1)S(1)}, bf16[48,1280]{1,0:T(8,128)(2,1)S(1)}, u32[]{:S(2)}, u32[]{:S(2)}) %collective-permute-start.10) | collective-permute-done | bytes 122912 | tf_op jit(solution)/shard_map/ppermute | solution.py:857
  40.3 1.3 collective-permute-done.11.refs_9_
  41.7 3.2 %collective-permute-done.7.refs_2_ = bf16[7,48,768]{2,1,0:T(8,128)(2,1)S(1)} collective-permute-done((bf16[7,48,768]{2,1,0:T(8,128)(2,1)}, bf16[7,48,768]{2,1,0:T(8,128)(2,1)S(1)}, u32[]{:S(2)}, u32[]{:S(2)}) %collective-permute-start.7) | collective-permute-done | bytes 516128 | tf_op jit(solution)/shard_map/ppermute | solution.py:857
  44.9 3.1 %collective-permute-start.14 = (bf16[7,48,768]{2,1,0:T(8,128)(2,1)S(1)}, bf16[7,48,768]{2,1,0:T(8,128)(2,1)S(1)}, u32[]{:S(2)}, u32[]{:S(2)}) collective-permute-start(bf16[7,48,768]{2,1,0:T(8,128)(2,1)S(1)} %collective-permute-done.8.refs_3_), channel_id=1, source_target_pairs={{0,8},{2,10},{4,12},{6,14},{8,0},{10,2},{12,4},{14,6},{16,24},{18,... | collective-permute-start | bytes 1548296 | tf_op jit(solution)/shard_map/ppermute | solution.py:857
  48.0 1.3 collective-permute-start.15
  51.7 7.7 %project.1 = (bf16[1152,1024]{1,0:T(8,128)(2,1)}, bf16[8,48,1024]{2,1,0:T(8,128)(2,1)}, bf16[8,48,1024]{2,1,0:T(8,128)(2,1)}, f32[8,768]{1,0:T(8,128)}, f32[8,128]{1,0:T(8,128)}, /*index=5*/f32[6,384,128]{2,1,0:T(8,128)}) custom-call(s32[7]{0:T(128)} %concatenate.10.place, bf16[512,768]{1,0:T(8,128)(2,1)} %bitcast.113, bf16[512,768]{1,0:T(8,128)(2,1)} %copy-done.24, ...), custom_call_target="tpu_custom_call" | custom-call | flops 1000 | bytes 1000 | tf_op jit(solution)/shard_map/project/pallas_call | solution.py:193
  59.4 1.1 collective-permute-done.16.refs_8_
  60.5 1.6 collective-permute-start.17
  63.0 0.9 pad_maximum_fusion.2
  64.2 10.6 %attend_theirs.1 = (bf16[384,512]{1,0:T(8,128)(2,1)}, bf16[6,1024,512]{2,1,0:T(8,128)(2,1)}, f32[6,1,512]{2,1,0:T(1,128)}) custom-call(s32[7]{0:T(128)} %concatenate.10.place, f32[8,128]{1,0:T(8,128)} %get-tuple-element.192.table, f32[6,384,128]{2,1,0:T(8,128)} %get-tuple-element.193.tile, bf16[1152,1024]{1,0:T(8,128)(2,1)} %get-tuple-element.185.q.k.v, ...), custom_call_target="tpu_custom_call" | custom-call | flops 1000 | bytes 1000 | tf_op jit(solution)/shard_map/attend_theirs/pallas_call | solution.py:288
  74.9 1.6 collective-permute-start.22
  77.0 10.4 %attend_mine.1 = (bf16[384,512]{1,0:T(8,128)(2,1)}, bf16[6,1024,512]{2,1,0:T(8,128)(2,1)}, f32[6,1,512]{2,1,0:T(1,128)}) custom-call(s32[7]{0:T(128)} %concatenate.10.place, f32[8,128]{1,0:T(8,128)} %get-tuple-element.192.table, f32[6,384,128]{2,1,0:T(8,128)} %get-tuple-element.193.tile, bf16[1152,1024]{1,0:T(8,128)(2,1)} %get-tuple-element.185.q.k.v, ...), custom_call_target="tpu_custom_call" | custom-call | flops 1000 | bytes 1000 | tf_op jit(solution)/shard_map/attend_mine/pallas_call | solution.py:288
  87.5 1.8 collective-permute-done.23.refs_10_
  90.4 3.0 %collective-permute-done.29.refs_18_ = bf16[2,48,768]{2,1,0:T(8,128)(2,1)S(1)} collective-permute-done((bf16[2,48,768]{2,1,0:T(8,128)(2,1)S(1)}, bf16[2,48,768]{2,1,0:T(8,128)(2,1)S(1)}, u32[]{:S(2)}, u32[]{:S(2)}) %collective-permute-start.29) | collective-permute-done | bytes 147488 | tf_op jit(solution)/shard_map/ppermute | solution.py:857
  94.7 23.1 %forward.1 = (bf16[4,512,384]{2,1,0:T(8,128)(2,1)}, bf16[4,512,384]{2,1,0:T(8,128)(2,1)}, bf16[5,512,768]{2,1,0:T(8,128)(2,1)}, bf16[2,8,48,512]{3,2,1,0:T(8,128...) custom-call(s32[7]{0:T(128)} %concatenate.10.place, ...), custom_call_target="tpu_custom_call" | custom-call | flops 8500000 | bytes 20000 | tf_op jit(solution)/shard_map/forward/pallas_call | solution.py:584
  118.6 1.5 collective-permute-start.30
  120.1 11.5 %attend_back_mine.1 = (bf16[384,512]{1,0:T(8,128)(2,1)}, f32[384,1024]{1,0:T(8,128)}, f32[384,1024]{1,0:T(8,128)}, f32[6,384,128]{2,1,0:T(8,128)}, f32[6,8,512]{2,1,0:T(8,128)}) custom-call(s32[7]{0:T(128)} %concatenate.10.place, bf16[384,512]{1,0:T(8,128)(2,1)} %get-tuple-element.218.grad, bf16[384,512]{1,0:T(8,128)(2,1)} %get-tuple-element.204.att_near.out, ...), custom_call_target="tpu_custom_call" | custom-call | flops 3221225 | bytes 6000 | tf_op jit(solution)/shard_map/attend_back_mine/pallas_call | solution.py:450
  132.5 1.3 copy-done.1
  133.8 8.3 %expand_weight_grad.1 = (bf16[4,3,48,768]{3,2,1,0:T(8,128)(2,1)}, bf16[4,3,48,768]{3,2,1,0:T(8,128)(2,1)}, bf16[2,2,2,48,768]{4,3,2,1,0:T(8,128)(2,1)}, bf16[2,2,2,48,768]{4,3,2,1,0:T(8,128)(2,1)}) custom-call(s32[7]{0:T(128)} %concatenate.10.place, bf16[2,8,48,512]{3,2,1,0:T(8,128)(2,1)} %get-tuple-element.225.turned, bf16[2,8,48,512]{3,2,1,0:T(8,128)(2,1)} %copy-done.22, ...), custom_call_target="tpu_custom_call" | custom-call | flops 3019898 | bytes 12000 | tf_op jit(solution)/shard_map/expand_weight_grad/pallas_call | solution.py:674
  142.7 1.2 copy-done.6
  143.9 6.3 %contract_weight_grad.1 = (bf16[8,2,48,768]{3,2,1,0:T(8,128)(2,1)}, bf16[8,2,48,768]{3,2,1,0:T(8,128)(2,1)}) custom-call(s32[7]{0:T(128)} %concatenate.10.place, bf16[4,512,384]{2,1,0:T(8,128)(2,1)} %get-tuple-element.216.hid, bf16[4,512,384]{2,1,0:T(8,128)(2,1)} %copy-done.6, bf16[512,768]{1,0:T(8,128)(2,1)} %bitcast.119, bf16[512,768]{1,0:T(8,128)(2,1)} %copy-done.21), custom_call_target="tpu_custom_call" | custom-call | flops 2415919 | bytes 9000 | tf_op jit(solution)/shard_map/contract_weight_grad/pallas_call | solution.py:627
  150.8 1.6 collective-permute-start.35
  152.4 13.1 %attend_back_theirs.1.whole.refs_10_ = bf16[6,208,1024]{2,1,0:T(8,128)(2,1)} custom-call(s32[7]{0:T(128)} %concatenate.10.place, bf16[384,512]{1,0:T(8,128)(2,1)} %copy-done.37, bf16[384,512]{1,0:T(8,128)(2,1)} %get-tuple-element.201.out, f32[6,1,512]{2,1,0:T(1,128)} %get-tuple-element.234.inverse, bf16[1152,1024]{1,0:T(8,128)(2,1)} %get-tuple-element.185.q.k.v, ...), custom_call_target="tpu_custom_call" | custom-call | flops 3221225 | bytes 6000 | tf_op jit(solution)/shard_map/attend_back_theirs/pallas_call | solution.py:450
  165.6 1.0 fusion.4
  167.1 1.6 collective-permute-start.38
  168.7 6.8 %weight_grad.1 = (bf16[8,48,1280]{2,1,0:T(8,128)(2,1)}, bf16[8,48,1280]{2,1,0:T(8,128)(2,1)}) custom-call(s32[7]{0:T(128)} %concatenate.10.place, bf16[8,48,1024]{2,1,0:T(8,128)(2,1)} %get-tuple-element.250.mine, bf16[8,48,1024]{2,1,0:T(8,128)(2,1)} %get-tuple-element.251.other, bf16[6,208,1024]{2,1,0:T(8,128)(2,1)} %attend_back_theirs.1.whole.refs_10_), custom_call_target="tpu_custom_call" | custom-call | flops 1811939 | bytes 6000 | tf_op jit(solution)/shard_map/weight_grad/pallas_call | solution.py:718
  175.7 2.5 %collective-permute-done.36 = bf16[8,2,48,768]{3,2,1,0:T(8,128)(2,1)S(1)} collective-permute-done((bf16[8,2,48,768]{3,2,1,0:T(8,128)(2,1)}, bf16[8,2,48,768]{3,2,1,0:T(8,128)(2,1)S(1)}, u32[]{:S(2)}, u32[]{:S(2)}) %collective-permute-start.36) | collective-permute-done | bytes 1179680 | tf_op jit(solution)/shard_map/ppermute | solution.py:857
  178.2 6.3 %project_back.1 = (bf16[512,768]{1,0:T(8,128)(2,1)}, bf16[512,768]{1,0:T(8,128)(2,1)}) custom-call(s32[7]{0:T(128)} %concatenate.10.place, bf16[48,1280]{1,0:T(8,128)(2,1)} %narrow_shard.1.refs_0_, bf16[48,1280]{1,0:T(8,128)(2,1)} %copy-done.13, bf16[48,1280]{1,0:T(8,128)(2,1)} %copy-done.33, bf16[48,1280]{1,0:T(8,128)(2,1)} %copy-done.12, ...), custom_call_target="tpu_custom_call" | custom-call | flops 20000000000 | bytes 10000000 | tf_op jit(solution)/shard_map/project_back/pallas_call | solution.py:749
  184.6 0.9 fusion.2
  186.4 1.0 fusion
  187.3 1.6 collective-permute-start.40
  188.9 1.5 collective-permute-start.41
  191.0 1.2 fusion.7
  192.2 1.9 collective-permute-start.42
  194.2 1.1 fusion.14
  195.3 1.1 collective-permute-start.43
  196.4 5.4 %collective-permute-done.40 = bf16[2,2,2,48,768]{4,3,2,1,0:T(8,128)(2,1)} collective-permute-done((bf16[2,2,2,48,768]{4,3,2,1,0:T(8,128)(2,1)}, bf16[2,2,2,48,768]{4,3,2,1,0:T(8,128)(2,1)}, u32[]{:S(2)}, u32[]{:S(2)}) %collective-permute-start.40) | collective-permute-done | bytes 589856 | tf_op jit(solution)/shard_map/ppermute | solution.py:857
  201.8 1.1 fusion.1
  202.9 1.6 collective-permute-start.44
  204.5 6.7 %collective-permute-done.41 = bf16[2,2,48,1280]{3,2,1,0:T(8,128)(2,1)} collective-permute-done((bf16[2,2,48,1280]{3,2,1,0:T(8,128)(2,1)}, bf16[2,2,48,1280]{3,2,1,0:T(8,128)(2,1)}, u32[]{:S(2)}, u32[]{:S(2)}) %collective-permute-start.41) | collective-permute-done | bytes 491552 | tf_op jit(solution)/shard_map/ppermute | solution.py:857
  211.3 1.0 fusion.3
  212.9 1.3 fusion.6
  214.1 1.1 fusion.13
  215.3 1.6 collective-permute-start.47
  216.9 1.0 fusion.11
  218.6 1.0 fusion.17
  219.6 2.3 collective-permute-start.49
  221.9 0.9 collective-permute-done.47.b_far
  223.6 4.2 %finish_wide.1 = (bf16[512,768]{1,0:T(8,128)(2,1)}, f32[48,3072]{1,0:T(8,128)}, f32[48,768]{1,0:T(8,128)}, f32[1,48]{1,0:T(1,128)}) custom-call(s32[7]{0:T(128)} %concatenate.10.place, bf16[512,768]{1,0:T(8,128)(2,1)} %bitcast.115, f32[8,768]{1,0:T(8,128)} %get-tuple-element.206.small, bf16[512,768]{1,0:T(8,128)(2,1)} %get-tuple-element.255.near, ...), custom_call_target="tpu_custom_call" | custom-call | flops 1 | bytes 2000 | tf_op jit(solution)/shard_map/finish_wide/pallas_call | solution.py:830
  227.8 1.0 fusion.10.a_near
  228.9 1.6 collective-permute-start.50
  230.4 1.0 fusion.16.g_near
  232.0 4.4 %collective-permute-done.51.g_far = bf16[48,1280]{1,0:T(8,128)(2,1)S(1)} collective-permute-done((bf16[48,1280]{1,0:T(8,128)(2,1)S(1)}, bf16[48,1280]{1,0:T(8,128)(2,1)S(1)}, u32[]{:S(2)}, u32[]{:S(2)}) %collective-permute-start.51) | collective-permute-done | bytes 122912 | tf_op jit(solution)/shard_map/ppermute | solution.py:857
  237.7 2.4 %finish.1 = (f32[192,768]{1,0:T(8,128)}, f32[48,768]{1,0:T(8,128)}, f32[48,768]{1,0:T(8,128)}, f32[48,768]{1,0:T(8,128)}, f32[1,48]{1,0:T(1,128)}, /*index=5*/f32[2,12]{1,0:T(2,128)}) custom-call(s32[7]{0:T(128)} %concatenate.10.place, bf16[2,48,768]{2,1,0:T(8,128)(2,1)} %copy-done.29, bf16[2,48,768]{2,1,0:T(8,128)(2,1)} %copy-done.43, ...), custom_call_target="tpu_custom_call" | custom-call | flops 1 | bytes 1000 | tf_op jit(solution)/shard_map/finish/pallas_call | solution.py:799
  (184 shorter events, 19.3 us)
Async XLA Ops:
  0.6 14.9 %collective-permute-start.3 = (bf16[512,768]{1,0:T(8,128)(2,1)}, bf16[512,768]{1,0:T(8,128)(2,1)S(1)}, u32[]{:S(2)}, u32[]{:S(2)}) collective-permute-start(bf16[512,768]{1,0:T(8,128)(2,1)} %bitcast.117), channel_id=1, source_target_pairs={{0,2},{2,0},{4,6},{6,4},{8,10},{10,8},{12,14},{14,12},{16,18},{18,... | collective-permute-start | bytes 2359304 | tf_op jit(solution)/shard_map/ppermute | solution.py:857
  1.2 22.4 %collective-permute-start.6 = (bf16[512,768]{1,0:T(8,128)(2,1)}, bf16[512,768]{1,0:T(8,128)(2,1)S(1)}, u32[]{:S(2)}, u32[]{:S(2)}) collective-permute-start(bf16[512,768]{1,0:T(8,128)(2,1)} %bitcast.112), channel_id=1, source_target_pairs={{0,1},{1,0},{2,3},{3,2},{4,5},{5,4},{6,7},{7,6},{8,9},{9,8},{10,11... | collective-permute-start | bytes 2359304 | tf_op jit(solution)/shard_map/ppermute | solution.py:857
  6.1 34.1 %copy-start.11 = (bf16[48,1280]{1,0:T(8,128)(2,1)S(1)}, bf16[48,1280]{1,0:T(8,128)(2,1)}, u32[]{:S(2)}) copy-start(bf16[48,1280]{1,0:T(8,128)(2,1)} %narrow_shard.1.refs_0_) | copy-start | bytes 368644
  6.1 9.3 %collective-permute-start = (bf16[48,1280]{1,0:T(8,128)(2,1)}, bf16[48,1280]{1,0:T(8,128)(2,1)S(1)}, u32[]{:S(2)}, u32[]{:S(2)}) collective-permute-start(bf16[48,1280]{1,0:T(8,128)(2,1)} %narrow_shard.1.refs_0_), channel_id=1, source_target_pairs={{0,16},{2,18},{4,20},{6,22},{8,24},{10,26},{12,28},{14,30},{16,0},... | collective-permute-start | bytes 368648 | tf_op jit(solution)/shard_map/ppermute | solution.py:857
  8.7 6.8 %collective-permute-start.1 = (bf16[48,1280]{1,0:T(8,128)(2,1)}, bf16[48,1280]{1,0:T(8,128)(2,1)S(1)}, u32[]{:S(2)}, u32[]{:S(2)}) collective-permute-start(bf16[48,1280]{1,0:T(8,128)(2,1)} %narrow_shard.1.refs_0_), channel_id=1, source_target_pairs={{0,8},{2,10},{4,12},{6,14},{8,0},{10,2},{12,4},{14,6},{16,24},{18,... | collective-permute-start | bytes 368648 | tf_op jit(solution)/shard_map/ppermute | solution.py:857
  10.3 5.3 %collective-permute-start.2 = (bf16[48,1280]{1,0:T(8,128)(2,1)}, bf16[48,1280]{1,0:T(8,128)(2,1)S(1)}, u32[]{:S(2)}, u32[]{:S(2)}) collective-permute-start(bf16[48,1280]{1,0:T(8,128)(2,1)} %narrow_shard.1.refs_0_), channel_id=1, source_target_pairs={{0,4},{2,6},{4,0},{6,2},{8,12},{10,14},{12,8},{14,10},{16,20},{18,... | collective-permute-start | bytes 368648 | tf_op jit(solution)/shard_map/ppermute | solution.py:857
  15.4 34.0 %copy-start.12 = (bf16[48,1280]{1,0:T(8,128)(2,1)}, bf16[48,1280]{1,0:T(8,128)(2,1)S(1)}, u32[]{:S(2)}) copy-start(bf16[48,1280]{1,0:T(8,128)(2,1)S(1)} %collective-permute-done.refs_3_) | copy-start | bytes 368644
  15.5 33.8 %copy-start.33 = (bf16[48,1280]{1,0:T(8,128)(2,1)}, bf16[48,1280]{1,0:T(8,128)(2,1)S(1)}, u32[]{:S(2)}) copy-start(bf16[48,1280]{1,0:T(8,128)(2,1)S(1)} %collective-permute-done.1.refs_2_) | copy-start | bytes 368644
  15.5 33.8 %copy-start.13 = (bf16[48,1280]{1,0:T(8,128)(2,1)}, bf16[48,1280]{1,0:T(8,128)(2,1)S(1)}, u32[]{:S(2)}) copy-start(bf16[48,1280]{1,0:T(8,128)(2,1)S(1)} %collective-permute-done.2.refs_1_) | copy-start | bytes 368644
  15.5 33.9 %copy-start.21 = (bf16[512,768]{1,0:T(8,128)(2,1)}, bf16[512,768]{1,0:T(8,128)(2,1)S(1)}, u32[]{:S(2)}) copy-start(bf16[512,768]{1,0:T(8,128)(2,1)S(1)} %collective-permute-done.3.cot_far) | copy-start | bytes 2359300
  15.6 8.5 %collective-permute-start.4 = (bf16[2,48,1280]{2,1,0:T(8,128)(2,1)S(1)}, bf16[2,48,1280]{2,1,0:T(8,128)(2,1)S(1)}, u32[]{:S(2)}, u32[]{:S(2)}) collective-permute-start(bf16[2,48,1280]{2,1,0:T(8,128)(2,1)S(1)} %pad_maximum_fusion.8), channel_id=1, source_target_pairs={{0,8},{2,10},{4,12},{6,14},{8,0},{10,2},{12,4},{14,6},{16,24},{18,... | collective-permute-start | bytes 737288 | tf_op jit(solution)/shard_map/ppermute | solution.py:857
  17.1 7.0 %collective-permute-start.5 = (bf16[48,1280]{1,0:T(8,128)(2,1)S(1)}, bf16[48,1280]{1,0:T(8,128)(2,1)S(1)}, u32[]{:S(2)}, u32[]{:S(2)}) collective-permute-start(bf16[48,1280]{1,0:T(8,128)(2,1)S(1)} %collective-permute-done.refs_3_), channel_id=1, source_target_pairs={{0,4},{2,6},{4,0},{6,2},{8,12},{10,14},{12,8},{14,10},{16,20},{18,... | collective-permute-start | bytes 368648 | tf_op jit(solution)/shard_map/ppermute | solution.py:857
  21.2 23.7 %collective-permute-start.7 = (bf16[7,48,768]{2,1,0:T(8,128)(2,1)}, bf16[7,48,768]{2,1,0:T(8,128)(2,1)S(1)}, u32[]{:S(2)}, u32[]{:S(2)}) collective-permute-start(bf16[7,48,768]{2,1,0:T(8,128)(2,1)} %get-tuple-element.174), channel_id=1, source_target_pairs={{0,8},{2,10},{4,12},{6,14},{8,0},{10,2},{12,4},{14,6},{16,24},{18,... | collective-permute-start | bytes 1548296 | tf_op jit(solution)/shard_map/ppermute | solution.py:857
  21.8 23.1 %collective-permute-start.8 = (bf16[7,48,768]{2,1,0:T(8,128)(2,1)}, bf16[7,48,768]{2,1,0:T(8,128)(2,1)S(1)}, u32[]{:S(2)}, u32[]{:S(2)}) collective-permute-start(bf16[7,48,768]{2,1,0:T(8,128)(2,1)} %get-tuple-element.174), channel_id=1, source_target_pairs={{0,16},{2,18},{4,20},{6,22},{8,24},{10,26},{12,28},{14,30},{16,0},... | collective-permute-start | bytes 1548296 | tf_op jit(solution)/shard_map/ppermute | solution.py:857
  23.6 25.9 %copy-start.24 = (bf16[512,768]{1,0:T(8,128)(2,1)}, bf16[512,768]{1,0:T(8,128)(2,1)S(1)}, u32[]{:S(2)}) copy-start(bf16[512,768]{1,0:T(8,128)(2,1)S(1)} %collective-permute-done.6.x_far) | copy-start | bytes 2359300
  23.6 21.3 %collective-permute-start.9 = (bf16[7,48,768]{2,1,0:T(8,128)(2,1)}, bf16[7,48,768]{2,1,0:T(8,128)(2,1)S(1)}, u32[]{:S(2)}, u32[]{:S(2)}) collective-permute-start(bf16[7,48,768]{2,1,0:T(8,128)(2,1)} %get-tuple-element.174), channel_id=1, source_target_pairs={{0,4},{2,6},{4,0},{6,2},{8,12},{10,14},{12,8},{14,10},{16,20},{18,... | collective-permute-start | bytes 1548296 | tf_op jit(solution)/shard_map/ppermute | solution.py:857
  24.1 25.4 %copy-start.34 = (bf16[48,1280]{1,0:T(8,128)(2,1)}, bf16[48,1280]{1,0:T(8,128)(2,1)S(1)}, u32[]{:S(2)}) copy-start(bf16[48,1280]{1,0:T(8,128)(2,1)S(1)} %collective-permute-done.5.refs_5_) | copy-start | bytes 368644
  24.1 25.4 %copy-start.8 = (bf16[2,48,1280]{2,1,0:T(8,128)(2,1)}, bf16[2,48,1280]{2,1,0:T(8,128)(2,1)S(1)}, u32[]{:S(2)}) copy-start(bf16[2,48,1280]{2,1,0:T(8,128)(2,1)S(1)} %collective-permute-done.4.refs_4_) | copy-start | bytes 737284
  24.2 20.7 %collective-permute-start.12 = (bf16[3,48,1280]{2,1,0:T(8,128)(2,1)S(1)}, bf16[3,48,1280]{2,1,0:T(8,128)(2,1)}, u32[]{:S(2)}, u32[]{:S(2)}) collective-permute-start(bf16[3,48,1280]{2,1,0:T(8,128)(2,1)S(1)} %pad_maximum_fusion.5), channel_id=1, source_target_pairs={{0,2},{2,0},{4,6},{6,4},{8,10},{10,8},{12,14},{14,12},{16,18},{18,... | collective-permute-start | bytes 1105928 | tf_op jit(solution)/shard_map/ppermute | solution.py:857
  24.3 15.9 %collective-permute-start.10 = (bf16[48,1280]{1,0:T(8,128)(2,1)S(1)}, bf16[48,1280]{1,0:T(8,128)(2,1)S(1)}, u32[]{:S(2)}, u32[]{:S(2)}) collective-permute-start(bf16[48,1280]{1,0:T(8,128)(2,1)S(1)} %slice_bitcast_fusion.6), channel_id=1, source_target_pairs={{0,4},{2,6},{4,0},{6,2},{8,12},{10,14},{12,8},{14,10},{16,20},{18,... | collective-permute-start | bytes 368648 | tf_op jit(solution)/shard_map/ppermute | solution.py:857
  40.2 1.3 collective-permute-start.11
  41.6 8.8 %collective-permute-start.13 = (bf16[4,48,1280]{2,1,0:T(8,128)(2,1)S(1)}, bf16[4,48,1280]{2,1,0:T(8,128)(2,1)S(1)}, u32[]{:S(2)}, u32[]{:S(2)}) collective-permute-start(bf16[4,48,1280]{2,1,0:T(8,128)(2,1)S(1)} %pad_maximum_fusion.3), channel_id=1, source_target_pairs={{0,2},{2,0},{4,6},{6,4},{8,10},{10,8},{12,14},{14,12},{16,18},{18,... | collective-permute-start | bytes 1474568 | tf_op jit(solution)/shard_map/ppermute | solution.py:857
  44.9 18.1 %copy-start = (bf16[7,48,768]{2,1,0:T(8,128)(2,1)}, bf16[7,48,768]{2,1,0:T(8,128)(2,1)S(1)}, u32[]{:S(2)}) copy-start(bf16[7,48,768]{2,1,0:T(8,128)(2,1)S(1)} %collective-permute-done.9.refs_1_) | copy-start | bytes 1548292
  44.9 15.6 %collective-permute-start.14 = (bf16[7,48,768]{2,1,0:T(8,128)(2,1)S(1)}, bf16[7,48,768]{2,1,0:T(8,128)(2,1)S(1)}, u32[]{:S(2)}, u32[]{:S(2)}) collective-permute-start(bf16[7,48,768]{2,1,0:T(8,128)(2,1)S(1)} %collective-permute-done.8.refs_3_), channel_id=1, source_target_pairs={{0,8},{2,10},{4,12},{6,14},{8,0},{10,2},{12,4},{14,6},{16,24},{18,... | collective-permute-start | bytes 1548296 | tf_op jit(solution)/shard_map/ppermute | solution.py:857
  48.0 12.5 %collective-permute-start.15 = (bf16[7,48,768]{2,1,0:T(8,128)(2,1)S(1)}, bf16[7,48,768]{2,1,0:T(8,128)(2,1)S(1)}, u32[]{:S(2)}, u32[]{:S(2)}) collective-permute-start(bf16[7,48,768]{2,1,0:T(8,128)(2,1)S(1)} %collective-permute-done.8.refs_3_), channel_id=1, source_target_pairs={{0,4},{2,6},{4,0},{6,2},{8,12},{10,14},{12,8},{14,10},{16,20},{18,... | collective-permute-start | bytes 1548296 | tf_op jit(solution)/shard_map/ppermute | solution.py:857
  49.5 10.9 %collective-permute-start.16 = (bf16[3,2,48,768]{3,2,1,0:T(8,128)(2,1)S(1)}, bf16[3,2,48,768]{3,2,1,0:T(8,128)(2,1)S(1)}, u32[]{:S(2)}, u32[]{:S(2)}) collective-permute-start(bf16[3,2,48,768]{3,2,1,0:T(8,128)(2,1)S(1)} %pad_maximum_fusion.4), channel_id=1, source_target_pairs={{0,1},{1,0},{2,3},{3,2},{4,5},{5,4},{6,7},{7,6},{8,9},{9,8},{10,11... | collective-permute-start | bytes 1327112 | tf_op jit(solution)/shard_map/ppermute | solution.py:857
  50.3 24.6 %collective-permute-start.20 = (bf16[3,7,48,768]{3,2,1,0:T(8,128)(2,1)S(1)}, bf16[3,7,48,768]{3,2,1,0:T(8,128)(2,1)S(1)}, u32[]{:S(2)}, u32[]{:S(2)}) collective-permute-start(bf16[3,7,48,768]{3,2,1,0:T(8,128)(2,1)S(1)} %pad_maximum_fusion), channel_id=1, source_target_pairs={{0,2},{2,0},{4,6},{6,4},{8,10},{10,8},{12,14},{14,12},{16,18},{18,... | collective-permute-start | bytes 4644872 | tf_op jit(solution)/shard_map/ppermute | solution.py:857
  51.2 12.7 %collective-permute-start.19 = (bf16[9,48,768]{2,1,0:T(8,128)(2,1)}, bf16[9,48,768]{2,1,0:T(8,128)(2,1)}, u32[]{:S(2)}, u32[]{:S(2)}) collective-permute-start(bf16[9,48,768]{2,1,0:T(8,128)(2,1)} %get-tuple-element.196.refs_0_), channel_id=1, source_target_pairs={{0,2},{2,0},{4,6},{6,4},{8,10},{10,8},{12,14},{14,12},{16,18},{18,... | collective-permute-start | bytes 1990664 | tf_op jit(solution)/shard_map/ppermute | solution.py:857
  60.4 29.4 %copy-start.23 = (bf16[3,2,48,768]{3,2,1,0:T(8,128)(2,1)}, bf16[3,2,48,768]{3,2,1,0:T(8,128)(2,1)S(1)}, u32[]{:S(2)}) copy-start(bf16[3,2,48,768]{3,2,1,0:T(8,128)(2,1)S(1)} %collective-permute-done.16.refs_8_) | copy-start | bytes 1327108
  60.5 14.4 %collective-permute-start.17 = (bf16[7,48,768]{2,1,0:T(8,128)(2,1)S(1)}, bf16[7,48,768]{2,1,0:T(8,128)(2,1)S(1)}, u32[]{:S(2)}, u32[]{:S(2)}) collective-permute-start(bf16[7,48,768]{2,1,0:T(8,128)(2,1)S(1)} %collective-permute-done.14.refs_4_), channel_id=1, source_target_pairs={{0,4},{2,6},{4,0},{6,2},{8,12},{10,14},{12,8},{14,10},{16,20},{18,... | collective-permute-start | bytes 1548296 | tf_op jit(solution)/shard_map/ppermute | solution.py:857
  62.2 25.3 %collective-permute-start.24 = (bf16[2,7,48,768]{3,2,1,0:T(8,128)(2,1)S(1)}, bf16[2,7,48,768]{3,2,1,0:T(8,128)(2,1)S(1)}, u32[]{:S(2)}, u32[]{:S(2)}) collective-permute-start(bf16[2,7,48,768]{3,2,1,0:T(8,128)(2,1)S(1)} %pad_maximum_fusion.1), channel_id=1, source_target_pairs={{0,2},{2,0},{4,6},{6,4},{8,10},{10,8},{12,14},{14,12},{16,18},{18,... | collective-permute-start | bytes 3096584 | tf_op jit(solution)/shard_map/ppermute | solution.py:857
  62.3 12.5 %collective-permute-start.18 = (bf16[2,2,48,768]{3,2,1,0:T(8,128)(2,1)S(1)}, bf16[2,2,48,768]{3,2,1,0:T(8,128)(2,1)S(1)}, u32[]{:S(2)}, u32[]{:S(2)}) collective-permute-start(bf16[2,2,48,768]{3,2,1,0:T(8,128)(2,1)S(1)} %pad_maximum_fusion.7), channel_id=1, source_target_pairs={{0,1},{1,0},{2,3},{3,2},{4,5},{5,4},{6,7},{7,6},{8,9},{9,8},{10,11... | collective-permute-start | bytes 884744 | tf_op jit(solution)/shard_map/ppermute | solution.py:857
  63.9 23.6 %collective-permute-start.21 = (bf16[9,48,768]{2,1,0:T(8,128)(2,1)}, bf16[9,48,768]{2,1,0:T(8,128)(2,1)}, u32[]{:S(2)}, u32[]{:S(2)}) collective-permute-start(bf16[9,48,768]{2,1,0:T(8,128)(2,1)} %pad_maximum_fusion.2), channel_id=1, source_target_pairs={{0,8},{2,10},{4,12},{6,14},{8,0},{10,2},{12,4},{14,6},{16,24},{18,... | collective-permute-start | bytes 1990664 | tf_op jit(solution)/shard_map/ppermute | solution.py:857
  74.9 14.4 %collective-permute-start.22 = (bf16[384,512]{1,0:T(8,128)(2,1)}, bf16[384,512]{1,0:T(8,128)(2,1)S(1)}, u32[]{:S(2)}, u32[]{:S(2)}) collective-permute-start(bf16[384,512]{1,0:T(8,128)(2,1)} %get-tuple-element.201.out), channel_id=1, source_target_pairs={{0,1},{1,0},{2,3},{3,2},{4,5},{5,4},{6,7},{7,6},{8,9},{9,8},{10,11... | collective-permute-start | bytes 1179656 | tf_op jit(solution)/shard_map/ppermute | solution.py:857
  76.4 12.8 %collective-permute-start.23 = (bf16[2,48,768]{2,1,0:T(8,128)(2,1)S(1)}, bf16[2,48,768]{2,1,0:T(8,128)(2,1)S(1)}, u32[]{:S(2)}, u32[]{:S(2)}) collective-permute-start(bf16[2,48,768]{2,1,0:T(8,128)(2,1)S(1)} %slice.34), channel_id=1, source_target_pairs={{0,1},{1,0},{2,3},{3,2},{4,5},{5,4},{6,7},{7,6},{8,9},{9,8},{10,11... | collective-permute-start | bytes 442376 | tf_op jit(solution)/shard_map/ppermute | solution.py:857
  89.3 4.2 %collective-permute-start.25 = (bf16[9,48,768]{2,1,0:T(8,128)(2,1)}, bf16[9,48,768]{2,1,0:T(8,128)(2,1)S(1)}, u32[]{:S(2)}, u32[]{:S(2)}) collective-permute-start(bf16[9,48,768]{2,1,0:T(8,128)(2,1)} %collective-permute-done.21.refs_6_), channel_id=1, source_target_pairs={{0,2},{2,0},{4,6},{6,4},{8,10},{10,8},{12,14},{14,12},{16,18},{18,... | collective-permute-start | bytes 1990664 | tf_op jit(solution)/shard_map/ppermute | solution.py:857
  89.4 4.1 %collective-permute-start.26 = (bf16[7,48,768]{2,1,0:T(8,128)(2,1)S(1)}, bf16[7,48,768]{2,1,0:T(8,128)(2,1)S(1)}, u32[]{:S(2)}, u32[]{:S(2)}) collective-permute-start(bf16[7,48,768]{2,1,0:T(8,128)(2,1)S(1)} %collective-permute-done.17.refs_7_), channel_id=1, source_target_pairs={{0,2},{2,0},{4,6},{6,4},{8,10},{10,8},{12,14},{14,12},{16,18},{18,... | collective-permute-start | bytes 1548296 | tf_op jit(solution)/shard_map/ppermute | solution.py:857
  89.8 3.6 %collective-permute-start.27 = (bf16[3,2,48,768]{3,2,1,0:T(8,128)(2,1)S(1)}, bf16[3,2,48,768]{3,2,1,0:T(8,128)(2,1)S(1)}, u32[]{:S(2)}, u32[]{:S(2)}) collective-permute-start(bf16[3,2,48,768]{3,2,1,0:T(8,128)(2,1)S(1)} %collective-permute-done.16.refs_8_), channel_id=1, source_target_pairs={{0,2},{2,0},{4,6},{6,4},{8,10},{10,8},{12,14},{14,12},{16,18},{18,... | collective-permute-start | bytes 1327112 | tf_op jit(solution)/shard_map/ppermute | solution.py:857
  89.9 3.5 %collective-permute-start.28 = (bf16[2,2,48,768]{3,2,1,0:T(8,128)(2,1)S(1)}, bf16[2,2,48,768]{3,2,1,0:T(8,128)(2,1)S(1)}, u32[]{:S(2)}, u32[]{:S(2)}) collective-permute-start(bf16[2,2,48,768]{3,2,1,0:T(8,128)(2,1)S(1)} %collective-permute-done.18.refs_9_), channel_id=1, source_target_pairs={{0,2},{2,0},{4,6},{6,4},{8,10},{10,8},{12,14},{14,12},{16,18},{18,... | collective-permute-start | bytes 884744 | tf_op jit(solution)/shard_map/ppermute | solution.py:857
  90.4 3.1 %collective-permute-start.29 = (bf16[2,48,768]{2,1,0:T(8,128)(2,1)S(1)}, bf16[2,48,768]{2,1,0:T(8,128)(2,1)S(1)}, u32[]{:S(2)}, u32[]{:S(2)}) collective-permute-start(bf16[2,48,768]{2,1,0:T(8,128)(2,1)S(1)} %collective-permute-done.23.refs_10_), channel_id=1, source_target_pairs={{0,2},{2,0},{4,6},{6,4},{8,10},{10,8},{12,14},{14,12},{16,18},{18,... | collective-permute-start | bytes 442376 | tf_op jit(solution)/shard_map/ppermute | solution.py:857
  117.9 13.7 %collective-permute-start.32 = (bf16[5,512,768]{2,1,0:T(8,128)(2,1)}, bf16[5,512,768]{2,1,0:T(8,128)(2,1)S(1)}, u32[]{:S(2)}, u32[]{:S(2)}) collective-permute-start(bf16[5,512,768]{2,1,0:T(8,128)(2,1)} %get-tuple-element.227.pre), channel_id=1, source_target_pairs={{0,2},{2,0},{4,6},{6,4},{8,10},{10,8},{12,14},{14,12},{16,18},{18,... | collective-permute-start | bytes 11796488 | tf_op jit(solution)/shard_map/ppermute | solution.py:857
  118.0 24.7 %collective-permute-start.33 = (bf16[4,512,384]{2,1,0:T(8,128)(2,1)}, bf16[4,512,384]{2,1,0:T(8,128)(2,1)S(1)}, u32[]{:S(2)}, u32[]{:S(2)}) collective-permute-start(bf16[4,512,384]{2,1,0:T(8,128)(2,1)} %get-tuple-element.230), channel_id=1, source_target_pairs={{0,2},{2,0},{4,6},{6,4},{8,10},{10,8},{12,14},{14,12},{16,18},{18,... | collective-permute-start | bytes 4718600 | tf_op jit(solution)/shard_map/ppermute | solution.py:857
  118.4 13.1 %collective-permute-start.31 = (bf16[2,8,48,512]{3,2,1,0:T(8,128)(2,1)}, bf16[2,8,48,512]{3,2,1,0:T(8,128)(2,1)S(1)}, u32[]{:S(2)}, u32[]{:S(2)}) collective-permute-start(bf16[2,8,48,512]{3,2,1,0:T(8,128)(2,1)} %get-tuple-element.226), channel_id=1, source_target_pairs={{0,2},{2,0},{4,6},{6,4},{8,10},{10,8},{12,14},{14,12},{16,18},{18,... | collective-permute-start | bytes 2359304 | tf_op jit(solution)/shard_map/ppermute | solution.py:857
  118.6 13.0 %collective-permute-start.30 = (bf16[384,512]{1,0:T(8,128)(2,1)}, bf16[384,512]{1,0:T(8,128)(2,1)S(1)}, u32[]{:S(2)}, u32[]{:S(2)}) collective-permute-start(bf16[384,512]{1,0:T(8,128)(2,1)} %get-tuple-element.223), channel_id=1, source_target_pairs={{0,1},{1,0},{2,3},{3,2},{4,5},{5,4},{6,7},{7,6},{8,9},{9,8},{10,11... | collective-permute-start | bytes 1179656 | tf_op jit(solution)/shard_map/ppermute | solution.py:857
  142.2 23.4 %collective-permute-start.34 = (bf16[4,3,48,768]{3,2,1,0:T(8,128)(2,1)}, bf16[4,3,48,768]{3,2,1,0:T(8,128)(2,1)S(1)}, u32[]{:S(2)}, u32[]{:S(2)}) collective-permute-start(bf16[4,3,48,768]{3,2,1,0:T(8,128)(2,1)} %get-tuple-element.228), channel_id=1, source_target_pairs={{0,4},{2,6},{4,0},{6,2},{8,12},{10,14},{12,8},{14,10},{16,20},{18,... | collective-permute-start | bytes 2654216 | tf_op jit(solution)/shard_map/ppermute | solution.py:857
  150.3 27.9 %collective-permute-start.36 = (bf16[8,2,48,768]{3,2,1,0:T(8,128)(2,1)}, bf16[8,2,48,768]{3,2,1,0:T(8,128)(2,1)S(1)}, u32[]{:S(2)}, u32[]{:S(2)}) collective-permute-start(bf16[8,2,48,768]{3,2,1,0:T(8,128)(2,1)} %get-tuple-element.232), channel_id=1, source_target_pairs={{0,1},{1,0},{2,3},{3,2},{4,5},{5,4},{6,7},{7,6},{8,9},{9,8},{10,11... | collective-permute-start | bytes 3538952 | tf_op jit(solution)/shard_map/ppermute | solution.py:857
  150.8 16.2 %collective-permute-start.35 = (bf16[2,2,2,48,768]{4,3,2,1,0:T(8,128)(2,1)}, bf16[2,2,2,48,768]{4,3,2,1,0:T(8,128)(2,1)S(1)}, u32[]{:S(2)}, u32[]{:S(2)}) collective-permute-start(bf16[2,2,2,48,768]{4,3,2,1,0:T(8,128)(2,1)} %get-tuple-element.246), channel_id=1, source_target_pairs={{0,8},{2,10},{4,12},{6,14},{8,0},{10,2},{12,4},{14,6},{16,24},{18,... | collective-permute-start | bytes 1769480 | tf_op jit(solution)/shard_map/ppermute | solution.py:857
  166.6 11.6 %collective-permute-start.37 = (bf16[2,3,48,768]{3,2,1,0:T(8,128)(2,1)}, bf16[2,3,48,768]{3,2,1,0:T(8,128)(2,1)}, u32[]{:S(2)}, u32[]{:S(2)}) collective-permute-start(bf16[2,3,48,768]{3,2,1,0:T(8,128)(2,1)} %fusion.4), channel_id=1, source_target_pairs={{0,8},{2,10},{4,12},{6,14},{8,0},{10,2},{12,4},{14,6},{16,24},{18,... | collective-permute-start | bytes 1327112 | tf_op jit(solution)/shard_map/ppermute | solution.py:857
  167.1 8.5 %collective-permute-start.38 = (bf16[2,2,48,768]{3,2,1,0:T(8,128)(2,1)S(1)}, bf16[2,2,48,768]{3,2,1,0:T(8,128)(2,1)S(1)}, u32[]{:S(2)}, u32[]{:S(2)}) collective-permute-start(bf16[2,2,48,768]{3,2,1,0:T(8,128)(2,1)S(1)} %fusion.8), channel_id=1, source_target_pairs={{0,4},{2,6},{4,0},{6,2},{8,12},{10,14},{12,8},{14,10},{16,20},{18,... | collective-permute-start | bytes 884744 | tf_op jit(solution)/shard_map/ppermute | solution.py:857
  175.6 9.0 %collective-permute-start.39 = (bf16[8,48,1280]{2,1,0:T(8,128)(2,1)}, bf16[8,48,1280]{2,1,0:T(8,128)(2,1)S(1)}, u32[]{:S(2)}, u32[]{:S(2)}) collective-permute-start(bf16[8,48,1280]{2,1,0:T(8,128)(2,1)} %get-tuple-element.257), channel_id=1, source_target_pairs={{0,2},{2,0},{4,6},{6,4},{8,10},{10,8},{12,14},{14,12},{16,18},{18,... | collective-permute-start | bytes 2949128 | tf_op jit(solution)/shard_map/ppermute | solution.py:857
  187.3 14.5 %collective-permute-start.40 = (bf16[2,2,2,48,768]{4,3,2,1,0:T(8,128)(2,1)}, bf16[2,2,2,48,768]{4,3,2,1,0:T(8,128)(2,1)}, u32[]{:S(2)}, u32[]{:S(2)}) collective-permute-start(bf16[2,2,2,48,768]{4,3,2,1,0:T(8,128)(2,1)} %fusion), channel_id=1, source_target_pairs={{0,4},{2,6},{4,0},{6,2},{8,12},{10,14},{12,8},{14,10},{16,20},{18,... | collective-permute-start | bytes 1769480 | tf_op jit(solution)/shard_map/ppermute | solution.py:857
  188.9 22.4 %collective-permute-start.41 = (bf16[2,2,48,1280]{3,2,1,0:T(8,128)(2,1)}, bf16[2,2,48,1280]{3,2,1,0:T(8,128)(2,1)}, u32[]{:S(2)}, u32[]{:S(2)}) collective-permute-start(bf16[2,2,48,1280]{3,2,1,0:T(8,128)(2,1)} %fusion.2), channel_id=1, source_target_pairs={{0,8},{2,10},{4,12},{6,14},{8,0},{10,2},{12,4},{14,6},{16,24},{18,... | collective-permute-start | bytes 1474568 | tf_op jit(solution)/shard_map/ppermute | solution.py:857
  190.4 20.9 %copy-start.17 = (bf16[8,48,1280]{2,1,0:T(8,128)(2,1)S(1)}, bf16[8,48,1280]{2,1,0:T(8,128)(2,1)}, u32[]{:S(2)}) copy-start(bf16[8,48,1280]{2,1,0:T(8,128)(2,1)} %copy-done.16) | copy-start | bytes 2949124
  190.4 31.5 %collective-permute-start.46 = (bf16[512,768]{1,0:T(8,128)(2,1)}, bf16[512,768]{1,0:T(8,128)(2,1)S(1)}, u32[]{:S(2)}, u32[]{:S(2)}) collective-permute-start(bf16[512,768]{1,0:T(8,128)(2,1)} %get-tuple-element.302), channel_id=1, source_target_pairs={{0,1},{1,0},{2,3},{3,2},{4,5},{5,4},{6,7},{7,6},{8,9},{9,8},{10,11... | collective-permute-start | bytes 2359304 | tf_op jit(solution)/shard_map/ppermute | solution.py:857
  192.2 20.6 %collective-permute-start.42 = (bf16[3,48,768]{2,1,0:T(8,128)(2,1)S(1)}, bf16[3,48,768]{2,1,0:T(8,128)(2,1)S(1)}, u32[]{:S(2)}, u32[]{:S(2)}) collective-permute-start(bf16[3,48,768]{2,1,0:T(8,128)(2,1)S(1)} %fusion.7), channel_id=1, source_target_pairs={{0,16},{2,18},{4,20},{6,22},{8,24},{10,26},{12,28},{14,30},{16,0},... | collective-permute-start | bytes 663560 | tf_op jit(solution)/shard_map/ppermute | solution.py:857
  195.3 18.8 %copy-start.42 = (bf16[2,2,48,768]{3,2,1,0:T(8,128)(2,1)S(1)}, bf16[2,2,48,768]{3,2,1,0:T(8,128)(2,1)}, u32[]{:S(2)}) copy-start(bf16[2,2,48,768]{3,2,1,0:T(8,128)(2,1)} %copy-done.41) | copy-start | bytes 884740
  195.3 18.8 %collective-permute-start.43 = (bf16[2,48,768]{2,1,0:T(8,128)(2,1)S(1)}, bf16[2,48,768]{2,1,0:T(8,128)(2,1)S(1)}, u32[]{:S(2)}, u32[]{:S(2)}) collective-permute-start(bf16[2,48,768]{2,1,0:T(8,128)(2,1)S(1)} %fusion.14), channel_id=1, source_target_pairs={{0,16},{2,18},{4,20},{6,22},{8,24},{10,26},{12,28},{14,30},{16,0},... | collective-permute-start | bytes 442376 | tf_op jit(solution)/shard_map/ppermute | solution.py:857
  202.9 14.0 %collective-permute-start.44 = (bf16[2,2,48,768]{3,2,1,0:T(8,128)(2,1)S(1)}, bf16[2,2,48,768]{3,2,1,0:T(8,128)(2,1)S(1)}, u32[]{:S(2)}, u32[]{:S(2)}) collective-permute-start(bf16[2,2,48,768]{3,2,1,0:T(8,128)(2,1)S(1)} %fusion.1), channel_id=1, source_target_pairs={{0,8},{2,10},{4,12},{6,14},{8,0},{10,2},{12,4},{14,6},{16,24},{18,... | collective-permute-start | bytes 884744 | tf_op jit(solution)/shard_map/ppermute | solution.py:857
  212.3 6.3 %collective-permute-start.45 = (bf16[2,48,1280]{2,1,0:T(8,128)(2,1)S(1)}, bf16[2,48,1280]{2,1,0:T(8,128)(2,1)S(1)}, u32[]{:S(2)}, u32[]{:S(2)}) collective-permute-start(bf16[2,48,1280]{2,1,0:T(8,128)(2,1)S(1)} %fusion.3), channel_id=1, source_target_pairs={{0,4},{2,6},{4,0},{6,2},{8,12},{10,14},{12,8},{14,10},{16,20},{18,... | collective-permute-start | bytes 737288 | tf_op jit(solution)/shard_map/ppermute | solution.py:857
  215.3 7.6 %collective-permute-start.47 = (bf16[5,48,768]{2,1,0:T(8,128)(2,1)S(1)}, bf16[5,48,768]{2,1,0:T(8,128)(2,1)S(1)}, u32[]{:S(2)}, u32[]{:S(2)}) collective-permute-start(bf16[5,48,768]{2,1,0:T(8,128)(2,1)S(1)} %pad_maximum_fusion.6.b_near), channel_id=1, source_target_pairs={{0,1},{1,0},{2,3},{3,2},{4,5},{5,4},{6,7},{7,6},{8,9},{9,8},{10,11... | collective-permute-start | bytes 1105928 | tf_op jit(solution)/shard_map/ppermute | solution.py:857
  217.9 9.9 %collective-permute-start.48 = (bf16[2,48,768]{2,1,0:T(8,128)(2,1)S(1)}, bf16[2,48,768]{2,1,0:T(8,128)(2,1)S(1)}, u32[]{:S(2)}, u32[]{:S(2)}) collective-permute-start(bf16[2,48,768]{2,1,0:T(8,128)(2,1)S(1)} %fusion.11), channel_id=1, source_target_pairs={{0,16},{2,18},{4,20},{6,22},{8,24},{10,26},{12,28},{14,30},{16,0},... | collective-permute-start | bytes 442376 | tf_op jit(solution)/shard_map/ppermute | solution.py:857
  219.6 10.9 %collective-permute-start.49 = (bf16[48,1280]{1,0:T(8,128)(2,1)S(1)}, bf16[48,1280]{1,0:T(8,128)(2,1)S(1)}, u32[]{:S(2)}, u32[]{:S(2)}) collective-permute-start(bf16[48,1280]{1,0:T(8,128)(2,1)S(1)} %fusion.17), channel_id=1, source_target_pairs={{0,16},{2,18},{4,20},{6,22},{8,24},{10,26},{12,28},{14,30},{16,0},... | collective-permute-start | bytes 368648 | tf_op jit(solution)/shard_map/ppermute | solution.py:857
  228.9 7.5 %collective-permute-start.50 = (bf16[2,48,768]{2,1,0:T(8,128)(2,1)S(1)}, bf16[2,48,768]{2,1,0:T(8,128)(2,1)S(1)}, u32[]{:S(2)}, u32[]{:S(2)}) collective-permute-start(bf16[2,48,768]{2,1,0:T(8,128)(2,1)S(1)} %fusion.10.a_near), channel_id=1, source_target_pairs={{0,1},{1,0},{2,3},{3,2},{4,5},{5,4},{6,7},{7,6},{8,9},{9,8},{10,11... | collective-permute-start | bytes 442376 | tf_op jit(solution)/shard_map/ppermute | solution.py:857
  231.4 4.9 %collective-permute-start.51 = (bf16[48,1280]{1,0:T(8,128)(2,1)S(1)}, bf16[48,1280]{1,0:T(8,128)(2,1)S(1)}, u32[]{:S(2)}, u32[]{:S(2)}) collective-permute-start(bf16[48,1280]{1,0:T(8,128)(2,1)S(1)} %fusion.16.g_near), channel_id=1, source_target_pairs={{0,1},{1,0},{2,3},{3,2},{4,5},{5,4},{6,7},{7,6},{8,9},{9,8},{10,11... | collective-permute-start | bytes 368648 | tf_op jit(solution)/shard_map/ppermute | solution.py:857
  (37 other events, 194.1 us)

commit v5 on v4

--- a/solution.py
+++ b/solution.py
@@ -27,8 +27,8 @@
     )
 
 
-def params():
-    return pltpu.CompilerParams(vmem_limit_bytes=VMEM)
+def params(limit=VMEM):
+    return pltpu.CompilerParams(vmem_limit_bytes=limit)
 
 
 def cost(flops, byte_count, exps=0):
@@ -451,7 +451,7 @@
         functools.partial(attend_back_kernel, bool(carry), mine),
         out_shape=out_shape,
         grid_spec=grid,
-        compiler_params=params(),
+        compiler_params=params(VMEM if carry else 66_000_000),
         cost_estimate=cost(count * 1024 * 512 * 1024, 6_000_000),
         name="attend_back_mine" if mine else "attend_back_theirs",
     )(place, grad, out, inverse, qkv, qkv, qkv, kept, *carry)
@@ -758,9 +758,25 @@
             pltpu.SemaphoreType.DMA((6,)),
         ],
         compiler_params=params(),
-        cost_estimate=pl.CostEstimate(flops=20_000_000_000, bytes_accessed=10_000_000, transcendentals=0),
+        cost_estimate=cost(2 * 1024 * 768 * 1152, 10_000_000),
         name="project_back",
     )(place, *blocks, whole)
+
+
+def pass_kernel(place, result):
+    for at in range(7):
+        result[at] = place[at]
+
+
+def hand_on(place):
+    return pl.pallas_call(
+        pass_kernel,
+        out_shape=jax.ShapeDtypeStruct((7,), jnp.int32),
+        in_specs=[SCALARS],
+        out_specs=SCALARS,
+        cost_estimate=pl.CostEstimate(flops=20_000_000_000, bytes_accessed=1000, transcendentals=0),
+        name="hand_on",
+    )(place)
 
 
 def finish_kernel(place, a_near, a_far, g_near, g_far, qw, kw, vw, gain, contract, q, k, v, gain_grad, bias):
@@ -1013,12 +1029,13 @@
     g_near, g_far = line.run(weight_grad, normed_kept, normed_sent, whole)
     g_parts = parts(g_near, by_core(g_far), "high", "low", "y")
     line.wait(a_got, b_got, c_got)
-    part_near, part_far = line.run(project_back, narrow, whole)
-    part_got = by_x(part_far)
+    line.place = hand_on(line.place)
     g_parts = keep(g_parts, "low", by_z(total(line, g_parts, own, "low")))
     a_parts = keep(a_parts, "y", by_y(total(line, a_parts, own, "y")))
     b_parts = keep(b_parts, "high", by_zz(total(line, b_parts, own, "high")))
     c_parts = keep(c_parts, "high", by_zz(total(line, c_parts, own, "high")))
+    part_near, part_far = line.run(project_back, narrow, whole)
+    part_got = by_x(part_far)
     a_parts = keep(a_parts, "low", by_z(total(line, a_parts, own, "low")))
     g_parts = keep(g_parts, "y", by_y(total(line, g_parts, own, "y")))
     b_low = jnp.concatenate([total(line, b_parts, own), total(line, c_parts, own)], axis=0)
@@ -1027,13 +1044,13 @@
     line.wait(b_low)
     a_parts = keep(a_parts, "high", by_zz(total(line, a_parts, own, "high")))
     g_parts = keep(g_parts, "high", by_zz(total(line, g_parts, own, "high")))
-    result, expand_sum, output_sum, gain_two = line.run(
-        finish_wide, tokens, small, part_near, part_got, middle_grad, b_low, b_other, expand_weight, feedforward_gain
-    )
     a_low = total(line, a_parts, own)
     a_other = by_x(a_low)
     g_low = total(line, g_parts, own)
     g_other = by_x(g_low)
+    result, expand_sum, output_sum, gain_two = line.run(
+        finish_wide, tokens, small, part_near, part_got, middle_grad, b_low, b_other, expand_weight, feedforward_gain
+    )
     contract_sum, *grads, gain_one, bias_grad = line.run(
         finish, a_low, a_other, g_low, g_other, query_weight, key_weight, value_weight, attention_gain
     )

time: 242 us -> 235 us (0.971)
  waiting for transfers between devices: 35.8 us -> 30.7 us
  local copies, waits for them, and re-layouts: 9.14 us -> 5.53 us
    ppermute x52, waiting for transfers between devices: 35.8 us -> 30.7 us  [swap(): return lax.ppermute(array, axis, [(i, i ^ bit) for i in range(count)])]
    unnamed x98 -> x90, local copies, waits for them, and re-layouts: 8.43 us -> 4.83 us
  transfers between devices with their start and end apart: 52 -> 52, of which waited for: 15 -> 15; matrix products, arithmetic and copies ran while one was open for 6% -> 6% of each run, Pallas kernels for 38% -> 39%
where the time goes in v5:
time: 235 us; the launch traced here: 233 us
  Pallas kernels  117 us (50%)
  starting transfers between devices  60 us (26%)
  waiting for transfers between devices  30.7 us (13%)
  other arithmetic  17.1 us (7%)
  local copies, waits for them, and re-layouts  5.53 us (2%)
  between operations  3.41 us (1%)
    ppermute x52, starting transfers between devices, swap(): return lax.ppermute(array, axis, [(i, i ^ bit) for i in range(count)])  60 us
    ppermute x52, waiting for transfers between devices, swap(): return lax.ppermute(array, axis, [(i, i ^ bit) for i in range(count)])  30.7 us
    pallas_call x2, Pallas kernels, attend_back(): pl.pallas_call(functools.partial(attend_back_kernel, bool(carry), mine),...  24.6 us
    pallas_call x1, Pallas kernels, forward(): pl.pallas_call(forward_kernel, out_shape=(hidden, hidden, jax.ShapeDtypeS...  23.1 us
    pallas_call x2, Pallas kernels, attend(): pl.pallas_call(functools.partial(attend_kernel, mine), out_shape=(jax.Sha...  21 us
    convert_element_type x14, other arithmetic, total(): made = lax.optimization_barrier(made.astype(bf16))  15.1 us
    pallas_call x1, Pallas kernels, expand_weight_grad(): pl.pallas_call(expand_grad_kernel, out_shape=(first, first, second, secon...  8.34 us
    pallas_call x1, Pallas kernels, project(): pl.pallas_call(project_kernel, out_shape=(jax.ShapeDtypeStruct((1152, 102...  7.72 us
  transfers between devices with their start and end apart: 52, of which 15 were waited for; matrix products, arithmetic and copies ran while one was open for 6% of the time, Pallas kernels for 39%

profile of v5, /device:TPU:0, one launch (start us, length us, event | category | flops | bytes accessed | tf_op | source)
XLA Modules:
  0.0 233.4 jit_solution(6183462776771288152)
XLA Ops:
  1.2 2.6 %collective-permute-start.6 = (bf16[512,768]{1,0:T(8,128)(2,1)}, bf16[512,768]{1,0:T(8,128)(2,1)S(1)}, u32[]{:S(2)}, u32[]{:S(2)}) collective-permute-start(bf16[512,768]{1,0:T(8,128)(2,1)} %bitcast.112), channel_id=1, source_target_pairs={{0,1},{1,0},{2,3},{3,2},{4,5},{5,4},{6,7},{7,6},{8,9},{9,8},{10,11... | collective-permute-start | bytes 2359304 | tf_op jit(solution)/shard_map/ppermute | solution.py:873
  4.3 1.8 narrow_shard.1.refs_0_
  6.1 2.6 %collective-permute-start = (bf16[48,1280]{1,0:T(8,128)(2,1)}, bf16[48,1280]{1,0:T(8,128)(2,1)S(1)}, u32[]{:S(2)}, u32[]{:S(2)}) collective-permute-start(bf16[48,1280]{1,0:T(8,128)(2,1)} %narrow_shard.1.refs_0_), channel_id=1, source_target_pairs={{0,16},{2,18},{4,20},{6,22},{8,24},{10,26},{12,28},{14,30},{16,0},... | collective-permute-start | bytes 368648 | tf_op jit(solution)/shard_map/ppermute | solution.py:873
  8.7 1.6 collective-permute-start.1
  10.3 1.5 collective-permute-start.2
  11.8 2.9 %wide_shard.1 = (bf16[7,48,768]{2,1,0:T(8,128)(2,1)}, bf16[9,48,768]{2,1,0:T(8,128)(2,1)}) custom-call(s32[4]{0:T(128)} %pad_add_fusion.place, bf16[48,3072]{1,0:T(8,128)(2,1)} %up.1, bf16[48,768]{1,0:T(8,128)(2,1)} %output.1, bf16[192,768]{1,0:T(8,128)(2,1)} %contract.1), custom_call_target="tpu_custom_call" | custom-call | flops 1000 | bytes 1000 | tf_op jit(solution)/shard_map/wide_shard/pallas_call | solution.py:101
  15.6 1.5 collective-permute-start.4
  17.1 1.5 collective-permute-start.5
  21.8 1.8 collective-permute-start.8
  24.3 12.0 %collective-permute-start.10 = (bf16[48,1280]{1,0:T(8,128)(2,1)S(1)}, bf16[48,1280]{1,0:T(8,128)(2,1)S(1)}, u32[]{:S(2)}, u32[]{:S(2)}) collective-permute-start(bf16[48,1280]{1,0:T(8,128)(2,1)S(1)} %slice_bitcast_fusion.6), channel_id=1, source_target_pairs={{0,4},{2,6},{4,0},{6,2},{8,12},{10,14},{12,8},{14,10},{16,20},{18,... | collective-permute-start | bytes 368648 | tf_op jit(solution)/shard_map/ppermute | solution.py:873
  36.2 4.0 %collective-permute-done.10.refs_6_ = bf16[48,1280]{1,0:T(8,128)(2,1)S(1)} collective-permute-done((bf16[48,1280]{1,0:T(8,128)(2,1)S(1)}, bf16[48,1280]{1,0:T(8,128)(2,1)S(1)}, u32[]{:S(2)}, u32[]{:S(2)}) %collective-permute-start.10) | collective-permute-done | bytes 122912 | tf_op jit(solution)/shard_map/ppermute | solution.py:873
  40.3 1.2 collective-permute-done.11.refs_9_
  41.7 3.1 %collective-permute-done.7.refs_2_ = bf16[7,48,768]{2,1,0:T(8,128)(2,1)S(1)} collective-permute-done((bf16[7,48,768]{2,1,0:T(8,128)(2,1)}, bf16[7,48,768]{2,1,0:T(8,128)(2,1)S(1)}, u32[]{:S(2)}, u32[]{:S(2)}) %collective-permute-start.7) | collective-permute-done | bytes 516128 | tf_op jit(solution)/shard_map/ppermute | solution.py:873
  44.9 3.1 %collective-permute-start.14 = (bf16[7,48,768]{2,1,0:T(8,128)(2,1)S(1)}, bf16[7,48,768]{2,1,0:T(8,128)(2,1)S(1)}, u32[]{:S(2)}, u32[]{:S(2)}) collective-permute-start(bf16[7,48,768]{2,1,0:T(8,128)(2,1)S(1)} %collective-permute-done.8.refs_3_), channel_id=1, source_target_pairs={{0,8},{2,10},{4,12},{6,14},{8,0},{10,2},{12,4},{14,6},{16,24},{18,... | collective-permute-start | bytes 1548296 | tf_op jit(solution)/shard_map/ppermute | solution.py:873
  48.0 1.3 collective-permute-start.15
  51.2 7.7 %project.1 = (bf16[1152,1024]{1,0:T(8,128)(2,1)}, bf16[8,48,1024]{2,1,0:T(8,128)(2,1)}, bf16[8,48,1024]{2,1,0:T(8,128)(2,1)}, f32[8,768]{1,0:T(8,128)}, f32[8,128]{1,0:T(8,128)}, /*index=5*/f32[6,384,128]{2,1,0:T(8,128)}) custom-call(s32[7]{0:T(128)} %concatenate.10.place, bf16[512,768]{1,0:T(8,128)(2,1)} %bitcast.113, bf16[512,768]{1,0:T(8,128)(2,1)} %copy-done.24, ...), custom_call_target="tpu_custom_call" | custom-call | flops 1000 | bytes 1000 | tf_op jit(solution)/shard_map/project/pallas_call | solution.py:193
  58.9 1.5 collective-permute-done.16.refs_8_
  60.5 1.6 collective-permute-start.17
  63.0 0.9 pad_maximum_fusion.2
  64.2 10.6 %attend_theirs.1 = (bf16[384,512]{1,0:T(8,128)(2,1)}, bf16[6,1024,512]{2,1,0:T(8,128)(2,1)}, f32[6,1,512]{2,1,0:T(1,128)}) custom-call(s32[7]{0:T(128)} %concatenate.10.place, f32[8,128]{1,0:T(8,128)} %get-tuple-element.192.table, f32[6,384,128]{2,1,0:T(8,128)} %get-tuple-element.193.tile, bf16[1152,1024]{1,0:T(8,128)(2,1)} %get-tuple-element.185.q.k.v, ...), custom_call_target="tpu_custom_call" | custom-call | flops 1000 | bytes 1000 | tf_op jit(solution)/shard_map/attend_theirs/pallas_call | solution.py:288
  74.9 1.6 collective-permute-start.22
  77.1 10.4 %attend_mine.1 = (bf16[384,512]{1,0:T(8,128)(2,1)}, bf16[6,1024,512]{2,1,0:T(8,128)(2,1)}, f32[6,1,512]{2,1,0:T(1,128)}) custom-call(s32[7]{0:T(128)} %concatenate.10.place, f32[8,128]{1,0:T(8,128)} %get-tuple-element.192.table, f32[6,384,128]{2,1,0:T(8,128)} %get-tuple-element.193.tile, bf16[1152,1024]{1,0:T(8,128)(2,1)} %get-tuple-element.185.q.k.v, ...), custom_call_target="tpu_custom_call" | custom-call | flops 1000 | bytes 1000 | tf_op jit(solution)/shard_map/attend_mine/pallas_call | solution.py:288
  87.5 1.8 collective-permute-done.23.refs_10_
  90.5 3.0 %collective-permute-done.29.refs_18_ = bf16[2,48,768]{2,1,0:T(8,128)(2,1)S(1)} collective-permute-done((bf16[2,48,768]{2,1,0:T(8,128)(2,1)S(1)}, bf16[2,48,768]{2,1,0:T(8,128)(2,1)S(1)}, u32[]{:S(2)}, u32[]{:S(2)}) %collective-permute-start.29) | collective-permute-done | bytes 147488 | tf_op jit(solution)/shard_map/ppermute | solution.py:873
  94.8 23.1 %forward.1 = (bf16[4,512,384]{2,1,0:T(8,128)(2,1)}, bf16[4,512,384]{2,1,0:T(8,128)(2,1)}, bf16[5,512,768]{2,1,0:T(8,128)(2,1)}, bf16[2,8,48,512]{3,2,1,0:T(8,128...) custom-call(s32[7]{0:T(128)} %concatenate.10.place, ...), custom_call_target="tpu_custom_call" | custom-call | flops 8500000 | bytes 20000 | tf_op jit(solution)/shard_map/forward/pallas_call | solution.py:584
  118.6 1.5 collective-permute-start.30
  120.1 11.5 %attend_back_mine.1 = (bf16[384,512]{1,0:T(8,128)(2,1)}, f32[384,1024]{1,0:T(8,128)}, f32[384,1024]{1,0:T(8,128)}, f32[6,384,128]{2,1,0:T(8,128)}, f32[6,8,512]{2,1,0:T(8,128)}) custom-call(s32[7]{0:T(128)} %concatenate.10.place, bf16[384,512]{1,0:T(8,128)(2,1)} %get-tuple-element.218.grad, bf16[384,512]{1,0:T(8,128)(2,1)} %get-tuple-element.204.att_near.out, ...), custom_call_target="tpu_custom_call" | custom-call | flops 3221225 | bytes 6000 | tf_op jit(solution)/shard_map/attend_back_mine/pallas_call | solution.py:450
  131.6 0.9 copy-done.22
  132.5 8.3 %expand_weight_grad.1 = (bf16[4,3,48,768]{3,2,1,0:T(8,128)(2,1)}, bf16[4,3,48,768]{3,2,1,0:T(8,128)(2,1)}, bf16[2,2,2,48,768]{4,3,2,1,0:T(8,128)(2,1)}, bf16[2,2,2,48,768]{4,3,2,1,0:T(8,128)(2,1)}) custom-call(s32[7]{0:T(128)} %concatenate.10.place, bf16[2,8,48,512]{3,2,1,0:T(8,128)(2,1)} %get-tuple-element.225.turned, bf16[2,8,48,512]{3,2,1,0:T(8,128)(2,1)} %copy-done.22, ...), custom_call_target="tpu_custom_call" | custom-call | flops 3019898 | bytes 12000 | tf_op jit(solution)/shard_map/expand_weight_grad/pallas_call | solution.py:674
  141.3 6.3 %contract_weight_grad.1 = (bf16[8,2,48,768]{3,2,1,0:T(8,128)(2,1)}, bf16[8,2,48,768]{3,2,1,0:T(8,128)(2,1)}) custom-call(s32[7]{0:T(128)} %concatenate.10.place, bf16[4,512,384]{2,1,0:T(8,128)(2,1)} %get-tuple-element.216.hid, bf16[4,512,384]{2,1,0:T(8,128)(2,1)} %collective-permute-done.33.hid_far, bf16[512,768]{1,0:T(8,128)(2,1)} %bitcast.119, ...), custom_call_target="tpu_custom_call" | custom-call | flops 2415919 | bytes 9000 | tf_op jit(solution)/shard_map/contract_weight_grad/pallas_call | solution.py:627
  148.2 1.7 collective-permute-start.35
  149.9 13.1 %attend_back_theirs.1.whole.refs_10_ = bf16[6,208,1024]{2,1,0:T(8,128)(2,1)} custom-call(s32[7]{0:T(128)} %concatenate.10.place, bf16[384,512]{1,0:T(8,128)(2,1)} %collective-permute-done.30.grad, bf16[384,512]{1,0:T(8,128)(2,1)} %get-tuple-element.201.out, f32[6,1,512]{2,1,0:T(1,128)} %get-tuple-element.234.inverse, ...), custom_call_target="tpu_custom_call" | custom-call | flops 3221225 | bytes 6000 | tf_op jit(solution)/shard_map/attend_back_theirs/pallas_call | solution.py:450
  163.0 1.0 fusion.4
  164.0 1.4 collective-permute-start.37
  166.0 6.9 %weight_grad.1 = (bf16[8,48,1280]{2,1,0:T(8,128)(2,1)}, bf16[8,48,1280]{2,1,0:T(8,128)(2,1)}) custom-call(s32[7]{0:T(128)} %concatenate.10.place, bf16[8,48,1024]{2,1,0:T(8,128)(2,1)} %get-tuple-element.250.mine, bf16[8,48,1024]{2,1,0:T(8,128)(2,1)} %get-tuple-element.251.other, bf16[6,208,1024]{2,1,0:T(8,128)(2,1)} %attend_back_theirs.1.whole.refs_10_), custom_call_target="tpu_custom_call" | custom-call | flops 1811939 | bytes 6000 | tf_op jit(solution)/shard_map/weight_grad/pallas_call | solution.py:718
  173.4 2.2 collective-permute-done.36
  175.6 1.2 hand_on.1.place
  176.8 2.1 fusion.2
  178.9 1.0 fusion
  179.8 1.5 collective-permute-start.40
  181.4 1.6 collective-permute-start.41
  183.0 1.2 fusion.7
  184.2 0.9 collective-permute-start.42
  185.1 1.1 fusion.14
  186.2 2.2 collective-permute-start.43
  188.4 6.3 %project_back.1 = (bf16[512,768]{1,0:T(8,128)(2,1)}, bf16[512,768]{1,0:T(8,128)(2,1)}) custom-call(s32[7]{0:T(128)} %hand_on.1.place, bf16[48,1280]{1,0:T(8,128)(2,1)} %narrow_shard.1.refs_0_, bf16[48,1280]{1,0:T(8,128)(2,1)} %copy-done.9, bf16[48,1280]{1,0:T(8,128)(2,1)} %copy-done.14, bf16[48,1280]{1,0:T(8,128)(2,1)} %copy-done.8, ...), custom_call_target="tpu_custom_call" | custom-call | flops 1811939 | bytes 10000 | tf_op jit(solution)/shard_map/project_back/pallas_call | solution.py:749
  195.3 1.1 fusion.1
  196.4 1.4 collective-permute-start.44
  197.8 5.9 %collective-permute-done.41 = bf16[2,2,48,1280]{3,2,1,0:T(8,128)(2,1)} collective-permute-done((bf16[2,2,48,1280]{3,2,1,0:T(8,128)(2,1)}, bf16[2,2,48,1280]{3,2,1,0:T(8,128)(2,1)}, u32[]{:S(2)}, u32[]{:S(2)}) %collective-permute-start.41) | collective-permute-done | bytes 491552 | tf_op jit(solution)/shard_map/ppermute | solution.py:873
  203.8 1.2 fusion.3
  205.5 1.3 fusion.6
  206.8 1.1 fusion.13
  207.9 1.5 collective-permute-start.49
  209.4 1.0 fusion.11
  210.5 0.7 collective-permute-done.45
  211.2 1.0 fusion.17
  212.2 2.3 collective-permute-start.47
  214.5 5.7 %collective-permute-done.46 = bf16[2,48,768]{2,1,0:T(8,128)(2,1)S(1)} collective-permute-done((bf16[2,48,768]{2,1,0:T(8,128)(2,1)S(1)}, bf16[2,48,768]{2,1,0:T(8,128)(2,1)S(1)}, u32[]{:S(2)}, u32[]{:S(2)}) %collective-permute-start.46) | collective-permute-done | bytes 147488 | tf_op jit(solution)/shard_map/ppermute | solution.py:873
  220.2 1.0 fusion.10.a_near
  221.9 1.0 fusion.16.g_near
  223.0 1.5 collective-permute-start.51
  224.5 0.8 copy-done.25
  225.5 4.2 %finish_wide.1 = (bf16[512,768]{1,0:T(8,128)(2,1)}, f32[48,3072]{1,0:T(8,128)}, f32[48,768]{1,0:T(8,128)}, f32[1,48]{1,0:T(1,128)}) custom-call(s32[7]{0:T(128)} %hand_on.1.place, bf16[512,768]{1,0:T(8,128)(2,1)} %bitcast.115, f32[8,768]{1,0:T(8,128)} %get-tuple-element.206.small, bf16[512,768]{1,0:T(8,128)(2,1)} %get-tuple-element.271.near, ...), custom_call_target="tpu_custom_call" | custom-call | flops 1 | bytes 2000 | tf_op jit(solution)/shard_map/finish_wide/pallas_call | solution.py:846
  231.0 2.4 %finish.1 = (f32[192,768]{1,0:T(8,128)}, f32[48,768]{1,0:T(8,128)}, f32[48,768]{1,0:T(8,128)}, f32[48,768]{1,0:T(8,128)}, f32[1,48]{1,0:T(1,128)}, /*index=5*/f32[2,12]{1,0:T(2,128)}) custom-call(s32[7]{0:T(128)} %hand_on.1.place, bf16[2,48,768]{2,1,0:T(8,128)(2,1)} %copy-done.29, bf16[2,48,768]{2,1,0:T(8,128)(2,1)} %copy-done.41, ...), custom_call_target="tpu_custom_call" | custom-call | flops 1 | bytes 1000 | tf_op jit(solution)/shard_map/finish/pallas_call | solution.py:815
  (177 shorter events, 16.4 us)
Async XLA Ops:
  0.6 14.9 %collective-permute-start.3 = (bf16[512,768]{1,0:T(8,128)(2,1)}, bf16[512,768]{1,0:T(8,128)(2,1)S(1)}, u32[]{:S(2)}, u32[]{:S(2)}) collective-permute-start(bf16[512,768]{1,0:T(8,128)(2,1)} %bitcast.117), channel_id=1, source_target_pairs={{0,2},{2,0},{4,6},{6,4},{8,10},{10,8},{12,14},{14,12},{16,18},{18,... | collective-permute-start | bytes 2359304 | tf_op jit(solution)/shard_map/ppermute | solution.py:873
  1.2 22.4 %collective-permute-start.6 = (bf16[512,768]{1,0:T(8,128)(2,1)}, bf16[512,768]{1,0:T(8,128)(2,1)S(1)}, u32[]{:S(2)}, u32[]{:S(2)}) collective-permute-start(bf16[512,768]{1,0:T(8,128)(2,1)} %bitcast.112), channel_id=1, source_target_pairs={{0,1},{1,0},{2,3},{3,2},{4,5},{5,4},{6,7},{7,6},{8,9},{9,8},{10,11... | collective-permute-start | bytes 2359304 | tf_op jit(solution)/shard_map/ppermute | solution.py:873
  6.1 34.1 %copy-start.7 = (bf16[48,1280]{1,0:T(8,128)(2,1)S(1)}, bf16[48,1280]{1,0:T(8,128)(2,1)}, u32[]{:S(2)}) copy-start(bf16[48,1280]{1,0:T(8,128)(2,1)} %narrow_shard.1.refs_0_) | copy-start | bytes 368644
  6.1 9.3 %collective-permute-start = (bf16[48,1280]{1,0:T(8,128)(2,1)}, bf16[48,1280]{1,0:T(8,128)(2,1)S(1)}, u32[]{:S(2)}, u32[]{:S(2)}) collective-permute-start(bf16[48,1280]{1,0:T(8,128)(2,1)} %narrow_shard.1.refs_0_), channel_id=1, source_target_pairs={{0,16},{2,18},{4,20},{6,22},{8,24},{10,26},{12,28},{14,30},{16,0},... | collective-permute-start | bytes 368648 | tf_op jit(solution)/shard_map/ppermute | solution.py:873
  8.7 6.8 %collective-permute-start.1 = (bf16[48,1280]{1,0:T(8,128)(2,1)}, bf16[48,1280]{1,0:T(8,128)(2,1)S(1)}, u32[]{:S(2)}, u32[]{:S(2)}) collective-permute-start(bf16[48,1280]{1,0:T(8,128)(2,1)} %narrow_shard.1.refs_0_), channel_id=1, source_target_pairs={{0,8},{2,10},{4,12},{6,14},{8,0},{10,2},{12,4},{14,6},{16,24},{18,... | collective-permute-start | bytes 368648 | tf_op jit(solution)/shard_map/ppermute | solution.py:873
  10.3 5.3 %collective-permute-start.2 = (bf16[48,1280]{1,0:T(8,128)(2,1)}, bf16[48,1280]{1,0:T(8,128)(2,1)S(1)}, u32[]{:S(2)}, u32[]{:S(2)}) collective-permute-start(bf16[48,1280]{1,0:T(8,128)(2,1)} %narrow_shard.1.refs_0_), channel_id=1, source_target_pairs={{0,4},{2,6},{4,0},{6,2},{8,12},{10,14},{12,8},{14,10},{16,20},{18,... | collective-permute-start | bytes 368648 | tf_op jit(solution)/shard_map/ppermute | solution.py:873
  15.4 34.0 %copy-start.8 = (bf16[48,1280]{1,0:T(8,128)(2,1)}, bf16[48,1280]{1,0:T(8,128)(2,1)S(1)}, u32[]{:S(2)}) copy-start(bf16[48,1280]{1,0:T(8,128)(2,1)S(1)} %collective-permute-done.refs_3_) | copy-start | bytes 368644
  15.5 33.8 %copy-start.14 = (bf16[48,1280]{1,0:T(8,128)(2,1)}, bf16[48,1280]{1,0:T(8,128)(2,1)S(1)}, u32[]{:S(2)}) copy-start(bf16[48,1280]{1,0:T(8,128)(2,1)S(1)} %collective-permute-done.1.refs_2_) | copy-start | bytes 368644
  15.5 33.9 %copy-start.9 = (bf16[48,1280]{1,0:T(8,128)(2,1)}, bf16[48,1280]{1,0:T(8,128)(2,1)S(1)}, u32[]{:S(2)}) copy-start(bf16[48,1280]{1,0:T(8,128)(2,1)S(1)} %collective-permute-done.2.refs_1_) | copy-start | bytes 368644
  15.5 33.9 %copy-start.21 = (bf16[512,768]{1,0:T(8,128)(2,1)}, bf16[512,768]{1,0:T(8,128)(2,1)S(1)}, u32[]{:S(2)}) copy-start(bf16[512,768]{1,0:T(8,128)(2,1)S(1)} %collective-permute-done.3.cot_far) | copy-start | bytes 2359300
  15.6 8.5 %collective-permute-start.4 = (bf16[2,48,1280]{2,1,0:T(8,128)(2,1)S(1)}, bf16[2,48,1280]{2,1,0:T(8,128)(2,1)S(1)}, u32[]{:S(2)}, u32[]{:S(2)}) collective-permute-start(bf16[2,48,1280]{2,1,0:T(8,128)(2,1)S(1)} %pad_maximum_fusion.8), channel_id=1, source_target_pairs={{0,8},{2,10},{4,12},{6,14},{8,0},{10,2},{12,4},{14,6},{16,24},{18,... | collective-permute-start | bytes 737288 | tf_op jit(solution)/shard_map/ppermute | solution.py:873
  17.1 7.0 %collective-permute-start.5 = (bf16[48,1280]{1,0:T(8,128)(2,1)S(1)}, bf16[48,1280]{1,0:T(8,128)(2,1)S(1)}, u32[]{:S(2)}, u32[]{:S(2)}) collective-permute-start(bf16[48,1280]{1,0:T(8,128)(2,1)S(1)} %collective-permute-done.refs_3_), channel_id=1, source_target_pairs={{0,4},{2,6},{4,0},{6,2},{8,12},{10,14},{12,8},{14,10},{16,20},{18,... | collective-permute-start | bytes 368648 | tf_op jit(solution)/shard_map/ppermute | solution.py:873
  21.2 23.7 %collective-permute-start.7 = (bf16[7,48,768]{2,1,0:T(8,128)(2,1)}, bf16[7,48,768]{2,1,0:T(8,128)(2,1)S(1)}, u32[]{:S(2)}, u32[]{:S(2)}) collective-permute-start(bf16[7,48,768]{2,1,0:T(8,128)(2,1)} %get-tuple-element.174), channel_id=1, source_target_pairs={{0,8},{2,10},{4,12},{6,14},{8,0},{10,2},{12,4},{14,6},{16,24},{18,... | collective-permute-start | bytes 1548296 | tf_op jit(solution)/shard_map/ppermute | solution.py:873
  21.8 23.1 %collective-permute-start.8 = (bf16[7,48,768]{2,1,0:T(8,128)(2,1)}, bf16[7,48,768]{2,1,0:T(8,128)(2,1)S(1)}, u32[]{:S(2)}, u32[]{:S(2)}) collective-permute-start(bf16[7,48,768]{2,1,0:T(8,128)(2,1)} %get-tuple-element.174), channel_id=1, source_target_pairs={{0,16},{2,18},{4,20},{6,22},{8,24},{10,26},{12,28},{14,30},{16,0},... | collective-permute-start | bytes 1548296 | tf_op jit(solution)/shard_map/ppermute | solution.py:873
  23.6 16.7 %copy-start.24 = (bf16[512,768]{1,0:T(8,128)(2,1)}, bf16[512,768]{1,0:T(8,128)(2,1)S(1)}, u32[]{:S(2)}) copy-start(bf16[512,768]{1,0:T(8,128)(2,1)S(1)} %collective-permute-done.6.x_far) | copy-start | bytes 2359300
  23.6 21.3 %collective-permute-start.9 = (bf16[7,48,768]{2,1,0:T(8,128)(2,1)}, bf16[7,48,768]{2,1,0:T(8,128)(2,1)S(1)}, u32[]{:S(2)}, u32[]{:S(2)}) collective-permute-start(bf16[7,48,768]{2,1,0:T(8,128)(2,1)} %get-tuple-element.174), channel_id=1, source_target_pairs={{0,4},{2,6},{4,0},{6,2},{8,12},{10,14},{12,8},{14,10},{16,20},{18,... | collective-permute-start | bytes 1548296 | tf_op jit(solution)/shard_map/ppermute | solution.py:873
  24.1 25.4 %copy-start.15 = (bf16[48,1280]{1,0:T(8,128)(2,1)}, bf16[48,1280]{1,0:T(8,128)(2,1)S(1)}, u32[]{:S(2)}) copy-start(bf16[48,1280]{1,0:T(8,128)(2,1)S(1)} %collective-permute-done.5.refs_5_) | copy-start | bytes 368644
  24.1 25.4 %copy-start.1 = (bf16[2,48,1280]{2,1,0:T(8,128)(2,1)}, bf16[2,48,1280]{2,1,0:T(8,128)(2,1)S(1)}, u32[]{:S(2)}) copy-start(bf16[2,48,1280]{2,1,0:T(8,128)(2,1)S(1)} %collective-permute-done.4.refs_4_) | copy-start | bytes 737284
  24.2 20.7 %collective-permute-start.12 = (bf16[3,48,1280]{2,1,0:T(8,128)(2,1)S(1)}, bf16[3,48,1280]{2,1,0:T(8,128)(2,1)S(1)}, u32[]{:S(2)}, u32[]{:S(2)}) collective-permute-start(bf16[3,48,1280]{2,1,0:T(8,128)(2,1)S(1)} %pad_maximum_fusion.5), channel_id=1, source_target_pairs={{0,2},{2,0},{4,6},{6,4},{8,10},{10,8},{12,14},{14,12},{16,18},{18,... | collective-permute-start | bytes 1105928 | tf_op jit(solution)/shard_map/ppermute | solution.py:873
  24.3 16.0 %collective-permute-start.10 = (bf16[48,1280]{1,0:T(8,128)(2,1)S(1)}, bf16[48,1280]{1,0:T(8,128)(2,1)S(1)}, u32[]{:S(2)}, u32[]{:S(2)}) collective-permute-start(bf16[48,1280]{1,0:T(8,128)(2,1)S(1)} %slice_bitcast_fusion.6), channel_id=1, source_target_pairs={{0,4},{2,6},{4,0},{6,2},{8,12},{10,14},{12,8},{14,10},{16,20},{18,... | collective-permute-start | bytes 368648 | tf_op jit(solution)/shard_map/ppermute | solution.py:873
  40.2 1.3 collective-permute-start.11
  41.6 8.8 %collective-permute-start.13 = (bf16[4,48,1280]{2,1,0:T(8,128)(2,1)S(1)}, bf16[4,48,1280]{2,1,0:T(8,128)(2,1)S(1)}, u32[]{:S(2)}, u32[]{:S(2)}) collective-permute-start(bf16[4,48,1280]{2,1,0:T(8,128)(2,1)S(1)} %pad_maximum_fusion.3), channel_id=1, source_target_pairs={{0,2},{2,0},{4,6},{6,4},{8,10},{10,8},{12,14},{14,12},{16,18},{18,... | collective-permute-start | bytes 1474568 | tf_op jit(solution)/shard_map/ppermute | solution.py:873
  44.9 18.1 %copy-start = (bf16[7,48,768]{2,1,0:T(8,128)(2,1)}, bf16[7,48,768]{2,1,0:T(8,128)(2,1)S(1)}, u32[]{:S(2)}) copy-start(bf16[7,48,768]{2,1,0:T(8,128)(2,1)S(1)} %collective-permute-done.9.refs_1_) | copy-start | bytes 1548292
  44.9 15.6 %collective-permute-start.14 = (bf16[7,48,768]{2,1,0:T(8,128)(2,1)S(1)}, bf16[7,48,768]{2,1,0:T(8,128)(2,1)S(1)}, u32[]{:S(2)}, u32[]{:S(2)}) collective-permute-start(bf16[7,48,768]{2,1,0:T(8,128)(2,1)S(1)} %collective-permute-done.8.refs_3_), channel_id=1, source_target_pairs={{0,8},{2,10},{4,12},{6,14},{8,0},{10,2},{12,4},{14,6},{16,24},{18,... | collective-permute-start | bytes 1548296 | tf_op jit(solution)/shard_map/ppermute | solution.py:873
  48.0 12.5 %collective-permute-start.15 = (bf16[7,48,768]{2,1,0:T(8,128)(2,1)S(1)}, bf16[7,48,768]{2,1,0:T(8,128)(2,1)S(1)}, u32[]{:S(2)}, u32[]{:S(2)}) collective-permute-start(bf16[7,48,768]{2,1,0:T(8,128)(2,1)S(1)} %collective-permute-done.8.refs_3_), channel_id=1, source_target_pairs={{0,4},{2,6},{4,0},{6,2},{8,12},{10,14},{12,8},{14,10},{16,20},{18,... | collective-permute-start | bytes 1548296 | tf_op jit(solution)/shard_map/ppermute | solution.py:873
  49.5 11.0 %collective-permute-start.16 = (bf16[3,2,48,768]{3,2,1,0:T(8,128)(2,1)S(1)}, bf16[3,2,48,768]{3,2,1,0:T(8,128)(2,1)S(1)}, u32[]{:S(2)}, u32[]{:S(2)}) collective-permute-start(bf16[3,2,48,768]{3,2,1,0:T(8,128)(2,1)S(1)} %pad_maximum_fusion.4), channel_id=1, source_target_pairs={{0,1},{1,0},{2,3},{3,2},{4,5},{5,4},{6,7},{7,6},{8,9},{9,8},{10,11... | collective-permute-start | bytes 1327112 | tf_op jit(solution)/shard_map/ppermute | solution.py:873
  50.3 24.6 %collective-permute-start.20 = (bf16[3,7,48,768]{3,2,1,0:T(8,128)(2,1)S(1)}, bf16[3,7,48,768]{3,2,1,0:T(8,128)(2,1)S(1)}, u32[]{:S(2)}, u32[]{:S(2)}) collective-permute-start(bf16[3,7,48,768]{3,2,1,0:T(8,128)(2,1)S(1)} %pad_maximum_fusion), channel_id=1, source_target_pairs={{0,2},{2,0},{4,6},{6,4},{8,10},{10,8},{12,14},{14,12},{16,18},{18,... | collective-permute-start | bytes 4644872 | tf_op jit(solution)/shard_map/ppermute | solution.py:873
  50.4 13.5 %collective-permute-start.19 = (bf16[9,48,768]{2,1,0:T(8,128)(2,1)}, bf16[9,48,768]{2,1,0:T(8,128)(2,1)}, u32[]{:S(2)}, u32[]{:S(2)}) collective-permute-start(bf16[9,48,768]{2,1,0:T(8,128)(2,1)} %get-tuple-element.196.refs_0_), channel_id=1, source_target_pairs={{0,2},{2,0},{4,6},{6,4},{8,10},{10,8},{12,14},{14,12},{16,18},{18,... | collective-permute-start | bytes 1990664 | tf_op jit(solution)/shard_map/ppermute | solution.py:873
  60.4 29.4 %copy-start.23 = (bf16[3,2,48,768]{3,2,1,0:T(8,128)(2,1)}, bf16[3,2,48,768]{3,2,1,0:T(8,128)(2,1)S(1)}, u32[]{:S(2)}) copy-start(bf16[3,2,48,768]{3,2,1,0:T(8,128)(2,1)S(1)} %collective-permute-done.16.refs_8_) | copy-start | bytes 1327108
  60.5 14.4 %collective-permute-start.17 = (bf16[7,48,768]{2,1,0:T(8,128)(2,1)S(1)}, bf16[7,48,768]{2,1,0:T(8,128)(2,1)S(1)}, u32[]{:S(2)}, u32[]{:S(2)}) collective-permute-start(bf16[7,48,768]{2,1,0:T(8,128)(2,1)S(1)} %collective-permute-done.14.refs_4_), channel_id=1, source_target_pairs={{0,4},{2,6},{4,0},{6,2},{8,12},{10,14},{12,8},{14,10},{16,20},{18,... | collective-permute-start | bytes 1548296 | tf_op jit(solution)/shard_map/ppermute | solution.py:873
  62.2 25.3 %collective-permute-start.24 = (bf16[2,7,48,768]{3,2,1,0:T(8,128)(2,1)S(1)}, bf16[2,7,48,768]{3,2,1,0:T(8,128)(2,1)S(1)}, u32[]{:S(2)}, u32[]{:S(2)}) collective-permute-start(bf16[2,7,48,768]{3,2,1,0:T(8,128)(2,1)S(1)} %pad_maximum_fusion.1), channel_id=1, source_target_pairs={{0,2},{2,0},{4,6},{6,4},{8,10},{10,8},{12,14},{14,12},{16,18},{18,... | collective-permute-start | bytes 3096584 | tf_op jit(solution)/shard_map/ppermute | solution.py:873
  62.4 12.5 %collective-permute-start.18 = (bf16[2,2,48,768]{3,2,1,0:T(8,128)(2,1)S(1)}, bf16[2,2,48,768]{3,2,1,0:T(8,128)(2,1)S(1)}, u32[]{:S(2)}, u32[]{:S(2)}) collective-permute-start(bf16[2,2,48,768]{3,2,1,0:T(8,128)(2,1)S(1)} %pad_maximum_fusion.7), channel_id=1, source_target_pairs={{0,1},{1,0},{2,3},{3,2},{4,5},{5,4},{6,7},{7,6},{8,9},{9,8},{10,11... | collective-permute-start | bytes 884744 | tf_op jit(solution)/shard_map/ppermute | solution.py:873
  63.9 23.6 %collective-permute-start.21 = (bf16[9,48,768]{2,1,0:T(8,128)(2,1)}, bf16[9,48,768]{2,1,0:T(8,128)(2,1)}, u32[]{:S(2)}, u32[]{:S(2)}) collective-permute-start(bf16[9,48,768]{2,1,0:T(8,128)(2,1)} %pad_maximum_fusion.2), channel_id=1, source_target_pairs={{0,8},{2,10},{4,12},{6,14},{8,0},{10,2},{12,4},{14,6},{16,24},{18,... | collective-permute-start | bytes 1990664 | tf_op jit(solution)/shard_map/ppermute | solution.py:873
  74.9 14.4 %collective-permute-start.22 = (bf16[384,512]{1,0:T(8,128)(2,1)}, bf16[384,512]{1,0:T(8,128)(2,1)S(1)}, u32[]{:S(2)}, u32[]{:S(2)}) collective-permute-start(bf16[384,512]{1,0:T(8,128)(2,1)} %get-tuple-element.201.out), channel_id=1, source_target_pairs={{0,1},{1,0},{2,3},{3,2},{4,5},{5,4},{6,7},{7,6},{8,9},{9,8},{10,11... | collective-permute-start | bytes 1179656 | tf_op jit(solution)/shard_map/ppermute | solution.py:873
  76.5 12.8 %collective-permute-start.23 = (bf16[2,48,768]{2,1,0:T(8,128)(2,1)S(1)}, bf16[2,48,768]{2,1,0:T(8,128)(2,1)S(1)}, u32[]{:S(2)}, u32[]{:S(2)}) collective-permute-start(bf16[2,48,768]{2,1,0:T(8,128)(2,1)S(1)} %slice.34), channel_id=1, source_target_pairs={{0,1},{1,0},{2,3},{3,2},{4,5},{5,4},{6,7},{7,6},{8,9},{9,8},{10,11... | collective-permute-start | bytes 442376 | tf_op jit(solution)/shard_map/ppermute | solution.py:873
  89.3 4.2 %collective-permute-start.25 = (bf16[9,48,768]{2,1,0:T(8,128)(2,1)}, bf16[9,48,768]{2,1,0:T(8,128)(2,1)S(1)}, u32[]{:S(2)}, u32[]{:S(2)}) collective-permute-start(bf16[9,48,768]{2,1,0:T(8,128)(2,1)} %collective-permute-done.21.refs_6_), channel_id=1, source_target_pairs={{0,2},{2,0},{4,6},{6,4},{8,10},{10,8},{12,14},{14,12},{16,18},{18,... | collective-permute-start | bytes 1990664 | tf_op jit(solution)/shard_map/ppermute | solution.py:873
  89.4 4.1 %collective-permute-start.26 = (bf16[7,48,768]{2,1,0:T(8,128)(2,1)S(1)}, bf16[7,48,768]{2,1,0:T(8,128)(2,1)S(1)}, u32[]{:S(2)}, u32[]{:S(2)}) collective-permute-start(bf16[7,48,768]{2,1,0:T(8,128)(2,1)S(1)} %collective-permute-done.17.refs_7_), channel_id=1, source_target_pairs={{0,2},{2,0},{4,6},{6,4},{8,10},{10,8},{12,14},{14,12},{16,18},{18,... | collective-permute-start | bytes 1548296 | tf_op jit(solution)/shard_map/ppermute | solution.py:873
  89.9 3.6 %collective-permute-start.27 = (bf16[3,2,48,768]{3,2,1,0:T(8,128)(2,1)S(1)}, bf16[3,2,48,768]{3,2,1,0:T(8,128)(2,1)S(1)}, u32[]{:S(2)}, u32[]{:S(2)}) collective-permute-start(bf16[3,2,48,768]{3,2,1,0:T(8,128)(2,1)S(1)} %collective-permute-done.16.refs_8_), channel_id=1, source_target_pairs={{0,2},{2,0},{4,6},{6,4},{8,10},{10,8},{12,14},{14,12},{16,18},{18,... | collective-permute-start | bytes 1327112 | tf_op jit(solution)/shard_map/ppermute | solution.py:873
  90.0 3.5 %collective-permute-start.28 = (bf16[2,2,48,768]{3,2,1,0:T(8,128)(2,1)S(1)}, bf16[2,2,48,768]{3,2,1,0:T(8,128)(2,1)S(1)}, u32[]{:S(2)}, u32[]{:S(2)}) collective-permute-start(bf16[2,2,48,768]{3,2,1,0:T(8,128)(2,1)S(1)} %collective-permute-done.18.refs_9_), channel_id=1, source_target_pairs={{0,2},{2,0},{4,6},{6,4},{8,10},{10,8},{12,14},{14,12},{16,18},{18,... | collective-permute-start | bytes 884744 | tf_op jit(solution)/shard_map/ppermute | solution.py:873
  90.4 3.1 %collective-permute-start.29 = (bf16[2,48,768]{2,1,0:T(8,128)(2,1)S(1)}, bf16[2,48,768]{2,1,0:T(8,128)(2,1)S(1)}, u32[]{:S(2)}, u32[]{:S(2)}) collective-permute-start(bf16[2,48,768]{2,1,0:T(8,128)(2,1)S(1)} %collective-permute-done.23.refs_10_), channel_id=1, source_target_pairs={{0,2},{2,0},{4,6},{6,4},{8,10},{10,8},{12,14},{14,12},{16,18},{18,... | collective-permute-start | bytes 442376 | tf_op jit(solution)/shard_map/ppermute | solution.py:873
  117.9 13.7 %collective-permute-start.32 = (bf16[5,512,768]{2,1,0:T(8,128)(2,1)}, bf16[5,512,768]{2,1,0:T(8,128)(2,1)}, u32[]{:S(2)}, u32[]{:S(2)}) collective-permute-start(bf16[5,512,768]{2,1,0:T(8,128)(2,1)} %get-tuple-element.227.pre), channel_id=1, source_target_pairs={{0,2},{2,0},{4,6},{6,4},{8,10},{10,8},{12,14},{14,12},{16,18},{18,... | collective-permute-start | bytes 11796488 | tf_op jit(solution)/shard_map/ppermute | solution.py:873
  118.1 23.2 %collective-permute-start.33 = (bf16[4,512,384]{2,1,0:T(8,128)(2,1)}, bf16[4,512,384]{2,1,0:T(8,128)(2,1)}, u32[]{:S(2)}, u32[]{:S(2)}) collective-permute-start(bf16[4,512,384]{2,1,0:T(8,128)(2,1)} %get-tuple-element.230), channel_id=1, source_target_pairs={{0,2},{2,0},{4,6},{6,4},{8,10},{10,8},{12,14},{14,12},{16,18},{18,... | collective-permute-start | bytes 4718600 | tf_op jit(solution)/shard_map/ppermute | solution.py:873
  118.5 13.1 %collective-permute-start.31 = (bf16[2,8,48,512]{3,2,1,0:T(8,128)(2,1)}, bf16[2,8,48,512]{3,2,1,0:T(8,128)(2,1)S(1)}, u32[]{:S(2)}, u32[]{:S(2)}) collective-permute-start(bf16[2,8,48,512]{3,2,1,0:T(8,128)(2,1)} %get-tuple-element.226), channel_id=1, source_target_pairs={{0,2},{2,0},{4,6},{6,4},{8,10},{10,8},{12,14},{14,12},{16,18},{18,... | collective-permute-start | bytes 2359304 | tf_op jit(solution)/shard_map/ppermute | solution.py:873
  118.6 13.0 %collective-permute-start.30 = (bf16[384,512]{1,0:T(8,128)(2,1)}, bf16[384,512]{1,0:T(8,128)(2,1)}, u32[]{:S(2)}, u32[]{:S(2)}) collective-permute-start(bf16[384,512]{1,0:T(8,128)(2,1)} %get-tuple-element.223), channel_id=1, source_target_pairs={{0,1},{1,0},{2,3},{3,2},{4,5},{5,4},{6,7},{7,6},{8,9},{9,8},{10,11... | collective-permute-start | bytes 1179656 | tf_op jit(solution)/shard_map/ppermute | solution.py:873
  140.8 22.1 %collective-permute-start.34 = (bf16[4,3,48,768]{3,2,1,0:T(8,128)(2,1)}, bf16[4,3,48,768]{3,2,1,0:T(8,128)(2,1)S(1)}, u32[]{:S(2)}, u32[]{:S(2)}) collective-permute-start(bf16[4,3,48,768]{3,2,1,0:T(8,128)(2,1)} %get-tuple-element.228), channel_id=1, source_target_pairs={{0,4},{2,6},{4,0},{6,2},{8,12},{10,14},{12,8},{14,10},{16,20},{18,... | collective-permute-start | bytes 2654216 | tf_op jit(solution)/shard_map/ppermute | solution.py:873
  147.6 27.9 %collective-permute-start.36 = (bf16[8,2,48,768]{3,2,1,0:T(8,128)(2,1)}, bf16[8,2,48,768]{3,2,1,0:T(8,128)(2,1)S(1)}, u32[]{:S(2)}, u32[]{:S(2)}) collective-permute-start(bf16[8,2,48,768]{3,2,1,0:T(8,128)(2,1)} %get-tuple-element.232), channel_id=1, source_target_pairs={{0,1},{1,0},{2,3},{3,2},{4,5},{5,4},{6,7},{7,6},{8,9},{9,8},{10,11... | collective-permute-start | bytes 3538952 | tf_op jit(solution)/shard_map/ppermute | solution.py:873
  148.2 17.2 %collective-permute-start.35 = (bf16[2,2,2,48,768]{4,3,2,1,0:T(8,128)(2,1)}, bf16[2,2,2,48,768]{4,3,2,1,0:T(8,128)(2,1)S(1)}, u32[]{:S(2)}, u32[]{:S(2)}) collective-permute-start(bf16[2,2,2,48,768]{4,3,2,1,0:T(8,128)(2,1)} %get-tuple-element.246), channel_id=1, source_target_pairs={{0,8},{2,10},{4,12},{6,14},{8,0},{10,2},{12,4},{14,6},{16,24},{18,... | collective-permute-start | bytes 1769480 | tf_op jit(solution)/shard_map/ppermute | solution.py:873
  149.9 15.5 %copy-start.27 = (bf16[2,2,2,48,768]{4,3,2,1,0:T(8,128)(2,1)S(1)}, bf16[2,2,2,48,768]{4,3,2,1,0:T(8,128)(2,1)}, u32[]{:S(2)}) copy-start(bf16[2,2,2,48,768]{4,3,2,1,0:T(8,128)(2,1)} %get-tuple-element.286) | copy-start | bytes 1769476
  164.0 11.6 %collective-permute-start.37 = (bf16[2,3,48,768]{3,2,1,0:T(8,128)(2,1)}, bf16[2,3,48,768]{3,2,1,0:T(8,128)(2,1)}, u32[]{:S(2)}, u32[]{:S(2)}) collective-permute-start(bf16[2,3,48,768]{3,2,1,0:T(8,128)(2,1)} %fusion.4), channel_id=1, source_target_pairs={{0,8},{2,10},{4,12},{6,14},{8,0},{10,2},{12,4},{14,6},{16,24},{18,... | collective-permute-start | bytes 1327112 | tf_op jit(solution)/shard_map/ppermute | solution.py:873
  165.4 7.9 %collective-permute-start.38 = (bf16[2,2,48,768]{3,2,1,0:T(8,128)(2,1)S(1)}, bf16[2,2,48,768]{3,2,1,0:T(8,128)(2,1)S(1)}, u32[]{:S(2)}, u32[]{:S(2)}) collective-permute-start(bf16[2,2,48,768]{3,2,1,0:T(8,128)(2,1)S(1)} %fusion.8), channel_id=1, source_target_pairs={{0,4},{2,6},{4,0},{6,2},{8,12},{10,14},{12,8},{14,10},{16,20},{18,... | collective-permute-start | bytes 884744 | tf_op jit(solution)/shard_map/ppermute | solution.py:873
  172.9 3.9 %collective-permute-start.39 = (bf16[8,48,1280]{2,1,0:T(8,128)(2,1)}, bf16[8,48,1280]{2,1,0:T(8,128)(2,1)}, u32[]{:S(2)}, u32[]{:S(2)}) collective-permute-start(bf16[8,48,1280]{2,1,0:T(8,128)(2,1)} %get-tuple-element.255), channel_id=1, source_target_pairs={{0,2},{2,0},{4,6},{6,4},{8,10},{10,8},{12,14},{14,12},{16,18},{18,... | collective-permute-start | bytes 2949128 | tf_op jit(solution)/shard_map/ppermute | solution.py:873
  179.8 15.5 %collective-permute-start.40 = (bf16[2,2,2,48,768]{4,3,2,1,0:T(8,128)(2,1)}, bf16[2,2,2,48,768]{4,3,2,1,0:T(8,128)(2,1)}, u32[]{:S(2)}, u32[]{:S(2)}) collective-permute-start(bf16[2,2,2,48,768]{4,3,2,1,0:T(8,128)(2,1)} %fusion), channel_id=1, source_target_pairs={{0,4},{2,6},{4,0},{6,2},{8,12},{10,14},{12,8},{14,10},{16,20},{18,... | collective-permute-start | bytes 1769480 | tf_op jit(solution)/shard_map/ppermute | solution.py:873
  181.4 22.4 %collective-permute-start.41 = (bf16[2,2,48,1280]{3,2,1,0:T(8,128)(2,1)}, bf16[2,2,48,1280]{3,2,1,0:T(8,128)(2,1)}, u32[]{:S(2)}, u32[]{:S(2)}) collective-permute-start(bf16[2,2,48,1280]{3,2,1,0:T(8,128)(2,1)} %fusion.2), channel_id=1, source_target_pairs={{0,8},{2,10},{4,12},{6,14},{8,0},{10,2},{12,4},{14,6},{16,24},{18,... | collective-permute-start | bytes 1474568 | tf_op jit(solution)/shard_map/ppermute | solution.py:873
  184.2 21.3 %collective-permute-start.42 = (bf16[3,48,768]{2,1,0:T(8,128)(2,1)S(1)}, bf16[3,48,768]{2,1,0:T(8,128)(2,1)S(1)}, u32[]{:S(2)}, u32[]{:S(2)}) collective-permute-start(bf16[3,48,768]{2,1,0:T(8,128)(2,1)S(1)} %fusion.7), channel_id=1, source_target_pairs={{0,16},{2,18},{4,20},{6,22},{8,24},{10,26},{12,28},{14,30},{16,0},... | collective-permute-start | bytes 663560 | tf_op jit(solution)/shard_map/ppermute | solution.py:873
  186.2 20.5 %collective-permute-start.43 = (bf16[2,48,768]{2,1,0:T(8,128)(2,1)S(1)}, bf16[2,48,768]{2,1,0:T(8,128)(2,1)S(1)}, u32[]{:S(2)}, u32[]{:S(2)}) collective-permute-start(bf16[2,48,768]{2,1,0:T(8,128)(2,1)S(1)} %fusion.14), channel_id=1, source_target_pairs={{0,16},{2,18},{4,20},{6,22},{8,24},{10,26},{12,28},{14,30},{16,0},... | collective-permute-start | bytes 442376 | tf_op jit(solution)/shard_map/ppermute | solution.py:873
  194.7 29.8 %collective-permute-start.48 = (bf16[512,768]{1,0:T(8,128)(2,1)}, bf16[512,768]{1,0:T(8,128)(2,1)S(1)}, u32[]{:S(2)}, u32[]{:S(2)}) collective-permute-start(bf16[512,768]{1,0:T(8,128)(2,1)} %get-tuple-element.314), channel_id=1, source_target_pairs={{0,1},{1,0},{2,3},{3,2},{4,5},{5,4},{6,7},{7,6},{8,9},{9,8},{10,11... | collective-permute-start | bytes 2359304 | tf_op jit(solution)/shard_map/ppermute | solution.py:873
  196.4 13.0 %collective-permute-start.44 = (bf16[2,2,48,768]{3,2,1,0:T(8,128)(2,1)S(1)}, bf16[2,2,48,768]{3,2,1,0:T(8,128)(2,1)S(1)}, u32[]{:S(2)}, u32[]{:S(2)}) collective-permute-start(bf16[2,2,48,768]{3,2,1,0:T(8,128)(2,1)S(1)} %fusion.1), channel_id=1, source_target_pairs={{0,8},{2,10},{4,12},{6,14},{8,0},{10,2},{12,4},{14,6},{16,24},{18,... | collective-permute-start | bytes 884744 | tf_op jit(solution)/shard_map/ppermute | solution.py:873
  204.9 6.3 %collective-permute-start.45 = (bf16[2,48,1280]{2,1,0:T(8,128)(2,1)S(1)}, bf16[2,48,1280]{2,1,0:T(8,128)(2,1)S(1)}, u32[]{:S(2)}, u32[]{:S(2)}) collective-permute-start(bf16[2,48,1280]{2,1,0:T(8,128)(2,1)S(1)} %fusion.3), channel_id=1, source_target_pairs={{0,4},{2,6},{4,0},{6,2},{8,12},{10,14},{12,8},{14,10},{16,20},{18,... | collective-permute-start | bytes 737288 | tf_op jit(solution)/shard_map/ppermute | solution.py:873
  207.9 16.6 %copy-start.12 = (bf16[5,48,768]{2,1,0:T(8,128)(2,1)}, bf16[5,48,768]{2,1,0:T(8,128)(2,1)S(1)}, u32[]{:S(2)}) copy-start(bf16[5,48,768]{2,1,0:T(8,128)(2,1)S(1)} %pad_maximum_fusion.6.b_near) | copy-start | bytes 1105924
  207.9 16.6 %collective-permute-start.49 = (bf16[5,48,768]{2,1,0:T(8,128)(2,1)S(1)}, bf16[5,48,768]{2,1,0:T(8,128)(2,1)S(1)}, u32[]{:S(2)}, u32[]{:S(2)}) collective-permute-start(bf16[5,48,768]{2,1,0:T(8,128)(2,1)S(1)} %pad_maximum_fusion.6.b_near), channel_id=1, source_target_pairs={{0,1},{1,0},{2,3},{3,2},{4,5},{5,4},{6,7},{7,6},{8,9},{9,8},{10,11... | collective-permute-start | bytes 1105928 | tf_op jit(solution)/shard_map/ppermute | solution.py:873
  210.4 9.8 %collective-permute-start.46 = (bf16[2,48,768]{2,1,0:T(8,128)(2,1)S(1)}, bf16[2,48,768]{2,1,0:T(8,128)(2,1)S(1)}, u32[]{:S(2)}, u32[]{:S(2)}) collective-permute-start(bf16[2,48,768]{2,1,0:T(8,128)(2,1)S(1)} %fusion.11), channel_id=1, source_target_pairs={{0,16},{2,18},{4,20},{6,22},{8,24},{10,26},{12,28},{14,30},{16,0},... | collective-permute-start | bytes 442376 | tf_op jit(solution)/shard_map/ppermute | solution.py:873
  212.2 9.7 %collective-permute-start.47 = (bf16[48,1280]{1,0:T(8,128)(2,1)S(1)}, bf16[48,1280]{1,0:T(8,128)(2,1)S(1)}, u32[]{:S(2)}, u32[]{:S(2)}) collective-permute-start(bf16[48,1280]{1,0:T(8,128)(2,1)S(1)} %fusion.17), channel_id=1, source_target_pairs={{0,16},{2,18},{4,20},{6,22},{8,24},{10,26},{12,28},{14,30},{16,0},... | collective-permute-start | bytes 368648 | tf_op jit(solution)/shard_map/ppermute | solution.py:873
  221.3 8.5 %collective-permute-start.50 = (bf16[2,48,768]{2,1,0:T(8,128)(2,1)S(1)}, bf16[2,48,768]{2,1,0:T(8,128)(2,1)S(1)}, u32[]{:S(2)}, u32[]{:S(2)}) collective-permute-start(bf16[2,48,768]{2,1,0:T(8,128)(2,1)S(1)} %fusion.10.a_near), channel_id=1, source_target_pairs={{0,1},{1,0},{2,3},{3,2},{4,5},{5,4},{6,7},{7,6},{8,9},{9,8},{10,11... | collective-permute-start | bytes 442376 | tf_op jit(solution)/shard_map/ppermute | solution.py:873
  223.0 6.7 %collective-permute-start.51 = (bf16[48,1280]{1,0:T(8,128)(2,1)S(1)}, bf16[48,1280]{1,0:T(8,128)(2,1)S(1)}, u32[]{:S(2)}, u32[]{:S(2)}) collective-permute-start(bf16[48,1280]{1,0:T(8,128)(2,1)S(1)} %fusion.16.g_near), channel_id=1, source_target_pairs={{0,1},{1,0},{2,3},{3,2},{4,5},{5,4},{6,7},{7,6},{8,9},{9,8},{10,11... | collective-permute-start | bytes 368648 | tf_op jit(solution)/shard_map/ppermute | solution.py:873
  (33 other events, 171.3 us)

commit v6 on v5

--- a/solution.py
+++ b/solution.py
@@ -826,35 +826,34 @@
     )(place, a_near, a_far, g_near, g_far, qw, kw, vw, gain.reshape(1, 48))
 
 
-def finish_wide_kernel(
-    place, x, small, near, far, middle_grad, b_near, b_far, up, gain, result, expand, output, gain_grad
-):
-    input_grad_kernel(place, x, small, near, far, middle_grad, result)
-    summed = b_near[...].astype(f32) + b_far[...].astype(f32)
-    joint = jnp.zeros((48, 768), f32)
-    for at in range(4):
-        cols = slice(at * 768, at * 768 + 768)
-        expand[:, cols] = summed[at]
-        joint = joint + summed[at] * up[:, cols].astype(f32)
-    output[...] = summed[4]
+def finish_wide_kernel(place, b_near, b_far, up, gain, expand, output, gain_grad):
+    near, far = b_near[...].astype(f32), b_far[...].astype(f32)
+    sides = (jnp.where(place[3] == 0, near, far), jnp.where(place[3] == 0, far, near))
+    joint = jnp.zeros((48, 384), f32)
+    for half, side in enumerate(sides):
+        for at in range(4):
+            cols = slice(at * 768 + half * 384, at * 768 + half * 384 + 384)
+            expand[:, cols] = side[at]
+            joint = joint + side[at] * up[:, cols].astype(f32)
+        output[:, half * 384 : half * 384 + 384] = side[4]
     column = jnp.broadcast_to(jnp.sum(joint, axis=1, keepdims=True), (48, 128))
     turned = jnp.concatenate([column, jnp.zeros((80, 128), f32)], axis=0).T
     gain_grad[...] = turned[0:1, 0:48] / gain[...].astype(f32)
 
 
-def finish_wide(place, x, small, near, far, middle_grad, b_near, b_far, up, gain):
+def finish_wide(place, b_near, b_far, up, gain):
     return pl.pallas_call(
         finish_wide_kernel,
         out_shape=(
-            jax.ShapeDtypeStruct((512, 768), bf16), jax.ShapeDtypeStruct((48, 3072), f32),
+            jax.ShapeDtypeStruct((48, 3072), f32),
             jax.ShapeDtypeStruct((48, 768), f32), jax.ShapeDtypeStruct((1, 48), f32),
         ),
-        in_specs=[SCALARS] + [FULL] * 9,
-        out_specs=(FULL,) * 4,
+        in_specs=[SCALARS] + [FULL] * 4,
+        out_specs=(FULL,) * 3,
         compiler_params=params(),
         cost_estimate=cost(1000, 2_000_000),
         name="finish_wide",
-    )(place, x, small, near, far, middle_grad, b_near, b_far, up, gain.reshape(1, 48))
+    )(place, b_near, b_far, up, gain.reshape(1, 48))
 
 
 def input_grad_kernel(place, x, small, near, far, middle_grad, result):
@@ -868,6 +867,18 @@
         result[rows] = (middle_grad[rows] + inward).astype(bf16)
 
 
+def input_grad(place, x, small, near, far, middle_grad):
+    return pl.pallas_call(
+        input_grad_kernel,
+        out_shape=jax.ShapeDtypeStruct((512, 768), bf16),
+        in_specs=[SCALARS] + [FULL] * 5,
+        out_specs=FULL,
+        compiler_params=params(),
+        cost_estimate=cost(512 * 768 * 20, 6_000_000),
+        name="input_grad",
+    )(place, x, small, near, far, middle_grad)
+
+
 def swap(array, axis, bit):
     count = lax.axis_size(axis)
     return lax.ppermute(array, axis, [(i, i ^ bit) for i in range(count)])
@@ -916,6 +927,14 @@
         made = term if made is None else made + term
     made = lax.optimization_barrier(made.astype(bf16))
     line.wait(made)
+    return made
+
+
+def sum_parts(parts, own, now=None):
+    made = None
+    for part in parts:
+        term = gather_part(part[0], part, own, now)
+        made = term if made is None else made + term
     return made
 
 
@@ -1032,25 +1051,29 @@
     line.place = hand_on(line.place)
     g_parts = keep(g_parts, "low", by_z(total(line, g_parts, own, "low")))
     a_parts = keep(a_parts, "y", by_y(total(line, a_parts, own, "y")))
-    b_parts = keep(b_parts, "high", by_zz(total(line, b_parts, own, "high")))
-    c_parts = keep(c_parts, "high", by_zz(total(line, c_parts, own, "high")))
+    arrays = after([part[0] for part in b_parts + c_parts], line.place)
+    held = [(array, *part[1:]) for array, part in zip(arrays, b_parts + c_parts)]
+    joint = jnp.concatenate([sum_parts(held[:3], own), sum_parts(held[3:], own)], axis=1).astype(bf16)
+    sent = lax.dynamic_slice_in_dim(joint, (1 - x) * 384, 384, axis=3)
+    kept = lax.dynamic_slice_in_dim(joint, x * 384, 384, axis=3)
+    sent, kept = lax.optimization_barrier((sent, kept))
+    line.wait(sent, kept)
+    bc_parts = [(kept, ("high", "n"), ()), (by_x(sent), ("high", "n"), ())]
     part_near, part_far = line.run(project_back, narrow, whole)
     part_got = by_x(part_far)
     a_parts = keep(a_parts, "low", by_z(total(line, a_parts, own, "low")))
+    bc_parts = keep(bc_parts, "high", by_zz(total(line, bc_parts, own, "high")))
     g_parts = keep(g_parts, "y", by_y(total(line, g_parts, own, "y")))
-    b_low = jnp.concatenate([total(line, b_parts, own), total(line, c_parts, own)], axis=0)
-    b_low = lax.optimization_barrier(b_low)
+    a_parts = keep(a_parts, "high", by_zz(total(line, a_parts, own, "high")))
+    b_low = total(line, bc_parts, own)
     b_other = by_x(b_low)
-    line.wait(b_low)
-    a_parts = keep(a_parts, "high", by_zz(total(line, a_parts, own, "high")))
     g_parts = keep(g_parts, "high", by_zz(total(line, g_parts, own, "high")))
+    result = line.run(input_grad, tokens, small, part_near, part_got, middle_grad)
     a_low = total(line, a_parts, own)
     a_other = by_x(a_low)
     g_low = total(line, g_parts, own)
     g_other = by_x(g_low)
-    result, expand_sum, output_sum, gain_two = line.run(
-        finish_wide, tokens, small, part_near, part_got, middle_grad, b_low, b_other, expand_weight, feedforward_gain
-    )
+    expand_sum, output_sum, gain_two = line.run(finish_wide, b_low, b_other, expand_weight, feedforward_gain)
     contract_sum, *grads, gain_one, bias_grad = line.run(
         finish, a_low, a_other, g_low, g_other, query_weight, key_weight, value_weight, attention_gain
     )

time: 235 us -> 232 us (0.987)
  waiting for transfers between devices: 30.7 us -> 25.7 us
    ppermute x52, waiting for transfers between devices: 30.7 us -> 25.7 us  [swap(): return lax.ppermute(array, axis, [(i, i ^ bit) for i in range(count)])]
    convert_element_type x14 -> x12, other arithmetic: 15.1 us -> 10.5 us  [total(): made = lax.optimization_barrier(made.astype(bf16))]
    pallas_call x1 -> x2, Pallas kernels: 4.2 us -> 5.89 us  [the longest x1 3.79 us: input_grad(): pl.pallas_call(input_grad_kernel, out_shape=jax.ShapeDtypeStruct((512, 76...]
    unnamed x90 -> x98, local copies, waits for them, and re-layouts: 4.83 us -> 5.42 us
  transfers between devices with their start and end apart: 52 -> 52, of which waited for: 15 -> 15; matrix products, arithmetic and copies ran while one was open for 6% -> 6% of each run, Pallas kernels for 39% -> 40%
where the time goes in v6:
time: 232 us; the launch traced here: 231 us
  Pallas kernels  118 us (51%)
  starting transfers between devices  61.4 us (26%)
  waiting for transfers between devices  25.7 us (11%)
  other arithmetic  15.6 us (7%)
  local copies, waits for them, and re-layouts  6.22 us (3%)
  between operations  3.39 us (1%)
    ppermute x52, starting transfers between devices, swap(): return lax.ppermute(array, axis, [(i, i ^ bit) for i in range(count)])  61.4 us
    ppermute x52, waiting for transfers between devices, swap(): return lax.ppermute(array, axis, [(i, i ^ bit) for i in range(count)])  25.7 us
    pallas_call x2, Pallas kernels, attend_back(): pl.pallas_call(functools.partial(attend_back_kernel, bool(carry), mine),...  24.6 us
    pallas_call x1, Pallas kernels, forward(): pl.pallas_call(forward_kernel, out_shape=(hidden, hidden, jax.ShapeDtypeS...  23.1 us
    pallas_call x2, Pallas kernels, attend(): pl.pallas_call(functools.partial(attend_kernel, mine), out_shape=(jax.Sha...  21 us
    convert_element_type x12, other arithmetic, total(): made = lax.optimization_barrier(made.astype(bf16))  10.5 us
    pallas_call x1, Pallas kernels, expand_weight_grad(): pl.pallas_call(expand_grad_kernel, out_shape=(first, first, second, secon...  8.34 us
    pallas_call x1, Pallas kernels, project(): pl.pallas_call(project_kernel, out_shape=(jax.ShapeDtypeStruct((1152, 102...  7.72 us
  transfers between devices with their start and end apart: 52, of which 15 were waited for; matrix products, arithmetic and copies ran while one was open for 6% of the time, Pallas kernels for 40%

profile of v6, /device:TPU:0, one launch (start us, length us, event | category | flops | bytes accessed | tf_op | source)
XLA Modules:
  0.0 230.8 jit_solution(14473936514597560024)
XLA Ops:
  1.2 2.6 %collective-permute-start.6 = (bf16[512,768]{1,0:T(8,128)(2,1)}, bf16[512,768]{1,0:T(8,128)(2,1)S(1)}, u32[]{:S(2)}, u32[]{:S(2)}) collective-permute-start(bf16[512,768]{1,0:T(8,128)(2,1)} %bitcast.106), channel_id=1, source_target_pairs={{0,1},{1,0},{2,3},{3,2},{4,5},{5,4},{6,7},{7,6},{8,9},{9,8},{10,11... | collective-permute-start | bytes 2359304 | tf_op jit(solution)/shard_map/ppermute | solution.py:884
  4.3 1.8 narrow_shard.1.refs_0_
  6.1 2.6 %collective-permute-start = (bf16[48,1280]{1,0:T(8,128)(2,1)}, bf16[48,1280]{1,0:T(8,128)(2,1)S(1)}, u32[]{:S(2)}, u32[]{:S(2)}) collective-permute-start(bf16[48,1280]{1,0:T(8,128)(2,1)} %narrow_shard.1.refs_0_), channel_id=1, source_target_pairs={{0,16},{2,18},{4,20},{6,22},{8,24},{10,26},{12,28},{14,30},{16,0},... | collective-permute-start | bytes 368648 | tf_op jit(solution)/shard_map/ppermute | solution.py:884
  8.7 1.6 collective-permute-start.1
  10.3 1.5 collective-permute-start.2
  11.8 2.9 %wide_shard.1 = (bf16[7,48,768]{2,1,0:T(8,128)(2,1)}, bf16[9,48,768]{2,1,0:T(8,128)(2,1)}) custom-call(s32[4]{0:T(128)} %pad_add_fusion.place, bf16[48,3072]{1,0:T(8,128)(2,1)} %up.1, bf16[48,768]{1,0:T(8,128)(2,1)} %output.1, bf16[192,768]{1,0:T(8,128)(2,1)} %contract.1), custom_call_target="tpu_custom_call" | custom-call | flops 1000 | bytes 1000 | tf_op jit(solution)/shard_map/wide_shard/pallas_call | solution.py:101
  15.6 1.5 collective-permute-start.4
  17.1 1.5 collective-permute-start.5
  21.8 1.8 collective-permute-start.8
  24.3 11.9 %collective-permute-start.10 = (bf16[48,1280]{1,0:T(8,128)(2,1)S(1)}, bf16[48,1280]{1,0:T(8,128)(2,1)S(1)}, u32[]{:S(2)}, u32[]{:S(2)}) collective-permute-start(bf16[48,1280]{1,0:T(8,128)(2,1)S(1)} %slice_bitcast_fusion.6), channel_id=1, source_target_pairs={{0,4},{2,6},{4,0},{6,2},{8,12},{10,14},{12,8},{14,10},{16,20},{18,... | collective-permute-start | bytes 368648 | tf_op jit(solution)/shard_map/ppermute | solution.py:884
  36.2 4.0 %collective-permute-done.10.refs_6_ = bf16[48,1280]{1,0:T(8,128)(2,1)S(1)} collective-permute-done((bf16[48,1280]{1,0:T(8,128)(2,1)S(1)}, bf16[48,1280]{1,0:T(8,128)(2,1)S(1)}, u32[]{:S(2)}, u32[]{:S(2)}) %collective-permute-start.10) | collective-permute-done | bytes 122912 | tf_op jit(solution)/shard_map/ppermute | solution.py:884
  40.2 1.2 collective-permute-done.11.refs_9_
  41.6 3.3 %collective-permute-done.7.refs_2_ = bf16[7,48,768]{2,1,0:T(8,128)(2,1)S(1)} collective-permute-done((bf16[7,48,768]{2,1,0:T(8,128)(2,1)}, bf16[7,48,768]{2,1,0:T(8,128)(2,1)S(1)}, u32[]{:S(2)}, u32[]{:S(2)}) %collective-permute-start.7) | collective-permute-done | bytes 516128 | tf_op jit(solution)/shard_map/ppermute | solution.py:884
  45.0 3.1 %collective-permute-start.14 = (bf16[7,48,768]{2,1,0:T(8,128)(2,1)S(1)}, bf16[7,48,768]{2,1,0:T(8,128)(2,1)S(1)}, u32[]{:S(2)}, u32[]{:S(2)}) collective-permute-start(bf16[7,48,768]{2,1,0:T(8,128)(2,1)S(1)} %collective-permute-done.8.refs_3_), channel_id=1, source_target_pairs={{0,8},{2,10},{4,12},{6,14},{8,0},{10,2},{12,4},{14,6},{16,24},{18,... | collective-permute-start | bytes 1548296 | tf_op jit(solution)/shard_map/ppermute | solution.py:884
  48.1 1.3 collective-permute-start.15
  51.2 7.7 %project.1 = (bf16[1152,1024]{1,0:T(8,128)(2,1)}, bf16[8,48,1024]{2,1,0:T(8,128)(2,1)}, bf16[8,48,1024]{2,1,0:T(8,128)(2,1)}, f32[8,768]{1,0:T(8,128)}, f32[8,128]{1,0:T(8,128)}, /*index=5*/f32[6,384,128]{2,1,0:T(8,128)}) custom-call(s32[7]{0:T(128)} %concatenate.11.place, bf16[512,768]{1,0:T(8,128)(2,1)} %bitcast.107, bf16[512,768]{1,0:T(8,128)(2,1)} %copy-done.27, ...), custom_call_target="tpu_custom_call" | custom-call | flops 1000 | bytes 1000 | tf_op jit(solution)/shard_map/project/pallas_call | solution.py:193
  58.9 1.4 collective-permute-done.16.refs_8_
  60.4 1.6 collective-permute-start.17
  62.9 0.9 pad_maximum_fusion.2
  64.2 10.6 %attend_theirs.1 = (bf16[384,512]{1,0:T(8,128)(2,1)}, bf16[6,1024,512]{2,1,0:T(8,128)(2,1)}, f32[6,1,512]{2,1,0:T(1,128)}) custom-call(s32[7]{0:T(128)} %concatenate.11.place, f32[8,128]{1,0:T(8,128)} %get-tuple-element.189.table, f32[6,384,128]{2,1,0:T(8,128)} %get-tuple-element.190.tile, bf16[1152,1024]{1,0:T(8,128)(2,1)} %get-tuple-element.182.q.k.v, ...), custom_call_target="tpu_custom_call" | custom-call | flops 1000 | bytes 1000 | tf_op jit(solution)/shard_map/attend_theirs/pallas_call | solution.py:288
  74.8 1.6 collective-permute-start.22
  77.0 10.4 %attend_mine.1 = (bf16[384,512]{1,0:T(8,128)(2,1)}, bf16[6,1024,512]{2,1,0:T(8,128)(2,1)}, f32[6,1,512]{2,1,0:T(1,128)}) custom-call(s32[7]{0:T(128)} %concatenate.11.place, f32[8,128]{1,0:T(8,128)} %get-tuple-element.189.table, f32[6,384,128]{2,1,0:T(8,128)} %get-tuple-element.190.tile, bf16[1152,1024]{1,0:T(8,128)(2,1)} %get-tuple-element.182.q.k.v, ...), custom_call_target="tpu_custom_call" | custom-call | flops 1000 | bytes 1000 | tf_op jit(solution)/shard_map/attend_mine/pallas_call | solution.py:288
  87.5 1.8 collective-permute-done.23.refs_10_
  90.4 3.0 %collective-permute-done.29.refs_18_ = bf16[2,48,768]{2,1,0:T(8,128)(2,1)S(1)} collective-permute-done((bf16[2,48,768]{2,1,0:T(8,128)(2,1)S(1)}, bf16[2,48,768]{2,1,0:T(8,128)(2,1)S(1)}, u32[]{:S(2)}, u32[]{:S(2)}) %collective-permute-start.29) | collective-permute-done | bytes 147488 | tf_op jit(solution)/shard_map/ppermute | solution.py:884
  94.7 23.1 %forward.1 = (bf16[4,512,384]{2,1,0:T(8,128)(2,1)}, bf16[4,512,384]{2,1,0:T(8,128)(2,1)}, bf16[5,512,768]{2,1,0:T(8,128)(2,1)}, bf16[2,8,48,512]{3,2,1,0:T(8,128...) custom-call(s32[7]{0:T(128)} %concatenate.11.place, ...), custom_call_target="tpu_custom_call" | custom-call | flops 8500000 | bytes 20000 | tf_op jit(solution)/shard_map/forward/pallas_call | solution.py:584
  118.5 1.5 collective-permute-start.30
  120.0 11.5 %attend_back_mine.1 = (bf16[384,512]{1,0:T(8,128)(2,1)}, f32[384,1024]{1,0:T(8,128)}, f32[384,1024]{1,0:T(8,128)}, f32[6,384,128]{2,1,0:T(8,128)}, f32[6,8,512]{2,1,0:T(8,128)}) custom-call(s32[7]{0:T(128)} %concatenate.11.place, bf16[384,512]{1,0:T(8,128)(2,1)} %get-tuple-element.215.grad, bf16[384,512]{1,0:T(8,128)(2,1)} %get-tuple-element.201.att_near.out, ...), custom_call_target="tpu_custom_call" | custom-call | flops 3221225 | bytes 6000 | tf_op jit(solution)/shard_map/attend_back_mine/pallas_call | solution.py:450
  131.6 0.9 copy-done.25
  132.5 8.3 %expand_weight_grad.1 = (bf16[4,3,48,768]{3,2,1,0:T(8,128)(2,1)}, bf16[4,3,48,768]{3,2,1,0:T(8,128)(2,1)}, bf16[2,2,2,48,768]{4,3,2,1,0:T(8,128)(2,1)}, bf16[2,2,2,48,768]{4,3,2,1,0:T(8,128)(2,1)}) custom-call(s32[7]{0:T(128)} %concatenate.11.place, bf16[2,8,48,512]{3,2,1,0:T(8,128)(2,1)} %get-tuple-element.222.turned, bf16[2,8,48,512]{3,2,1,0:T(8,128)(2,1)} %copy-done.25, ...), custom_call_target="tpu_custom_call" | custom-call | flops 3019898 | bytes 12000 | tf_op jit(solution)/shard_map/expand_weight_grad/pallas_call | solution.py:674
  141.4 6.3 %contract_weight_grad.1 = (bf16[8,2,48,768]{3,2,1,0:T(8,128)(2,1)}, bf16[8,2,48,768]{3,2,1,0:T(8,128)(2,1)}) custom-call(s32[7]{0:T(128)} %concatenate.11.place, bf16[4,512,384]{2,1,0:T(8,128)(2,1)} %get-tuple-element.213.hid, bf16[4,512,384]{2,1,0:T(8,128)(2,1)} %collective-permute-done.33.hid_far, bf16[512,768]{1,0:T(8,128)(2,1)} %bitcast.113, ...), custom_call_target="tpu_custom_call" | custom-call | flops 2415919 | bytes 9000 | tf_op jit(solution)/shard_map/contract_weight_grad/pallas_call | solution.py:627
  148.3 1.7 collective-permute-start.35
  150.0 13.1 %attend_back_theirs.1.whole.refs_10_ = bf16[6,208,1024]{2,1,0:T(8,128)(2,1)} custom-call(s32[7]{0:T(128)} %concatenate.11.place, bf16[384,512]{1,0:T(8,128)(2,1)} %collective-permute-done.30.grad, bf16[384,512]{1,0:T(8,128)(2,1)} %get-tuple-element.198.out, f32[6,1,512]{2,1,0:T(1,128)} %get-tuple-element.231.inverse, ...), custom_call_target="tpu_custom_call" | custom-call | flops 3221225 | bytes 6000 | tf_op jit(solution)/shard_map/attend_back_theirs/pallas_call | solution.py:450
  163.1 1.0 fusion.6
  164.1 1.3 collective-permute-start.37
  165.4 0.9 fusion.10
  166.9 6.8 %weight_grad.1 = (bf16[8,48,1280]{2,1,0:T(8,128)(2,1)}, bf16[8,48,1280]{2,1,0:T(8,128)(2,1)}) custom-call(s32[7]{0:T(128)} %concatenate.11.place, bf16[8,48,1024]{2,1,0:T(8,128)(2,1)} %get-tuple-element.247.mine, bf16[8,48,1024]{2,1,0:T(8,128)(2,1)} %get-tuple-element.248.other, bf16[6,208,1024]{2,1,0:T(8,128)(2,1)} %attend_back_theirs.1.whole.refs_10_), custom_call_target="tpu_custom_call" | custom-call | flops 1811939 | bytes 6000 | tf_op jit(solution)/shard_map/weight_grad/pallas_call | solution.py:718
  174.5 1.1 collective-permute-done.36
  175.7 1.2 hand_on.1.place
  177.0 2.1 fusion.4
  179.1 1.0 fusion.1
  180.0 1.6 collective-permute-start.40
  181.6 1.5 collective-permute-start.42
  183.1 1.1 fusion.3
  184.2 1.2 fusion
  185.4 0.8 fusion.7
  186.8 6.3 %project_back.1 = (bf16[512,768]{1,0:T(8,128)(2,1)}, bf16[512,768]{1,0:T(8,128)(2,1)}) custom-call(s32[7]{0:T(128)} %hand_on.1.place, bf16[48,1280]{1,0:T(8,128)(2,1)} %narrow_shard.1.refs_0_, bf16[48,1280]{1,0:T(8,128)(2,1)} %copy-done.9, bf16[48,1280]{1,0:T(8,128)(2,1)} %copy-done.13, bf16[48,1280]{1,0:T(8,128)(2,1)} %copy-done.8, ...), custom_call_target="tpu_custom_call" | custom-call | flops 1811939 | bytes 10000 | tf_op jit(solution)/shard_map/project_back/pallas_call | solution.py:749
  193.1 1.6 collective-permute-start.46
  195.5 1.7 collective-permute-start.43
  197.2 1.0 fusion.17
  198.2 1.5 collective-permute-start.44
  199.7 1.2 fusion.5
  200.9 1.1 collective-permute-start.45
  201.9 5.6 %collective-permute-done.43 = bf16[2,2,48,768]{3,2,1,0:T(8,128)(2,1)S(1)} collective-permute-done((bf16[2,2,48,768]{3,2,1,0:T(8,128)(2,1)S(1)}, bf16[2,2,48,768]{3,2,1,0:T(8,128)(2,1)S(1)}, u32[]{:S(2)}, u32[]{:S(2)}) %collective-permute-start.43) | collective-permute-done | bytes 294944 | tf_op jit(solution)/shard_map/ppermute | solution.py:884
  208.5 1.0 fusion.9.b_near
  209.5 1.1 fusion.16
  210.6 3.5 %collective-permute-start.48 = (bf16[48,1280]{1,0:T(8,128)(2,1)S(1)}, bf16[48,1280]{1,0:T(8,128)(2,1)S(1)}, u32[]{:S(2)}, u32[]{:S(2)}) collective-permute-start(bf16[48,1280]{1,0:T(8,128)(2,1)S(1)} %fusion.16), channel_id=1, source_target_pairs={{0,16},{2,18},{4,20},{6,22},{8,24},{10,26},{12,28},{14,30},{16,0},... | collective-permute-start | bytes 368648 | tf_op jit(solution)/shard_map/ppermute | solution.py:884
  214.8 0.9 copy-done.24
  215.7 3.8 %input_grad.1 = bf16[512,768]{1,0:T(8,128)(2,1)} custom-call(s32[7]{0:T(128)} %hand_on.1.place, bf16[512,768]{1,0:T(8,128)(2,1)} %bitcast.109, f32[8,768]{1,0:T(8,128)} %get-tuple-element.203.small, bf16[512,768]{1,0:T(8,128)(2,1)} %get-tuple-element.269.near, bf16[512,768]{1,0:T(8,128)(2,1)} %copy-done.24, f32[512,768]{1,0:T(8,128)} %get-tuple-element.297.middle_grad), custom_call_target="tpu_custom_call" | custom-call | flops 7864 | bytes 6000 | tf_op jit(solution)/shard_map/input_grad/pallas_call | solution.py:871
  219.6 1.4 collective-permute-start.50
  221.0 1.0 fusion.15.g_near
  222.0 0.9 collective-permute-start.51
  223.6 2.1 finish_wide.1
  225.7 1.3 collective-permute-done.51.g_far
  228.3 2.4 %finish.1 = (f32[192,768]{1,0:T(8,128)}, f32[48,768]{1,0:T(8,128)}, f32[48,768]{1,0:T(8,128)}, f32[48,768]{1,0:T(8,128)}, f32[1,48]{1,0:T(1,128)}, /*index=5*/f32[2,12]{1,0:T(2,128)}) custom-call(s32[7]{0:T(128)} %hand_on.1.place, bf16[2,48,768]{2,1,0:T(8,128)(2,1)} %copy-done.35, bf16[2,48,768]{2,1,0:T(8,128)(2,1)} %copy-done.45, ...), custom_call_target="tpu_custom_call" | custom-call | flops 1 | bytes 1000 | tf_op jit(solution)/shard_map/finish/pallas_call | solution.py:815
  (187 shorter events, 18.5 us)
Async XLA Ops:
  0.6 14.9 %collective-permute-start.3 = (bf16[512,768]{1,0:T(8,128)(2,1)}, bf16[512,768]{1,0:T(8,128)(2,1)S(1)}, u32[]{:S(2)}, u32[]{:S(2)}) collective-permute-start(bf16[512,768]{1,0:T(8,128)(2,1)} %bitcast.111), channel_id=1, source_target_pairs={{0,2},{2,0},{4,6},{6,4},{8,10},{10,8},{12,14},{14,12},{16,18},{18,... | collective-permute-start | bytes 2359304 | tf_op jit(solution)/shard_map/ppermute | solution.py:884
  1.2 22.5 %collective-permute-start.6 = (bf16[512,768]{1,0:T(8,128)(2,1)}, bf16[512,768]{1,0:T(8,128)(2,1)S(1)}, u32[]{:S(2)}, u32[]{:S(2)}) collective-permute-start(bf16[512,768]{1,0:T(8,128)(2,1)} %bitcast.106), channel_id=1, source_target_pairs={{0,1},{1,0},{2,3},{3,2},{4,5},{5,4},{6,7},{7,6},{8,9},{9,8},{10,11... | collective-permute-start | bytes 2359304 | tf_op jit(solution)/shard_map/ppermute | solution.py:884
  6.1 34.1 %copy-start.7 = (bf16[48,1280]{1,0:T(8,128)(2,1)S(1)}, bf16[48,1280]{1,0:T(8,128)(2,1)}, u32[]{:S(2)}) copy-start(bf16[48,1280]{1,0:T(8,128)(2,1)} %narrow_shard.1.refs_0_) | copy-start | bytes 368644
  6.1 9.3 %collective-permute-start = (bf16[48,1280]{1,0:T(8,128)(2,1)}, bf16[48,1280]{1,0:T(8,128)(2,1)S(1)}, u32[]{:S(2)}, u32[]{:S(2)}) collective-permute-start(bf16[48,1280]{1,0:T(8,128)(2,1)} %narrow_shard.1.refs_0_), channel_id=1, source_target_pairs={{0,16},{2,18},{4,20},{6,22},{8,24},{10,26},{12,28},{14,30},{16,0},... | collective-permute-start | bytes 368648 | tf_op jit(solution)/shard_map/ppermute | solution.py:884
  8.7 6.8 %collective-permute-start.1 = (bf16[48,1280]{1,0:T(8,128)(2,1)}, bf16[48,1280]{1,0:T(8,128)(2,1)S(1)}, u32[]{:S(2)}, u32[]{:S(2)}) collective-permute-start(bf16[48,1280]{1,0:T(8,128)(2,1)} %narrow_shard.1.refs_0_), channel_id=1, source_target_pairs={{0,8},{2,10},{4,12},{6,14},{8,0},{10,2},{12,4},{14,6},{16,24},{18,... | collective-permute-start | bytes 368648 | tf_op jit(solution)/shard_map/ppermute | solution.py:884
  10.3 5.3 %collective-permute-start.2 = (bf16[48,1280]{1,0:T(8,128)(2,1)}, bf16[48,1280]{1,0:T(8,128)(2,1)S(1)}, u32[]{:S(2)}, u32[]{:S(2)}) collective-permute-start(bf16[48,1280]{1,0:T(8,128)(2,1)} %narrow_shard.1.refs_0_), channel_id=1, source_target_pairs={{0,4},{2,6},{4,0},{6,2},{8,12},{10,14},{12,8},{14,10},{16,20},{18,... | collective-permute-start | bytes 368648 | tf_op jit(solution)/shard_map/ppermute | solution.py:884
  15.4 34.0 %copy-start.8 = (bf16[48,1280]{1,0:T(8,128)(2,1)}, bf16[48,1280]{1,0:T(8,128)(2,1)S(1)}, u32[]{:S(2)}) copy-start(bf16[48,1280]{1,0:T(8,128)(2,1)S(1)} %collective-permute-done.refs_3_) | copy-start | bytes 368644
  15.5 33.8 %copy-start.13 = (bf16[48,1280]{1,0:T(8,128)(2,1)}, bf16[48,1280]{1,0:T(8,128)(2,1)S(1)}, u32[]{:S(2)}) copy-start(bf16[48,1280]{1,0:T(8,128)(2,1)S(1)} %collective-permute-done.1.refs_2_) | copy-start | bytes 368644
  15.5 33.9 %copy-start.9 = (bf16[48,1280]{1,0:T(8,128)(2,1)}, bf16[48,1280]{1,0:T(8,128)(2,1)S(1)}, u32[]{:S(2)}) copy-start(bf16[48,1280]{1,0:T(8,128)(2,1)S(1)} %collective-permute-done.2.refs_1_) | copy-start | bytes 368644
  15.5 33.9 %copy-start.23 = (bf16[512,768]{1,0:T(8,128)(2,1)}, bf16[512,768]{1,0:T(8,128)(2,1)S(1)}, u32[]{:S(2)}) copy-start(bf16[512,768]{1,0:T(8,128)(2,1)S(1)} %collective-permute-done.3.cot_far) | copy-start | bytes 2359300
  15.6 8.6 %collective-permute-start.4 = (bf16[2,48,1280]{2,1,0:T(8,128)(2,1)S(1)}, bf16[2,48,1280]{2,1,0:T(8,128)(2,1)S(1)}, u32[]{:S(2)}, u32[]{:S(2)}) collective-permute-start(bf16[2,48,1280]{2,1,0:T(8,128)(2,1)S(1)} %pad_maximum_fusion.7), channel_id=1, source_target_pairs={{0,8},{2,10},{4,12},{6,14},{8,0},{10,2},{12,4},{14,6},{16,24},{18,... | collective-permute-start | bytes 737288 | tf_op jit(solution)/shard_map/ppermute | solution.py:884
  17.1 7.1 %collective-permute-start.5 = (bf16[48,1280]{1,0:T(8,128)(2,1)S(1)}, bf16[48,1280]{1,0:T(8,128)(2,1)S(1)}, u32[]{:S(2)}, u32[]{:S(2)}) collective-permute-start(bf16[48,1280]{1,0:T(8,128)(2,1)S(1)} %collective-permute-done.refs_3_), channel_id=1, source_target_pairs={{0,4},{2,6},{4,0},{6,2},{8,12},{10,14},{12,8},{14,10},{16,20},{18,... | collective-permute-start | bytes 368648 | tf_op jit(solution)/shard_map/ppermute | solution.py:884
  21.2 23.7 %collective-permute-start.7 = (bf16[7,48,768]{2,1,0:T(8,128)(2,1)}, bf16[7,48,768]{2,1,0:T(8,128)(2,1)S(1)}, u32[]{:S(2)}, u32[]{:S(2)}) collective-permute-start(bf16[7,48,768]{2,1,0:T(8,128)(2,1)} %get-tuple-element.171), channel_id=1, source_target_pairs={{0,8},{2,10},{4,12},{6,14},{8,0},{10,2},{12,4},{14,6},{16,24},{18,... | collective-permute-start | bytes 1548296 | tf_op jit(solution)/shard_map/ppermute | solution.py:884
  21.8 23.1 %collective-permute-start.8 = (bf16[7,48,768]{2,1,0:T(8,128)(2,1)}, bf16[7,48,768]{2,1,0:T(8,128)(2,1)S(1)}, u32[]{:S(2)}, u32[]{:S(2)}) collective-permute-start(bf16[7,48,768]{2,1,0:T(8,128)(2,1)} %get-tuple-element.171), channel_id=1, source_target_pairs={{0,16},{2,18},{4,20},{6,22},{8,24},{10,26},{12,28},{14,30},{16,0},... | collective-permute-start | bytes 1548296 | tf_op jit(solution)/shard_map/ppermute | solution.py:884
  23.7 16.6 %copy-start.27 = (bf16[512,768]{1,0:T(8,128)(2,1)}, bf16[512,768]{1,0:T(8,128)(2,1)S(1)}, u32[]{:S(2)}) copy-start(bf16[512,768]{1,0:T(8,128)(2,1)S(1)} %collective-permute-done.6.x_far) | copy-start | bytes 2359300
  23.7 21.3 %collective-permute-start.9 = (bf16[7,48,768]{2,1,0:T(8,128)(2,1)}, bf16[7,48,768]{2,1,0:T(8,128)(2,1)S(1)}, u32[]{:S(2)}, u32[]{:S(2)}) collective-permute-start(bf16[7,48,768]{2,1,0:T(8,128)(2,1)} %get-tuple-element.171), channel_id=1, source_target_pairs={{0,4},{2,6},{4,0},{6,2},{8,12},{10,14},{12,8},{14,10},{16,20},{18,... | collective-permute-start | bytes 1548296 | tf_op jit(solution)/shard_map/ppermute | solution.py:884
  24.2 25.3 %copy-start.14 = (bf16[48,1280]{1,0:T(8,128)(2,1)}, bf16[48,1280]{1,0:T(8,128)(2,1)S(1)}, u32[]{:S(2)}) copy-start(bf16[48,1280]{1,0:T(8,128)(2,1)S(1)} %collective-permute-done.5.refs_5_) | copy-start | bytes 368644
  24.2 25.3 %copy-start.1 = (bf16[2,48,1280]{2,1,0:T(8,128)(2,1)}, bf16[2,48,1280]{2,1,0:T(8,128)(2,1)S(1)}, u32[]{:S(2)}) copy-start(bf16[2,48,1280]{2,1,0:T(8,128)(2,1)S(1)} %collective-permute-done.4.refs_4_) | copy-start | bytes 737284
  24.2 20.7 %collective-permute-start.12 = (bf16[3,48,1280]{2,1,0:T(8,128)(2,1)S(1)}, bf16[3,48,1280]{2,1,0:T(8,128)(2,1)S(1)}, u32[]{:S(2)}, u32[]{:S(2)}) collective-permute-start(bf16[3,48,1280]{2,1,0:T(8,128)(2,1)S(1)} %pad_maximum_fusion.5), channel_id=1, source_target_pairs={{0,2},{2,0},{4,6},{6,4},{8,10},{10,8},{12,14},{14,12},{16,18},{18,... | collective-permute-start | bytes 1105928 | tf_op jit(solution)/shard_map/ppermute | solution.py:884
  24.3 15.8 %collective-permute-start.10 = (bf16[48,1280]{1,0:T(8,128)(2,1)S(1)}, bf16[48,1280]{1,0:T(8,128)(2,1)S(1)}, u32[]{:S(2)}, u32[]{:S(2)}) collective-permute-start(bf16[48,1280]{1,0:T(8,128)(2,1)S(1)} %slice_bitcast_fusion.6), channel_id=1, source_target_pairs={{0,4},{2,6},{4,0},{6,2},{8,12},{10,14},{12,8},{14,10},{16,20},{18,... | collective-permute-start | bytes 368648 | tf_op jit(solution)/shard_map/ppermute | solution.py:884
  40.2 1.3 collective-permute-start.11
  41.5 8.9 %collective-permute-start.13 = (bf16[4,48,1280]{2,1,0:T(8,128)(2,1)S(1)}, bf16[4,48,1280]{2,1,0:T(8,128)(2,1)S(1)}, u32[]{:S(2)}, u32[]{:S(2)}) collective-permute-start(bf16[4,48,1280]{2,1,0:T(8,128)(2,1)S(1)} %pad_maximum_fusion.3), channel_id=1, source_target_pairs={{0,2},{2,0},{4,6},{6,4},{8,10},{10,8},{12,14},{14,12},{16,18},{18,... | collective-permute-start | bytes 1474568 | tf_op jit(solution)/shard_map/ppermute | solution.py:884
  44.9 18.0 %copy-start = (bf16[7,48,768]{2,1,0:T(8,128)(2,1)}, bf16[7,48,768]{2,1,0:T(8,128)(2,1)S(1)}, u32[]{:S(2)}) copy-start(bf16[7,48,768]{2,1,0:T(8,128)(2,1)S(1)} %collective-permute-done.9.refs_1_) | copy-start | bytes 1548292
  45.0 15.4 %collective-permute-start.14 = (bf16[7,48,768]{2,1,0:T(8,128)(2,1)S(1)}, bf16[7,48,768]{2,1,0:T(8,128)(2,1)S(1)}, u32[]{:S(2)}, u32[]{:S(2)}) collective-permute-start(bf16[7,48,768]{2,1,0:T(8,128)(2,1)S(1)} %collective-permute-done.8.refs_3_), channel_id=1, source_target_pairs={{0,8},{2,10},{4,12},{6,14},{8,0},{10,2},{12,4},{14,6},{16,24},{18,... | collective-permute-start | bytes 1548296 | tf_op jit(solution)/shard_map/ppermute | solution.py:884
  48.1 12.3 %collective-permute-start.15 = (bf16[7,48,768]{2,1,0:T(8,128)(2,1)S(1)}, bf16[7,48,768]{2,1,0:T(8,128)(2,1)S(1)}, u32[]{:S(2)}, u32[]{:S(2)}) collective-permute-start(bf16[7,48,768]{2,1,0:T(8,128)(2,1)S(1)} %collective-permute-done.8.refs_3_), channel_id=1, source_target_pairs={{0,4},{2,6},{4,0},{6,2},{8,12},{10,14},{12,8},{14,10},{16,20},{18,... | collective-permute-start | bytes 1548296 | tf_op jit(solution)/shard_map/ppermute | solution.py:884
  49.5 10.9 %collective-permute-start.16 = (bf16[3,2,48,768]{3,2,1,0:T(8,128)(2,1)S(1)}, bf16[3,2,48,768]{3,2,1,0:T(8,128)(2,1)S(1)}, u32[]{:S(2)}, u32[]{:S(2)}) collective-permute-start(bf16[3,2,48,768]{3,2,1,0:T(8,128)(2,1)S(1)} %pad_maximum_fusion.4), channel_id=1, source_target_pairs={{0,1},{1,0},{2,3},{3,2},{4,5},{5,4},{6,7},{7,6},{8,9},{9,8},{10,11... | collective-permute-start | bytes 1327112 | tf_op jit(solution)/shard_map/ppermute | solution.py:884
  50.3 24.5 %collective-permute-start.20 = (bf16[3,7,48,768]{3,2,1,0:T(8,128)(2,1)S(1)}, bf16[3,7,48,768]{3,2,1,0:T(8,128)(2,1)S(1)}, u32[]{:S(2)}, u32[]{:S(2)}) collective-permute-start(bf16[3,7,48,768]{3,2,1,0:T(8,128)(2,1)S(1)} %pad_maximum_fusion), channel_id=1, source_target_pairs={{0,2},{2,0},{4,6},{6,4},{8,10},{10,8},{12,14},{14,12},{16,18},{18,... | collective-permute-start | bytes 4644872 | tf_op jit(solution)/shard_map/ppermute | solution.py:884
  50.4 13.4 %collective-permute-start.19 = (bf16[9,48,768]{2,1,0:T(8,128)(2,1)}, bf16[9,48,768]{2,1,0:T(8,128)(2,1)}, u32[]{:S(2)}, u32[]{:S(2)}) collective-permute-start(bf16[9,48,768]{2,1,0:T(8,128)(2,1)} %get-tuple-element.193.refs_0_), channel_id=1, source_target_pairs={{0,2},{2,0},{4,6},{6,4},{8,10},{10,8},{12,14},{14,12},{16,18},{18,... | collective-permute-start | bytes 1990664 | tf_op jit(solution)/shard_map/ppermute | solution.py:884
  60.4 29.4 %copy-start.26 = (bf16[3,2,48,768]{3,2,1,0:T(8,128)(2,1)}, bf16[3,2,48,768]{3,2,1,0:T(8,128)(2,1)S(1)}, u32[]{:S(2)}) copy-start(bf16[3,2,48,768]{3,2,1,0:T(8,128)(2,1)S(1)} %collective-permute-done.16.refs_8_) | copy-start | bytes 1327108
  60.4 14.4 %collective-permute-start.17 = (bf16[7,48,768]{2,1,0:T(8,128)(2,1)S(1)}, bf16[7,48,768]{2,1,0:T(8,128)(2,1)S(1)}, u32[]{:S(2)}, u32[]{:S(2)}) collective-permute-start(bf16[7,48,768]{2,1,0:T(8,128)(2,1)S(1)} %collective-permute-done.14.refs_4_), channel_id=1, source_target_pairs={{0,4},{2,6},{4,0},{6,2},{8,12},{10,14},{12,8},{14,10},{16,20},{18,... | collective-permute-start | bytes 1548296 | tf_op jit(solution)/shard_map/ppermute | solution.py:884
  62.1 25.3 %collective-permute-start.24 = (bf16[2,7,48,768]{3,2,1,0:T(8,128)(2,1)S(1)}, bf16[2,7,48,768]{3,2,1,0:T(8,128)(2,1)S(1)}, u32[]{:S(2)}, u32[]{:S(2)}) collective-permute-start(bf16[2,7,48,768]{3,2,1,0:T(8,128)(2,1)S(1)} %pad_maximum_fusion.1), channel_id=1, source_target_pairs={{0,2},{2,0},{4,6},{6,4},{8,10},{10,8},{12,14},{14,12},{16,18},{18,... | collective-permute-start | bytes 3096584 | tf_op jit(solution)/shard_map/ppermute | solution.py:884
  62.3 12.5 %collective-permute-start.18 = (bf16[2,2,48,768]{3,2,1,0:T(8,128)(2,1)S(1)}, bf16[2,2,48,768]{3,2,1,0:T(8,128)(2,1)S(1)}, u32[]{:S(2)}, u32[]{:S(2)}) collective-permute-start(bf16[2,2,48,768]{3,2,1,0:T(8,128)(2,1)S(1)} %pad_maximum_fusion.6), channel_id=1, source_target_pairs={{0,1},{1,0},{2,3},{3,2},{4,5},{5,4},{6,7},{7,6},{8,9},{9,8},{10,11... | collective-permute-start | bytes 884744 | tf_op jit(solution)/shard_map/ppermute | solution.py:884
  63.8 23.6 %collective-permute-start.21 = (bf16[9,48,768]{2,1,0:T(8,128)(2,1)}, bf16[9,48,768]{2,1,0:T(8,128)(2,1)}, u32[]{:S(2)}, u32[]{:S(2)}) collective-permute-start(bf16[9,48,768]{2,1,0:T(8,128)(2,1)} %pad_maximum_fusion.2), channel_id=1, source_target_pairs={{0,8},{2,10},{4,12},{6,14},{8,0},{10,2},{12,4},{14,6},{16,24},{18,... | collective-permute-start | bytes 1990664 | tf_op jit(solution)/shard_map/ppermute | solution.py:884
  74.8 15.1 %copy-start.42 = (bf16[2,2,48,768]{3,2,1,0:T(8,128)(2,1)}, bf16[2,2,48,768]{3,2,1,0:T(8,128)(2,1)S(1)}, u32[]{:S(2)}) copy-start(bf16[2,2,48,768]{3,2,1,0:T(8,128)(2,1)S(1)} %collective-permute-done.18.refs_9_) | copy-start | bytes 884740
  74.8 14.4 %collective-permute-start.22 = (bf16[384,512]{1,0:T(8,128)(2,1)}, bf16[384,512]{1,0:T(8,128)(2,1)S(1)}, u32[]{:S(2)}, u32[]{:S(2)}) collective-permute-start(bf16[384,512]{1,0:T(8,128)(2,1)} %get-tuple-element.198.out), channel_id=1, source_target_pairs={{0,1},{1,0},{2,3},{3,2},{4,5},{5,4},{6,7},{7,6},{8,9},{9,8},{10,11... | collective-permute-start | bytes 1179656 | tf_op jit(solution)/shard_map/ppermute | solution.py:884
  76.4 12.8 %collective-permute-start.23 = (bf16[2,48,768]{2,1,0:T(8,128)(2,1)S(1)}, bf16[2,48,768]{2,1,0:T(8,128)(2,1)S(1)}, u32[]{:S(2)}, u32[]{:S(2)}) collective-permute-start(bf16[2,48,768]{2,1,0:T(8,128)(2,1)S(1)} %slice.34), channel_id=1, source_target_pairs={{0,1},{1,0},{2,3},{3,2},{4,5},{5,4},{6,7},{7,6},{8,9},{9,8},{10,11... | collective-permute-start | bytes 442376 | tf_op jit(solution)/shard_map/ppermute | solution.py:884
  89.2 4.2 %collective-permute-start.25 = (bf16[9,48,768]{2,1,0:T(8,128)(2,1)}, bf16[9,48,768]{2,1,0:T(8,128)(2,1)S(1)}, u32[]{:S(2)}, u32[]{:S(2)}) collective-permute-start(bf16[9,48,768]{2,1,0:T(8,128)(2,1)} %collective-permute-done.21.refs_6_), channel_id=1, source_target_pairs={{0,2},{2,0},{4,6},{6,4},{8,10},{10,8},{12,14},{14,12},{16,18},{18,... | collective-permute-start | bytes 1990664 | tf_op jit(solution)/shard_map/ppermute | solution.py:884
  89.3 4.1 %collective-permute-start.26 = (bf16[7,48,768]{2,1,0:T(8,128)(2,1)S(1)}, bf16[7,48,768]{2,1,0:T(8,128)(2,1)S(1)}, u32[]{:S(2)}, u32[]{:S(2)}) collective-permute-start(bf16[7,48,768]{2,1,0:T(8,128)(2,1)S(1)} %collective-permute-done.17.refs_7_), channel_id=1, source_target_pairs={{0,2},{2,0},{4,6},{6,4},{8,10},{10,8},{12,14},{14,12},{16,18},{18,... | collective-permute-start | bytes 1548296 | tf_op jit(solution)/shard_map/ppermute | solution.py:884
  89.8 3.6 %collective-permute-start.27 = (bf16[3,2,48,768]{3,2,1,0:T(8,128)(2,1)S(1)}, bf16[3,2,48,768]{3,2,1,0:T(8,128)(2,1)S(1)}, u32[]{:S(2)}, u32[]{:S(2)}) collective-permute-start(bf16[3,2,48,768]{3,2,1,0:T(8,128)(2,1)S(1)} %collective-permute-done.16.refs_8_), channel_id=1, source_target_pairs={{0,2},{2,0},{4,6},{6,4},{8,10},{10,8},{12,14},{14,12},{16,18},{18,... | collective-permute-start | bytes 1327112 | tf_op jit(solution)/shard_map/ppermute | solution.py:884
  89.9 3.5 %collective-permute-start.28 = (bf16[2,2,48,768]{3,2,1,0:T(8,128)(2,1)S(1)}, bf16[2,2,48,768]{3,2,1,0:T(8,128)(2,1)S(1)}, u32[]{:S(2)}, u32[]{:S(2)}) collective-permute-start(bf16[2,2,48,768]{3,2,1,0:T(8,128)(2,1)S(1)} %collective-permute-done.18.refs_9_), channel_id=1, source_target_pairs={{0,2},{2,0},{4,6},{6,4},{8,10},{10,8},{12,14},{14,12},{16,18},{18,... | collective-permute-start | bytes 884744 | tf_op jit(solution)/shard_map/ppermute | solution.py:884
  90.3 3.1 %collective-permute-start.29 = (bf16[2,48,768]{2,1,0:T(8,128)(2,1)S(1)}, bf16[2,48,768]{2,1,0:T(8,128)(2,1)S(1)}, u32[]{:S(2)}, u32[]{:S(2)}) collective-permute-start(bf16[2,48,768]{2,1,0:T(8,128)(2,1)S(1)} %collective-permute-done.23.refs_10_), channel_id=1, source_target_pairs={{0,2},{2,0},{4,6},{6,4},{8,10},{10,8},{12,14},{14,12},{16,18},{18,... | collective-permute-start | bytes 442376 | tf_op jit(solution)/shard_map/ppermute | solution.py:884
  117.8 13.7 %collective-permute-start.32 = (bf16[5,512,768]{2,1,0:T(8,128)(2,1)}, bf16[5,512,768]{2,1,0:T(8,128)(2,1)}, u32[]{:S(2)}, u32[]{:S(2)}) collective-permute-start(bf16[5,512,768]{2,1,0:T(8,128)(2,1)} %get-tuple-element.224.pre), channel_id=1, source_target_pairs={{0,2},{2,0},{4,6},{6,4},{8,10},{10,8},{12,14},{14,12},{16,18},{18,... | collective-permute-start | bytes 11796488 | tf_op jit(solution)/shard_map/ppermute | solution.py:884
  118.0 23.3 %collective-permute-start.33 = (bf16[4,512,384]{2,1,0:T(8,128)(2,1)}, bf16[4,512,384]{2,1,0:T(8,128)(2,1)}, u32[]{:S(2)}, u32[]{:S(2)}) collective-permute-start(bf16[4,512,384]{2,1,0:T(8,128)(2,1)} %get-tuple-element.227), channel_id=1, source_target_pairs={{0,2},{2,0},{4,6},{6,4},{8,10},{10,8},{12,14},{14,12},{16,18},{18,... | collective-permute-start | bytes 4718600 | tf_op jit(solution)/shard_map/ppermute | solution.py:884
  118.4 13.1 %collective-permute-start.31 = (bf16[2,8,48,512]{3,2,1,0:T(8,128)(2,1)}, bf16[2,8,48,512]{3,2,1,0:T(8,128)(2,1)S(1)}, u32[]{:S(2)}, u32[]{:S(2)}) collective-permute-start(bf16[2,8,48,512]{3,2,1,0:T(8,128)(2,1)} %get-tuple-element.223), channel_id=1, source_target_pairs={{0,2},{2,0},{4,6},{6,4},{8,10},{10,8},{12,14},{14,12},{16,18},{18,... | collective-permute-start | bytes 2359304 | tf_op jit(solution)/shard_map/ppermute | solution.py:884
  118.5 13.0 %collective-permute-start.30 = (bf16[384,512]{1,0:T(8,128)(2,1)}, bf16[384,512]{1,0:T(8,128)(2,1)}, u32[]{:S(2)}, u32[]{:S(2)}) collective-permute-start(bf16[384,512]{1,0:T(8,128)(2,1)} %get-tuple-element.220), channel_id=1, source_target_pairs={{0,1},{1,0},{2,3},{3,2},{4,5},{5,4},{6,7},{7,6},{8,9},{9,8},{10,11... | collective-permute-start | bytes 1179656 | tf_op jit(solution)/shard_map/ppermute | solution.py:884
  140.8 22.3 %collective-permute-start.34 = (bf16[4,3,48,768]{3,2,1,0:T(8,128)(2,1)}, bf16[4,3,48,768]{3,2,1,0:T(8,128)(2,1)S(1)}, u32[]{:S(2)}, u32[]{:S(2)}) collective-permute-start(bf16[4,3,48,768]{3,2,1,0:T(8,128)(2,1)} %get-tuple-element.225), channel_id=1, source_target_pairs={{0,4},{2,6},{4,0},{6,2},{8,12},{10,14},{12,8},{14,10},{16,20},{18,... | collective-permute-start | bytes 2654216 | tf_op jit(solution)/shard_map/ppermute | solution.py:884
  147.7 27.9 %collective-permute-start.36 = (bf16[8,2,48,768]{3,2,1,0:T(8,128)(2,1)}, bf16[8,2,48,768]{3,2,1,0:T(8,128)(2,1)S(1)}, u32[]{:S(2)}, u32[]{:S(2)}) collective-permute-start(bf16[8,2,48,768]{3,2,1,0:T(8,128)(2,1)} %get-tuple-element.229), channel_id=1, source_target_pairs={{0,1},{1,0},{2,3},{3,2},{4,5},{5,4},{6,7},{7,6},{8,9},{9,8},{10,11... | collective-permute-start | bytes 3538952 | tf_op jit(solution)/shard_map/ppermute | solution.py:884
  148.3 17.1 %collective-permute-start.35 = (bf16[2,2,2,48,768]{4,3,2,0,1:T(8,128)(2,1)S(1)}, bf16[2,2,2,48,768]{4,3,2,0,1:T(8,128)(2,1)S(1)}, u32[]{:S(2)}, u32[]{:S(2)}) collective-permute-start(bf16[2,2,2,48,768]{4,3,2,0,1:T(8,128)(2,1)S(1)} %copy.32), channel_id=1, source_target_pairs={{0,8},{2,10},{4,12},{6,14},{8,0},{10,2},{12,4},{14,6},{16,24},{18,... | collective-permute-start | bytes 1769480 | tf_op jit(solution)/shard_map/ppermute | solution.py:884
  150.0 15.4 %copy-start.30 = (bf16[2,2,2,48,768]{4,3,2,1,0:T(8,128)(2,1)S(1)}, bf16[2,2,2,48,768]{4,3,2,1,0:T(8,128)(2,1)}, u32[]{:S(2)}) copy-start(bf16[2,2,2,48,768]{4,3,2,1,0:T(8,128)(2,1)} %get-tuple-element.263) | copy-start | bytes 1769476
  164.1 11.6 %collective-permute-start.37 = (bf16[2,3,48,768]{3,2,1,0:T(8,128)(2,1)}, bf16[2,3,48,768]{3,2,1,0:T(8,128)(2,1)}, u32[]{:S(2)}, u32[]{:S(2)}) collective-permute-start(bf16[2,3,48,768]{3,2,1,0:T(8,128)(2,1)} %fusion.6), channel_id=1, source_target_pairs={{0,8},{2,10},{4,12},{6,14},{8,0},{10,2},{12,4},{14,6},{16,24},{18,... | collective-permute-start | bytes 1327112 | tf_op jit(solution)/shard_map/ppermute | solution.py:884
  166.3 8.2 %collective-permute-start.38 = (bf16[2,2,48,768]{3,2,1,0:T(8,128)(2,1)}, bf16[2,2,48,768]{3,2,1,0:T(8,128)(2,1)}, u32[]{:S(2)}, u32[]{:S(2)}) collective-permute-start(bf16[2,2,48,768]{3,2,1,0:T(8,128)(2,1)} %fusion.10), channel_id=1, source_target_pairs={{0,4},{2,6},{4,0},{6,2},{8,12},{10,14},{12,8},{14,10},{16,20},{18,... | collective-permute-start | bytes 884744 | tf_op jit(solution)/shard_map/ppermute | solution.py:884
  173.8 3.2 %collective-permute-start.39 = (bf16[8,48,1280]{2,1,0:T(8,128)(2,1)}, bf16[8,48,1280]{2,1,0:T(8,128)(2,1)}, u32[]{:S(2)}, u32[]{:S(2)}) collective-permute-start(bf16[8,48,1280]{2,1,0:T(8,128)(2,1)} %get-tuple-element.252), channel_id=1, source_target_pairs={{0,2},{2,0},{4,6},{6,4},{8,10},{10,8},{12,14},{14,12},{16,18},{18,... | collective-permute-start | bytes 2949128 | tf_op jit(solution)/shard_map/ppermute | solution.py:884
  180.0 15.3 %collective-permute-start.40 = (bf16[2,2,2,48,768]{4,3,2,1,0:T(8,128)(2,1)}, bf16[2,2,2,48,768]{4,3,2,1,0:T(8,128)(2,1)S(1)}, u32[]{:S(2)}, u32[]{:S(2)}) collective-permute-start(bf16[2,2,2,48,768]{4,3,2,1,0:T(8,128)(2,1)} %fusion.1), channel_id=1, source_target_pairs={{0,4},{2,6},{4,0},{6,2},{8,12},{10,14},{12,8},{14,10},{16,20},{18,... | collective-permute-start | bytes 1769480 | tf_op jit(solution)/shard_map/ppermute | solution.py:884
  181.6 18.1 %collective-permute-start.42 = (bf16[2,2,48,1280]{3,2,1,0:T(8,128)(2,1)}, bf16[2,2,48,1280]{3,2,1,0:T(8,128)(2,1)}, u32[]{:S(2)}, u32[]{:S(2)}) collective-permute-start(bf16[2,2,48,1280]{3,2,1,0:T(8,128)(2,1)} %fusion.4), channel_id=1, source_target_pairs={{0,8},{2,10},{4,12},{6,14},{8,0},{10,2},{12,4},{14,6},{16,24},{18,... | collective-permute-start | bytes 1474568 | tf_op jit(solution)/shard_map/ppermute | solution.py:884
  186.2 11.0 %collective-permute-start.41 = (bf16[2,5,48,384]{3,2,1,0:T(8,128)(2,1)}, bf16[2,5,48,384]{3,2,1,0:T(8,128)(2,1)}, u32[]{:S(2)}, u32[]{:S(2)}) collective-permute-start(bf16[2,5,48,384]{3,2,1,0:T(8,128)(2,1)} %get-tuple-element.266), channel_id=1, source_target_pairs={{0,1},{1,0},{2,3},{3,2},{4,5},{5,4},{6,7},{7,6},{8,9},{9,8},{10,11... | collective-permute-start | bytes 1105928 | tf_op jit(solution)/shard_map/ppermute | solution.py:884
  193.1 21.7 %collective-permute-start.46 = (bf16[512,768]{1,0:T(8,128)(2,1)}, bf16[512,768]{1,0:T(8,128)(2,1)S(1)}, u32[]{:S(2)}, u32[]{:S(2)}) collective-permute-start(bf16[512,768]{1,0:T(8,128)(2,1)} %get-tuple-element.296), channel_id=1, source_target_pairs={{0,1},{1,0},{2,3},{3,2},{4,5},{5,4},{6,7},{7,6},{8,9},{9,8},{10,11... | collective-permute-start | bytes 2359304 | tf_op jit(solution)/shard_map/ppermute | solution.py:884
  195.5 12.1 %collective-permute-start.43 = (bf16[2,2,48,768]{3,2,1,0:T(8,128)(2,1)S(1)}, bf16[2,2,48,768]{3,2,1,0:T(8,128)(2,1)S(1)}, u32[]{:S(2)}, u32[]{:S(2)}) collective-permute-start(bf16[2,2,48,768]{3,2,1,0:T(8,128)(2,1)S(1)} %fusion.2), channel_id=1, source_target_pairs={{0,8},{2,10},{4,12},{6,14},{8,0},{10,2},{12,4},{14,6},{16,24},{18,... | collective-permute-start | bytes 884744 | tf_op jit(solution)/shard_map/ppermute | solution.py:884
  198.2 10.3 %collective-permute-start.44 = (bf16[5,48,384]{2,1,0:T(8,128)(2,1)S(1)}, bf16[5,48,384]{2,1,0:T(8,128)(2,1)S(1)}, u32[]{:S(2)}, u32[]{:S(2)}) collective-permute-start(bf16[5,48,384]{2,1,0:T(8,128)(2,1)S(1)} %fusion.17), channel_id=1, source_target_pairs={{0,16},{2,18},{4,20},{6,22},{8,24},{10,26},{12,28},{14,30},{16,0},... | collective-permute-start | bytes 552968 | tf_op jit(solution)/shard_map/ppermute | solution.py:884
  200.9 8.6 %collective-permute-start.45 = (bf16[2,48,1280]{2,1,0:T(8,128)(2,1)S(1)}, bf16[2,48,1280]{2,1,0:T(8,128)(2,1)S(1)}, u32[]{:S(2)}, u32[]{:S(2)}) collective-permute-start(bf16[2,48,1280]{2,1,0:T(8,128)(2,1)S(1)} %fusion.5), channel_id=1, source_target_pairs={{0,4},{2,6},{4,0},{6,2},{8,12},{10,14},{12,8},{14,10},{16,20},{18,... | collective-permute-start | bytes 737288 | tf_op jit(solution)/shard_map/ppermute | solution.py:884
  207.7 11.8 %collective-permute-start.47 = (bf16[2,48,768]{2,1,0:T(8,128)(2,1)S(1)}, bf16[2,48,768]{2,1,0:T(8,128)(2,1)S(1)}, u32[]{:S(2)}, u32[]{:S(2)}) collective-permute-start(bf16[2,48,768]{2,1,0:T(8,128)(2,1)S(1)} %fusion.13), channel_id=1, source_target_pairs={{0,16},{2,18},{4,20},{6,22},{8,24},{10,26},{12,28},{14,30},{16,0},... | collective-permute-start | bytes 442376 | tf_op jit(solution)/shard_map/ppermute | solution.py:884
  210.6 10.4 %collective-permute-start.48 = (bf16[48,1280]{1,0:T(8,128)(2,1)S(1)}, bf16[48,1280]{1,0:T(8,128)(2,1)S(1)}, u32[]{:S(2)}, u32[]{:S(2)}) collective-permute-start(bf16[48,1280]{1,0:T(8,128)(2,1)S(1)} %fusion.16), channel_id=1, source_target_pairs={{0,16},{2,18},{4,20},{6,22},{8,24},{10,26},{12,28},{14,30},{16,0},... | collective-permute-start | bytes 368648 | tf_op jit(solution)/shard_map/ppermute | solution.py:884
  214.1 8.9 %collective-permute-start.49 = (bf16[5,48,384]{2,1,0:T(8,128)(2,1)S(1)}, bf16[5,48,384]{2,1,0:T(8,128)(2,1)S(1)}, u32[]{:S(2)}, u32[]{:S(2)}) collective-permute-start(bf16[5,48,384]{2,1,0:T(8,128)(2,1)S(1)} %fusion.9.b_near), channel_id=1, source_target_pairs={{0,1},{1,0},{2,3},{3,2},{4,5},{5,4},{6,7},{7,6},{8,9},{9,8},{10,11... | collective-permute-start | bytes 552968 | tf_op jit(solution)/shard_map/ppermute | solution.py:884
  219.6 7.5 %collective-permute-start.50 = (bf16[2,48,768]{2,1,0:T(8,128)(2,1)S(1)}, bf16[2,48,768]{2,1,0:T(8,128)(2,1)S(1)}, u32[]{:S(2)}, u32[]{:S(2)}) collective-permute-start(bf16[2,48,768]{2,1,0:T(8,128)(2,1)S(1)} %fusion.12.a_near), channel_id=1, source_target_pairs={{0,1},{1,0},{2,3},{3,2},{4,5},{5,4},{6,7},{7,6},{8,9},{9,8},{10,11... | collective-permute-start | bytes 442376 | tf_op jit(solution)/shard_map/ppermute | solution.py:884
  222.0 5.0 %collective-permute-start.51 = (bf16[48,1280]{1,0:T(8,128)(2,1)S(1)}, bf16[48,1280]{1,0:T(8,128)(2,1)S(1)}, u32[]{:S(2)}, u32[]{:S(2)}) collective-permute-start(bf16[48,1280]{1,0:T(8,128)(2,1)S(1)} %fusion.15.g_near), channel_id=1, source_target_pairs={{0,1},{1,0},{2,3},{3,2},{4,5},{5,4},{6,7},{7,6},{8,9},{9,8},{10,11... | collective-permute-start | bytes 368648 | tf_op jit(solution)/shard_map/ppermute | solution.py:884
  (37 other events, 186.2 us)

commit v7 on v6

--- a/solution.py
+++ b/solution.py
@@ -16,6 +16,7 @@
 far_edges = (12, 16, 23, 32, 46, 64, 91)
 HIDDEN = -(2.0**30)
 VMEM = 56 * 1024 * 1024
+MOST = 66_900_000
 ANY = pl.BlockSpec(memory_space=pl.ANY)
 FULL = pl.BlockSpec(memory_space=pltpu.VMEM)
 SCALARS = pl.BlockSpec(memory_space=pltpu.SMEM)
@@ -451,7 +452,7 @@
         functools.partial(attend_back_kernel, bool(carry), mine),
         out_shape=out_shape,
         grid_spec=grid,
-        compiler_params=params(VMEM if carry else 66_000_000),
+        compiler_params=params(VMEM if carry else MOST),
         cost_estimate=cost(count * 1024 * 512 * 1024, 6_000_000),
         name="attend_back_mine" if mine else "attend_back_theirs",
     )(place, grad, out, inverse, qkv, qkv, qkv, kept, *carry)
@@ -850,7 +851,7 @@
         ),
         in_specs=[SCALARS] + [FULL] * 4,
         out_specs=(FULL,) * 3,
-        compiler_params=params(),
+        compiler_params=params(MOST),
         cost_estimate=cost(1000, 2_000_000),
         name="finish_wide",
     )(place, b_near, b_far, up, gain.reshape(1, 48))

time: 232 us -> 230 us (level)
  local copies, waits for them, and re-layouts: 6.22 us -> 3.28 us
    unnamed x98 -> x88, local copies, waits for them, and re-layouts: 5.42 us -> 2.55 us
  transfers between devices with their start and end apart: 52 -> 52, of which waited for: 15 -> 16; matrix products, arithmetic and copies ran while one was open for 6% -> 6% of each run, Pallas kernels for 40% -> 41%
where the time goes in v7:
time: 230 us; the launch traced here: 229 us
  Pallas kernels  118 us (51%)
  starting transfers between devices  60.7 us (26%)
  waiting for transfers between devices  27 us (12%)
  other arithmetic  16.3 us (7%)
  between operations  3.36 us (1%)
  local copies, waits for them, and re-layouts  3.28 us (1%)
    ppermute x52, starting transfers between devices, swap(): return lax.ppermute(array, axis, [(i, i ^ bit) for i in range(count)])  60.7 us
    ppermute x52, waiting for transfers between devices, swap(): return lax.ppermute(array, axis, [(i, i ^ bit) for i in range(count)])  27 us
    pallas_call x2, Pallas kernels, attend_back(): pl.pallas_call(functools.partial(attend_back_kernel, bool(carry), mine),...  24.6 us
    pallas_call x1, Pallas kernels, forward(): pl.pallas_call(forward_kernel, out_shape=(hidden, hidden, jax.ShapeDtypeS...  23 us
    pallas_call x2, Pallas kernels, attend(): pl.pallas_call(functools.partial(attend_kernel, mine), out_shape=(jax.Sha...  21 us
    convert_element_type x12, other arithmetic, total(): made = lax.optimization_barrier(made.astype(bf16))  11.2 us
    pallas_call x1, Pallas kernels, expand_weight_grad(): pl.pallas_call(expand_grad_kernel, out_shape=(first, first, second, secon...  8.37 us
    pallas_call x1, Pallas kernels, project(): pl.pallas_call(project_kernel, out_shape=(jax.ShapeDtypeStruct((1152, 102...  7.72 us
  transfers between devices with their start and end apart: 52, of which 16 were waited for; matrix products, arithmetic and copies ran while one was open for 6% of the time, Pallas kernels for 41%

profile of v7, /device:TPU:0, one launch (start us, length us, event | category | flops | bytes accessed | tf_op | source)
XLA Modules:
  0.0 229.0 jit_solution(4079268172163861309)
XLA Ops:
  1.2 2.6 %collective-permute-start.6 = (bf16[512,768]{1,0:T(8,128)(2,1)}, bf16[512,768]{1,0:T(8,128)(2,1)S(1)}, u32[]{:S(2)}, u32[]{:S(2)}) collective-permute-start(bf16[512,768]{1,0:T(8,128)(2,1)} %bitcast.106), channel_id=1, source_target_pairs={{0,1},{1,0},{2,3},{3,2},{4,5},{5,4},{6,7},{7,6},{8,9},{9,8},{10,11... | collective-permute-start | bytes 2359304 | tf_op jit(solution)/shard_map/ppermute | solution.py:885
  4.3 1.8 narrow_shard.1.refs_0_
  6.1 2.6 %collective-permute-start = (bf16[48,1280]{1,0:T(8,128)(2,1)}, bf16[48,1280]{1,0:T(8,128)(2,1)S(1)}, u32[]{:S(2)}, u32[]{:S(2)}) collective-permute-start(bf16[48,1280]{1,0:T(8,128)(2,1)} %narrow_shard.1.refs_0_), channel_id=1, source_target_pairs={{0,16},{2,18},{4,20},{6,22},{8,24},{10,26},{12,28},{14,30},{16,0},... | collective-permute-start | bytes 368648 | tf_op jit(solution)/shard_map/ppermute | solution.py:885
  8.7 1.6 collective-permute-start.1
  10.3 1.5 collective-permute-start.2
  11.8 2.9 %wide_shard.1 = (bf16[7,48,768]{2,1,0:T(8,128)(2,1)}, bf16[9,48,768]{2,1,0:T(8,128)(2,1)}) custom-call(s32[4]{0:T(128)} %pad_add_fusion.place, bf16[48,3072]{1,0:T(8,128)(2,1)} %up.1, bf16[48,768]{1,0:T(8,128)(2,1)} %output.1, bf16[192,768]{1,0:T(8,128)(2,1)} %contract.1), custom_call_target="tpu_custom_call" | custom-call | flops 1000 | bytes 1000 | tf_op jit(solution)/shard_map/wide_shard/pallas_call | solution.py:102
  15.6 1.5 collective-permute-start.4
  17.1 1.5 collective-permute-start.5
  21.7 1.8 collective-permute-start.8
  24.3 12.0 %collective-permute-start.10 = (bf16[48,1280]{1,0:T(8,128)(2,1)S(1)}, bf16[48,1280]{1,0:T(8,128)(2,1)S(1)}, u32[]{:S(2)}, u32[]{:S(2)}) collective-permute-start(bf16[48,1280]{1,0:T(8,128)(2,1)S(1)} %slice_bitcast_fusion.6), channel_id=1, source_target_pairs={{0,4},{2,6},{4,0},{6,2},{8,12},{10,14},{12,8},{14,10},{16,20},{18,... | collective-permute-start | bytes 368648 | tf_op jit(solution)/shard_map/ppermute | solution.py:885
  36.2 4.0 %collective-permute-done.10.refs_6_ = bf16[48,1280]{1,0:T(8,128)(2,1)S(1)} collective-permute-done((bf16[48,1280]{1,0:T(8,128)(2,1)S(1)}, bf16[48,1280]{1,0:T(8,128)(2,1)S(1)}, u32[]{:S(2)}, u32[]{:S(2)}) %collective-permute-start.10) | collective-permute-done | bytes 122912 | tf_op jit(solution)/shard_map/ppermute | solution.py:885
  40.3 1.2 collective-permute-done.11.refs_9_
  41.7 3.1 %collective-permute-done.7.refs_2_ = bf16[7,48,768]{2,1,0:T(8,128)(2,1)S(1)} collective-permute-done((bf16[7,48,768]{2,1,0:T(8,128)(2,1)}, bf16[7,48,768]{2,1,0:T(8,128)(2,1)S(1)}, u32[]{:S(2)}, u32[]{:S(2)}) %collective-permute-start.7) | collective-permute-done | bytes 516128 | tf_op jit(solution)/shard_map/ppermute | solution.py:885
  44.9 3.1 %collective-permute-start.14 = (bf16[7,48,768]{2,1,0:T(8,128)(2,1)S(1)}, bf16[7,48,768]{2,1,0:T(8,128)(2,1)S(1)}, u32[]{:S(2)}, u32[]{:S(2)}) collective-permute-start(bf16[7,48,768]{2,1,0:T(8,128)(2,1)S(1)} %collective-permute-done.8.refs_3_), channel_id=1, source_target_pairs={{0,8},{2,10},{4,12},{6,14},{8,0},{10,2},{12,4},{14,6},{16,24},{18,... | collective-permute-start | bytes 1548296 | tf_op jit(solution)/shard_map/ppermute | solution.py:885
  48.0 1.3 collective-permute-start.15
  51.2 7.7 %project.1 = (bf16[1152,1024]{1,0:T(8,128)(2,1)}, bf16[8,48,1024]{2,1,0:T(8,128)(2,1)}, bf16[8,48,1024]{2,1,0:T(8,128)(2,1)}, f32[8,768]{1,0:T(8,128)}, f32[8,128]{1,0:T(8,128)}, /*index=5*/f32[6,384,128]{2,1,0:T(8,128)}) custom-call(s32[7]{0:T(128)} %concatenate.11.place, bf16[512,768]{1,0:T(8,128)(2,1)} %bitcast.107, bf16[512,768]{1,0:T(8,128)(2,1)} %copy-done.26, ...), custom_call_target="tpu_custom_call" | custom-call | flops 1000 | bytes 1000 | tf_op jit(solution)/shard_map/project/pallas_call | solution.py:194
  58.9 1.5 collective-permute-done.16.refs_8_
  60.5 1.6 collective-permute-start.17
  63.0 0.9 pad_maximum_fusion.2
  64.2 10.6 %attend_theirs.1 = (bf16[384,512]{1,0:T(8,128)(2,1)}, bf16[6,1024,512]{2,1,0:T(8,128)(2,1)}, f32[6,1,512]{2,1,0:T(1,128)}) custom-call(s32[7]{0:T(128)} %concatenate.11.place, f32[8,128]{1,0:T(8,128)} %get-tuple-element.189.table, f32[6,384,128]{2,1,0:T(8,128)} %get-tuple-element.190.tile, bf16[1152,1024]{1,0:T(8,128)(2,1)} %get-tuple-element.182.q.k.v, ...), custom_call_target="tpu_custom_call" | custom-call | flops 1000 | bytes 1000 | tf_op jit(solution)/shard_map/attend_theirs/pallas_call | solution.py:289
  74.9 1.6 collective-permute-start.22
  77.1 10.4 %attend_mine.1 = (bf16[384,512]{1,0:T(8,128)(2,1)}, bf16[6,1024,512]{2,1,0:T(8,128)(2,1)}, f32[6,1,512]{2,1,0:T(1,128)}) custom-call(s32[7]{0:T(128)} %concatenate.11.place, f32[8,128]{1,0:T(8,128)} %get-tuple-element.189.table, f32[6,384,128]{2,1,0:T(8,128)} %get-tuple-element.190.tile, bf16[1152,1024]{1,0:T(8,128)(2,1)} %get-tuple-element.182.q.k.v, ...), custom_call_target="tpu_custom_call" | custom-call | flops 1000 | bytes 1000 | tf_op jit(solution)/shard_map/attend_mine/pallas_call | solution.py:289
  87.5 1.8 collective-permute-done.23.refs_10_
  90.5 3.0 %collective-permute-done.29.refs_18_ = bf16[2,48,768]{2,1,0:T(8,128)(2,1)S(1)} collective-permute-done((bf16[2,48,768]{2,1,0:T(8,128)(2,1)S(1)}, bf16[2,48,768]{2,1,0:T(8,128)(2,1)S(1)}, u32[]{:S(2)}, u32[]{:S(2)}) %collective-permute-start.29) | collective-permute-done | bytes 147488 | tf_op jit(solution)/shard_map/ppermute | solution.py:885
  94.8 23.0 %forward.1 = (bf16[4,512,384]{2,1,0:T(8,128)(2,1)}, bf16[4,512,384]{2,1,0:T(8,128)(2,1)}, bf16[5,512,768]{2,1,0:T(8,128)(2,1)}, bf16[2,8,48,512]{3,2,1,0:T(8,128...) custom-call(s32[7]{0:T(128)} %concatenate.11.place, ...), custom_call_target="tpu_custom_call" | custom-call | flops 8500000 | bytes 20000 | tf_op jit(solution)/shard_map/forward/pallas_call | solution.py:585
  118.6 1.5 collective-permute-start.30
  120.1 11.5 %attend_back_mine.1 = (bf16[384,512]{1,0:T(8,128)(2,1)}, f32[384,1024]{1,0:T(8,128)}, f32[384,1024]{1,0:T(8,128)}, f32[6,384,128]{2,1,0:T(8,128)}, f32[6,8,512]{2,1,0:T(8,128)}) custom-call(s32[7]{0:T(128)} %concatenate.11.place, bf16[384,512]{1,0:T(8,128)(2,1)} %get-tuple-element.215.grad, bf16[384,512]{1,0:T(8,128)(2,1)} %get-tuple-element.201.att_near.out, ...), custom_call_target="tpu_custom_call" | custom-call | flops 3221225 | bytes 6000 | tf_op jit(solution)/shard_map/attend_back_mine/pallas_call | solution.py:451
  131.6 8.4 %expand_weight_grad.1 = (bf16[4,3,48,768]{3,2,1,0:T(8,128)(2,1)}, bf16[4,3,48,768]{3,2,1,0:T(8,128)(2,1)}, bf16[2,2,2,48,768]{4,3,2,1,0:T(8,128)(2,1)}, bf16[2,2,2,48,768]{4,3,2,1,0:T(8,128)(2,1)}) custom-call(s32[7]{0:T(128)} %concatenate.11.place, bf16[2,8,48,512]{3,2,1,0:T(8,128)(2,1)} %get-tuple-element.222.turned, ...), custom_call_target="tpu_custom_call" | custom-call | flops 3019898 | bytes 12000 | tf_op jit(solution)/shard_map/expand_weight_grad/pallas_call | solution.py:675
  140.5 6.3 %contract_weight_grad.1 = (bf16[8,2,48,768]{3,2,1,0:T(8,128)(2,1)}, bf16[8,2,48,768]{3,2,1,0:T(8,128)(2,1)}) custom-call(s32[7]{0:T(128)} %concatenate.11.place, bf16[4,512,384]{2,1,0:T(8,128)(2,1)} %get-tuple-element.213.hid, bf16[4,512,384]{2,1,0:T(8,128)(2,1)} %collective-permute-done.33.hid_far, bf16[512,768]{1,0:T(8,128)(2,1)} %bitcast.113, ...), custom_call_target="tpu_custom_call" | custom-call | flops 2415919 | bytes 9000 | tf_op jit(solution)/shard_map/contract_weight_grad/pallas_call | solution.py:628
  147.4 1.7 collective-permute-start.35
  149.1 13.1 %attend_back_theirs.1.whole.refs_10_ = bf16[6,208,1024]{2,1,0:T(8,128)(2,1)} custom-call(s32[7]{0:T(128)} %concatenate.11.place, bf16[384,512]{1,0:T(8,128)(2,1)} %collective-permute-done.30.grad, bf16[384,512]{1,0:T(8,128)(2,1)} %get-tuple-element.198.out, f32[6,1,512]{2,1,0:T(1,128)} %get-tuple-element.231.inverse, ...), custom_call_target="tpu_custom_call" | custom-call | flops 3221225 | bytes 6000 | tf_op jit(solution)/shard_map/attend_back_theirs/pallas_call | solution.py:451
  162.3 1.0 fusion.6
  163.3 1.3 collective-permute-start.37
  164.6 0.9 fusion.10
  166.1 6.9 %weight_grad.1 = (bf16[8,48,1280]{2,1,0:T(8,128)(2,1)}, bf16[8,48,1280]{2,1,0:T(8,128)(2,1)}) custom-call(s32[7]{0:T(128)} %concatenate.11.place, bf16[8,48,1024]{2,1,0:T(8,128)(2,1)} %get-tuple-element.247.mine, bf16[8,48,1024]{2,1,0:T(8,128)(2,1)} %get-tuple-element.248.other, bf16[6,208,1024]{2,1,0:T(8,128)(2,1)} %attend_back_theirs.1.whole.refs_10_), custom_call_target="tpu_custom_call" | custom-call | flops 1811939 | bytes 6000 | tf_op jit(solution)/shard_map/weight_grad/pallas_call | solution.py:719
  173.7 1.1 collective-permute-done.36
  174.9 1.2 hand_on.1.place
  176.1 2.1 fusion.4
  178.3 1.0 fusion.1
  179.2 1.5 collective-permute-start.40
  180.8 1.5 collective-permute-start.42
  182.3 1.1 fusion.3
  183.4 1.2 fusion
  184.5 0.8 fusion.7
  185.9 6.3 %project_back.1 = (bf16[512,768]{1,0:T(8,128)(2,1)}, bf16[512,768]{1,0:T(8,128)(2,1)}) custom-call(s32[7]{0:T(128)} %hand_on.1.place, bf16[48,1280]{1,0:T(8,128)(2,1)} %narrow_shard.1.refs_0_, bf16[48,1280]{1,0:T(8,128)(2,1)} %copy-done.9, bf16[48,1280]{1,0:T(8,128)(2,1)} %copy-done.13, bf16[48,1280]{1,0:T(8,128)(2,1)} %copy-done.8, ...), custom_call_target="tpu_custom_call" | custom-call | flops 1811939 | bytes 10000 | tf_op jit(solution)/shard_map/project_back/pallas_call | solution.py:750
  192.2 1.6 collective-permute-start.46
  194.7 1.7 collective-permute-start.43
  196.4 1.0 fusion.17
  197.4 1.5 collective-permute-start.44
  198.9 1.2 fusion.5
  200.7 6.2 %collective-permute-done.43 = bf16[2,2,48,768]{3,2,1,0:T(8,128)(2,1)S(1)} collective-permute-done((bf16[2,2,48,768]{3,2,1,0:T(8,128)(2,1)S(1)}, bf16[2,2,48,768]{3,2,1,0:T(8,128)(2,1)S(1)}, u32[]{:S(2)}, u32[]{:S(2)}) %collective-permute-start.43) | collective-permute-done | bytes 294944 | tf_op jit(solution)/shard_map/ppermute | solution.py:885
  206.9 0.9 collective-permute-start.47
  208.0 1.0 fusion.9.b_near
  209.0 1.1 fusion.16
  210.1 2.0 collective-permute-start.48
  212.1 1.3 collective-permute-start.49
  213.4 0.9 copy-done.24
  214.3 3.8 %input_grad.1 = bf16[512,768]{1,0:T(8,128)(2,1)} custom-call(s32[7]{0:T(128)} %hand_on.1.place, bf16[512,768]{1,0:T(8,128)(2,1)} %bitcast.109, f32[8,768]{1,0:T(8,128)} %get-tuple-element.203.small, bf16[512,768]{1,0:T(8,128)(2,1)} %get-tuple-element.269.near, bf16[512,768]{1,0:T(8,128)(2,1)} %copy-done.24, f32[512,768]{1,0:T(8,128)} %get-tuple-element.297.middle_grad), custom_call_target="tpu_custom_call" | custom-call | flops 7864 | bytes 6000 | tf_op jit(solution)/shard_map/input_grad/pallas_call | solution.py:872
  219.2 1.3 collective-permute-start.50
  220.5 1.0 fusion.15.g_near
  221.5 0.8 collective-permute-start.51
  222.4 2.1 finish_wide.1
  224.5 2.1 collective-permute-done.51.g_far
  226.6 2.4 %finish.1 = (f32[192,768]{1,0:T(8,128)}, f32[48,768]{1,0:T(8,128)}, f32[48,768]{1,0:T(8,128)}, f32[48,768]{1,0:T(8,128)}, f32[1,48]{1,0:T(1,128)}, /*index=5*/f32[2,12]{1,0:T(2,128)}) custom-call(s32[7]{0:T(128)} %hand_on.1.place, bf16[2,48,768]{2,1,0:T(8,128)(2,1)} %fusion.12.a_near, bf16[2,48,768]{2,1,0:T(8,128)(2,1)} %collective-permute-done.50.a_far, ...), custom_call_target="tpu_custom_call" | custom-call | flops 1 | bytes 1000 | tf_op jit(solution)/shard_map/finish/pallas_call | solution.py:816
  (177 shorter events, 16.8 us)
Async XLA Ops:
  0.6 14.9 %collective-permute-start.3 = (bf16[512,768]{1,0:T(8,128)(2,1)}, bf16[512,768]{1,0:T(8,128)(2,1)S(1)}, u32[]{:S(2)}, u32[]{:S(2)}) collective-permute-start(bf16[512,768]{1,0:T(8,128)(2,1)} %bitcast.111), channel_id=1, source_target_pairs={{0,2},{2,0},{4,6},{6,4},{8,10},{10,8},{12,14},{14,12},{16,18},{18,... | collective-permute-start | bytes 2359304 | tf_op jit(solution)/shard_map/ppermute | solution.py:885
  1.2 22.4 %collective-permute-start.6 = (bf16[512,768]{1,0:T(8,128)(2,1)}, bf16[512,768]{1,0:T(8,128)(2,1)S(1)}, u32[]{:S(2)}, u32[]{:S(2)}) collective-permute-start(bf16[512,768]{1,0:T(8,128)(2,1)} %bitcast.106), channel_id=1, source_target_pairs={{0,1},{1,0},{2,3},{3,2},{4,5},{5,4},{6,7},{7,6},{8,9},{9,8},{10,11... | collective-permute-start | bytes 2359304 | tf_op jit(solution)/shard_map/ppermute | solution.py:885
  6.1 34.1 %copy-start.7 = (bf16[48,1280]{1,0:T(8,128)(2,1)S(1)}, bf16[48,1280]{1,0:T(8,128)(2,1)}, u32[]{:S(2)}) copy-start(bf16[48,1280]{1,0:T(8,128)(2,1)} %narrow_shard.1.refs_0_) | copy-start | bytes 368644
  6.1 9.3 %collective-permute-start = (bf16[48,1280]{1,0:T(8,128)(2,1)}, bf16[48,1280]{1,0:T(8,128)(2,1)S(1)}, u32[]{:S(2)}, u32[]{:S(2)}) collective-permute-start(bf16[48,1280]{1,0:T(8,128)(2,1)} %narrow_shard.1.refs_0_), channel_id=1, source_target_pairs={{0,16},{2,18},{4,20},{6,22},{8,24},{10,26},{12,28},{14,30},{16,0},... | collective-permute-start | bytes 368648 | tf_op jit(solution)/shard_map/ppermute | solution.py:885
  8.7 6.8 %collective-permute-start.1 = (bf16[48,1280]{1,0:T(8,128)(2,1)}, bf16[48,1280]{1,0:T(8,128)(2,1)S(1)}, u32[]{:S(2)}, u32[]{:S(2)}) collective-permute-start(bf16[48,1280]{1,0:T(8,128)(2,1)} %narrow_shard.1.refs_0_), channel_id=1, source_target_pairs={{0,8},{2,10},{4,12},{6,14},{8,0},{10,2},{12,4},{14,6},{16,24},{18,... | collective-permute-start | bytes 368648 | tf_op jit(solution)/shard_map/ppermute | solution.py:885
  10.3 5.3 %collective-permute-start.2 = (bf16[48,1280]{1,0:T(8,128)(2,1)}, bf16[48,1280]{1,0:T(8,128)(2,1)S(1)}, u32[]{:S(2)}, u32[]{:S(2)}) collective-permute-start(bf16[48,1280]{1,0:T(8,128)(2,1)} %narrow_shard.1.refs_0_), channel_id=1, source_target_pairs={{0,4},{2,6},{4,0},{6,2},{8,12},{10,14},{12,8},{14,10},{16,20},{18,... | collective-permute-start | bytes 368648 | tf_op jit(solution)/shard_map/ppermute | solution.py:885
  15.4 34.0 %copy-start.8 = (bf16[48,1280]{1,0:T(8,128)(2,1)}, bf16[48,1280]{1,0:T(8,128)(2,1)S(1)}, u32[]{:S(2)}) copy-start(bf16[48,1280]{1,0:T(8,128)(2,1)S(1)} %collective-permute-done.refs_3_) | copy-start | bytes 368644
  15.5 33.8 %copy-start.13 = (bf16[48,1280]{1,0:T(8,128)(2,1)}, bf16[48,1280]{1,0:T(8,128)(2,1)S(1)}, u32[]{:S(2)}) copy-start(bf16[48,1280]{1,0:T(8,128)(2,1)S(1)} %collective-permute-done.1.refs_2_) | copy-start | bytes 368644
  15.5 33.9 %copy-start.9 = (bf16[48,1280]{1,0:T(8,128)(2,1)}, bf16[48,1280]{1,0:T(8,128)(2,1)S(1)}, u32[]{:S(2)}) copy-start(bf16[48,1280]{1,0:T(8,128)(2,1)S(1)} %collective-permute-done.2.refs_1_) | copy-start | bytes 368644
  15.5 24.8 %copy-start.23 = (bf16[512,768]{1,0:T(8,128)(2,1)}, bf16[512,768]{1,0:T(8,128)(2,1)S(1)}, u32[]{:S(2)}) copy-start(bf16[512,768]{1,0:T(8,128)(2,1)S(1)} %collective-permute-done.3.cot_far) | copy-start | bytes 2359300
  15.6 8.5 %collective-permute-start.4 = (bf16[2,48,1280]{2,1,0:T(8,128)(2,1)S(1)}, bf16[2,48,1280]{2,1,0:T(8,128)(2,1)S(1)}, u32[]{:S(2)}, u32[]{:S(2)}) collective-permute-start(bf16[2,48,1280]{2,1,0:T(8,128)(2,1)S(1)} %pad_maximum_fusion.7), channel_id=1, source_target_pairs={{0,8},{2,10},{4,12},{6,14},{8,0},{10,2},{12,4},{14,6},{16,24},{18,... | collective-permute-start | bytes 737288 | tf_op jit(solution)/shard_map/ppermute | solution.py:885
  17.1 7.0 %collective-permute-start.5 = (bf16[48,1280]{1,0:T(8,128)(2,1)S(1)}, bf16[48,1280]{1,0:T(8,128)(2,1)S(1)}, u32[]{:S(2)}, u32[]{:S(2)}) collective-permute-start(bf16[48,1280]{1,0:T(8,128)(2,1)S(1)} %collective-permute-done.refs_3_), channel_id=1, source_target_pairs={{0,4},{2,6},{4,0},{6,2},{8,12},{10,14},{12,8},{14,10},{16,20},{18,... | collective-permute-start | bytes 368648 | tf_op jit(solution)/shard_map/ppermute | solution.py:885
  21.1 23.7 %collective-permute-start.7 = (bf16[7,48,768]{2,1,0:T(8,128)(2,1)}, bf16[7,48,768]{2,1,0:T(8,128)(2,1)S(1)}, u32[]{:S(2)}, u32[]{:S(2)}) collective-permute-start(bf16[7,48,768]{2,1,0:T(8,128)(2,1)} %get-tuple-element.171), channel_id=1, source_target_pairs={{0,8},{2,10},{4,12},{6,14},{8,0},{10,2},{12,4},{14,6},{16,24},{18,... | collective-permute-start | bytes 1548296 | tf_op jit(solution)/shard_map/ppermute | solution.py:885
  21.7 23.1 %collective-permute-start.8 = (bf16[7,48,768]{2,1,0:T(8,128)(2,1)}, bf16[7,48,768]{2,1,0:T(8,128)(2,1)S(1)}, u32[]{:S(2)}, u32[]{:S(2)}) collective-permute-start(bf16[7,48,768]{2,1,0:T(8,128)(2,1)} %get-tuple-element.171), channel_id=1, source_target_pairs={{0,16},{2,18},{4,20},{6,22},{8,24},{10,26},{12,28},{14,30},{16,0},... | collective-permute-start | bytes 1548296 | tf_op jit(solution)/shard_map/ppermute | solution.py:885
  23.6 16.7 %copy-start.26 = (bf16[512,768]{1,0:T(8,128)(2,1)}, bf16[512,768]{1,0:T(8,128)(2,1)S(1)}, u32[]{:S(2)}) copy-start(bf16[512,768]{1,0:T(8,128)(2,1)S(1)} %collective-permute-done.6.x_far) | copy-start | bytes 2359300
  23.6 21.3 %collective-permute-start.9 = (bf16[7,48,768]{2,1,0:T(8,128)(2,1)}, bf16[7,48,768]{2,1,0:T(8,128)(2,1)S(1)}, u32[]{:S(2)}, u32[]{:S(2)}) collective-permute-start(bf16[7,48,768]{2,1,0:T(8,128)(2,1)} %get-tuple-element.171), channel_id=1, source_target_pairs={{0,4},{2,6},{4,0},{6,2},{8,12},{10,14},{12,8},{14,10},{16,20},{18,... | collective-permute-start | bytes 1548296 | tf_op jit(solution)/shard_map/ppermute | solution.py:885
  24.1 25.4 %copy-start.14 = (bf16[48,1280]{1,0:T(8,128)(2,1)}, bf16[48,1280]{1,0:T(8,128)(2,1)S(1)}, u32[]{:S(2)}) copy-start(bf16[48,1280]{1,0:T(8,128)(2,1)S(1)} %collective-permute-done.5.refs_5_) | copy-start | bytes 368644
  24.1 25.4 %copy-start.1 = (bf16[2,48,1280]{2,1,0:T(8,128)(2,1)}, bf16[2,48,1280]{2,1,0:T(8,128)(2,1)S(1)}, u32[]{:S(2)}) copy-start(bf16[2,48,1280]{2,1,0:T(8,128)(2,1)S(1)} %collective-permute-done.4.refs_4_) | copy-start | bytes 737284
  24.2 20.7 %collective-permute-start.12 = (bf16[3,48,1280]{2,1,0:T(8,128)(2,1)S(1)}, bf16[3,48,1280]{2,1,0:T(8,128)(2,1)S(1)}, u32[]{:S(2)}, u32[]{:S(2)}) collective-permute-start(bf16[3,48,1280]{2,1,0:T(8,128)(2,1)S(1)} %pad_maximum_fusion.5), channel_id=1, source_target_pairs={{0,2},{2,0},{4,6},{6,4},{8,10},{10,8},{12,14},{14,12},{16,18},{18,... | collective-permute-start | bytes 1105928 | tf_op jit(solution)/shard_map/ppermute | solution.py:885
  24.3 16.0 %collective-permute-start.10 = (bf16[48,1280]{1,0:T(8,128)(2,1)S(1)}, bf16[48,1280]{1,0:T(8,128)(2,1)S(1)}, u32[]{:S(2)}, u32[]{:S(2)}) collective-permute-start(bf16[48,1280]{1,0:T(8,128)(2,1)S(1)} %slice_bitcast_fusion.6), channel_id=1, source_target_pairs={{0,4},{2,6},{4,0},{6,2},{8,12},{10,14},{12,8},{14,10},{16,20},{18,... | collective-permute-start | bytes 368648 | tf_op jit(solution)/shard_map/ppermute | solution.py:885
  40.2 1.3 collective-permute-start.11
  41.6 8.8 %collective-permute-start.13 = (bf16[4,48,1280]{2,1,0:T(8,128)(2,1)S(1)}, bf16[4,48,1280]{2,1,0:T(8,128)(2,1)S(1)}, u32[]{:S(2)}, u32[]{:S(2)}) collective-permute-start(bf16[4,48,1280]{2,1,0:T(8,128)(2,1)S(1)} %pad_maximum_fusion.3), channel_id=1, source_target_pairs={{0,2},{2,0},{4,6},{6,4},{8,10},{10,8},{12,14},{14,12},{16,18},{18,... | collective-permute-start | bytes 1474568 | tf_op jit(solution)/shard_map/ppermute | solution.py:885
  44.9 18.1 %copy-start = (bf16[7,48,768]{2,1,0:T(8,128)(2,1)}, bf16[7,48,768]{2,1,0:T(8,128)(2,1)S(1)}, u32[]{:S(2)}) copy-start(bf16[7,48,768]{2,1,0:T(8,128)(2,1)S(1)} %collective-permute-done.9.refs_1_) | copy-start | bytes 1548292
  44.9 15.6 %collective-permute-start.14 = (bf16[7,48,768]{2,1,0:T(8,128)(2,1)S(1)}, bf16[7,48,768]{2,1,0:T(8,128)(2,1)S(1)}, u32[]{:S(2)}, u32[]{:S(2)}) collective-permute-start(bf16[7,48,768]{2,1,0:T(8,128)(2,1)S(1)} %collective-permute-done.8.refs_3_), channel_id=1, source_target_pairs={{0,8},{2,10},{4,12},{6,14},{8,0},{10,2},{12,4},{14,6},{16,24},{18,... | collective-permute-start | bytes 1548296 | tf_op jit(solution)/shard_map/ppermute | solution.py:885
  48.0 12.5 %collective-permute-start.15 = (bf16[7,48,768]{2,1,0:T(8,128)(2,1)S(1)}, bf16[7,48,768]{2,1,0:T(8,128)(2,1)S(1)}, u32[]{:S(2)}, u32[]{:S(2)}) collective-permute-start(bf16[7,48,768]{2,1,0:T(8,128)(2,1)S(1)} %collective-permute-done.8.refs_3_), channel_id=1, source_target_pairs={{0,4},{2,6},{4,0},{6,2},{8,12},{10,14},{12,8},{14,10},{16,20},{18,... | collective-permute-start | bytes 1548296 | tf_op jit(solution)/shard_map/ppermute | solution.py:885
  49.5 11.0 %collective-permute-start.16 = (bf16[3,2,48,768]{3,2,1,0:T(8,128)(2,1)S(1)}, bf16[3,2,48,768]{3,2,1,0:T(8,128)(2,1)S(1)}, u32[]{:S(2)}, u32[]{:S(2)}) collective-permute-start(bf16[3,2,48,768]{3,2,1,0:T(8,128)(2,1)S(1)} %pad_maximum_fusion.4), channel_id=1, source_target_pairs={{0,1},{1,0},{2,3},{3,2},{4,5},{5,4},{6,7},{7,6},{8,9},{9,8},{10,11... | collective-permute-start | bytes 1327112 | tf_op jit(solution)/shard_map/ppermute | solution.py:885
  50.3 24.6 %collective-permute-start.20 = (bf16[3,7,48,768]{3,2,1,0:T(8,128)(2,1)S(1)}, bf16[3,7,48,768]{3,2,1,0:T(8,128)(2,1)S(1)}, u32[]{:S(2)}, u32[]{:S(2)}) collective-permute-start(bf16[3,7,48,768]{3,2,1,0:T(8,128)(2,1)S(1)} %pad_maximum_fusion), channel_id=1, source_target_pairs={{0,2},{2,0},{4,6},{6,4},{8,10},{10,8},{12,14},{14,12},{16,18},{18,... | collective-permute-start | bytes 4644872 | tf_op jit(solution)/shard_map/ppermute | solution.py:885
  50.4 13.5 %collective-permute-start.19 = (bf16[9,48,768]{2,1,0:T(8,128)(2,1)}, bf16[9,48,768]{2,1,0:T(8,128)(2,1)}, u32[]{:S(2)}, u32[]{:S(2)}) collective-permute-start(bf16[9,48,768]{2,1,0:T(8,128)(2,1)} %get-tuple-element.193.refs_0_), channel_id=1, source_target_pairs={{0,2},{2,0},{4,6},{6,4},{8,10},{10,8},{12,14},{14,12},{16,18},{18,... | collective-permute-start | bytes 1990664 | tf_op jit(solution)/shard_map/ppermute | solution.py:885
  60.4 29.4 %copy-start.25 = (bf16[3,2,48,768]{3,2,1,0:T(8,128)(2,1)}, bf16[3,2,48,768]{3,2,1,0:T(8,128)(2,1)S(1)}, u32[]{:S(2)}) copy-start(bf16[3,2,48,768]{3,2,1,0:T(8,128)(2,1)S(1)} %collective-permute-done.16.refs_8_) | copy-start | bytes 1327108
  60.5 14.4 %collective-permute-start.17 = (bf16[7,48,768]{2,1,0:T(8,128)(2,1)S(1)}, bf16[7,48,768]{2,1,0:T(8,128)(2,1)S(1)}, u32[]{:S(2)}, u32[]{:S(2)}) collective-permute-start(bf16[7,48,768]{2,1,0:T(8,128)(2,1)S(1)} %collective-permute-done.14.refs_4_), channel_id=1, source_target_pairs={{0,4},{2,6},{4,0},{6,2},{8,12},{10,14},{12,8},{14,10},{16,20},{18,... | collective-permute-start | bytes 1548296 | tf_op jit(solution)/shard_map/ppermute | solution.py:885
  62.2 25.3 %collective-permute-start.24 = (bf16[2,7,48,768]{3,2,1,0:T(8,128)(2,1)S(1)}, bf16[2,7,48,768]{3,2,1,0:T(8,128)(2,1)S(1)}, u32[]{:S(2)}, u32[]{:S(2)}) collective-permute-start(bf16[2,7,48,768]{3,2,1,0:T(8,128)(2,1)S(1)} %pad_maximum_fusion.1), channel_id=1, source_target_pairs={{0,2},{2,0},{4,6},{6,4},{8,10},{10,8},{12,14},{14,12},{16,18},{18,... | collective-permute-start | bytes 3096584 | tf_op jit(solution)/shard_map/ppermute | solution.py:885
  62.4 12.5 %collective-permute-start.18 = (bf16[2,2,48,768]{3,2,1,0:T(8,128)(2,1)S(1)}, bf16[2,2,48,768]{3,2,1,0:T(8,128)(2,1)S(1)}, u32[]{:S(2)}, u32[]{:S(2)}) collective-permute-start(bf16[2,2,48,768]{3,2,1,0:T(8,128)(2,1)S(1)} %pad_maximum_fusion.6), channel_id=1, source_target_pairs={{0,1},{1,0},{2,3},{3,2},{4,5},{5,4},{6,7},{7,6},{8,9},{9,8},{10,11... | collective-permute-start | bytes 884744 | tf_op jit(solution)/shard_map/ppermute | solution.py:885
  63.9 23.6 %collective-permute-start.21 = (bf16[9,48,768]{2,1,0:T(8,128)(2,1)}, bf16[9,48,768]{2,1,0:T(8,128)(2,1)}, u32[]{:S(2)}, u32[]{:S(2)}) collective-permute-start(bf16[9,48,768]{2,1,0:T(8,128)(2,1)} %pad_maximum_fusion.2), channel_id=1, source_target_pairs={{0,8},{2,10},{4,12},{6,14},{8,0},{10,2},{12,4},{14,6},{16,24},{18,... | collective-permute-start | bytes 1990664 | tf_op jit(solution)/shard_map/ppermute | solution.py:885
  74.8 15.1 %copy-start.40 = (bf16[2,2,48,768]{3,2,1,0:T(8,128)(2,1)}, bf16[2,2,48,768]{3,2,1,0:T(8,128)(2,1)S(1)}, u32[]{:S(2)}) copy-start(bf16[2,2,48,768]{3,2,1,0:T(8,128)(2,1)S(1)} %collective-permute-done.18.refs_9_) | copy-start | bytes 884740
  74.9 14.4 %collective-permute-start.22 = (bf16[384,512]{1,0:T(8,128)(2,1)}, bf16[384,512]{1,0:T(8,128)(2,1)S(1)}, u32[]{:S(2)}, u32[]{:S(2)}) collective-permute-start(bf16[384,512]{1,0:T(8,128)(2,1)} %get-tuple-element.198.out), channel_id=1, source_target_pairs={{0,1},{1,0},{2,3},{3,2},{4,5},{5,4},{6,7},{7,6},{8,9},{9,8},{10,11... | collective-permute-start | bytes 1179656 | tf_op jit(solution)/shard_map/ppermute | solution.py:885
  76.5 12.8 %collective-permute-start.23 = (bf16[2,48,768]{2,1,0:T(8,128)(2,1)S(1)}, bf16[2,48,768]{2,1,0:T(8,128)(2,1)S(1)}, u32[]{:S(2)}, u32[]{:S(2)}) collective-permute-start(bf16[2,48,768]{2,1,0:T(8,128)(2,1)S(1)} %slice.34), channel_id=1, source_target_pairs={{0,1},{1,0},{2,3},{3,2},{4,5},{5,4},{6,7},{7,6},{8,9},{9,8},{10,11... | collective-permute-start | bytes 442376 | tf_op jit(solution)/shard_map/ppermute | solution.py:885
  89.3 4.2 %collective-permute-start.25 = (bf16[9,48,768]{2,1,0:T(8,128)(2,1)}, bf16[9,48,768]{2,1,0:T(8,128)(2,1)S(1)}, u32[]{:S(2)}, u32[]{:S(2)}) collective-permute-start(bf16[9,48,768]{2,1,0:T(8,128)(2,1)} %collective-permute-done.21.refs_6_), channel_id=1, source_target_pairs={{0,2},{2,0},{4,6},{6,4},{8,10},{10,8},{12,14},{14,12},{16,18},{18,... | collective-permute-start | bytes 1990664 | tf_op jit(solution)/shard_map/ppermute | solution.py:885
  89.4 4.1 %collective-permute-start.26 = (bf16[7,48,768]{2,1,0:T(8,128)(2,1)S(1)}, bf16[7,48,768]{2,1,0:T(8,128)(2,1)S(1)}, u32[]{:S(2)}, u32[]{:S(2)}) collective-permute-start(bf16[7,48,768]{2,1,0:T(8,128)(2,1)S(1)} %collective-permute-done.17.refs_7_), channel_id=1, source_target_pairs={{0,2},{2,0},{4,6},{6,4},{8,10},{10,8},{12,14},{14,12},{16,18},{18,... | collective-permute-start | bytes 1548296 | tf_op jit(solution)/shard_map/ppermute | solution.py:885
  89.9 3.6 %collective-permute-start.27 = (bf16[3,2,48,768]{3,2,1,0:T(8,128)(2,1)S(1)}, bf16[3,2,48,768]{3,2,1,0:T(8,128)(2,1)S(1)}, u32[]{:S(2)}, u32[]{:S(2)}) collective-permute-start(bf16[3,2,48,768]{3,2,1,0:T(8,128)(2,1)S(1)} %collective-permute-done.16.refs_8_), channel_id=1, source_target_pairs={{0,2},{2,0},{4,6},{6,4},{8,10},{10,8},{12,14},{14,12},{16,18},{18,... | collective-permute-start | bytes 1327112 | tf_op jit(solution)/shard_map/ppermute | solution.py:885
  90.0 3.5 %collective-permute-start.28 = (bf16[2,2,48,768]{3,2,1,0:T(8,128)(2,1)S(1)}, bf16[2,2,48,768]{3,2,1,0:T(8,128)(2,1)S(1)}, u32[]{:S(2)}, u32[]{:S(2)}) collective-permute-start(bf16[2,2,48,768]{3,2,1,0:T(8,128)(2,1)S(1)} %collective-permute-done.18.refs_9_), channel_id=1, source_target_pairs={{0,2},{2,0},{4,6},{6,4},{8,10},{10,8},{12,14},{14,12},{16,18},{18,... | collective-permute-start | bytes 884744 | tf_op jit(solution)/shard_map/ppermute | solution.py:885
  90.4 3.1 %collective-permute-start.29 = (bf16[2,48,768]{2,1,0:T(8,128)(2,1)S(1)}, bf16[2,48,768]{2,1,0:T(8,128)(2,1)S(1)}, u32[]{:S(2)}, u32[]{:S(2)}) collective-permute-start(bf16[2,48,768]{2,1,0:T(8,128)(2,1)S(1)} %collective-permute-done.23.refs_10_), channel_id=1, source_target_pairs={{0,2},{2,0},{4,6},{6,4},{8,10},{10,8},{12,14},{14,12},{16,18},{18,... | collective-permute-start | bytes 442376 | tf_op jit(solution)/shard_map/ppermute | solution.py:885
  117.9 13.7 %collective-permute-start.32 = (bf16[5,512,768]{2,1,0:T(8,128)(2,1)}, bf16[5,512,768]{2,1,0:T(8,128)(2,1)}, u32[]{:S(2)}, u32[]{:S(2)}) collective-permute-start(bf16[5,512,768]{2,1,0:T(8,128)(2,1)} %get-tuple-element.224.pre), channel_id=1, source_target_pairs={{0,2},{2,0},{4,6},{6,4},{8,10},{10,8},{12,14},{14,12},{16,18},{18,... | collective-permute-start | bytes 11796488 | tf_op jit(solution)/shard_map/ppermute | solution.py:885
  118.1 22.5 %collective-permute-start.33 = (bf16[4,512,384]{2,1,0:T(8,128)(2,1)}, bf16[4,512,384]{2,1,0:T(8,128)(2,1)}, u32[]{:S(2)}, u32[]{:S(2)}) collective-permute-start(bf16[4,512,384]{2,1,0:T(8,128)(2,1)} %get-tuple-element.227), channel_id=1, source_target_pairs={{0,2},{2,0},{4,6},{6,4},{8,10},{10,8},{12,14},{14,12},{16,18},{18,... | collective-permute-start | bytes 4718600 | tf_op jit(solution)/shard_map/ppermute | solution.py:885
  118.4 13.1 %collective-permute-start.31 = (bf16[2,8,48,512]{3,2,1,0:T(8,128)(2,1)}, bf16[2,8,48,512]{3,2,1,0:T(8,128)(2,1)}, u32[]{:S(2)}, u32[]{:S(2)}) collective-permute-start(bf16[2,8,48,512]{3,2,1,0:T(8,128)(2,1)} %get-tuple-element.223), channel_id=1, source_target_pairs={{0,2},{2,0},{4,6},{6,4},{8,10},{10,8},{12,14},{14,12},{16,18},{18,... | collective-permute-start | bytes 2359304 | tf_op jit(solution)/shard_map/ppermute | solution.py:885
  118.6 13.0 %collective-permute-start.30 = (bf16[384,512]{1,0:T(8,128)(2,1)}, bf16[384,512]{1,0:T(8,128)(2,1)}, u32[]{:S(2)}, u32[]{:S(2)}) collective-permute-start(bf16[384,512]{1,0:T(8,128)(2,1)} %get-tuple-element.220), channel_id=1, source_target_pairs={{0,1},{1,0},{2,3},{3,2},{4,5},{5,4},{6,7},{7,6},{8,9},{9,8},{10,11... | collective-permute-start | bytes 1179656 | tf_op jit(solution)/shard_map/ppermute | solution.py:885
  140.0 22.3 %collective-permute-start.34 = (bf16[4,3,48,768]{3,2,1,0:T(8,128)(2,1)}, bf16[4,3,48,768]{3,2,1,0:T(8,128)(2,1)S(1)}, u32[]{:S(2)}, u32[]{:S(2)}) collective-permute-start(bf16[4,3,48,768]{3,2,1,0:T(8,128)(2,1)} %get-tuple-element.225), channel_id=1, source_target_pairs={{0,4},{2,6},{4,0},{6,2},{8,12},{10,14},{12,8},{14,10},{16,20},{18,... | collective-permute-start | bytes 2654216 | tf_op jit(solution)/shard_map/ppermute | solution.py:885
  146.8 27.9 %collective-permute-start.36 = (bf16[8,2,48,768]{3,2,1,0:T(8,128)(2,1)}, bf16[8,2,48,768]{3,2,1,0:T(8,128)(2,1)S(1)}, u32[]{:S(2)}, u32[]{:S(2)}) collective-permute-start(bf16[8,2,48,768]{3,2,1,0:T(8,128)(2,1)} %get-tuple-element.229), channel_id=1, source_target_pairs={{0,1},{1,0},{2,3},{3,2},{4,5},{5,4},{6,7},{7,6},{8,9},{9,8},{10,11... | collective-permute-start | bytes 3538952 | tf_op jit(solution)/shard_map/ppermute | solution.py:885
  147.4 17.2 %collective-permute-start.35 = (bf16[2,2,2,48,768]{4,3,2,0,1:T(8,128)(2,1)S(1)}, bf16[2,2,2,48,768]{4,3,2,0,1:T(8,128)(2,1)S(1)}, u32[]{:S(2)}, u32[]{:S(2)}) collective-permute-start(bf16[2,2,2,48,768]{4,3,2,0,1:T(8,128)(2,1)S(1)} %copy.32), channel_id=1, source_target_pairs={{0,8},{2,10},{4,12},{6,14},{8,0},{10,2},{12,4},{14,6},{16,24},{18,... | collective-permute-start | bytes 1769480 | tf_op jit(solution)/shard_map/ppermute | solution.py:885
  149.1 15.4 %copy-start.29 = (bf16[2,2,2,48,768]{4,3,2,1,0:T(8,128)(2,1)S(1)}, bf16[2,2,2,48,768]{4,3,2,1,0:T(8,128)(2,1)}, u32[]{:S(2)}) copy-start(bf16[2,2,2,48,768]{4,3,2,1,0:T(8,128)(2,1)} %get-tuple-element.263) | copy-start | bytes 1769476
  163.3 11.6 %collective-permute-start.37 = (bf16[2,3,48,768]{3,2,1,0:T(8,128)(2,1)}, bf16[2,3,48,768]{3,2,1,0:T(8,128)(2,1)}, u32[]{:S(2)}, u32[]{:S(2)}) collective-permute-start(bf16[2,3,48,768]{3,2,1,0:T(8,128)(2,1)} %fusion.6), channel_id=1, source_target_pairs={{0,8},{2,10},{4,12},{6,14},{8,0},{10,2},{12,4},{14,6},{16,24},{18,... | collective-permute-start | bytes 1327112 | tf_op jit(solution)/shard_map/ppermute | solution.py:885
  165.5 8.2 %collective-permute-start.38 = (bf16[2,2,48,768]{3,2,1,0:T(8,128)(2,1)}, bf16[2,2,48,768]{3,2,1,0:T(8,128)(2,1)}, u32[]{:S(2)}, u32[]{:S(2)}) collective-permute-start(bf16[2,2,48,768]{3,2,1,0:T(8,128)(2,1)} %fusion.10), channel_id=1, source_target_pairs={{0,4},{2,6},{4,0},{6,2},{8,12},{10,14},{12,8},{14,10},{16,20},{18,... | collective-permute-start | bytes 884744 | tf_op jit(solution)/shard_map/ppermute | solution.py:885
  173.0 3.1 %collective-permute-start.39 = (bf16[8,48,1280]{2,1,0:T(8,128)(2,1)}, bf16[8,48,1280]{2,1,0:T(8,128)(2,1)}, u32[]{:S(2)}, u32[]{:S(2)}) collective-permute-start(bf16[8,48,1280]{2,1,0:T(8,128)(2,1)} %get-tuple-element.252), channel_id=1, source_target_pairs={{0,2},{2,0},{4,6},{6,4},{8,10},{10,8},{12,14},{14,12},{16,18},{18,... | collective-permute-start | bytes 2949128 | tf_op jit(solution)/shard_map/ppermute | solution.py:885
  179.2 15.4 %collective-permute-start.40 = (bf16[2,2,2,48,768]{4,3,2,1,0:T(8,128)(2,1)}, bf16[2,2,2,48,768]{4,3,2,1,0:T(8,128)(2,1)S(1)}, u32[]{:S(2)}, u32[]{:S(2)}) collective-permute-start(bf16[2,2,2,48,768]{4,3,2,1,0:T(8,128)(2,1)} %fusion.1), channel_id=1, source_target_pairs={{0,4},{2,6},{4,0},{6,2},{8,12},{10,14},{12,8},{14,10},{16,20},{18,... | collective-permute-start | bytes 1769480 | tf_op jit(solution)/shard_map/ppermute | solution.py:885
  180.8 18.1 %collective-permute-start.42 = (bf16[2,2,48,1280]{3,2,1,0:T(8,128)(2,1)}, bf16[2,2,48,1280]{3,2,1,0:T(8,128)(2,1)}, u32[]{:S(2)}, u32[]{:S(2)}) collective-permute-start(bf16[2,2,48,1280]{3,2,1,0:T(8,128)(2,1)} %fusion.4), channel_id=1, source_target_pairs={{0,8},{2,10},{4,12},{6,14},{8,0},{10,2},{12,4},{14,6},{16,24},{18,... | collective-permute-start | bytes 1474568 | tf_op jit(solution)/shard_map/ppermute | solution.py:885
  185.4 11.0 %collective-permute-start.41 = (bf16[2,5,48,384]{3,2,1,0:T(8,128)(2,1)}, bf16[2,5,48,384]{3,2,1,0:T(8,128)(2,1)}, u32[]{:S(2)}, u32[]{:S(2)}) collective-permute-start(bf16[2,5,48,384]{3,2,1,0:T(8,128)(2,1)} %get-tuple-element.266), channel_id=1, source_target_pairs={{0,1},{1,0},{2,3},{3,2},{4,5},{5,4},{6,7},{7,6},{8,9},{9,8},{10,11... | collective-permute-start | bytes 1105928 | tf_op jit(solution)/shard_map/ppermute | solution.py:885
  192.2 21.2 %collective-permute-start.46 = (bf16[512,768]{1,0:T(8,128)(2,1)}, bf16[512,768]{1,0:T(8,128)(2,1)S(1)}, u32[]{:S(2)}, u32[]{:S(2)}) collective-permute-start(bf16[512,768]{1,0:T(8,128)(2,1)} %get-tuple-element.296), channel_id=1, source_target_pairs={{0,1},{1,0},{2,3},{3,2},{4,5},{5,4},{6,7},{7,6},{8,9},{9,8},{10,11... | collective-permute-start | bytes 2359304 | tf_op jit(solution)/shard_map/ppermute | solution.py:885
  194.7 12.1 %collective-permute-start.43 = (bf16[2,2,48,768]{3,2,1,0:T(8,128)(2,1)S(1)}, bf16[2,2,48,768]{3,2,1,0:T(8,128)(2,1)S(1)}, u32[]{:S(2)}, u32[]{:S(2)}) collective-permute-start(bf16[2,2,48,768]{3,2,1,0:T(8,128)(2,1)S(1)} %fusion.2), channel_id=1, source_target_pairs={{0,8},{2,10},{4,12},{6,14},{8,0},{10,2},{12,4},{14,6},{16,24},{18,... | collective-permute-start | bytes 884744 | tf_op jit(solution)/shard_map/ppermute | solution.py:885
  197.4 10.6 %collective-permute-start.44 = (bf16[5,48,384]{2,1,0:T(8,128)(2,1)S(1)}, bf16[5,48,384]{2,1,0:T(8,128)(2,1)S(1)}, u32[]{:S(2)}, u32[]{:S(2)}) collective-permute-start(bf16[5,48,384]{2,1,0:T(8,128)(2,1)S(1)} %fusion.17), channel_id=1, source_target_pairs={{0,16},{2,18},{4,20},{6,22},{8,24},{10,26},{12,28},{14,30},{16,0},... | collective-permute-start | bytes 552968 | tf_op jit(solution)/shard_map/ppermute | solution.py:885
  200.1 9.0 %collective-permute-start.45 = (bf16[2,48,1280]{2,1,0:T(8,128)(2,1)S(1)}, bf16[2,48,1280]{2,1,0:T(8,128)(2,1)S(1)}, u32[]{:S(2)}, u32[]{:S(2)}) collective-permute-start(bf16[2,48,1280]{2,1,0:T(8,128)(2,1)S(1)} %fusion.5), channel_id=1, source_target_pairs={{0,4},{2,6},{4,0},{6,2},{8,12},{10,14},{12,8},{14,10},{16,20},{18,... | collective-permute-start | bytes 737288 | tf_op jit(solution)/shard_map/ppermute | solution.py:885
  206.9 11.5 %collective-permute-start.47 = (bf16[2,48,768]{2,1,0:T(8,128)(2,1)S(1)}, bf16[2,48,768]{2,1,0:T(8,128)(2,1)S(1)}, u32[]{:S(2)}, u32[]{:S(2)}) collective-permute-start(bf16[2,48,768]{2,1,0:T(8,128)(2,1)S(1)} %fusion.13), channel_id=1, source_target_pairs={{0,16},{2,18},{4,20},{6,22},{8,24},{10,26},{12,28},{14,30},{16,0},... | collective-permute-start | bytes 442376 | tf_op jit(solution)/shard_map/ppermute | solution.py:885
  210.1 10.4 %collective-permute-start.48 = (bf16[48,1280]{1,0:T(8,128)(2,1)S(1)}, bf16[48,1280]{1,0:T(8,128)(2,1)S(1)}, u32[]{:S(2)}, u32[]{:S(2)}) collective-permute-start(bf16[48,1280]{1,0:T(8,128)(2,1)S(1)} %fusion.16), channel_id=1, source_target_pairs={{0,16},{2,18},{4,20},{6,22},{8,24},{10,26},{12,28},{14,30},{16,0},... | collective-permute-start | bytes 368648 | tf_op jit(solution)/shard_map/ppermute | solution.py:885
  212.1 10.3 %collective-permute-start.49 = (bf16[5,48,384]{2,1,0:T(8,128)(2,1)S(1)}, bf16[5,48,384]{2,1,0:T(8,128)(2,1)}, u32[]{:S(2)}, u32[]{:S(2)}) collective-permute-start(bf16[5,48,384]{2,1,0:T(8,128)(2,1)S(1)} %fusion.9.b_near), channel_id=1, source_target_pairs={{0,1},{1,0},{2,3},{3,2},{4,5},{5,4},{6,7},{7,6},{8,9},{9,8},{10,11... | collective-permute-start | bytes 552968 | tf_op jit(solution)/shard_map/ppermute | solution.py:885
  219.2 7.4 %collective-permute-start.50 = (bf16[2,48,768]{2,1,0:T(8,128)(2,1)}, bf16[2,48,768]{2,1,0:T(8,128)(2,1)}, u32[]{:S(2)}, u32[]{:S(2)}) collective-permute-start(bf16[2,48,768]{2,1,0:T(8,128)(2,1)} %fusion.12.a_near), channel_id=1, source_target_pairs={{0,1},{1,0},{2,3},{3,2},{4,5},{5,4},{6,7},{7,6},{8,9},{9,8},{10,11... | collective-permute-start | bytes 442376 | tf_op jit(solution)/shard_map/ppermute | solution.py:885
  221.5 5.1 %collective-permute-start.51 = (bf16[48,1280]{1,0:T(8,128)(2,1)S(1)}, bf16[48,1280]{1,0:T(8,128)(2,1)}, u32[]{:S(2)}, u32[]{:S(2)}) collective-permute-start(bf16[48,1280]{1,0:T(8,128)(2,1)S(1)} %fusion.15.g_near), channel_id=1, source_target_pairs={{0,1},{1,0},{2,3},{3,2},{4,5},{5,4},{6,7},{7,6},{8,9},{9,8},{10,11... | collective-permute-start | bytes 368648 | tf_op jit(solution)/shard_map/ppermute | solution.py:885
  (32 other events, 175.1 us)

commit v8 on v7

--- a/solution.py
+++ b/solution.py
@@ -62,8 +62,9 @@
     side[...] = jnp.zeros((8, 128), f32)
     side[0:1, 0:48] = gain_one[...].astype(f32)
     side[1:2, 0:48] = gain_two[...].astype(f32)
-    side[2:3, 0:12] = table[0:1].astype(f32)
-    side[2:3, 12:24] = table[1:2].astype(f32)
+    rows = table[...].astype(f32)
+    side[2:3, 0:12] = rows[0:1]
+    side[2:3, 12:24] = rows[1:2]
     wide = jnp.concatenate([side[...], jnp.zeros((120, 128), f32)], axis=0).T
     out[:, 1152:1280] = wide[0:48].astype(bf16)
 
@@ -703,8 +704,8 @@
         spot = iota((384, 128), 0) % 48
         bucket = ((iota((384, 128), 0) // 48) * 2 + kind) * 2 + spot // 6
         chosen = jnp.where((iota((384, 128), 1) == bucket) & (spot < 12), 1.0, 0.0)
-        per_head = dot(chosen.astype(bf16), bias[0:8], 1, 1)
-        pattern = (iota((384, 8), 1) == (iota((384, 8), 0) % 48) % 6).astype(f32)
+        per_head = dot(chosen.astype(bf16), bias[...], 1, 1)
+        pattern = (iota((384, 16), 1) == (iota((384, 16), 0) % 48) % 6).astype(f32)
         column = jnp.sum(per_head * pattern, axis=1, keepdims=True)
         side = jnp.where(iota((384, 128), 1) == 0, column, 0.0)
         dest[:, :, 1152:1280] = side.astype(bf16).reshape(8, 48, 128)

time: 230 us -> 230 us (level)
  no operation moved by 1% of the time
where the time goes in v8:
time: 230 us; the launch traced here: 229 us
  Pallas kernels  118 us (51%)
  starting transfers between devices  60.7 us (26%)
  waiting for transfers between devices  27 us (12%)
  other arithmetic  16.3 us (7%)
  between operations  3.36 us (1%)
  local copies, waits for them, and re-layouts  3.28 us (1%)
    ppermute x52, starting transfers between devices, swap(): return lax.ppermute(array, axis, [(i, i ^ bit) for i in range(count)])  60.7 us
    ppermute x52, waiting for transfers between devices, swap(): return lax.ppermute(array, axis, [(i, i ^ bit) for i in range(count)])  27 us
    pallas_call x2, Pallas kernels, attend_back(): pl.pallas_call(functools.partial(attend_back_kernel, bool(carry), mine),...  24.6 us
    pallas_call x1, Pallas kernels, forward(): pl.pallas_call(forward_kernel, out_shape=(hidden, hidden, jax.ShapeDtypeS...  23 us
    pallas_call x2, Pallas kernels, attend(): pl.pallas_call(functools.partial(attend_kernel, mine), out_shape=(jax.Sha...  21 us
    convert_element_type x12, other arithmetic, total(): made = lax.optimization_barrier(made.astype(bf16))  11.2 us
    pallas_call x1, Pallas kernels, expand_weight_grad(): pl.pallas_call(expand_grad_kernel, out_shape=(first, first, second, secon...  8.37 us
    pallas_call x1, Pallas kernels, project(): pl.pallas_call(project_kernel, out_shape=(jax.ShapeDtypeStruct((1152, 102...  7.72 us
  transfers between devices with their start and end apart: 52, of which 16 were waited for; matrix products, arithmetic and copies ran while one was open for 6% of the time, Pallas kernels for 41%

profile of v8, /device:TPU:0, one launch (start us, length us, event | category | flops | bytes accessed | tf_op | source)
XLA Modules:
  0.0 229.0 jit_solution(15142446545041457495)
XLA Ops:
  1.2 2.6 %collective-permute-start.6 = (bf16[512,768]{1,0:T(8,128)(2,1)}, bf16[512,768]{1,0:T(8,128)(2,1)S(1)}, u32[]{:S(2)}, u32[]{:S(2)}) collective-permute-start(bf16[512,768]{1,0:T(8,128)(2,1)} %bitcast.106), channel_id=1, source_target_pairs={{0,1},{1,0},{2,3},{3,2},{4,5},{5,4},{6,7},{7,6},{8,9},{9,8},{10,11... | collective-permute-start | bytes 2359304 | tf_op jit(solution)/shard_map/ppermute | solution.py:886
  4.3 1.8 narrow_shard.1.refs_0_
  6.1 2.6 %collective-permute-start = (bf16[48,1280]{1,0:T(8,128)(2,1)}, bf16[48,1280]{1,0:T(8,128)(2,1)S(1)}, u32[]{:S(2)}, u32[]{:S(2)}) collective-permute-start(bf16[48,1280]{1,0:T(8,128)(2,1)} %narrow_shard.1.refs_0_), channel_id=1, source_target_pairs={{0,16},{2,18},{4,20},{6,22},{8,24},{10,26},{12,28},{14,30},{16,0},... | collective-permute-start | bytes 368648 | tf_op jit(solution)/shard_map/ppermute | solution.py:886
  8.7 1.6 collective-permute-start.1
  10.3 1.5 collective-permute-start.2
  11.8 2.9 %wide_shard.1 = (bf16[7,48,768]{2,1,0:T(8,128)(2,1)}, bf16[9,48,768]{2,1,0:T(8,128)(2,1)}) custom-call(s32[4]{0:T(128)} %pad_add_fusion.place, bf16[48,3072]{1,0:T(8,128)(2,1)} %up.1, bf16[48,768]{1,0:T(8,128)(2,1)} %output.1, bf16[192,768]{1,0:T(8,128)(2,1)} %contract.1), custom_call_target="tpu_custom_call" | custom-call | flops 1000 | bytes 1000 | tf_op jit(solution)/shard_map/wide_shard/pallas_call | solution.py:103
  15.6 1.5 collective-permute-start.4
  17.1 1.5 collective-permute-start.5
  21.7 1.8 collective-permute-start.8
  24.3 12.0 %collective-permute-start.10 = (bf16[48,1280]{1,0:T(8,128)(2,1)S(1)}, bf16[48,1280]{1,0:T(8,128)(2,1)S(1)}, u32[]{:S(2)}, u32[]{:S(2)}) collective-permute-start(bf16[48,1280]{1,0:T(8,128)(2,1)S(1)} %slice_bitcast_fusion.6), channel_id=1, source_target_pairs={{0,4},{2,6},{4,0},{6,2},{8,12},{10,14},{12,8},{14,10},{16,20},{18,... | collective-permute-start | bytes 368648 | tf_op jit(solution)/shard_map/ppermute | solution.py:886
  36.2 4.0 %collective-permute-done.10.refs_6_ = bf16[48,1280]{1,0:T(8,128)(2,1)S(1)} collective-permute-done((bf16[48,1280]{1,0:T(8,128)(2,1)S(1)}, bf16[48,1280]{1,0:T(8,128)(2,1)S(1)}, u32[]{:S(2)}, u32[]{:S(2)}) %collective-permute-start.10) | collective-permute-done | bytes 122912 | tf_op jit(solution)/shard_map/ppermute | solution.py:886
  40.3 1.2 collective-permute-done.11.refs_9_
  41.7 3.1 %collective-permute-done.7.refs_2_ = bf16[7,48,768]{2,1,0:T(8,128)(2,1)S(1)} collective-permute-done((bf16[7,48,768]{2,1,0:T(8,128)(2,1)}, bf16[7,48,768]{2,1,0:T(8,128)(2,1)S(1)}, u32[]{:S(2)}, u32[]{:S(2)}) %collective-permute-start.7) | collective-permute-done | bytes 516128 | tf_op jit(solution)/shard_map/ppermute | solution.py:886
  44.9 3.1 %collective-permute-start.14 = (bf16[7,48,768]{2,1,0:T(8,128)(2,1)S(1)}, bf16[7,48,768]{2,1,0:T(8,128)(2,1)S(1)}, u32[]{:S(2)}, u32[]{:S(2)}) collective-permute-start(bf16[7,48,768]{2,1,0:T(8,128)(2,1)S(1)} %collective-permute-done.8.refs_3_), channel_id=1, source_target_pairs={{0,8},{2,10},{4,12},{6,14},{8,0},{10,2},{12,4},{14,6},{16,24},{18,... | collective-permute-start | bytes 1548296 | tf_op jit(solution)/shard_map/ppermute | solution.py:886
  48.0 1.3 collective-permute-start.15
  51.2 7.7 %project.1 = (bf16[1152,1024]{1,0:T(8,128)(2,1)}, bf16[8,48,1024]{2,1,0:T(8,128)(2,1)}, bf16[8,48,1024]{2,1,0:T(8,128)(2,1)}, f32[8,768]{1,0:T(8,128)}, f32[8,128]{1,0:T(8,128)}, /*index=5*/f32[6,384,128]{2,1,0:T(8,128)}) custom-call(s32[7]{0:T(128)} %concatenate.11.place, bf16[512,768]{1,0:T(8,128)(2,1)} %bitcast.107, bf16[512,768]{1,0:T(8,128)(2,1)} %copy-done.26, ...), custom_call_target="tpu_custom_call" | custom-call | flops 1000 | bytes 1000 | tf_op jit(solution)/shard_map/project/pallas_call | solution.py:195
  58.9 1.5 collective-permute-done.16.refs_8_
  60.5 1.6 collective-permute-start.17
  63.0 0.9 pad_maximum_fusion.2
  64.2 10.6 %attend_theirs.1 = (bf16[384,512]{1,0:T(8,128)(2,1)}, bf16[6,1024,512]{2,1,0:T(8,128)(2,1)}, f32[6,1,512]{2,1,0:T(1,128)}) custom-call(s32[7]{0:T(128)} %concatenate.11.place, f32[8,128]{1,0:T(8,128)} %get-tuple-element.189.table, f32[6,384,128]{2,1,0:T(8,128)} %get-tuple-element.190.tile, bf16[1152,1024]{1,0:T(8,128)(2,1)} %get-tuple-element.182.q.k.v, ...), custom_call_target="tpu_custom_call" | custom-call | flops 1000 | bytes 1000 | tf_op jit(solution)/shard_map/attend_theirs/pallas_call | solution.py:290
  74.9 1.6 collective-permute-start.22
  77.1 10.4 %attend_mine.1 = (bf16[384,512]{1,0:T(8,128)(2,1)}, bf16[6,1024,512]{2,1,0:T(8,128)(2,1)}, f32[6,1,512]{2,1,0:T(1,128)}) custom-call(s32[7]{0:T(128)} %concatenate.11.place, f32[8,128]{1,0:T(8,128)} %get-tuple-element.189.table, f32[6,384,128]{2,1,0:T(8,128)} %get-tuple-element.190.tile, bf16[1152,1024]{1,0:T(8,128)(2,1)} %get-tuple-element.182.q.k.v, ...), custom_call_target="tpu_custom_call" | custom-call | flops 1000 | bytes 1000 | tf_op jit(solution)/shard_map/attend_mine/pallas_call | solution.py:290
  87.5 1.8 collective-permute-done.23.refs_10_
  90.5 3.0 %collective-permute-done.29.refs_18_ = bf16[2,48,768]{2,1,0:T(8,128)(2,1)S(1)} collective-permute-done((bf16[2,48,768]{2,1,0:T(8,128)(2,1)S(1)}, bf16[2,48,768]{2,1,0:T(8,128)(2,1)S(1)}, u32[]{:S(2)}, u32[]{:S(2)}) %collective-permute-start.29) | collective-permute-done | bytes 147488 | tf_op jit(solution)/shard_map/ppermute | solution.py:886
  94.8 23.0 %forward.1 = (bf16[4,512,384]{2,1,0:T(8,128)(2,1)}, bf16[4,512,384]{2,1,0:T(8,128)(2,1)}, bf16[5,512,768]{2,1,0:T(8,128)(2,1)}, bf16[2,8,48,512]{3,2,1,0:T(8,128...) custom-call(s32[7]{0:T(128)} %concatenate.11.place, ...), custom_call_target="tpu_custom_call" | custom-call | flops 8500000 | bytes 20000 | tf_op jit(solution)/shard_map/forward/pallas_call | solution.py:586
  118.6 1.5 collective-permute-start.30
  120.1 11.5 %attend_back_mine.1 = (bf16[384,512]{1,0:T(8,128)(2,1)}, f32[384,1024]{1,0:T(8,128)}, f32[384,1024]{1,0:T(8,128)}, f32[6,384,128]{2,1,0:T(8,128)}, f32[6,8,512]{2,1,0:T(8,128)}) custom-call(s32[7]{0:T(128)} %concatenate.11.place, bf16[384,512]{1,0:T(8,128)(2,1)} %get-tuple-element.215.grad, bf16[384,512]{1,0:T(8,128)(2,1)} %get-tuple-element.201.att_near.out, ...), custom_call_target="tpu_custom_call" | custom-call | flops 3221225 | bytes 6000 | tf_op jit(solution)/shard_map/attend_back_mine/pallas_call | solution.py:452
  131.6 8.4 %expand_weight_grad.1 = (bf16[4,3,48,768]{3,2,1,0:T(8,128)(2,1)}, bf16[4,3,48,768]{3,2,1,0:T(8,128)(2,1)}, bf16[2,2,2,48,768]{4,3,2,1,0:T(8,128)(2,1)}, bf16[2,2,2,48,768]{4,3,2,1,0:T(8,128)(2,1)}) custom-call(s32[7]{0:T(128)} %concatenate.11.place, bf16[2,8,48,512]{3,2,1,0:T(8,128)(2,1)} %get-tuple-element.222.turned, ...), custom_call_target="tpu_custom_call" | custom-call | flops 3019898 | bytes 12000 | tf_op jit(solution)/shard_map/expand_weight_grad/pallas_call | solution.py:676
  140.5 6.3 %contract_weight_grad.1 = (bf16[8,2,48,768]{3,2,1,0:T(8,128)(2,1)}, bf16[8,2,48,768]{3,2,1,0:T(8,128)(2,1)}) custom-call(s32[7]{0:T(128)} %concatenate.11.place, bf16[4,512,384]{2,1,0:T(8,128)(2,1)} %get-tuple-element.213.hid, bf16[4,512,384]{2,1,0:T(8,128)(2,1)} %collective-permute-done.33.hid_far, bf16[512,768]{1,0:T(8,128)(2,1)} %bitcast.113, ...), custom_call_target="tpu_custom_call" | custom-call | flops 2415919 | bytes 9000 | tf_op jit(solution)/shard_map/contract_weight_grad/pallas_call | solution.py:629
  147.4 1.7 collective-permute-start.35
  149.1 13.1 %attend_back_theirs.1.whole.refs_10_ = bf16[6,208,1024]{2,1,0:T(8,128)(2,1)} custom-call(s32[7]{0:T(128)} %concatenate.11.place, bf16[384,512]{1,0:T(8,128)(2,1)} %collective-permute-done.30.grad, bf16[384,512]{1,0:T(8,128)(2,1)} %get-tuple-element.198.out, f32[6,1,512]{2,1,0:T(1,128)} %get-tuple-element.231.inverse, ...), custom_call_target="tpu_custom_call" | custom-call | flops 3221225 | bytes 6000 | tf_op jit(solution)/shard_map/attend_back_theirs/pallas_call | solution.py:452
  162.3 1.0 fusion.6
  163.3 1.3 collective-permute-start.37
  164.6 0.9 fusion.10
  166.1 6.9 %weight_grad.1 = (bf16[8,48,1280]{2,1,0:T(8,128)(2,1)}, bf16[8,48,1280]{2,1,0:T(8,128)(2,1)}) custom-call(s32[7]{0:T(128)} %concatenate.11.place, bf16[8,48,1024]{2,1,0:T(8,128)(2,1)} %get-tuple-element.247.mine, bf16[8,48,1024]{2,1,0:T(8,128)(2,1)} %get-tuple-element.248.other, bf16[6,208,1024]{2,1,0:T(8,128)(2,1)} %attend_back_theirs.1.whole.refs_10_), custom_call_target="tpu_custom_call" | custom-call | flops 1811939 | bytes 6000 | tf_op jit(solution)/shard_map/weight_grad/pallas_call | solution.py:720
  173.7 1.1 collective-permute-done.36
  174.9 1.2 hand_on.1.place
  176.1 2.1 fusion.4
  178.3 1.0 fusion.1
  179.2 1.5 collective-permute-start.40
  180.8 1.5 collective-permute-start.42
  182.3 1.1 fusion.3
  183.4 1.2 fusion
  184.5 0.8 fusion.7
  185.9 6.3 %project_back.1 = (bf16[512,768]{1,0:T(8,128)(2,1)}, bf16[512,768]{1,0:T(8,128)(2,1)}) custom-call(s32[7]{0:T(128)} %hand_on.1.place, bf16[48,1280]{1,0:T(8,128)(2,1)} %narrow_shard.1.refs_0_, bf16[48,1280]{1,0:T(8,128)(2,1)} %copy-done.9, bf16[48,1280]{1,0:T(8,128)(2,1)} %copy-done.13, bf16[48,1280]{1,0:T(8,128)(2,1)} %copy-done.8, ...), custom_call_target="tpu_custom_call" | custom-call | flops 1811939 | bytes 10000 | tf_op jit(solution)/shard_map/project_back/pallas_call | solution.py:751
  192.2 1.6 collective-permute-start.46
  194.7 1.7 collective-permute-start.43
  196.4 1.0 fusion.17
  197.4 1.5 collective-permute-start.44
  198.9 1.2 fusion.5
  200.7 6.2 %collective-permute-done.43 = bf16[2,2,48,768]{3,2,1,0:T(8,128)(2,1)S(1)} collective-permute-done((bf16[2,2,48,768]{3,2,1,0:T(8,128)(2,1)S(1)}, bf16[2,2,48,768]{3,2,1,0:T(8,128)(2,1)S(1)}, u32[]{:S(2)}, u32[]{:S(2)}) %collective-permute-start.43) | collective-permute-done | bytes 294944 | tf_op jit(solution)/shard_map/ppermute | solution.py:886
  206.9 0.9 collective-permute-start.47
  208.0 1.0 fusion.9.b_near
  209.0 1.1 fusion.16
  210.1 2.0 collective-permute-start.48
  212.1 1.3 collective-permute-start.49
  213.4 0.9 copy-done.24
  214.3 3.8 %input_grad.1 = bf16[512,768]{1,0:T(8,128)(2,1)} custom-call(s32[7]{0:T(128)} %hand_on.1.place, bf16[512,768]{1,0:T(8,128)(2,1)} %bitcast.109, f32[8,768]{1,0:T(8,128)} %get-tuple-element.203.small, bf16[512,768]{1,0:T(8,128)(2,1)} %get-tuple-element.269.near, bf16[512,768]{1,0:T(8,128)(2,1)} %copy-done.24, f32[512,768]{1,0:T(8,128)} %get-tuple-element.297.middle_grad), custom_call_target="tpu_custom_call" | custom-call | flops 7864 | bytes 6000 | tf_op jit(solution)/shard_map/input_grad/pallas_call | solution.py:873
  219.2 1.3 collective-permute-start.50
  220.5 1.0 fusion.15.g_near
  221.5 0.8 collective-permute-start.51
  222.4 2.1 finish_wide.1
  224.5 2.1 collective-permute-done.51.g_far
  226.6 2.4 %finish.1 = (f32[192,768]{1,0:T(8,128)}, f32[48,768]{1,0:T(8,128)}, f32[48,768]{1,0:T(8,128)}, f32[48,768]{1,0:T(8,128)}, f32[1,48]{1,0:T(1,128)}, /*index=5*/f32[2,12]{1,0:T(2,128)}) custom-call(s32[7]{0:T(128)} %hand_on.1.place, bf16[2,48,768]{2,1,0:T(8,128)(2,1)} %fusion.12.a_near, bf16[2,48,768]{2,1,0:T(8,128)(2,1)} %collective-permute-done.50.a_far, ...), custom_call_target="tpu_custom_call" | custom-call | flops 1 | bytes 1000 | tf_op jit(solution)/shard_map/finish/pallas_call | solution.py:817
  (177 shorter events, 16.8 us)
Async XLA Ops:
  0.6 14.9 %collective-permute-start.3 = (bf16[512,768]{1,0:T(8,128)(2,1)}, bf16[512,768]{1,0:T(8,128)(2,1)S(1)}, u32[]{:S(2)}, u32[]{:S(2)}) collective-permute-start(bf16[512,768]{1,0:T(8,128)(2,1)} %bitcast.111), channel_id=1, source_target_pairs={{0,2},{2,0},{4,6},{6,4},{8,10},{10,8},{12,14},{14,12},{16,18},{18,... | collective-permute-start | bytes 2359304 | tf_op jit(solution)/shard_map/ppermute | solution.py:886
  1.2 22.4 %collective-permute-start.6 = (bf16[512,768]{1,0:T(8,128)(2,1)}, bf16[512,768]{1,0:T(8,128)(2,1)S(1)}, u32[]{:S(2)}, u32[]{:S(2)}) collective-permute-start(bf16[512,768]{1,0:T(8,128)(2,1)} %bitcast.106), channel_id=1, source_target_pairs={{0,1},{1,0},{2,3},{3,2},{4,5},{5,4},{6,7},{7,6},{8,9},{9,8},{10,11... | collective-permute-start | bytes 2359304 | tf_op jit(solution)/shard_map/ppermute | solution.py:886
  6.1 34.1 %copy-start.7 = (bf16[48,1280]{1,0:T(8,128)(2,1)S(1)}, bf16[48,1280]{1,0:T(8,128)(2,1)}, u32[]{:S(2)}) copy-start(bf16[48,1280]{1,0:T(8,128)(2,1)} %narrow_shard.1.refs_0_) | copy-start | bytes 368644
  6.1 9.3 %collective-permute-start = (bf16[48,1280]{1,0:T(8,128)(2,1)}, bf16[48,1280]{1,0:T(8,128)(2,1)S(1)}, u32[]{:S(2)}, u32[]{:S(2)}) collective-permute-start(bf16[48,1280]{1,0:T(8,128)(2,1)} %narrow_shard.1.refs_0_), channel_id=1, source_target_pairs={{0,16},{2,18},{4,20},{6,22},{8,24},{10,26},{12,28},{14,30},{16,0},... | collective-permute-start | bytes 368648 | tf_op jit(solution)/shard_map/ppermute | solution.py:886
  8.7 6.8 %collective-permute-start.1 = (bf16[48,1280]{1,0:T(8,128)(2,1)}, bf16[48,1280]{1,0:T(8,128)(2,1)S(1)}, u32[]{:S(2)}, u32[]{:S(2)}) collective-permute-start(bf16[48,1280]{1,0:T(8,128)(2,1)} %narrow_shard.1.refs_0_), channel_id=1, source_target_pairs={{0,8},{2,10},{4,12},{6,14},{8,0},{10,2},{12,4},{14,6},{16,24},{18,... | collective-permute-start | bytes 368648 | tf_op jit(solution)/shard_map/ppermute | solution.py:886
  10.3 5.3 %collective-permute-start.2 = (bf16[48,1280]{1,0:T(8,128)(2,1)}, bf16[48,1280]{1,0:T(8,128)(2,1)S(1)}, u32[]{:S(2)}, u32[]{:S(2)}) collective-permute-start(bf16[48,1280]{1,0:T(8,128)(2,1)} %narrow_shard.1.refs_0_), channel_id=1, source_target_pairs={{0,4},{2,6},{4,0},{6,2},{8,12},{10,14},{12,8},{14,10},{16,20},{18,... | collective-permute-start | bytes 368648 | tf_op jit(solution)/shard_map/ppermute | solution.py:886
  15.4 34.0 %copy-start.8 = (bf16[48,1280]{1,0:T(8,128)(2,1)}, bf16[48,1280]{1,0:T(8,128)(2,1)S(1)}, u32[]{:S(2)}) copy-start(bf16[48,1280]{1,0:T(8,128)(2,1)S(1)} %collective-permute-done.refs_3_) | copy-start | bytes 368644
  15.5 33.8 %copy-start.13 = (bf16[48,1280]{1,0:T(8,128)(2,1)}, bf16[48,1280]{1,0:T(8,128)(2,1)S(1)}, u32[]{:S(2)}) copy-start(bf16[48,1280]{1,0:T(8,128)(2,1)S(1)} %collective-permute-done.1.refs_2_) | copy-start | bytes 368644
  15.5 33.9 %copy-start.9 = (bf16[48,1280]{1,0:T(8,128)(2,1)}, bf16[48,1280]{1,0:T(8,128)(2,1)S(1)}, u32[]{:S(2)}) copy-start(bf16[48,1280]{1,0:T(8,128)(2,1)S(1)} %collective-permute-done.2.refs_1_) | copy-start | bytes 368644
  15.5 24.8 %copy-start.23 = (bf16[512,768]{1,0:T(8,128)(2,1)}, bf16[512,768]{1,0:T(8,128)(2,1)S(1)}, u32[]{:S(2)}) copy-start(bf16[512,768]{1,0:T(8,128)(2,1)S(1)} %collective-permute-done.3.cot_far) | copy-start | bytes 2359300
  15.6 8.5 %collective-permute-start.4 = (bf16[2,48,1280]{2,1,0:T(8,128)(2,1)S(1)}, bf16[2,48,1280]{2,1,0:T(8,128)(2,1)S(1)}, u32[]{:S(2)}, u32[]{:S(2)}) collective-permute-start(bf16[2,48,1280]{2,1,0:T(8,128)(2,1)S(1)} %pad_maximum_fusion.7), channel_id=1, source_target_pairs={{0,8},{2,10},{4,12},{6,14},{8,0},{10,2},{12,4},{14,6},{16,24},{18,... | collective-permute-start | bytes 737288 | tf_op jit(solution)/shard_map/ppermute | solution.py:886
  17.1 7.0 %collective-permute-start.5 = (bf16[48,1280]{1,0:T(8,128)(2,1)S(1)}, bf16[48,1280]{1,0:T(8,128)(2,1)S(1)}, u32[]{:S(2)}, u32[]{:S(2)}) collective-permute-start(bf16[48,1280]{1,0:T(8,128)(2,1)S(1)} %collective-permute-done.refs_3_), channel_id=1, source_target_pairs={{0,4},{2,6},{4,0},{6,2},{8,12},{10,14},{12,8},{14,10},{16,20},{18,... | collective-permute-start | bytes 368648 | tf_op jit(solution)/shard_map/ppermute | solution.py:886
  21.1 23.7 %collective-permute-start.7 = (bf16[7,48,768]{2,1,0:T(8,128)(2,1)}, bf16[7,48,768]{2,1,0:T(8,128)(2,1)S(1)}, u32[]{:S(2)}, u32[]{:S(2)}) collective-permute-start(bf16[7,48,768]{2,1,0:T(8,128)(2,1)} %get-tuple-element.171), channel_id=1, source_target_pairs={{0,8},{2,10},{4,12},{6,14},{8,0},{10,2},{12,4},{14,6},{16,24},{18,... | collective-permute-start | bytes 1548296 | tf_op jit(solution)/shard_map/ppermute | solution.py:886
  21.7 23.1 %collective-permute-start.8 = (bf16[7,48,768]{2,1,0:T(8,128)(2,1)}, bf16[7,48,768]{2,1,0:T(8,128)(2,1)S(1)}, u32[]{:S(2)}, u32[]{:S(2)}) collective-permute-start(bf16[7,48,768]{2,1,0:T(8,128)(2,1)} %get-tuple-element.171), channel_id=1, source_target_pairs={{0,16},{2,18},{4,20},{6,22},{8,24},{10,26},{12,28},{14,30},{16,0},... | collective-permute-start | bytes 1548296 | tf_op jit(solution)/shard_map/ppermute | solution.py:886
  23.6 16.7 %copy-start.26 = (bf16[512,768]{1,0:T(8,128)(2,1)}, bf16[512,768]{1,0:T(8,128)(2,1)S(1)}, u32[]{:S(2)}) copy-start(bf16[512,768]{1,0:T(8,128)(2,1)S(1)} %collective-permute-done.6.x_far) | copy-start | bytes 2359300
  23.6 21.3 %collective-permute-start.9 = (bf16[7,48,768]{2,1,0:T(8,128)(2,1)}, bf16[7,48,768]{2,1,0:T(8,128)(2,1)S(1)}, u32[]{:S(2)}, u32[]{:S(2)}) collective-permute-start(bf16[7,48,768]{2,1,0:T(8,128)(2,1)} %get-tuple-element.171), channel_id=1, source_target_pairs={{0,4},{2,6},{4,0},{6,2},{8,12},{10,14},{12,8},{14,10},{16,20},{18,... | collective-permute-start | bytes 1548296 | tf_op jit(solution)/shard_map/ppermute | solution.py:886
  24.1 25.4 %copy-start.14 = (bf16[48,1280]{1,0:T(8,128)(2,1)}, bf16[48,1280]{1,0:T(8,128)(2,1)S(1)}, u32[]{:S(2)}) copy-start(bf16[48,1280]{1,0:T(8,128)(2,1)S(1)} %collective-permute-done.5.refs_5_) | copy-start | bytes 368644
  24.1 25.4 %copy-start.1 = (bf16[2,48,1280]{2,1,0:T(8,128)(2,1)}, bf16[2,48,1280]{2,1,0:T(8,128)(2,1)S(1)}, u32[]{:S(2)}) copy-start(bf16[2,48,1280]{2,1,0:T(8,128)(2,1)S(1)} %collective-permute-done.4.refs_4_) | copy-start | bytes 737284
  24.2 20.7 %collective-permute-start.12 = (bf16[3,48,1280]{2,1,0:T(8,128)(2,1)S(1)}, bf16[3,48,1280]{2,1,0:T(8,128)(2,1)S(1)}, u32[]{:S(2)}, u32[]{:S(2)}) collective-permute-start(bf16[3,48,1280]{2,1,0:T(8,128)(2,1)S(1)} %pad_maximum_fusion.5), channel_id=1, source_target_pairs={{0,2},{2,0},{4,6},{6,4},{8,10},{10,8},{12,14},{14,12},{16,18},{18,... | collective-permute-start | bytes 1105928 | tf_op jit(solution)/shard_map/ppermute | solution.py:886
  24.3 16.0 %collective-permute-start.10 = (bf16[48,1280]{1,0:T(8,128)(2,1)S(1)}, bf16[48,1280]{1,0:T(8,128)(2,1)S(1)}, u32[]{:S(2)}, u32[]{:S(2)}) collective-permute-start(bf16[48,1280]{1,0:T(8,128)(2,1)S(1)} %slice_bitcast_fusion.6), channel_id=1, source_target_pairs={{0,4},{2,6},{4,0},{6,2},{8,12},{10,14},{12,8},{14,10},{16,20},{18,... | collective-permute-start | bytes 368648 | tf_op jit(solution)/shard_map/ppermute | solution.py:886
  40.2 1.3 collective-permute-start.11
  41.6 8.8 %collective-permute-start.13 = (bf16[4,48,1280]{2,1,0:T(8,128)(2,1)S(1)}, bf16[4,48,1280]{2,1,0:T(8,128)(2,1)S(1)}, u32[]{:S(2)}, u32[]{:S(2)}) collective-permute-start(bf16[4,48,1280]{2,1,0:T(8,128)(2,1)S(1)} %pad_maximum_fusion.3), channel_id=1, source_target_pairs={{0,2},{2,0},{4,6},{6,4},{8,10},{10,8},{12,14},{14,12},{16,18},{18,... | collective-permute-start | bytes 1474568 | tf_op jit(solution)/shard_map/ppermute | solution.py:886
  44.9 18.1 %copy-start = (bf16[7,48,768]{2,1,0:T(8,128)(2,1)}, bf16[7,48,768]{2,1,0:T(8,128)(2,1)S(1)}, u32[]{:S(2)}) copy-start(bf16[7,48,768]{2,1,0:T(8,128)(2,1)S(1)} %collective-permute-done.9.refs_1_) | copy-start | bytes 1548292
  44.9 15.6 %collective-permute-start.14 = (bf16[7,48,768]{2,1,0:T(8,128)(2,1)S(1)}, bf16[7,48,768]{2,1,0:T(8,128)(2,1)S(1)}, u32[]{:S(2)}, u32[]{:S(2)}) collective-permute-start(bf16[7,48,768]{2,1,0:T(8,128)(2,1)S(1)} %collective-permute-done.8.refs_3_), channel_id=1, source_target_pairs={{0,8},{2,10},{4,12},{6,14},{8,0},{10,2},{12,4},{14,6},{16,24},{18,... | collective-permute-start | bytes 1548296 | tf_op jit(solution)/shard_map/ppermute | solution.py:886
  48.0 12.5 %collective-permute-start.15 = (bf16[7,48,768]{2,1,0:T(8,128)(2,1)S(1)}, bf16[7,48,768]{2,1,0:T(8,128)(2,1)S(1)}, u32[]{:S(2)}, u32[]{:S(2)}) collective-permute-start(bf16[7,48,768]{2,1,0:T(8,128)(2,1)S(1)} %collective-permute-done.8.refs_3_), channel_id=1, source_target_pairs={{0,4},{2,6},{4,0},{6,2},{8,12},{10,14},{12,8},{14,10},{16,20},{18,... | collective-permute-start | bytes 1548296 | tf_op jit(solution)/shard_map/ppermute | solution.py:886
  49.5 11.0 %collective-permute-start.16 = (bf16[3,2,48,768]{3,2,1,0:T(8,128)(2,1)S(1)}, bf16[3,2,48,768]{3,2,1,0:T(8,128)(2,1)S(1)}, u32[]{:S(2)}, u32[]{:S(2)}) collective-permute-start(bf16[3,2,48,768]{3,2,1,0:T(8,128)(2,1)S(1)} %pad_maximum_fusion.4), channel_id=1, source_target_pairs={{0,1},{1,0},{2,3},{3,2},{4,5},{5,4},{6,7},{7,6},{8,9},{9,8},{10,11... | collective-permute-start | bytes 1327112 | tf_op jit(solution)/shard_map/ppermute | solution.py:886
  50.3 24.6 %collective-permute-start.20 = (bf16[3,7,48,768]{3,2,1,0:T(8,128)(2,1)S(1)}, bf16[3,7,48,768]{3,2,1,0:T(8,128)(2,1)S(1)}, u32[]{:S(2)}, u32[]{:S(2)}) collective-permute-start(bf16[3,7,48,768]{3,2,1,0:T(8,128)(2,1)S(1)} %pad_maximum_fusion), channel_id=1, source_target_pairs={{0,2},{2,0},{4,6},{6,4},{8,10},{10,8},{12,14},{14,12},{16,18},{18,... | collective-permute-start | bytes 4644872 | tf_op jit(solution)/shard_map/ppermute | solution.py:886
  50.4 13.5 %collective-permute-start.19 = (bf16[9,48,768]{2,1,0:T(8,128)(2,1)}, bf16[9,48,768]{2,1,0:T(8,128)(2,1)}, u32[]{:S(2)}, u32[]{:S(2)}) collective-permute-start(bf16[9,48,768]{2,1,0:T(8,128)(2,1)} %get-tuple-element.193.refs_0_), channel_id=1, source_target_pairs={{0,2},{2,0},{4,6},{6,4},{8,10},{10,8},{12,14},{14,12},{16,18},{18,... | collective-permute-start | bytes 1990664 | tf_op jit(solution)/shard_map/ppermute | solution.py:886
  60.4 29.4 %copy-start.25 = (bf16[3,2,48,768]{3,2,1,0:T(8,128)(2,1)}, bf16[3,2,48,768]{3,2,1,0:T(8,128)(2,1)S(1)}, u32[]{:S(2)}) copy-start(bf16[3,2,48,768]{3,2,1,0:T(8,128)(2,1)S(1)} %collective-permute-done.16.refs_8_) | copy-start | bytes 1327108
  60.5 14.4 %collective-permute-start.17 = (bf16[7,48,768]{2,1,0:T(8,128)(2,1)S(1)}, bf16[7,48,768]{2,1,0:T(8,128)(2,1)S(1)}, u32[]{:S(2)}, u32[]{:S(2)}) collective-permute-start(bf16[7,48,768]{2,1,0:T(8,128)(2,1)S(1)} %collective-permute-done.14.refs_4_), channel_id=1, source_target_pairs={{0,4},{2,6},{4,0},{6,2},{8,12},{10,14},{12,8},{14,10},{16,20},{18,... | collective-permute-start | bytes 1548296 | tf_op jit(solution)/shard_map/ppermute | solution.py:886
  62.2 25.3 %collective-permute-start.24 = (bf16[2,7,48,768]{3,2,1,0:T(8,128)(2,1)S(1)}, bf16[2,7,48,768]{3,2,1,0:T(8,128)(2,1)S(1)}, u32[]{:S(2)}, u32[]{:S(2)}) collective-permute-start(bf16[2,7,48,768]{3,2,1,0:T(8,128)(2,1)S(1)} %pad_maximum_fusion.1), channel_id=1, source_target_pairs={{0,2},{2,0},{4,6},{6,4},{8,10},{10,8},{12,14},{14,12},{16,18},{18,... | collective-permute-start | bytes 3096584 | tf_op jit(solution)/shard_map/ppermute | solution.py:886
  62.4 12.5 %collective-permute-start.18 = (bf16[2,2,48,768]{3,2,1,0:T(8,128)(2,1)S(1)}, bf16[2,2,48,768]{3,2,1,0:T(8,128)(2,1)S(1)}, u32[]{:S(2)}, u32[]{:S(2)}) collective-permute-start(bf16[2,2,48,768]{3,2,1,0:T(8,128)(2,1)S(1)} %pad_maximum_fusion.6), channel_id=1, source_target_pairs={{0,1},{1,0},{2,3},{3,2},{4,5},{5,4},{6,7},{7,6},{8,9},{9,8},{10,11... | collective-permute-start | bytes 884744 | tf_op jit(solution)/shard_map/ppermute | solution.py:886
  63.9 23.6 %collective-permute-start.21 = (bf16[9,48,768]{2,1,0:T(8,128)(2,1)}, bf16[9,48,768]{2,1,0:T(8,128)(2,1)}, u32[]{:S(2)}, u32[]{:S(2)}) collective-permute-start(bf16[9,48,768]{2,1,0:T(8,128)(2,1)} %pad_maximum_fusion.2), channel_id=1, source_target_pairs={{0,8},{2,10},{4,12},{6,14},{8,0},{10,2},{12,4},{14,6},{16,24},{18,... | collective-permute-start | bytes 1990664 | tf_op jit(solution)/shard_map/ppermute | solution.py:886
  74.8 15.1 %copy-start.40 = (bf16[2,2,48,768]{3,2,1,0:T(8,128)(2,1)}, bf16[2,2,48,768]{3,2,1,0:T(8,128)(2,1)S(1)}, u32[]{:S(2)}) copy-start(bf16[2,2,48,768]{3,2,1,0:T(8,128)(2,1)S(1)} %collective-permute-done.18.refs_9_) | copy-start | bytes 884740
  74.9 14.4 %collective-permute-start.22 = (bf16[384,512]{1,0:T(8,128)(2,1)}, bf16[384,512]{1,0:T(8,128)(2,1)S(1)}, u32[]{:S(2)}, u32[]{:S(2)}) collective-permute-start(bf16[384,512]{1,0:T(8,128)(2,1)} %get-tuple-element.198.out), channel_id=1, source_target_pairs={{0,1},{1,0},{2,3},{3,2},{4,5},{5,4},{6,7},{7,6},{8,9},{9,8},{10,11... | collective-permute-start | bytes 1179656 | tf_op jit(solution)/shard_map/ppermute | solution.py:886
  76.5 12.8 %collective-permute-start.23 = (bf16[2,48,768]{2,1,0:T(8,128)(2,1)S(1)}, bf16[2,48,768]{2,1,0:T(8,128)(2,1)S(1)}, u32[]{:S(2)}, u32[]{:S(2)}) collective-permute-start(bf16[2,48,768]{2,1,0:T(8,128)(2,1)S(1)} %slice.34), channel_id=1, source_target_pairs={{0,1},{1,0},{2,3},{3,2},{4,5},{5,4},{6,7},{7,6},{8,9},{9,8},{10,11... | collective-permute-start | bytes 442376 | tf_op jit(solution)/shard_map/ppermute | solution.py:886
  89.3 4.2 %collective-permute-start.25 = (bf16[9,48,768]{2,1,0:T(8,128)(2,1)}, bf16[9,48,768]{2,1,0:T(8,128)(2,1)S(1)}, u32[]{:S(2)}, u32[]{:S(2)}) collective-permute-start(bf16[9,48,768]{2,1,0:T(8,128)(2,1)} %collective-permute-done.21.refs_6_), channel_id=1, source_target_pairs={{0,2},{2,0},{4,6},{6,4},{8,10},{10,8},{12,14},{14,12},{16,18},{18,... | collective-permute-start | bytes 1990664 | tf_op jit(solution)/shard_map/ppermute | solution.py:886
  89.4 4.1 %collective-permute-start.26 = (bf16[7,48,768]{2,1,0:T(8,128)(2,1)S(1)}, bf16[7,48,768]{2,1,0:T(8,128)(2,1)S(1)}, u32[]{:S(2)}, u32[]{:S(2)}) collective-permute-start(bf16[7,48,768]{2,1,0:T(8,128)(2,1)S(1)} %collective-permute-done.17.refs_7_), channel_id=1, source_target_pairs={{0,2},{2,0},{4,6},{6,4},{8,10},{10,8},{12,14},{14,12},{16,18},{18,... | collective-permute-start | bytes 1548296 | tf_op jit(solution)/shard_map/ppermute | solution.py:886
  89.9 3.6 %collective-permute-start.27 = (bf16[3,2,48,768]{3,2,1,0:T(8,128)(2,1)S(1)}, bf16[3,2,48,768]{3,2,1,0:T(8,128)(2,1)S(1)}, u32[]{:S(2)}, u32[]{:S(2)}) collective-permute-start(bf16[3,2,48,768]{3,2,1,0:T(8,128)(2,1)S(1)} %collective-permute-done.16.refs_8_), channel_id=1, source_target_pairs={{0,2},{2,0},{4,6},{6,4},{8,10},{10,8},{12,14},{14,12},{16,18},{18,... | collective-permute-start | bytes 1327112 | tf_op jit(solution)/shard_map/ppermute | solution.py:886
  90.0 3.5 %collective-permute-start.28 = (bf16[2,2,48,768]{3,2,1,0:T(8,128)(2,1)S(1)}, bf16[2,2,48,768]{3,2,1,0:T(8,128)(2,1)S(1)}, u32[]{:S(2)}, u32[]{:S(2)}) collective-permute-start(bf16[2,2,48,768]{3,2,1,0:T(8,128)(2,1)S(1)} %collective-permute-done.18.refs_9_), channel_id=1, source_target_pairs={{0,2},{2,0},{4,6},{6,4},{8,10},{10,8},{12,14},{14,12},{16,18},{18,... | collective-permute-start | bytes 884744 | tf_op jit(solution)/shard_map/ppermute | solution.py:886
  90.4 3.1 %collective-permute-start.29 = (bf16[2,48,768]{2,1,0:T(8,128)(2,1)S(1)}, bf16[2,48,768]{2,1,0:T(8,128)(2,1)S(1)}, u32[]{:S(2)}, u32[]{:S(2)}) collective-permute-start(bf16[2,48,768]{2,1,0:T(8,128)(2,1)S(1)} %collective-permute-done.23.refs_10_), channel_id=1, source_target_pairs={{0,2},{2,0},{4,6},{6,4},{8,10},{10,8},{12,14},{14,12},{16,18},{18,... | collective-permute-start | bytes 442376 | tf_op jit(solution)/shard_map/ppermute | solution.py:886
  117.9 13.7 %collective-permute-start.32 = (bf16[5,512,768]{2,1,0:T(8,128)(2,1)}, bf16[5,512,768]{2,1,0:T(8,128)(2,1)}, u32[]{:S(2)}, u32[]{:S(2)}) collective-permute-start(bf16[5,512,768]{2,1,0:T(8,128)(2,1)} %get-tuple-element.224.pre), channel_id=1, source_target_pairs={{0,2},{2,0},{4,6},{6,4},{8,10},{10,8},{12,14},{14,12},{16,18},{18,... | collective-permute-start | bytes 11796488 | tf_op jit(solution)/shard_map/ppermute | solution.py:886
  118.1 22.5 %collective-permute-start.33 = (bf16[4,512,384]{2,1,0:T(8,128)(2,1)}, bf16[4,512,384]{2,1,0:T(8,128)(2,1)}, u32[]{:S(2)}, u32[]{:S(2)}) collective-permute-start(bf16[4,512,384]{2,1,0:T(8,128)(2,1)} %get-tuple-element.227), channel_id=1, source_target_pairs={{0,2},{2,0},{4,6},{6,4},{8,10},{10,8},{12,14},{14,12},{16,18},{18,... | collective-permute-start | bytes 4718600 | tf_op jit(solution)/shard_map/ppermute | solution.py:886
  118.4 13.1 %collective-permute-start.31 = (bf16[2,8,48,512]{3,2,1,0:T(8,128)(2,1)}, bf16[2,8,48,512]{3,2,1,0:T(8,128)(2,1)}, u32[]{:S(2)}, u32[]{:S(2)}) collective-permute-start(bf16[2,8,48,512]{3,2,1,0:T(8,128)(2,1)} %get-tuple-element.223), channel_id=1, source_target_pairs={{0,2},{2,0},{4,6},{6,4},{8,10},{10,8},{12,14},{14,12},{16,18},{18,... | collective-permute-start | bytes 2359304 | tf_op jit(solution)/shard_map/ppermute | solution.py:886
  118.6 13.0 %collective-permute-start.30 = (bf16[384,512]{1,0:T(8,128)(2,1)}, bf16[384,512]{1,0:T(8,128)(2,1)}, u32[]{:S(2)}, u32[]{:S(2)}) collective-permute-start(bf16[384,512]{1,0:T(8,128)(2,1)} %get-tuple-element.220), channel_id=1, source_target_pairs={{0,1},{1,0},{2,3},{3,2},{4,5},{5,4},{6,7},{7,6},{8,9},{9,8},{10,11... | collective-permute-start | bytes 1179656 | tf_op jit(solution)/shard_map/ppermute | solution.py:886
  140.0 22.3 %collective-permute-start.34 = (bf16[4,3,48,768]{3,2,1,0:T(8,128)(2,1)}, bf16[4,3,48,768]{3,2,1,0:T(8,128)(2,1)S(1)}, u32[]{:S(2)}, u32[]{:S(2)}) collective-permute-start(bf16[4,3,48,768]{3,2,1,0:T(8,128)(2,1)} %get-tuple-element.225), channel_id=1, source_target_pairs={{0,4},{2,6},{4,0},{6,2},{8,12},{10,14},{12,8},{14,10},{16,20},{18,... | collective-permute-start | bytes 2654216 | tf_op jit(solution)/shard_map/ppermute | solution.py:886
  146.8 27.9 %collective-permute-start.36 = (bf16[8,2,48,768]{3,2,1,0:T(8,128)(2,1)}, bf16[8,2,48,768]{3,2,1,0:T(8,128)(2,1)S(1)}, u32[]{:S(2)}, u32[]{:S(2)}) collective-permute-start(bf16[8,2,48,768]{3,2,1,0:T(8,128)(2,1)} %get-tuple-element.229), channel_id=1, source_target_pairs={{0,1},{1,0},{2,3},{3,2},{4,5},{5,4},{6,7},{7,6},{8,9},{9,8},{10,11... | collective-permute-start | bytes 3538952 | tf_op jit(solution)/shard_map/ppermute | solution.py:886
  147.4 17.2 %collective-permute-start.35 = (bf16[2,2,2,48,768]{4,3,2,0,1:T(8,128)(2,1)S(1)}, bf16[2,2,2,48,768]{4,3,2,0,1:T(8,128)(2,1)S(1)}, u32[]{:S(2)}, u32[]{:S(2)}) collective-permute-start(bf16[2,2,2,48,768]{4,3,2,0,1:T(8,128)(2,1)S(1)} %copy.32), channel_id=1, source_target_pairs={{0,8},{2,10},{4,12},{6,14},{8,0},{10,2},{12,4},{14,6},{16,24},{18,... | collective-permute-start | bytes 1769480 | tf_op jit(solution)/shard_map/ppermute | solution.py:886
  149.1 15.4 %copy-start.29 = (bf16[2,2,2,48,768]{4,3,2,1,0:T(8,128)(2,1)S(1)}, bf16[2,2,2,48,768]{4,3,2,1,0:T(8,128)(2,1)}, u32[]{:S(2)}) copy-start(bf16[2,2,2,48,768]{4,3,2,1,0:T(8,128)(2,1)} %get-tuple-element.263) | copy-start | bytes 1769476
  163.3 11.6 %collective-permute-start.37 = (bf16[2,3,48,768]{3,2,1,0:T(8,128)(2,1)}, bf16[2,3,48,768]{3,2,1,0:T(8,128)(2,1)}, u32[]{:S(2)}, u32[]{:S(2)}) collective-permute-start(bf16[2,3,48,768]{3,2,1,0:T(8,128)(2,1)} %fusion.6), channel_id=1, source_target_pairs={{0,8},{2,10},{4,12},{6,14},{8,0},{10,2},{12,4},{14,6},{16,24},{18,... | collective-permute-start | bytes 1327112 | tf_op jit(solution)/shard_map/ppermute | solution.py:886
  165.5 8.2 %collective-permute-start.38 = (bf16[2,2,48,768]{3,2,1,0:T(8,128)(2,1)}, bf16[2,2,48,768]{3,2,1,0:T(8,128)(2,1)}, u32[]{:S(2)}, u32[]{:S(2)}) collective-permute-start(bf16[2,2,48,768]{3,2,1,0:T(8,128)(2,1)} %fusion.10), channel_id=1, source_target_pairs={{0,4},{2,6},{4,0},{6,2},{8,12},{10,14},{12,8},{14,10},{16,20},{18,... | collective-permute-start | bytes 884744 | tf_op jit(solution)/shard_map/ppermute | solution.py:886
  173.0 3.1 %collective-permute-start.39 = (bf16[8,48,1280]{2,1,0:T(8,128)(2,1)}, bf16[8,48,1280]{2,1,0:T(8,128)(2,1)}, u32[]{:S(2)}, u32[]{:S(2)}) collective-permute-start(bf16[8,48,1280]{2,1,0:T(8,128)(2,1)} %get-tuple-element.252), channel_id=1, source_target_pairs={{0,2},{2,0},{4,6},{6,4},{8,10},{10,8},{12,14},{14,12},{16,18},{18,... | collective-permute-start | bytes 2949128 | tf_op jit(solution)/shard_map/ppermute | solution.py:886
  179.2 15.4 %collective-permute-start.40 = (bf16[2,2,2,48,768]{4,3,2,1,0:T(8,128)(2,1)}, bf16[2,2,2,48,768]{4,3,2,1,0:T(8,128)(2,1)S(1)}, u32[]{:S(2)}, u32[]{:S(2)}) collective-permute-start(bf16[2,2,2,48,768]{4,3,2,1,0:T(8,128)(2,1)} %fusion.1), channel_id=1, source_target_pairs={{0,4},{2,6},{4,0},{6,2},{8,12},{10,14},{12,8},{14,10},{16,20},{18,... | collective-permute-start | bytes 1769480 | tf_op jit(solution)/shard_map/ppermute | solution.py:886
  180.8 18.1 %collective-permute-start.42 = (bf16[2,2,48,1280]{3,2,1,0:T(8,128)(2,1)}, bf16[2,2,48,1280]{3,2,1,0:T(8,128)(2,1)}, u32[]{:S(2)}, u32[]{:S(2)}) collective-permute-start(bf16[2,2,48,1280]{3,2,1,0:T(8,128)(2,1)} %fusion.4), channel_id=1, source_target_pairs={{0,8},{2,10},{4,12},{6,14},{8,0},{10,2},{12,4},{14,6},{16,24},{18,... | collective-permute-start | bytes 1474568 | tf_op jit(solution)/shard_map/ppermute | solution.py:886
  185.4 11.0 %collective-permute-start.41 = (bf16[2,5,48,384]{3,2,1,0:T(8,128)(2,1)}, bf16[2,5,48,384]{3,2,1,0:T(8,128)(2,1)}, u32[]{:S(2)}, u32[]{:S(2)}) collective-permute-start(bf16[2,5,48,384]{3,2,1,0:T(8,128)(2,1)} %get-tuple-element.266), channel_id=1, source_target_pairs={{0,1},{1,0},{2,3},{3,2},{4,5},{5,4},{6,7},{7,6},{8,9},{9,8},{10,11... | collective-permute-start | bytes 1105928 | tf_op jit(solution)/shard_map/ppermute | solution.py:886
  192.2 21.2 %collective-permute-start.46 = (bf16[512,768]{1,0:T(8,128)(2,1)}, bf16[512,768]{1,0:T(8,128)(2,1)S(1)}, u32[]{:S(2)}, u32[]{:S(2)}) collective-permute-start(bf16[512,768]{1,0:T(8,128)(2,1)} %get-tuple-element.296), channel_id=1, source_target_pairs={{0,1},{1,0},{2,3},{3,2},{4,5},{5,4},{6,7},{7,6},{8,9},{9,8},{10,11... | collective-permute-start | bytes 2359304 | tf_op jit(solution)/shard_map/ppermute | solution.py:886
  194.7 12.1 %collective-permute-start.43 = (bf16[2,2,48,768]{3,2,1,0:T(8,128)(2,1)S(1)}, bf16[2,2,48,768]{3,2,1,0:T(8,128)(2,1)S(1)}, u32[]{:S(2)}, u32[]{:S(2)}) collective-permute-start(bf16[2,2,48,768]{3,2,1,0:T(8,128)(2,1)S(1)} %fusion.2), channel_id=1, source_target_pairs={{0,8},{2,10},{4,12},{6,14},{8,0},{10,2},{12,4},{14,6},{16,24},{18,... | collective-permute-start | bytes 884744 | tf_op jit(solution)/shard_map/ppermute | solution.py:886
  197.4 10.6 %collective-permute-start.44 = (bf16[5,48,384]{2,1,0:T(8,128)(2,1)S(1)}, bf16[5,48,384]{2,1,0:T(8,128)(2,1)S(1)}, u32[]{:S(2)}, u32[]{:S(2)}) collective-permute-start(bf16[5,48,384]{2,1,0:T(8,128)(2,1)S(1)} %fusion.17), channel_id=1, source_target_pairs={{0,16},{2,18},{4,20},{6,22},{8,24},{10,26},{12,28},{14,30},{16,0},... | collective-permute-start | bytes 552968 | tf_op jit(solution)/shard_map/ppermute | solution.py:886
  200.1 9.0 %collective-permute-start.45 = (bf16[2,48,1280]{2,1,0:T(8,128)(2,1)S(1)}, bf16[2,48,1280]{2,1,0:T(8,128)(2,1)S(1)}, u32[]{:S(2)}, u32[]{:S(2)}) collective-permute-start(bf16[2,48,1280]{2,1,0:T(8,128)(2,1)S(1)} %fusion.5), channel_id=1, source_target_pairs={{0,4},{2,6},{4,0},{6,2},{8,12},{10,14},{12,8},{14,10},{16,20},{18,... | collective-permute-start | bytes 737288 | tf_op jit(solution)/shard_map/ppermute | solution.py:886
  206.9 11.6 %collective-permute-start.47 = (bf16[2,48,768]{2,1,0:T(8,128)(2,1)S(1)}, bf16[2,48,768]{2,1,0:T(8,128)(2,1)S(1)}, u32[]{:S(2)}, u32[]{:S(2)}) collective-permute-start(bf16[2,48,768]{2,1,0:T(8,128)(2,1)S(1)} %fusion.13), channel_id=1, source_target_pairs={{0,16},{2,18},{4,20},{6,22},{8,24},{10,26},{12,28},{14,30},{16,0},... | collective-permute-start | bytes 442376 | tf_op jit(solution)/shard_map/ppermute | solution.py:886
  210.1 10.4 %collective-permute-start.48 = (bf16[48,1280]{1,0:T(8,128)(2,1)S(1)}, bf16[48,1280]{1,0:T(8,128)(2,1)S(1)}, u32[]{:S(2)}, u32[]{:S(2)}) collective-permute-start(bf16[48,1280]{1,0:T(8,128)(2,1)S(1)} %fusion.16), channel_id=1, source_target_pairs={{0,16},{2,18},{4,20},{6,22},{8,24},{10,26},{12,28},{14,30},{16,0},... | collective-permute-start | bytes 368648 | tf_op jit(solution)/shard_map/ppermute | solution.py:886
  212.1 10.3 %collective-permute-start.49 = (bf16[5,48,384]{2,1,0:T(8,128)(2,1)S(1)}, bf16[5,48,384]{2,1,0:T(8,128)(2,1)}, u32[]{:S(2)}, u32[]{:S(2)}) collective-permute-start(bf16[5,48,384]{2,1,0:T(8,128)(2,1)S(1)} %fusion.9.b_near), channel_id=1, source_target_pairs={{0,1},{1,0},{2,3},{3,2},{4,5},{5,4},{6,7},{7,6},{8,9},{9,8},{10,11... | collective-permute-start | bytes 552968 | tf_op jit(solution)/shard_map/ppermute | solution.py:886
  219.2 7.4 %collective-permute-start.50 = (bf16[2,48,768]{2,1,0:T(8,128)(2,1)}, bf16[2,48,768]{2,1,0:T(8,128)(2,1)}, u32[]{:S(2)}, u32[]{:S(2)}) collective-permute-start(bf16[2,48,768]{2,1,0:T(8,128)(2,1)} %fusion.12.a_near), channel_id=1, source_target_pairs={{0,1},{1,0},{2,3},{3,2},{4,5},{5,4},{6,7},{7,6},{8,9},{9,8},{10,11... | collective-permute-start | bytes 442376 | tf_op jit(solution)/shard_map/ppermute | solution.py:886
  221.5 5.1 %collective-permute-start.51 = (bf16[48,1280]{1,0:T(8,128)(2,1)S(1)}, bf16[48,1280]{1,0:T(8,128)(2,1)}, u32[]{:S(2)}, u32[]{:S(2)}) collective-permute-start(bf16[48,1280]{1,0:T(8,128)(2,1)S(1)} %fusion.15.g_near), channel_id=1, source_target_pairs={{0,1},{1,0},{2,3},{3,2},{4,5},{5,4},{6,7},{7,6},{8,9},{9,8},{10,11... | collective-permute-start | bytes 368648 | tf_op jit(solution)/shard_map/ppermute | solution.py:886
  (32 other events, 175.1 us)
